TPU v7x, 32 devices: a whole 2x2x4 slice. The times are simulated.
32 devices in a mesh: seq: 8 (over z, y), head: 4 (over x, core).
Axes of the slice: x: 2, y: 2, z: 4, core: 2. Of those that a mesh axis runs over, the one named last changes fastest.
Arguments:
- tokens: bfloat16 [64, 512, 1024], P('seq', 'head'), may hold values from -6 to 6
- cotangent: bfloat16 [64, 512, 1024], P('seq', 'head'), may hold values from -6 to 6
- lengths: int32 [64], replicated, may hold values from 64 to 512, as said below
- seq_order: int32 [64], replicated, may hold values from 0 to 63, as said below
- w_qkv: bfloat16 [1024, 3072], P('head'), may hold values from -0.1875 to 0.1875
- w_out: bfloat16 [1024, 1024], P('head'), may hold values from -1.5 to 1.5
- w_up: bfloat16 [1024, 4096], P('head'), may hold values from -0.1875 to 0.1875
- w_down: bfloat16 [4096, 1024], P('head'), may hold values from -0.09375 to 0.09375
- bias_q: bfloat16 [1024], P('head'), may hold values from -3 to 3
- bias_v: bfloat16 [1024], P('head'), may hold values from -3 to 3
- bias_out: bfloat16 [1024], P('head'), may hold values from -3 to 3
- bias_up: bfloat16 [4096], P('head'), may hold values from -3 to 3
- bias_down: bfloat16 [1024], P('head'), may hold values from -3 to 3
- gain_attn: bfloat16 [1024], P('head'), may hold values from 0.25 to 1.75
- shift_attn: bfloat16 [1024], P('head'), may hold values from -3 to 3
- gain_mlp: bfloat16 [1024], P('head'), may hold values from 0.25 to 1.75
- shift_mlp: bfloat16 [1024], P('head'), may hold values from -3 to 3
Outputs:
- activations: bfloat16 [64, 512, 1024], P('seq', 'head')
- input_grad: bfloat16 [64, 512, 1024], P('seq', 'head')
- grad_qkv: float32 [1024, 3072], P('head')
- grad_out: float32 [1024, 1024], P('head')
- grad_up: float32 [1024, 4096], P('head')
- grad_down: float32 [4096, 1024], P('head')
- grad_bias_q: float32 [1024], P('head')
- grad_bias_v: float32 [1024], P('head')
- grad_bias_out: float32 [1024], P('head')
- grad_bias_up: float32 [4096], P('head')
- grad_bias_down: float32 [1024], P('head')
- grad_gain_attn: float32 [1024], P('head')
- grad_shift_attn: float32 [1024], P('head')
- grad_gain_mlp: float32 [1024], P('head')
- grad_shift_mlp: float32 [1024], P('head')
Inputs may be any that keep to these rules, and one draw needn't show every extreme that they name: In the placed order each group of 8 consecutive sequences has lengths summing to 2304, one of them 512 long. `seq_order`: A permutation of the sequences. Placed slot c of a group comes from the given group o_c further along (counted round), with o_0 = 0, o_1 = 1, o_c = c * 1 for 1 < c < 7 and o_c = 7 for the last slot; the 8 sequences of one given group go to 8 different groups, one to each slot number, in an order drawn from the seed.
All inputs are finite; a program needn't handle non-finite values.
Results may differ from a plain program's by a relative error of at most 0.017.
Values may be sent and summed in bfloat16 or wider, within the bound.
No kernel may reach another device: no remote copies, remote signals or barrier semaphores. Data moves between devices by JAX's collectives and lax.ppermute only.
A program may use at most 256 MiB of HBM per device.

v0:
```python
import jax
import jax.numpy as jnp
from jax import lax
from jax.sharding import PartitionSpec as P

HEAD_SIZE = 64


def layer_norm(inputs, gain, shift):
    average = jnp.mean(inputs, axis=-1, keepdims=True)
    centered = inputs - average
    variance = jnp.mean(centered * centered, axis=-1, keepdims=True)
    return centered * lax.rsqrt(variance + 1e-12) * gain + shift


def gelu_exact(inputs):
    return jax.nn.gelu(inputs, approximate=False)


def contract_rows(left, right):
    return lax.dot_general(
        left, right, (((0,), (0,)), ((), ())), preferred_element_type=jnp.float32
    )


def contract_cols(left, right):
    return lax.dot_general(
        left, right, (((1,), (1,)), ((), ())), preferred_element_type=jnp.float32
    )


def on_device(
    tokens,
    cotangent,
    lengths,
    seq_order,
    w_qkv,
    w_out,
    w_up,
    w_down,
    bias_q,
    bias_v,
    bias_out,
    bias_up,
    bias_down,
    gain_attn,
    shift_attn,
    gain_mlp,
    shift_mlp,
):
    group_count = lax.axis_size("seq")
    shard_count = lax.axis_size("head")
    group_id = lax.axis_index("seq")
    shard_id = lax.axis_index("head")
    slot_count, span_rows, model_width = tokens.shape
    seq_len = span_rows * shard_count
    part_width = model_width // shard_count
    heads_here = part_width // HEAD_SIZE
    total_seqs = seq_order.shape[0]
    scale = HEAD_SIZE ** (-0.5)
    local_ids = group_id * slot_count + jnp.arange(slot_count, dtype=jnp.int32)
    placed_ids = jnp.take(seq_order, local_ids)
    target = placed_ids // slot_count
    matches = seq_order[None, :] == local_ids[:, None]
    anchor_ids = jnp.sum(
        jnp.where(matches, jnp.arange(total_seqs, dtype=jnp.int32)[None, :], 0), axis=1
    )
    anchor = anchor_ids // slot_count
    seq_lens = jnp.sum(jnp.where(matches, lengths[None, :], 0), axis=1)
    outgoing = jnp.zeros((group_count, span_rows, model_width), jnp.bfloat16).at[target].set(tokens)
    incoming = lax.all_to_all(outgoing, "seq", split_axis=0, concat_axis=0, tiled=True)
    placed = jnp.take(incoming, anchor, axis=0)
    (
        full_qkv,
        full_out,
        full_up,
        full_down,
        query_bias,
        value_bias,
        out_bias,
        up_bias,
        down_bias,
        attn_gain,
        attn_shift,
        mlp_gain,
        mlp_shift,
    ) = (
        lax.all_gather(w_qkv, "head", axis=0, tiled=True),
        lax.all_gather(w_out, "head", axis=0, tiled=True),
        lax.all_gather(w_up, "head", axis=0, tiled=True),
        lax.all_gather(w_down, "head", axis=0, tiled=True),
        lax.all_gather(bias_q, "head", axis=0, tiled=True),
        lax.all_gather(bias_v, "head", axis=0, tiled=True),
        lax.all_gather(bias_out, "head", axis=0, tiled=True),
        lax.all_gather(bias_up, "head", axis=0, tiled=True),
        lax.all_gather(bias_down, "head", axis=0, tiled=True),
        lax.all_gather(gain_attn, "head", axis=0, tiled=True),
        lax.all_gather(shift_attn, "head", axis=0, tiled=True),
        lax.all_gather(gain_mlp, "head", axis=0, tiled=True),
        lax.all_gather(shift_mlp, "head", axis=0, tiled=True),
    )
    query_bias = query_bias.astype(jnp.float32)
    value_bias = value_bias.astype(jnp.float32)
    out_bias = out_bias.astype(jnp.float32)
    up_bias = up_bias.astype(jnp.float32)
    down_bias = down_bias.astype(jnp.float32)
    attn_gain = attn_gain.astype(jnp.float32)
    attn_shift = attn_shift.astype(jnp.float32)
    mlp_gain = mlp_gain.astype(jnp.float32)
    mlp_shift = mlp_shift.astype(jnp.float32)
    rows_in = placed.reshape(-1, model_width)
    joint_bias = jnp.concatenate([query_bias, jnp.zeros_like(query_bias), value_bias])
    qkv_rows = (jnp.dot(rows_in, full_qkv, preferred_element_type=jnp.float32) + joint_bias).astype(
        jnp.bfloat16
    )
    spread_qkv = qkv_rows.reshape(slot_count, span_rows, 3, shard_count, part_width)
    headed = lax.all_to_all(spread_qkv, "head", split_axis=3, concat_axis=1, tiled=True)
    queries = headed[:, :, 0, 0].reshape(slot_count, seq_len, heads_here, HEAD_SIZE)
    keys_all = headed[:, :, 1, 0].reshape(slot_count, seq_len, heads_here, HEAD_SIZE)
    values_all = headed[:, :, 2, 0].reshape(slot_count, seq_len, heads_here, HEAD_SIZE)
    key_keep = jnp.arange(seq_len, dtype=jnp.int32)[None, :] < seq_lens[:, None]

    def scores_of(query_block, key_block, keep_row):
        raw = (
            jnp.einsum("qhe,khe->hqk", query_block, key_block, preferred_element_type=jnp.float32)
            * scale
        )
        return jnp.where(keep_row[None, None, :], raw, -1e30)

    def attend(packed):
        query_block, key_block, value_block, keep_row = packed
        scores = scores_of(query_block, key_block, keep_row)
        highest = jnp.max(scores, axis=-1, keepdims=True)
        expo = jnp.exp(scores - highest)
        total = jnp.sum(expo, axis=-1, keepdims=True)
        probs_low = (expo / total).astype(jnp.bfloat16)
        mixed = jnp.einsum(
            "hqk,khe->qhe", probs_low, value_block, preferred_element_type=jnp.float32
        )
        return (
            mixed.astype(jnp.bfloat16).reshape(seq_len, part_width),
            (highest + jnp.log(total))[..., 0],
        )

    context, log_total = lax.map(attend, (queries, keys_all, values_all, key_keep))
    returned_ctx = lax.all_to_all(
        context[:, :, None, :], "head", split_axis=1, concat_axis=2, tiled=True
    )
    ctx_rows = returned_ctx.reshape(-1, model_width)
    resid_attn = (
        rows_in.astype(jnp.float32)
        + jnp.dot(ctx_rows, full_out, preferred_element_type=jnp.float32)
        + out_bias
    )
    hidden = layer_norm(resid_attn, attn_gain, attn_shift)
    hidden_low = hidden.astype(jnp.bfloat16)
    pre_act = jnp.dot(hidden_low, full_up, preferred_element_type=jnp.float32) + up_bias
    act_low = gelu_exact(pre_act).astype(jnp.bfloat16)
    resid_mlp = hidden + jnp.dot(act_low, full_down, preferred_element_type=jnp.float32) + down_bias
    final = layer_norm(resid_mlp, mlp_gain, mlp_shift)
    row_keep = (shard_id * span_rows + jnp.arange(span_rows, dtype=jnp.int32))[None, :] < seq_lens[
        :, None
    ]
    keep_col = row_keep.reshape(-1, 1)
    activations = (
        jnp.where(keep_col, final, 0.0)
        .astype(jnp.bfloat16)
        .reshape(slot_count, span_rows, model_width)
    )
    grad_final = jnp.where(keep_col, cotangent.reshape(-1, model_width).astype(jnp.float32), 0.0)
    _, back_mlp_norm = jax.vjp(layer_norm, resid_mlp, mlp_gain, mlp_shift)
    grad_resid2, grad_gain_m, grad_shift_m = back_mlp_norm(grad_final)
    grad_branch = grad_resid2.astype(jnp.bfloat16)
    down_grad = contract_rows(act_low, grad_branch)
    down_bias_grad = jnp.sum(grad_branch, axis=0, dtype=jnp.float32)
    grad_act = contract_cols(grad_branch, full_down)
    _, back_gelu = jax.vjp(gelu_exact, pre_act)
    grad_pre = back_gelu(grad_act)[0].astype(jnp.bfloat16)
    up_grad = contract_rows(hidden_low, grad_pre)
    up_bias_grad = jnp.sum(grad_pre, axis=0, dtype=jnp.float32)
    grad_hidden = grad_resid2 + contract_cols(grad_pre, full_up)
    _, back_attn_norm = jax.vjp(layer_norm, resid_attn, attn_gain, attn_shift)
    grad_resid1, grad_gain_a, grad_shift_a = back_attn_norm(grad_hidden)
    grad_attn = grad_resid1.astype(jnp.bfloat16)
    out_grad = contract_rows(ctx_rows, grad_attn)
    out_bias_grad = jnp.sum(grad_attn, axis=0, dtype=jnp.float32)
    grad_context = contract_cols(grad_attn, full_out).astype(jnp.bfloat16)
    grad_headed = lax.all_to_all(
        grad_context.reshape(slot_count, span_rows, shard_count, part_width),
        "head",
        split_axis=2,
        concat_axis=1,
        tiled=True,
    )
    grad_ctx = grad_headed[:, :, 0].reshape(slot_count, seq_len, heads_here, HEAD_SIZE)

    def attend_back(packed):
        query_block, key_block, value_block, keep_row, log_row, grad_block = packed
        scores = scores_of(query_block, key_block, keep_row)
        probs = jnp.exp(scores - log_row[..., None])
        probs_low = probs.astype(jnp.bfloat16)
        grad_value = jnp.einsum(
            "hqk,qhe->khe", probs_low, grad_block, preferred_element_type=jnp.float32
        )
        grad_probs = jnp.einsum(
            "qhe,khe->hqk", grad_block, value_block, preferred_element_type=jnp.float32
        )
        inner = jnp.sum(probs * grad_probs, axis=-1, keepdims=True)
        grad_scores = (probs * (grad_probs - inner)).astype(jnp.bfloat16)
        grad_query = (
            jnp.einsum("hqk,khe->qhe", grad_scores, key_block, preferred_element_type=jnp.float32)
            * scale
        )
        grad_key = (
            jnp.einsum("hqk,qhe->khe", grad_scores, query_block, preferred_element_type=jnp.float32)
            * scale
        )
        stacked = jnp.stack([grad_query, grad_key, grad_value], axis=1).astype(jnp.bfloat16)
        return stacked.reshape(seq_len, 3, 1, part_width)

    grad_parts = lax.map(
        attend_back, (queries, keys_all, values_all, key_keep, log_total, grad_ctx)
    )
    grad_tokens = lax.all_to_all(grad_parts, "head", split_axis=1, concat_axis=3, tiled=True)
    grad_qkv_rows = grad_tokens.reshape(-1, 3 * model_width)
    qkv_grad = contract_rows(rows_in, grad_qkv_rows)
    column_sums = jnp.sum(grad_qkv_rows, axis=0, dtype=jnp.float32)
    query_bias_grad = column_sums[:model_width]
    value_bias_grad = column_sums[2 * model_width :]
    grad_input = grad_resid1 + contract_cols(grad_qkv_rows, full_qkv)
    back_rows = grad_input.astype(jnp.bfloat16).reshape(slot_count, span_rows, model_width)
    outgoing_back = (
        jnp.zeros((group_count, span_rows, model_width), jnp.bfloat16).at[anchor].set(back_rows)
    )
    returned = lax.all_to_all(outgoing_back, "seq", split_axis=0, concat_axis=0, tiled=True)
    input_grad = jnp.take(returned, target, axis=0)
    shares = (
        lax.psum_scatter(
            qkv_grad.astype(jnp.bfloat16), "head", scatter_dimension=0, tiled=True
        ).astype(jnp.float32),
        lax.psum_scatter(
            out_grad.astype(jnp.bfloat16), "head", scatter_dimension=0, tiled=True
        ).astype(jnp.float32),
        lax.psum_scatter(
            up_grad.astype(jnp.bfloat16), "head", scatter_dimension=0, tiled=True
        ).astype(jnp.float32),
        lax.psum_scatter(
            down_grad.astype(jnp.bfloat16), "head", scatter_dimension=0, tiled=True
        ).astype(jnp.float32),
        lax.psum_scatter(
            query_bias_grad.astype(jnp.bfloat16), "head", scatter_dimension=0, tiled=True
        ).astype(jnp.float32),
        lax.psum_scatter(
            value_bias_grad.astype(jnp.bfloat16), "head", scatter_dimension=0, tiled=True
        ).astype(jnp.float32),
        lax.psum_scatter(
            out_bias_grad.astype(jnp.bfloat16), "head", scatter_dimension=0, tiled=True
        ).astype(jnp.float32),
        lax.psum_scatter(
            up_bias_grad.astype(jnp.bfloat16), "head", scatter_dimension=0, tiled=True
        ).astype(jnp.float32),
        lax.psum_scatter(
            down_bias_grad.astype(jnp.bfloat16), "head", scatter_dimension=0, tiled=True
        ).astype(jnp.float32),
        lax.psum_scatter(
            grad_gain_a.astype(jnp.bfloat16), "head", scatter_dimension=0, tiled=True
        ).astype(jnp.float32),
        lax.psum_scatter(
            grad_shift_a.astype(jnp.bfloat16), "head", scatter_dimension=0, tiled=True
        ).astype(jnp.float32),
        lax.psum_scatter(
            grad_gain_m.astype(jnp.bfloat16), "head", scatter_dimension=0, tiled=True
        ).astype(jnp.float32),
        lax.psum_scatter(
            grad_shift_m.astype(jnp.bfloat16), "head", scatter_dimension=0, tiled=True
        ).astype(jnp.float32),
    )
    totals = lax.psum(
        (
            shares[0],
            shares[1],
            shares[2],
            shares[3],
            shares[4],
            shares[5],
            shares[6],
            shares[7],
            shares[8],
            shares[9],
            shares[10],
            shares[11],
            shares[12],
        ),
        "seq",
    )
    return (activations, input_grad) + tuple(totals)


def solution(mesh):
    in_specs = (
        P("seq", "head", None),
        P("seq", "head", None),
        P(),
        P(),
        P("head", None),
        P("head", None),
        P("head", None),
        P("head", None),
        P("head"),
        P("head"),
        P("head"),
        P("head"),
        P("head"),
        P("head"),
        P("head"),
        P("head"),
        P("head"),
    )
    out_specs = (
        P("seq", "head", None),
        P("seq", "head", None),
        P("head", None),
        P("head", None),
        P("head", None),
        P("head", None),
        P("head"),
        P("head"),
        P("head"),
        P("head"),
        P("head"),
        P("head"),
        P("head"),
        P("head"),
        P("head"),
    )
    return jax.shard_map(
        on_device, mesh=mesh, in_specs=in_specs, out_specs=out_specs, check_vma=False
    )
```

profile of v0, /device:TPU:0, one launch (start us, length us, event | category | flops | bytes accessed | tf_op | source)
XLA Modules:
  0.0 1370.0 jit_solution(7659194562647064785)
XLA Ops:
  10.9 5.0 scatter_fusion
  15.9 7.3 all-to-all-start
  23.2 5.1 all-gather
  28.3 5.1 all-gather.1
  34.1 37.3 %all-to-all-done = bf16[8,128,1024]{2,1,0:T(8,128)(2,1)S(1)} async-done(((bf16[8,128,1024]{2,1,0:T(8,128)(2,1)}), bf16[8,128,1024]{2,1,0:T(8,128)(2,1)S(1)}, u32[]{:S(2)}, u32[]{:S(2)}) %all-to-all-start) | async-done | bytes 2097184 | tf_op jit(solution)/shard_map/all_to_all | solution.py:71
  75.3 12.1 add_convert_fusion.1
  87.4 12.2 reshape.399
  99.5 6.7 copy.112
  106.3 5.2 all-to-all-start.1
  113.1 113.5 %all-to-all-done.1 = bf16[8,128,3,4,256]{4,1,2,0,3:T(8,128)(2,1)} async-done(((bf16[8,128,3,4,256]{4,1,2,0,3:T(8,128)(2,1)}), bf16[8,128,3,4,256]{4,1,2,0,3:T(8,128)(2,1)}, u32[]{:S(2)}, u32[]{:S(2)}) %all-to-all-start.1) | async-done | bytes 6291488 | tf_op jit(solution)/shard_map/all_to_all | solution.py:117
  226.6 3.3 copy.113
  229.9 2.4 fusion.94
  232.3 2.4 copy.114
  234.7 2.9 copy.115
  237.6 3.9 copy.116
  241.5 51.4 %while.22 = (s32[]{:T(128)}, bf16[8,512,256]{1,2,0:T(8,128)(2,1)}, f32[8,4,512]{2,1,0:T(4,128)}, bf16[8,512,4,64]{1,3,2,0:T(8,128)(2,1)}, pred[8,512]{1,0:T(8,12...) while((s32[]{:T(128)}, bf16[8,512,256]{1,2,0:T(8,128)(2,1)}, ...), condition=%wide.region_6.8_spmd, body=%wide.region_3.7_spmd.sunk | while | flops 281147392 | bytes 14226521 | solution.py:145
  292.9 4.9 copy.117
  297.9 4.6 all-to-all-start.2
  303.2 39.6 %all-gather.2 = bf16[4,1,256]{2,1,0:T(2,128)(2,1)S(1)} all-gather(bf16[1,1,256]{2,1,0:T(2,128)(2,1)S(1)} %reshape.452), channel_id=1, replica_groups=mesh['seq'=8,'head'=4] {'head'}, dimensions={0}, use_global_device_ids=true | all-gather | bytes 2560 | tf_op jit(solution)/shard_map/all_gather | solution.py:94
  342.8 5.1 all-gather.3
  347.9 5.1 all-gather.4
  353.0 5.2 all_gather.47
  358.2 5.1 all-gather.5
  363.8 5.1 all-gather.6
  369.5 5.1 all-gather.7
  375.8 4.8 copy.118
  380.6 5.1 fusion.95
  388.9 50.7 %multiply_convert_fusion.1 = (bf16[1024,4096]{1,0:T(8,128)(2,1)}, f32[1024,4096]{1,0:T(8,128)}, f32[1024,4096]{1,0:T(8,128)}) fusion(f32[4096]{0:T(1024)S(1)} %convert_element_type.178, bf16[1024,4096]{1,0:T(8,128)(2,1)} %all-gather.17.cloned.1.call-done, f32[1024,1024]{1,0:T(8,128)} %copy-done.5, f32[1024]{0:T(1024)S(1)} %bitcast.238, ...), kind=kOutput, calls=%fused_computation.66 | convolution fusion | flops 8872001536 | bytes 54558720 | tf_op jit(solution)/shard_map/dot_general | solution.py:157
  439.6 15.2 %fusion.96 = (f32[1024]{0:T(1024)S(1)}, f32[1024,1024]{1,0:T(8,128)S(1)}) fusion(f32[1024]{0:T(1024)S(1)} %bitcast.241, bf16[1024,4096]{1,0:T(8,128)(2,1)} %get-tuple-element.185, bf16[4096,1024]{1,0:T(8,128)(2,1)} %all-gather.19.cloned.1.call-done, f32[1024]{0:T(1024)S(1)} %bitcast.239, f32[1024]{0:T(1024)S(1)} %bitcast.229, f32[1024]{0:T(1024)S(1)} %fusion.79, ...), kind=kOutput, calls=%fused_computation.192 | convolution fusion | flops 8597273600 | bytes 25190400 | tf_op jit(solution)/shard_map/dot_general | solution.py:159
  456.4 2.4 multiply_reduce_fusion.1
  458.9 3.6 fusion.92
  465.5 24.0 %fusion.89 = (bf16[4096]{0:T(1024)(128)(2,1)}, bf16[1024,4096]{1,0:T(8,128)(2,1)}) fusion(f32[1024,4096]{1,0:T(8,128)} %get-tuple-element.186, f32[1024,4096]{1,0:T(8,128)} %get-tuple-element.203, f32[4096]{0:T(1024)S(1)} %convert_element_type.178, bf16[1024,1024]{1,0:T(8,128)(2,1)S(1)} %get-tuple-element.174, ...), kind=kOutput, calls=%fused_computation.186 | convolution fusion | flops 8657039360 | bytes 52453376 | tf_op jit(solution)/shard_map/dot_general | solution.py:27
  489.6 17.6 %multiply_reduce_fusion.2 = (bf16[1024]{0:T(1024)(128)(2,1)}, f32[1024]{0:T(1024)S(1)}, bf16[1024]{0:T(1024)(128)(2,1)}, f32[1024,1024]{1,0:T(8,128)S(1)}) fusion(f32[1024,1024]{1,0:T(8,128)} %copy-done.5, f32[1024]{0:T(1024)S(1)} %fusion.79, f32[1024]{0:T(1024)S(1)} %broadcast_multiply_fusion.1, f32[1024]{0:T(1024)S(1)} %bitcast.230, ...), kind=kOutput, calls=%fused_computation.95 | convolution fusion | flops 8600417280 | bytes 29384704 | tf_op jit(solution)/shard_map/dot_general | solution.py:27
  513.4 3.7 fusion.70
  517.2 15.4 %convolution_convert_fusion = bf16[4096,1024]{1,0:T(8,128)(2,1)} fusion(bf16[1024,4096]{1,0:T(8,128)(2,1)} %get-tuple-element.185, bf16[1024,1024]{1,0:T(8,128)(2,1)S(1)} %get-tuple-element.174), kind=kOutput, calls=%fused_computation.81 | convolution fusion | flops 8594128896 | bytes 18874368 | tf_op jit(solution)/shard_map/dot_general | solution.py:21
  534.1 5.3 convolution_convert_fusion.2
  539.4 3.3 reshape.402
  544.5 3.6 all-to-all-start.3
  548.1 16.0 %convolution_convert_fusion.1 = bf16[1024,4096]{1,0:T(8,128)(2,1)} fusion(bf16[1024,4096]{1,0:T(8,128)(2,1)} %get-tuple-element.176, f32[1024,1024]{1,0:T(8,128)} %copy-done.5, f32[1024]{0:T(1024)S(1)} %bitcast.240, f32[1024]{0:T(1024)S(1)} %bitcast.232, f32[1024]{0:T(1024)S(1)} %fusion.79, f32[1024]{0:T(1024)S(1)} %broadcast_multiply_fusion.1), kind=kOutput, calls=%fused_computation.82 | convolution fusion | flops 8599371776 | bytes 20987904 | tf_op jit(solution)/shard_map/dot_general | solution.py:21
  564.2 9.5 all-to-all-done.3
  573.7 2.6 copy.120
  576.4 2.8 reshape_squeeze.15
  579.2 92.7 %while.23 = (s32[]{:T(128)}, bf16[8,512,3,1,256]{1,4,3,2,0:T(8,128)(2,1)}, bf16[8,512,4,64]{1,3,2,0:T(8,128)(2,1)}, pred[8,512]{1,0:T(8,128)(4,1)S(1)}, bf16[8,5...) while((s32[]{:T(128)}, ...), condition=%wide.region_17.19_spmd, body=%wide.region_15.18_spmd.sunk | while | flops 689829888 | bytes 35715176 | solution.py:221
  581.7 2.4 multiply_reduce_fusion.8
  593.3 2.4 multiply_reduce_fusion.8
  604.8 2.4 multiply_reduce_fusion.8
  616.4 2.4 multiply_reduce_fusion.8
  627.9 2.4 multiply_reduce_fusion.8
  639.8 2.4 multiply_reduce_fusion.8
  651.4 2.4 multiply_reduce_fusion.8
  662.9 2.4 multiply_reduce_fusion.8
  671.9 9.3 copy.121
  681.2 83.5 %all_to_all.73 = bf16[8,512,3,1,256]{4,0,3,2,1:T(8,128)(2,1)S(1)} all-to-all(bf16[8,512,3,1,256]{4,0,3,2,1:T(8,128)(2,1)} %copy.121), channel_id=1, replica_groups=mesh['seq'=8,'head'=4] {'head'}, dimensions={1} | all-to-all | bytes 12582912 | tf_op jit(solution)/shard_map/all_to_all | solution.py:224
  764.7 4.0 copy.122
  768.8 9.1 copy.123
  777.9 11.4 fusion.57
  790.0 12.4 add_convert_fusion.2
  804.0 5.8 scatter_fusion.1
  809.8 5.5 all-to-all-start.5
  817.9 3.9 reduce.6
  821.9 11.6 all-reduce.10
  833.8 30.0 %all-to-all-done.5 = bf16[8,128,1024]{2,1,0:T(8,128)(2,1)} async-done(((bf16[8,128,1024]{2,1,0:T(8,128)(2,1)}), bf16[8,128,1024]{2,1,0:T(8,128)(2,1)}, u32[]{:S(2)}, u32[]{:S(2)}) %all-to-all-start.5) | async-done | bytes 2097184 | tf_op jit(solution)/shard_map/all_to_all | solution.py:235
  863.8 2.3 gather_fusion.2
  867.7 495.3 %all-reduce.12 = (f32[256,3072]{1,0:T(8,128)}, f32[256,1024]{1,0:T(8,128)}, f32[256,4096]{1,0:T(8,128)}, f32[1024,1024]{1,0:T(8,128)}, f32[256]{0:T(256)}, /*ind...) all-reduce(bf16[256,3072]{1,0:T(8,128)(2,1)} %reduce-scatter.5.clon, ...), channel_id=1, replica_groups=mesh['seq'=8,'head'=4] {'seq'}, use_global_device_ids=true, to_apply=%region_20.22 | all-reduce | flops 3148800 | bytes 18898944 | tf_op jit(solution)/shard_map/psum | solution.py:278
  (294 shorter events, 160.0 us)
Async XLA Ops:
  7.2 3.7 copy-start.8
  7.2 68.1 %all-gather.13.cloned.1.call-start = ((), (), s32[]{:S(2)}) async-start(), calls=%async_computation.10 | async-start | bytes 7864320 | tf_op jit(solution)/shard_map/all_gather | solution.py:88
  9.3 6.6 copy-start.32
  10.9 12.3 copy-start.37
  10.9 17.4 %copy-start.38 = (bf16[256]{0:T(256)(128)(2,1)S(1)}, bf16[256]{0:T(256)(128)(2,1)}, u32[]{:S(2)}) copy-start(bf16[256]{0:T(256)(128)(2,1)} %param.32) | copy-start | bytes 1540
  10.9 22.5 %copy-start = (s32[64]{0:T(128)S(1)}, s32[64]{0:T(128)}, u32[]{:S(2)}) copy-start(s32[64]{0:T(128)} %param.26) | copy-start | bytes 772
  10.9 22.5 %copy-start.34 = (s32[64]{0:T(128)S(1)}, s32[64]{0:T(128)}, u32[]{:S(2)}) copy-start(s32[64]{0:T(128)} %param.25) | copy-start | bytes 772
  15.9 55.5 %all-to-all-start = ((bf16[8,128,1024]{2,1,0:T(8,128)(2,1)}), bf16[8,128,1024]{2,1,0:T(8,128)(2,1)S(1)}, u32[]{:S(2)}, u32[]{:S(2)}) async-start(bf16[8,128,1024]{2,1,0:T(8,128)(2,1)} %scatter_fusion), calls=%async_computation | async-start | bytes 4194304 | tf_op jit(solution)/shard_map/all_to_all | solution.py:71
  33.5 0.5 copy-start.35
  75.2 12.1 copy-start.11
  106.3 120.3 %all-to-all-start.1 = ((bf16[8,128,3,4,256]{4,1,2,0,3:T(8,128)(2,1)}), bf16[8,128,3,4,256]{4,1,2,0,3:T(8,128)(2,1)}, u32[]{:S(2)}, u32[]{:S(2)}) async-start(bf16[8,128,3,4,256]{4,1,2,0,3:T(8,128)(2,1)} %copy.112), calls=%async_computation.1 | async-start | bytes 12582912 | tf_op jit(solution)/shard_map/all_to_all | solution.py:117
  111.5 269.1 %all-gather.15.cloned.1.call-start = ((), (), s32[]{:S(2)}) async-start(), calls=%async_computation.11 | async-start | bytes 2621440 | tf_op jit(solution)/shard_map/all_gather | solution.py:89
  112.3 276.6 %all-gather.17.cloned.1.call-start = ((), (), s32[]{:S(2)}) async-start(), calls=%async_computation.12 | async-start | bytes 10485760 | tf_op jit(solution)/shard_map/all_gather | solution.py:90
  292.9 5.0 copy-start.3
  292.9 5.0 copy-start.16
  297.8 5.3 copy-start.39
  297.8 45.0 %copy-start.40 = (bf16[256]{0:T(256)(128)(2,1)S(1)}, bf16[256]{0:T(256)(128)(2,1)}, u32[]{:S(2)}) copy-start(bf16[256]{0:T(256)(128)(2,1)} %param.36) | copy-start | bytes 1540
  297.8 50.1 %copy-start.41 = (bf16[256]{0:T(256)(128)(2,1)S(1)}, bf16[256]{0:T(256)(128)(2,1)}, u32[]{:S(2)}) copy-start(bf16[256]{0:T(256)(128)(2,1)} %param.37) | copy-start | bytes 1540
  297.8 55.1 %copy-start.29 = (bf16[1024]{0:T(1024)(128)(2,1)S(1)}, bf16[1024]{0:T(1024)(128)(2,1)}, u32[]{:S(2)}) copy-start(bf16[1024]{0:T(1024)(128)(2,1)} %param.34) | copy-start | bytes 6148
  297.8 60.3 %copy-start.42 = (bf16[256]{0:T(256)(128)(2,1)S(1)}, bf16[256]{0:T(256)(128)(2,1)}, u32[]{:S(2)}) copy-start(bf16[256]{0:T(256)(128)(2,1)} %param.35) | copy-start | bytes 1540
  297.9 66.0 %copy-start.43 = (bf16[256]{0:T(256)(128)(2,1)S(1)}, bf16[256]{0:T(256)(128)(2,1)}, u32[]{:S(2)}) copy-start(bf16[256]{0:T(256)(128)(2,1)} %param.38) | copy-start | bytes 1540
  297.9 71.6 %copy-start.44 = (bf16[256]{0:T(256)(128)(2,1)S(1)}, bf16[256]{0:T(256)(128)(2,1)}, u32[]{:S(2)}) copy-start(bf16[256]{0:T(256)(128)(2,1)} %param.39) | copy-start | bytes 1540
  297.9 77.9 %all-to-all-start.2 = ((bf16[8,512,1,256]{3,0,2,1:T(8,128)(2,1)}), bf16[8,512,1,256]{3,0,2,1:T(8,128)(2,1)}, u32[]{:S(2)}, u32[]{:S(2)}) async-start(bf16[8,512,1,256]{3,0,2,1:T(8,128)(2,1)} %bitcast.212), calls=%async_computation.2 | async-start | bytes 4194304 | tf_op jit(solution)/shard_map/all_to_all | solution.py:146
  302.5 78.1 %copy-start.12 = (bf16[8,128,1024]{2,1,0:T(8,128)(2,1)S(1)}, bf16[8,128,1024]{2,1,0:T(8,128)(2,1)}, u32[]{:S(2)}) copy-start(bf16[8,128,1024]{2,1,0:T(8,128)(2,1)} %copy-done.11) | copy-start | bytes 6291460
  302.5 137.1 %all-gather.19.cloned.1.call-start = ((), (), s32[]{:S(2)}) async-start(), calls=%async_computation.13 | async-start | bytes 10485760 | tf_op jit(solution)/shard_map/all_gather | solution.py:91
  303.1 514.8 %reduce-scatter.7.cloned.1.call-start = ((), (), s32[]{:S(2)}) async-start(), calls=%async_computation.15 | async-start | bytes 2621440 | tf_op jit(solution)/shard_map/reduce_scatter | solution.py:241
  385.7 2.0 copy-start.5
  388.3 0.6 copy-start.19
  388.9 50.7 %copy-start.28 = (f32[4,1,256]{2,1,0:T(1,128)S(1)}, f32[4,1,256]{2,1,0:T(1,128)}, u32[]{:S(2)}) copy-start(f32[4,1,256]{2,1,0:T(1,128)} %convert_element_type.222) | copy-start | bytes 12292
  454.8 1.6 copy-start.1
  454.8 1.6 copy-start.18
  454.8 1.6 copy-start.22
  455.4 3.4 copy-start.21
  462.5 2.0 copy-start.7
  489.6 17.6 %copy-start.20 = (f32[1024]{0:T(1024)S(1)}, f32[1024]{0:T(1024)}, u32[]{:S(2)}) copy-start(f32[1024]{0:T(1024)} %copy-done.19) | copy-start | bytes 12292
  489.6 17.6 %copy-start.6 = (f32[1024,1024]{1,0:T(8,128)S(1)}, f32[1024,1024]{1,0:T(8,128)}, u32[]{:S(2)}) copy-start(f32[1024,1024]{1,0:T(8,128)} %copy-done.5) | copy-start | bytes 12582916
  508.9 2.1 copy-start.4
  508.9 4.5 copy-start.14
  512.1 1.3 copy-start.9
  517.1 350.5 %reduce-scatter.11.cloned.1.call-start = ((), (), s32[]{:S(2)}) async-start(), calls=%async_computation.17 | async-start | bytes 10485760 | tf_op jit(solution)/shard_map/reduce_scatter | solution.py:247
  532.6 1.6 copy-start.10
  544.5 29.3 %all-to-all-start.3 = ((bf16[8,128,4,256]{3,1,0,2:T(8,128)(2,1)}), bf16[8,128,4,256]{3,1,0,2:T(8,128)(2,1)S(1)}, u32[]{:S(2)}, u32[]{:S(2)}) async-start(bf16[8,128,4,256]{3,1,0,2:T(8,128)(2,1)} %copy.119), calls=%async_computation.3 | async-start | bytes 4194304 | tf_op jit(solution)/shard_map/all_to_all | solution.py:188
  548.1 319.6 %reduce-scatter.9.cloned.1.call-start = ((), (), s32[]{:S(2)}) async-start(), calls=%async_computation.16 | async-start | bytes 10485760 | tf_op jit(solution)/shard_map/reduce_scatter | solution.py:244
  564.2 303.5 %reduce-scatter.5.cloned.1.call-start = ((), (), s32[]{:S(2)}) async-start(), calls=%async_computation.14 | async-start | bytes 7864320 | tf_op jit(solution)/shard_map/reduce_scatter | solution.py:238
  573.7 5.4 copy-start.17
  768.8 9.1 copy-start.13
  789.3 0.7 copy-start.36
  804.0 11.3 copy-start.45
  804.0 13.2 copy-start.33
  804.0 13.3 copy-start.2
  804.0 13.3 copy-start.27
  809.8 54.0 %all-to-all-start.5 = ((bf16[8,128,1024]{2,1,0:T(8,128)(2,1)}), bf16[8,128,1024]{2,1,0:T(8,128)(2,1)}, u32[]{:S(2)}, u32[]{:S(2)}) async-start(bf16[8,128,1024]{2,1,0:T(8,128)(2,1)} %scatter_fusion.1), calls=%async_computation.5 | async-start | bytes 4194304 | tf_op jit(solution)/shard_map/all_to_all | solution.py:235
  817.3 4.5 copy-start.23
  817.3 4.5 copy-start.24
  817.3 4.5 copy-start.25
  817.3 4.5 copy-start.26
  817.4 4.5 copy-start.30
  817.4 4.5 copy-start.31
  833.8 33.9 %copy-start.15 = (bf16[256,1024]{1,0:T(8,128)(2,1)S(1)}, bf16[256,1024]{1,0:T(8,128)(2,1)}, u32[]{:S(2)}) copy-start(bf16[256,1024]{1,0:T(8,128)(2,1)} %reduce-scatter.7.cloned.1.call-done) | copy-start | bytes 1572868
Sparse Core Ops, SparseCore 0:
  9.6 49.1 all-gather.12
  113.9 33.4 all-gather.14
  149.0 91.0 all-gather.16
  304.6 70.4 all-gather.18
  517.3 28.5 reduce-scatter.6
  548.5 75.8 reduce-scatter.10
  627.0 80.7 reduce-scatter.8
  789.5 58.8 reduce-scatter.4
where the time goes:
time: 1380 us; the launch traced here: 1370 us
  blocking collectives  671 us (49%)
  matrix products  290 us (21%)
  waiting for transfers between devices  193 us (14%)
  local copies, waits for them, and re-layouts  120 us (9%)
  other arithmetic  52.8 us (4%)
  starting transfers between devices  26.6 us (2%)
  between operations  16.3 us (1%)
    psum x1, blocking collectives, on_device(): lax.psum((shares[0], shares[1], shares[2], shares[3], shares[4], shares[5...  495 us
    all_to_all x1, waiting for transfers between devices, on_device(): lax.all_to_all(spread_qkv, 'head', split_axis=3, concat_axis=1, tiled=True)  113 us
    all_to_all x1, blocking collectives, on_device(): lax.all_to_all(grad_parts, 'head', split_axis=1, concat_axis=3, tiled=True)  83.5 us
    dot_general x4, matrix products, contract_cols(): lax.dot_general(left, right, (((1,), (1,)), ((), ())), preferred_element_...  59.4 us
    dot_general x1, matrix products, on_device(): jnp.dot(hidden_low, full_up, preferred_element_type=jnp.float32) + up_bias  50.7 us
    dot_general x4, matrix products, contract_rows(): lax.dot_general(left, right, (((0,), (0,)), ((), ())), preferred_element_...  46.6 us
    all_gather x1, blocking collectives, on_device(): lax.all_gather(bias_out, 'head', axis=0, tiled=True)  39.6 us
    all_to_all x1, waiting for transfers between devices, on_device(): lax.all_to_all(outgoing, 'seq', split_axis=0, concat_axis=0, tiled=True)  37.3 us
  transfers between devices with their start and end apart: 13, of which 4 were waited for; matrix products, arithmetic and copies ran while one was open for 26% of the time, Pallas kernels for 0%

commit v1 on v0

v1 whole, which is shorter than its diff:
```python
import functools
import itertools

import jax
import jax.numpy as jnp
import numpy as np
from jax import lax
from jax.experimental import pallas as pl
from jax.experimental.pallas import tpu as pltpu
from jax.sharding import PartitionSpec as P

HEAD_SIZE = 64
CAP = 1472
HALF = CAP // 2
EPS = 1e-12
BF = jnp.bfloat16
F32 = jnp.float32
VMEM_SPEC = pl.BlockSpec(memory_space=pltpu.VMEM)
SMEM_SPEC = pl.BlockSpec(memory_space=pltpu.SMEM)
ANY_SPEC = pl.BlockSpec(memory_space=pl.ANY)


def mm(left, right):
    return jnp.dot(left, right, preferred_element_type=F32)


def mm_rows(left, right):
    return lax.dot_general(left, right, (((0,), (0,)), ((), ())), preferred_element_type=F32)


def mm_cols(left, right):
    return lax.dot_general(left, right, (((1,), (1,)), ((), ())), preferred_element_type=F32)


def _route_kernel(count, single, dst_ref, *refs):
    if single:
        src_ref, out_ref, sems = refs
        sources = [src_ref.at[k] for k in range(count)]
    else:
        sources = list(refs[:count])
        out_ref, sems = refs[count:]
    copies = []
    for k in range(count):
        copy = pltpu.make_async_copy(sources[k], out_ref.at[dst_ref[k]], sems.at[k])
        copy.start()
        copies.append(copy)
    for copy in copies:
        copy.wait()


def route(blocks, dst):
    single = not isinstance(blocks, (list, tuple))
    args = [blocks] if single else list(blocks)
    count = args[0].shape[0] if single else len(args)
    shape = args[0].shape[1:] if single else args[0].shape
    return pl.pallas_call(
        functools.partial(_route_kernel, count, single),
        out_shape=jax.ShapeDtypeStruct((count,) + shape, args[0].dtype),
        in_specs=[SMEM_SPEC] + [ANY_SPEC] * len(args),
        out_specs=ANY_SPEC,
        scratch_shapes=[pltpu.SemaphoreType.DMA((count,))],
        cost_estimate=pl.CostEstimate(flops=0, bytes_accessed=4 << 20, transcendentals=0),
        name="route",
    )(dst, *args)


def _pack_kernel(meta_ref, a0, a1, a2, a3, out_ref):
    here = meta_ref[12]
    out_ref[...] = jnp.zeros_like(out_ref)
    for slot in range(4):
        offset, length = meta_ref[slot], meta_ref[4 + slot]
        for src, flip in ((a0, 0), (a1, 2), (a2, 1), (a3, 3)):
            start = (here ^ flip) * 128
            pieces = jnp.clip((length - start + 15) // 16, 0, 8)

            @pl.loop(0, pieces)
            def _(i):
                row = pl.multiple_of(offset + start + i * 16, 16)
                out_ref[pl.ds(row, 16), :] = src[slot, pl.ds(pl.multiple_of(i * 16, 16), 16), :]


def pack(meta, own, from_x, from_core, from_both):
    return pl.pallas_call(
        _pack_kernel,
        out_shape=jax.ShapeDtypeStruct((CAP, own.shape[-1]), own.dtype),
        in_specs=[SMEM_SPEC] + [VMEM_SPEC] * 4,
        out_specs=VMEM_SPEC,
        compiler_params=pltpu.CompilerParams(vmem_limit_bytes=40 << 20),
        cost_estimate=pl.CostEstimate(flops=0, bytes_accessed=8 << 20, transcendentals=0),
        name="pack",
    )(meta, own, from_x, from_core, from_both)


def _unpack_kernel(meta_ref, mine_ref, other_ref, own_ref, far_ref, rows_ref, sems):
    here, core = meta_ref[12], meta_ref[13]
    first = pltpu.make_async_copy(
        mine_ref, rows_ref.at[pl.ds(pl.multiple_of(core * HALF, 16), HALF)], sems.at[0]
    )
    second = pltpu.make_async_copy(
        other_ref, rows_ref.at[pl.ds(pl.multiple_of((1 - core) * HALF, 16), HALF)], sems.at[1]
    )
    first.start()
    second.start()
    first.wait()
    second.wait()
    width = rows_ref.shape[1]
    for slot in range(4):
        offset, length = meta_ref[slot], meta_ref[4 + slot]
        for dst, flip in ((own_ref, 0), (far_ref, 2)):
            start = (here ^ flip) * 128

            @pl.loop(0, 8)
            def _(i):
                position = start + i * 16
                row = pl.multiple_of(jnp.minimum(offset + position, CAP - 16), 16)
                keep = lax.broadcasted_iota(jnp.int32, (16, width), 0) + position < length
                part = rows_ref[pl.ds(row, 16), :].astype(F32)
                dst[slot, pl.ds(pl.multiple_of(i * 16, 16), 16), :] = jnp.where(
                    keep, part, 0.0
                ).astype(BF)


def unpack(meta, mine, other):
    width = mine.shape[1]
    shape = jax.ShapeDtypeStruct((4, 128, width), BF)
    return pl.pallas_call(
        _unpack_kernel,
        out_shape=(shape, shape),
        in_specs=[SMEM_SPEC, ANY_SPEC, ANY_SPEC],
        out_specs=(VMEM_SPEC, VMEM_SPEC),
        scratch_shapes=[pltpu.VMEM((CAP, width), BF), pltpu.SemaphoreType.DMA((2,))],
        compiler_params=pltpu.CompilerParams(vmem_limit_bytes=40 << 20),
        cost_estimate=pl.CostEstimate(flops=0, bytes_accessed=5 << 20, transcendentals=0),
        name="unpack",
    )(meta, mine, other)


def _attend_kernel(meta_ref, qkv_ref, ctx_ref, lse_ref):
    ctx_ref[...] = jnp.zeros_like(ctx_ref)
    width = ctx_ref.shape[1]

    def one(slot, blocks):
        span = blocks * 128
        offset = pl.multiple_of(meta_ref[slot], 16)
        length = meta_ref[4 + slot]
        rows = pl.ds(offset, span)

        @pl.loop(0, width // 128)
        def _(pair):
            lane0 = pl.multiple_of(pair * 128, 128)
            keys = qkv_ref[rows, pl.ds(pl.multiple_of(width + lane0, 128), 128)]
            values = qkv_ref[rows, pl.ds(pl.multiple_of(2 * width + lane0, 128), 128)]
            values_t = values.astype(F32).T.astype(BF)
            for first in range(0, span, 256):
                step = min(span - first, 256)
                queries = qkv_ref[
                    pl.ds(pl.multiple_of(offset + first, 16), step), pl.ds(lane0, 128)
                ]
                queries = queries * jnp.asarray(HEAD_SIZE**-0.5, BF)
                lane = lax.broadcasted_iota(jnp.int32, (step, 128), 1)
                parts = []
                for half in range(2):
                    picked = jnp.where((lane >= 64) == (half == 1), queries, jnp.zeros_like(queries))
                    scores = mm_cols(keys, picked)
                    key_id = lax.broadcasted_iota(jnp.int32, scores.shape, 0)
                    scores = jnp.where(key_id < length, scores, -1e30)
                    highest = jnp.max(scores, axis=0, keepdims=True)
                    expo = jnp.exp(scores - highest)
                    total = jnp.sum(expo, axis=0, keepdims=True)
                    probs = (expo * (1.0 / total)).astype(BF)
                    parts.append(mm(values_t[64 * half : 64 * half + 64], probs))
                    lse_ref[slot, pair * 2 + half, :, first : first + step] = highest + jnp.log(total)
                mixed = jnp.concatenate(parts, axis=0).T
                ctx_ref[pl.ds(pl.multiple_of(offset + first, 16), step), pl.ds(lane0, 128)] = (
                    mixed.astype(BF)
                )

    @pl.loop(0, 4)
    def _(slot):
        for blocks in range(1, 5):
            pl.when(meta_ref[8 + slot] == blocks)(functools.partial(one, slot, blocks))


def attend(meta, qkv):
    width = qkv.shape[1] // 3
    return pl.pallas_call(
        _attend_kernel,
        out_shape=(
            jax.ShapeDtypeStruct((CAP, width), BF),
            jax.ShapeDtypeStruct((4, width // HEAD_SIZE, 1, 512), F32),
        ),
        in_specs=[SMEM_SPEC, VMEM_SPEC],
        out_specs=(VMEM_SPEC, VMEM_SPEC),
        compiler_params=pltpu.CompilerParams(vmem_limit_bytes=40 << 20),
        cost_estimate=pl.CostEstimate(
            flops=8 << 30, bytes_accessed=6 << 20, transcendentals=4 << 20
        ),
        name="attend",
    )(meta, qkv)


def _attend_back_kernel(meta_ref, qkv_ref, lse_ref, gctx_ref, out_ref):
    out_ref[...] = jnp.zeros_like(out_ref)
    width = gctx_ref.shape[1]

    def one(slot, blocks):
        span = blocks * 128
        offset = pl.multiple_of(meta_ref[slot], 16)
        length = meta_ref[4 + slot]
        rows = pl.ds(offset, span)

        @pl.loop(0, width // 128)
        def _(pair):
            lane0 = pl.multiple_of(pair * 128, 128)
            key_lanes = pl.ds(pl.multiple_of(width + lane0, 128), 128)
            value_lanes = pl.ds(pl.multiple_of(2 * width + lane0, 128), 128)
            keys = qkv_ref[rows, key_lanes]
            values = qkv_ref[rows, value_lanes]
            keys_t = keys.astype(F32).T.astype(BF)
            grad_keys = jnp.zeros((span, 128), F32)
            grad_values = jnp.zeros((span, 128), F32)
            for first in range(0, span, 256):
                step = min(span - first, 256)
                here = pl.ds(pl.multiple_of(offset + first, 16), step)
                queries = qkv_ref[here, pl.ds(lane0, 128)] * jnp.asarray(HEAD_SIZE**-0.5, BF)
                grad_ctx = gctx_ref[here, pl.ds(lane0, 128)]
                lane = lax.broadcasted_iota(jnp.int32, (step, 128), 1)
                row = lax.broadcasted_iota(jnp.int32, (step, 128), 0) + first
                grad_ctx = jnp.where(row < length, grad_ctx, jnp.zeros_like(grad_ctx))
                parts = []
                for half in range(2):
                    side = (lane >= 64) == (half == 1)
                    picked = jnp.where(side, queries, jnp.zeros_like(queries))
                    picked_grad = jnp.where(side, grad_ctx, jnp.zeros_like(grad_ctx))
                    scores = mm_cols(keys, picked)
                    log_total = lse_ref[slot, pair * 2 + half, :, first : first + step]
                    key_id = lax.broadcasted_iota(jnp.int32, scores.shape, 0)
                    probs = jnp.where(key_id < length, jnp.exp(scores - log_total), 0.0)
                    grad_values = grad_values + mm(probs.astype(BF), picked_grad)
                    grad_probs = mm_cols(values, picked_grad)
                    inner = jnp.sum(probs * grad_probs, axis=0, keepdims=True)
                    grad_scores = (probs * (grad_probs - inner)).astype(BF)
                    grad_keys = grad_keys + mm(grad_scores, picked)
                    parts.append(mm(keys_t[64 * half : 64 * half + 64], grad_scores))
                grad_queries = jnp.concatenate(parts, axis=0).T * HEAD_SIZE**-0.5
                out_ref[here, pl.ds(lane0, 128)] = grad_queries.astype(BF)
            out_ref[rows, key_lanes] = grad_keys.astype(BF)
            out_ref[rows, value_lanes] = grad_values.astype(BF)

    @pl.loop(0, 4)
    def _(slot):
        for blocks in range(1, 5):
            pl.when(meta_ref[8 + slot] == blocks)(functools.partial(one, slot, blocks))


def attend_back(meta, qkv, lse, grad_ctx):
    return pl.pallas_call(
        _attend_back_kernel,
        out_shape=jax.ShapeDtypeStruct(qkv.shape, BF),
        in_specs=[SMEM_SPEC] + [VMEM_SPEC] * 3,
        out_specs=VMEM_SPEC,
        compiler_params=pltpu.CompilerParams(vmem_limit_bytes=48 << 20),
        cost_estimate=pl.CostEstimate(
            flops=20 << 30, bytes_accessed=12 << 20, transcendentals=4 << 20
        ),
        name="attend_back",
    )(meta, qkv, lse, grad_ctx)


def normed(inputs):
    average = jnp.mean(inputs, axis=-1, keepdims=True)
    centered = inputs - average
    variance = jnp.mean(centered * centered, axis=-1, keepdims=True)
    rstd = lax.rsqrt(variance + EPS)
    return centered * rstd, rstd


def norm_back(unit, rstd, grad, gain):
    scaled = grad * gain
    return (
        scaled
        - jnp.mean(scaled, axis=-1, keepdims=True)
        - unit * jnp.mean(scaled * unit, axis=-1, keepdims=True)
    ) * rstd


def total_over_seq(part, group_count):
    if group_count != 8:
        return lax.psum(part, "seq")
    count, width = part.shape
    index = lax.axis_index("seq")
    here_y, here_z = index % 2, index // 2
    swap_y = [(i, i ^ 1) for i in range(8)]
    halves = part.reshape(2, count // 2, width)
    send = lax.dynamic_index_in_dim(halves, 1 - here_y, 0, keepdims=False).astype(BF)
    keep = lax.dynamic_index_in_dim(halves, here_y, 0, keepdims=False)
    keep = keep + lax.ppermute(send, "seq", swap_y).astype(F32)
    keep = keep.reshape(4, count // 8, width)
    right = left = None
    for step in (1, 2, 3):
        to_right = lax.dynamic_index_in_dim(
            keep, jnp.clip(here_z + 4 - step, 0, 3), 0, keepdims=False
        )
        to_left = lax.dynamic_index_in_dim(
            keep, jnp.clip(here_z - 4 + step, 0, 3), 0, keepdims=False
        )
        if right is not None:
            to_right = to_right + right.astype(F32)
            to_left = to_left + left.astype(F32)
        right = lax.ppermute(
            to_right.astype(BF),
            "seq",
            [(2 * z + y, 2 * z + 2 + y) for z in range(step) for y in range(2) if z < 3],
        )
        left = lax.ppermute(
            to_left.astype(BF),
            "seq",
            [(2 * z + y, 2 * z - 2 + y) for z in range(4 - step, 4) for y in range(2) if z > 0],
        )
    own = lax.dynamic_index_in_dim(keep, here_z, 0, keepdims=False)
    own = (own + right.astype(F32) + left.astype(F32)).astype(BF)
    pieces = [own] * 4
    right = left = own
    found = [[own, here_z]]
    for step in (1, 2, 3):
        right = lax.ppermute(
            right,
            "seq",
            [(2 * z + y, 2 * z + 2 + y) for z in range(step - 1, 3) for y in range(2)],
        )
        left = lax.ppermute(
            left,
            "seq",
            [(2 * z + y, 2 * z - 2 + y) for z in range(1, 5 - step) for y in range(2)],
        )
        found += [[right, here_z - step], [left, here_z + step]]
    for spot in range(4):
        for piece, where in found[1:]:
            pieces[spot] = jnp.where(where == spot, piece, pieces[spot])
    mine = jnp.concatenate(pieces, axis=0)
    other = lax.ppermute(mine, "seq", swap_y)
    lower = jnp.where(here_y == 0, mine, other)
    upper = jnp.where(here_y == 0, other, mine)
    return jnp.concatenate([lower, upper], axis=0).astype(F32)


def on_device(
    tokens,
    cotangent,
    lengths,
    seq_order,
    w_qkv,
    w_out,
    w_up,
    w_down,
    bias_q,
    bias_v,
    bias_out,
    bias_up,
    bias_down,
    gain_attn,
    shift_attn,
    gain_mlp,
    shift_mlp,
):
    group_count = lax.axis_size("seq")
    group_id = lax.axis_index("seq")
    here = lax.axis_index("head").astype(jnp.int32)
    core, chip = here % 2, here // 2
    slots, span_rows, width = tokens.shape
    part = width // 4
    ff_part = w_up.shape[1] // 4
    offsets = [k * group_count // slots for k in range(slots)]
    offsets[1], offsets[-1] = 1, group_count - 1
    swap_x = [(i, i ^ 2) for i in range(4)]
    swap_core = [(i, i ^ 1) for i in range(4)]

    def over_x(value):
        return lax.ppermute(value, "head", swap_x)

    def over_core(value):
        return lax.ppermute(value, "head", swap_core)

    def column_halves(weight, kinds):
        blocks = weight.reshape(weight.shape[0], kinds, 4, -1)

        def pick(flip):
            return lax.dynamic_slice_in_dim(blocks, here ^ flip, 1, axis=2)

        kept = jnp.concatenate([pick(0), pick(2)], axis=2).reshape(weight.shape[0], -1)
        sent = jnp.concatenate([pick(1), pick(3)], axis=2).reshape(weight.shape[0], -1)
        return kept, sent

    def gathered_columns(weight, kinds):
        kept, sent = column_halves(weight, kinds)
        far_kept, far_sent = column_halves(over_x(weight), kinds)
        full = jnp.zeros((4 * weight.shape[0], kept.shape[1]), BF)
        for flip, block in (
            (0, kept),
            (1, over_core(sent)),
            (2, far_kept),
            (3, over_core(far_sent)),
        ):
            full = lax.dynamic_update_slice_in_dim(full, block, (here ^ flip) * part, axis=0)
        return full

    full_qkv = gathered_columns(w_qkv, 3)
    full_out = jnp.concatenate([w_out, over_x(w_out)], axis=0)
    full_up = gathered_columns(w_up, 1)
    full_down = jnp.concatenate([w_down, over_x(w_down)], axis=0)
    small = lax.all_gather(
        jnp.concatenate(
            [
                bias_q,
                bias_v,
                bias_out,
                bias_down,
                gain_attn,
                shift_attn,
                gain_mlp,
                shift_mlp,
                bias_up,
            ]
        ),
        "head",
        axis=0,
        tiled=False,
    ).astype(F32)

    def vector(place):
        return small[:, place * part : (place + 1) * part].reshape(1, width)

    def local_columns(rows):
        return jnp.concatenate(
            [
                lax.dynamic_index_in_dim(rows, here, 0, keepdims=False),
                lax.dynamic_index_in_dim(rows, here ^ 2, 0, keepdims=False),
            ]
        )

    query_bias = local_columns(small[:, 0:part])
    value_bias = local_columns(small[:, part : 2 * part])
    up_bias = local_columns(small[:, 8 * part :])[None, :]
    out_bias, down_bias = vector(2), vector(3)
    attn_gain, attn_shift, mlp_gain, mlp_shift = vector(4), vector(5), vector(6), vector(7)
    joint_bias = jnp.concatenate([query_bias, jnp.zeros_like(query_bias), value_bias])[None, :]

    slot_ids = jnp.arange(slots, dtype=jnp.int32)
    local_ids = group_id * slots + slot_ids
    given_slot = lax.dynamic_slice_in_dim(seq_order, group_id * slots, slots) % slots
    given_of_slot = jnp.sum(
        jnp.where(given_slot[None, :] == slot_ids[:, None], slot_ids[None, :], 0), axis=1
    )
    matches = seq_order[None, :] == local_ids[:, None]
    slot_lens = jnp.sum(jnp.where(matches, lengths[None, :], 0), axis=1)
    aligned = (slot_lens + 15) // 16 * 16
    choices = np.zeros((35, slots), np.int32)
    for row, picks in enumerate(itertools.combinations(range(1, slots), 3)):
        choices[row, [0, *picks]] = 1
    sides = jnp.sum(choices * aligned[None, :], axis=1)
    larger = jnp.maximum(sides, jnp.sum(aligned) - sides)
    squares = jnp.sum(choices * (slot_lens * slot_lens)[None, :], axis=1)
    heavier = jnp.maximum(squares, jnp.sum(slot_lens * slot_lens) - squares)
    score = larger * 1024 + heavier // 4096
    best = jnp.min(score)
    chosen = jnp.argmax(score == best)
    in_first = jnp.sum(
        jnp.where(jnp.arange(35)[:, None] == chosen, choices, 0), axis=0, dtype=jnp.int32
    )
    is_own = jnp.where(chip == 0, in_first, 1 - in_first)
    before = np.tril(np.ones((slots, slots), np.int32), -1)
    rank_own = jnp.sum(before * is_own[None, :], axis=1)
    rank_far = jnp.sum(before * (1 - is_own)[None, :], axis=1)
    list_pos = jnp.where(is_own == 1, rank_own, 4 + rank_far).astype(jnp.int32)
    at_place = list_pos[None, :] == slot_ids[:, None]
    slot_at = jnp.sum(jnp.where(at_place, slot_ids[None, :], 0), axis=1)
    own_lens = jnp.sum(jnp.where(at_place, slot_lens[None, :], 0), axis=1)[:4]
    own_aligned = (own_lens + 15) // 16 * 16
    own_offsets = jnp.sum(np.tril(np.ones((4, 4), np.int32), -1) * own_aligned[None, :], axis=1)
    meta = jnp.concatenate(
        [
            own_offsets,
            own_lens,
            (own_lens + 127) // 128,
            here[None],
            core[None],
            jnp.zeros((2,), jnp.int32),
        ]
    ).astype(jnp.int32)
    row_ids = core * HALF + jnp.arange(HALF, dtype=jnp.int32)
    row_keep = jnp.any(
        (row_ids[:, None] >= own_offsets[None, :])
        & (row_ids[:, None] < (own_offsets + own_lens)[None, :]),
        axis=1,
        keepdims=True,
    )

    def to_chip(lists):
        own, far = lists[:4], over_x(lists[4:])
        return pack(meta, own, far, over_core(own), over_core(far))

    outgoing = route(tokens, given_slot.astype(jnp.int32))
    arrived = [outgoing[0]]
    for k in range(1, slots):
        arrived.append(
            lax.ppermute(
                outgoing[k],
                "seq",
                [(i, (i - offsets[k]) % group_count) for i in range(group_count)],
            )
        )
    rows_in = to_chip(route(arrived, list_pos))
    cot_rows = to_chip(route(cotangent, list_pos))

    def halves(value):
        return (
            lax.dynamic_slice_in_dim(value, core * HALF, HALF, axis=0),
            lax.dynamic_slice_in_dim(value, (1 - core) * HALF, HALF, axis=0),
        )

    def in_order(mine, other):
        lower = jnp.where(core == 0, mine, other)
        upper = jnp.where(core == 0, other, mine)
        return jnp.concatenate([lower, upper], axis=0)

    def core_sum(mine_left, other_left, right, product):
        arriving = over_core(product(other_left, right).astype(BF))
        return product(mine_left, right) + arriving.astype(F32)

    qkv = (mm(rows_in, full_qkv) + joint_bias).astype(BF)
    context, lse = attend(meta, qkv)
    ctx_mine, ctx_other = halves(context)
    rows_mine, _ = halves(rows_in)
    resid_attn = (
        core_sum(ctx_mine, ctx_other, full_out, mm) + rows_mine.astype(F32) + out_bias
    )
    unit_attn, rstd_attn = normed(resid_attn)
    hidden = unit_attn * attn_gain + attn_shift
    low_mine = hidden.astype(BF)
    low_other = over_core(low_mine)

    def up(low):
        pre = mm(low, full_up) + up_bias
        cdf = 0.5 * (1.0 + lax.erf(pre * np.float32(0.5**0.5)))
        slope = cdf + pre * jnp.exp(-0.5 * pre * pre) * np.float32((2 * np.pi) ** -0.5)
        return (pre * cdf).astype(BF), slope.astype(BF)

    act_mine, slope_mine = up(low_mine)
    act_other, slope_other = up(low_other)
    resid_mlp = core_sum(act_mine, act_other, full_down, mm) + hidden + down_bias
    unit_mlp, rstd_mlp = normed(resid_mlp)
    final_mine = (unit_mlp * mlp_gain + mlp_shift).astype(BF)

    cot_mine, _ = halves(cot_rows)
    grad_y = jnp.where(row_keep, cot_mine.astype(F32), 0.0)
    grad_mlp2 = norm_back(unit_mlp, rstd_mlp, grad_y, mlp_gain)
    sum_gain_mlp = jnp.sum(grad_y * unit_mlp, axis=0)
    sum_shift_mlp = jnp.sum(grad_y, axis=0)
    branch_mine = grad_mlp2.astype(BF)
    branch_other = over_core(branch_mine)
    sum_bias_down = jnp.sum(branch_mine, axis=0, dtype=F32)
    pre_mine = (mm_cols(branch_mine, full_down) * slope_mine.astype(F32)).astype(BF)
    pre_other = (mm_cols(branch_other, full_down) * slope_other.astype(F32)).astype(BF)
    sum_bias_up = jnp.sum(pre_mine, axis=0, dtype=F32) + jnp.sum(pre_other, axis=0, dtype=F32)
    branch = jnp.concatenate([branch_mine, branch_other], axis=0)
    act = jnp.concatenate([act_mine, act_other], axis=0)
    low = jnp.concatenate([low_mine, low_other], axis=0)
    grad_pre = jnp.concatenate([pre_mine, pre_other], axis=0)

    def chip_sum(far_product, own_product):
        arriving = over_x(far_product.astype(BF))
        return own_product + arriving.astype(F32)

    down_part = chip_sum(mm_rows(act[:, ff_part:], branch), mm_rows(act[:, :ff_part], branch))
    grad_hidden = core_sum(pre_mine, pre_other, full_up, mm_cols) + grad_mlp2

    def feature_block(value, flip):
        return lax.dynamic_slice_in_dim(value, (here ^ flip) * part, part, axis=1)

    def column_grads(left, right, kinds):
        blocks = right.shape[1] // (2 * kinds)

        def merged(mine, other):
            mine = mine.reshape(part, kinds, 2, blocks)
            other = other.reshape(part, kinds, 2, blocks)
            low_core = jnp.where(core == 0, mine, other)
            high_core = jnp.where(core == 0, other, mine)
            near = jnp.stack([low_core[:, :, 0], high_core[:, :, 0]], axis=2)
            far = jnp.stack([low_core[:, :, 1], high_core[:, :, 1]], axis=2)
            first = jnp.where(chip == 0, near, far)
            last = jnp.where(chip == 0, far, near)
            return jnp.concatenate([first, last], axis=2).reshape(part, -1)

        both = mm_rows(feature_block(left, 3), right).astype(BF)
        near = mm_rows(feature_block(left, 1), right).astype(BF)
        got_far = over_core(both)
        got_near = over_core(near)
        far_mine = mm_rows(feature_block(left, 2), right).astype(BF)
        arriving = over_x(merged(far_mine, got_far))
        own_mine = mm_rows(feature_block(left, 0), right)
        return merged(own_mine, got_near.astype(F32)) + arriving.astype(F32)

    up_part = column_grads(low, grad_pre, 1)

    grad_attn2 = norm_back(unit_attn, rstd_attn, grad_hidden, attn_gain)
    sum_gain_attn = jnp.sum(grad_hidden * unit_attn, axis=0)
    sum_shift_attn = jnp.sum(grad_hidden, axis=0)
    attn_mine = grad_attn2.astype(BF)
    attn_other = over_core(attn_mine)
    sum_bias_out = jnp.sum(attn_mine, axis=0, dtype=F32)
    grad_ctx = in_order(
        mm_cols(attn_mine, full_out).astype(BF), mm_cols(attn_other, full_out).astype(BF)
    )
    ctx_local = jnp.concatenate([ctx_mine, ctx_other], axis=0)
    attn_local = jnp.concatenate([attn_mine, attn_other], axis=0)
    out_part = chip_sum(
        mm_rows(ctx_local[:, part:], attn_local), mm_rows(ctx_local[:, :part], attn_local)
    )
    grad_qkv = attend_back(meta, qkv, lse, grad_ctx)
    gqkv_mine, gqkv_other = halves(grad_qkv)
    gx_mine = (core_sum(gqkv_mine, gqkv_other, full_qkv, mm_cols) + grad_attn2).astype(BF)
    qkv_part = column_grads(rows_in, grad_qkv, 3)
    qkv_sums = jnp.sum(grad_qkv, axis=0, dtype=F32)
    sum_bias_q, sum_bias_v = qkv_sums[: 2 * part], qkv_sums[4 * part :]

    def to_slots(mine):
        own, far = unpack(meta, mine, over_core(mine))
        arriving = over_x(far)
        parts = [own[k] for k in range(4)] + [arriving[k] for k in range(4)]
        return route(parts, slot_at.astype(jnp.int32))

    activations = to_slots(final_mine)
    back = to_slots(gx_mine)
    returned = [back[0]]
    for k in range(1, slots):
        returned.append(
            lax.ppermute(
                back[k],
                "seq",
                [(i, (i + offsets[k]) % group_count) for i in range(group_count)],
            )
        )
    input_grad = route(returned, given_of_slot.astype(jnp.int32))

    def whole_row(value):
        return value.reshape(4, part)

    def spread(value, size):
        result = jnp.zeros((4, size), F32)
        result = lax.dynamic_update_slice(result, value[None, :size], (here, 0))
        return lax.dynamic_update_slice(result, value[None, size:], (here ^ 2, 0))

    terms = jnp.concatenate(
        [
            spread(sum_bias_q, part),
            spread(sum_bias_v, part),
            whole_row(sum_bias_out),
            whole_row(sum_bias_down),
            whole_row(sum_gain_attn),
            whole_row(sum_shift_attn),
            whole_row(sum_gain_mlp),
            whole_row(sum_shift_mlp),
            spread(sum_bias_up, ff_part),
        ],
        axis=1,
    )

    def shard(value, flip):
        return lax.dynamic_index_in_dim(value, here ^ flip, 0, keepdims=True)

    from_core = over_core(jnp.concatenate([shard(terms, 1), shard(terms, 3)]).astype(BF))
    near_term = shard(terms, 0) + from_core[:1].astype(F32)
    far_term = shard(terms, 2) + from_core[1:].astype(F32)
    term = (near_term + over_x(far_term.astype(BF)).astype(F32))[0]
    lanes = term.shape[0] // part
    term = jnp.pad(term.reshape(lanes, part).T, ((0, 0), (0, 128 - lanes)))

    grad_down = total_over_seq(down_part, group_count)
    grad_up = total_over_seq(up_part, group_count)
    last = total_over_seq(jnp.concatenate([qkv_part, out_part, term], axis=1), group_count)
    grad_w_qkv = last[:, : 3 * width]
    grad_w_out = last[:, 3 * width : 4 * width]
    sums = last[:, 4 * width : 4 * width + lanes].T.reshape(-1)

    def piece(place):
        return sums[place * part : (place + 1) * part]

    return (
        activations,
        input_grad,
        grad_w_qkv,
        grad_w_out,
        grad_up,
        grad_down,
        piece(0),
        piece(1),
        piece(2),
        sums[8 * part :],
        piece(3),
        piece(4),
        piece(5),
        piece(6),
        piece(7),
    )


def solution(mesh):
    rows = P("seq", "head", None)
    weight, vector = P("head", None), P("head")
    in_specs = (rows, rows, P(), P()) + (weight,) * 4 + (vector,) * 9
    out_specs = (rows, rows) + (weight,) * 4 + (vector,) * 9
    return jax.shard_map(
        on_device, mesh=mesh, in_specs=in_specs, out_specs=out_specs, check_vma=False
    )
```

time: 1380 us -> 1120 us (0.81)
  blocking collectives: 671 us -> 5.19 us
  Pallas kernels: 0 us -> 451 us
  matrix products: 290 us -> 129 us
  starting transfers between devices: 26.6 us -> 135 us
  waiting for transfers between devices: 193 us -> 116 us
  local copies, waits for them, and re-layouts: 120 us -> 176 us
  other arithmetic: 52.8 us -> 93.7 us
    psum x1 -> x0, blocking collectives: 495 us -> none  [on_device(): lax.psum((shares[0], shares[1], shares[2], shares[3], shares[4], shares[5...]
    pallas_call x0 -> x12, Pallas kernels: none -> 451 us  [the longest x6 392 us: route(): pl.pallas_call(functools.partial(_route_kernel, count, single), out_shape...]
    all_to_all x5 -> x0, waiting for transfers between devices: 190 us -> none  [the longest x1 113 us: on_device(): lax.all_to_all(spread_qkv, 'head', split_axis=3, concat_axis=1, tiled=True)]
    dot_general x68 -> x27, matrix products: 290 us -> 129 us  [the longest x12 53.3 us: mm_rows(): lax.dot_general(left, right, (((0,), (0,)), ((), ())), preferred_element_...]
    ppermute x0 -> x91, starting transfers between devices: none -> 135 us  [the longest x9 43.1 us: total_over_seq(): lax.ppermute(to_right.astype(BF), 'seq', [(2 * z + y, 2 * z + 2 + y) for...]
    ppermute x0 -> x91, waiting for transfers between devices: none -> 116 us  [the longest x13 37.1 us: over_x(): return lax.ppermute(value, 'head', swap_x)]
    all_to_all x1 -> x0, blocking collectives: 83.5 us -> none  [on_device(): lax.all_to_all(grad_parts, 'head', split_axis=1, concat_axis=3, tiled=True)]
    all_gather x9 -> x1, blocking collectives: 80.3 us -> 5.19 us  [on_device(): lax.all_gather(jnp.concatenate([bias_q, bias_v, bias_out, bias_down, gain...]
  transfers between devices with their start and end apart: 13 -> 91, of which waited for: 4 -> 19; matrix products, arithmetic and copies ran while one was open for 26% -> 32% of each run, Pallas kernels for 0% -> 35%
where the time goes in v1:
time: 1120 us; the launch traced here: 1110 us
  Pallas kernels  451 us (40%)
  local copies, waits for them, and re-layouts  176 us (16%)
  starting transfers between devices  135 us (12%)
  matrix products  129 us (12%)
  waiting for transfers between devices  116 us (10%)
  other arithmetic  93.7 us (8%)
    pallas_call x6, Pallas kernels, route(): pl.pallas_call(functools.partial(_route_kernel, count, single), out_shape...  392 us
    dot_general x12, matrix products, mm_rows(): lax.dot_general(left, right, (((0,), (0,)), ((), ())), preferred_element_...  53.3 us
    dot_general x8, matrix products, mm_cols(): lax.dot_general(left, right, (((1,), (1,)), ((), ())), preferred_element_...  43.9 us
    ppermute x9, starting transfers between devices, total_over_seq(): lax.ppermute(to_right.astype(BF), 'seq', [(2 * z + y, 2 * z + 2 + y) for...  43.1 us
    ppermute x13, waiting for transfers between devices, over_x(): return lax.ppermute(value, 'head', swap_x)  37.1 us
    dot_general x7, matrix products, mm(): return jnp.dot(left, right, preferred_element_type=F32)  31.7 us
    unnamed x233, local copies, waits for them, and re-layouts  30 us
    dynamic_slice x4, local copies, waits for them, and re-layouts, pick(): return lax.dynamic_slice_in_dim(blocks, here ^ flip, 1, axis=2)  27.1 us
  transfers between devices with their start and end apart: 91, of which 19 were waited for; matrix products, arithmetic and copies ran while one was open for 32% of the time, Pallas kernels for 35%

profile of v1, /device:TPU:0, one launch (start us, length us, event | category | flops | bytes accessed | tf_op | source)
XLA Modules:
  0.0 1109.0 jit_solution(7310779122167890783)
XLA Ops:
  3.4 65.4 %route.6 = bf16[8,128,1024]{2,1,0:T(8,128)(2,1)} custom-call(s32[8]{0:T(128)} %get-tuple-element.222.dst_ref, bf16[8,128,1024]{2,1,0:T(8,128)(2,1)} %refs_0_.2), custom_call_target="tpu_custom_call" | custom-call | bytes 4194304 | tf_op jit(solution)/shard_map/route/pallas_call | solution.py:56
  71.7 6.0 collective-permute-start
  88.3 5.2 all-gather
  107.8 15.1 %collective-permute-done.3.refs_4_ = bf16[128,1024]{1,0:T(8,128)(2,1)} collective-permute-done((bf16[128,1024]{1,0:T(8,128)(2,1)}, bf16[128,1024]{1,0:T(8,128)(2,1)}, u32[]{:S(2)}, u32[]{:S(2)}) %collective-permute-start.3) | collective-permute-done | bytes 262176 | tf_op jit(solution)/shard_map/ppermute | solution.py:506
  125.4 65.4 %route.7 = bf16[8,128,1024]{2,1,0:T(8,128)(2,1)} custom-call(s32[8]{0:T(128)} %copy-done.70, bf16[128,1024]{1,0:T(8,128)(2,1)} %get-tuple-element.128.refs_0_, bf16[128,1024]{1,0:T(8,128)(2,1)} %collective-permute-done.refs_1_, bf16[128,1024]{1,0:T(8,128)(2,1)} %collective-permute-done.1.refs_2_, bf16[128,1024]{1,0:T(8,128)(2,1)} %collective-permute-done.2.refs_3_, ...), custom_call_target="tpu_custom_call" | custom-call | bytes 4194304 | tf_op jit(solution)/shard_map/route/pallas_call | solution.py:56
  194.5 23.2 %collective-permute-done.7.a1 = bf16[4,128,1024]{2,1,0:T(8,128)(2,1)S(1)} collective-permute-done((bf16[4,128,1024]{2,1,0:T(8,128)(2,1)S(1)}, bf16[4,128,1024]{2,1,0:T(8,128)(2,1)S(1)}, u32[]{:S(2)}, u32[]{:S(2)}) %collective-permute-start.7) | collective-permute-done | bytes 1048608 | tf_op jit(solution)/shard_map/ppermute | solution.py:379
  217.7 4.6 reshape.561
  222.3 7.4 constant_dynamic-slice_fusion.21
  258.8 5.5 fusion.qkv_ref
  264.3 24.2 %attend.1 = (bf16[1472,512]{1,0:T(8,128)(2,1)S(1)}, f32[4,8,1,512]{3,2,1,0:T(1,128)S(1)}) custom-call(s32[16]{0:T(128)S(1)} %concatenate.167.meta_ref, bf16[1472,1536]{1,0:T(8,128)(2,1)S(1)} %fusion.qkv_ref), custom_call_target="tpu_custom_call" | custom-call | flops 8589934592 | bytes 6291456 | tf_op jit(solution)/shard_map/attend/pallas_call | solution.py:186
  292.6 4.5 reshape.564
  297.1 8.2 constant_dynamic-slice_fusion.11
  305.2 5.7 pad_maximum_fusion.29
  312.7 65.4 %route.9 = bf16[8,128,1024]{2,1,0:T(8,128)(2,1)} custom-call(s32[8]{0:T(128)} %copy-done.70, bf16[8,128,1024]{2,1,0:T(8,128)(2,1)} %refs_0_.3), custom_call_target="tpu_custom_call" | custom-call | bytes 4194304 | tf_op jit(solution)/shard_map/route/pallas_call | solution.py:56
  386.3 4.5 reshape.567
  390.8 8.2 constant_dynamic-slice_fusion.7
  402.8 4.8 pad_maximum_fusion.31
  413.8 5.4 fusion.130
  419.2 9.0 multiply_convert_fusion.3
  432.3 5.6 collective-permute-done.24.a2
  450.8 8.4 convert_reduce_fusion.2
  459.2 8.8 convert_reduce_fusion.1
  468.1 4.5 convolution_convert_fusion.7
  476.0 6.6 fusion.26
  494.1 6.4 broadcast_select_fusion.13
  503.1 4.4 fusion.123
  513.6 5.0 broadcast_select_fusion.1
  523.2 4.4 convert_select_fusion.2
  544.2 8.3 multiply_reduce_fusion.1
  555.0 4.3 broadcast_select_fusion.3
  561.2 5.8 copy.52
  569.2 65.4 %route.8 = bf16[8,128,1024]{2,1,0:T(8,128)(2,1)} custom-call(s32[8]{0:T(128)} %get-tuple-element.50.dst_ref, bf16[128,1024]{1,0:T(8,128)(2,1)} %get-tuple-element.178.refs_0_, bf16[128,1024]{1,0:T(8,128)(2,1)} %get-tuple-element.177.refs_1_, bf16[128,1024]{1,0:T(8,128)(2,1)} %get-tuple-element.176.refs_2_, bf16[128,1024]{1,0:T(8,128)(2,1)} %get-tuple-element.175.refs_3_, ...), custom_call_target="tpu_custom_call" | custom-call | bytes 4194304 | tf_op jit(solution)/shard_map/route/pallas_call | solution.py:56
  634.6 7.0 convert_add_fusion
  646.8 25.0 %attend_back.1 = bf16[1472,1536]{1,0:T(8,128)(2,1)S(1)} custom-call(s32[16]{0:T(128)S(1)} %concatenate.167.meta_ref, bf16[1472,1536]{1,0:T(8,128)(2,1)} %copy-done.12, f32[4,8,1,512]{3,2,1,0:T(1,128)S(1)} %get-tuple-element.26.lse_ref, bf16[1472,512]{1,0:T(8,128)(2,1)S(1)} %pad_maximum_fusion.21.gctx_ref), custom_call_target="tpu_custom_call" | custom-call | flops 21474836480 | bytes 12582912 | tf_op jit(solution)/shard_map/attend_back/pallas_call | solution.py:257
  679.9 4.9 convolution_convert_fusion.3
  695.7 8.2 collective-permute-start.78
  710.9 4.7 collective-permute-start.79
  723.2 4.3 collective-permute-start.80
  743.7 5.6 convert_select_fusion.4
  755.2 5.5 broadcast_select_fusion.5
  766.0 5.2 collective-permute-start.63
  778.0 4.6 collective-permute-start.87
  792.1 5.0 pad_maximum_fusion.2
  797.1 5.1 reshape.570
  806.4 6.5 add_convert_fusion.mine_ref
  813.0 7.1 collective-permute-start.65
  822.2 13.9 %collective-permute-done.41 = bf16[256,3072]{1,0:T(8,128)(2,1)S(1)} collective-permute-done((bf16[256,3072]{1,0:T(8,128)(2,1)}, bf16[256,3072]{1,0:T(8,128)(2,1)S(1)}, u32[]{:S(2)}, u32[]{:S(2)}) %collective-permute-start.41) | collective-permute-done | bytes 1572896 | tf_op jit(solution)/shard_map/ppermute | solution.py:379
  838.7 5.6 collective-permute-done.68
  845.8 4.6 collective-permute-start.72
  855.6 5.4 collective-permute-done.45
  861.2 4.5 collective-permute-start.46
  876.0 4.4 collective-permute-done.47
  881.3 5.0 collective-permute-start.48
  893.7 7.8 collective-permute-done.51
  902.9 4.6 collective-permute-start.55
  916.2 65.4 %route.10 = bf16[8,128,1024]{2,1,0:T(8,128)(2,1)} custom-call(s32[8]{0:T(128)} %get-tuple-element.50.dst_ref, bf16[128,1024]{1,0:T(8,128)(2,1)} %get-tuple-element.170.refs_0_, bf16[128,1024]{1,0:T(8,128)(2,1)} %get-tuple-element.169.refs_1_, bf16[128,1024]{1,0:T(8,128)(2,1)} %get-tuple-element.168.refs_2_, bf16[128,1024]{1,0:T(8,128)(2,1)} %get-tuple-element.167.refs_3_, ...), custom_call_target="tpu_custom_call" | custom-call | bytes 4194304 | tf_op jit(solution)/shard_map/route/pallas_call | solution.py:56
  986.1 5.5 collective-permute-start.33
  991.6 5.2 collective-permute-done.54
  997.3 4.4 collective-permute-start.58
  1003.5 4.3 collective-permute-start.37
  1007.8 6.4 collective-permute-done.34.refs_3_
  1014.3 7.4 collective-permute-start.38
  1024.3 7.4 collective-permute-done.38.refs_7_
  1032.4 65.4 %route.11 = bf16[8,128,1024]{2,1,0:T(8,128)(2,1)} custom-call(s32[8]{0:T(128)} %select_reduce_fusion.dst_ref, bf16[128,1024]{1,0:T(8,128)(2,1)} %get-tuple-element.108.refs_0_, bf16[128,1024]{1,0:T(8,128)(2,1)} %collective-permute-done.32.refs_1_, bf16[128,1024]{1,0:T(8,128)(2,1)} %copy-done.57, bf16[128,1024]{1,0:T(8,128)(2,1)} %copy-done.58, ...), custom_call_target="tpu_custom_call" | custom-call | bytes 4194304 | tf_op jit(solution)/shard_map/route/pallas_call | solution.py:56
  (573 shorter events, 304.3 us)
Async XLA Ops:
  71.7 29.6 %collective-permute-start = (bf16[128,1024]{1,0:T(8,128)(2,1)}, bf16[128,1024]{1,0:T(8,128)(2,1)}, u32[]{:S(2)}, u32[]{:S(2)}) collective-permute-start(bf16[128,1024]{1,0:T(8,128)(2,1)} %get-tuple-element.127), channel_id=1, source_target_pairs={{0,28},{4,0},{8,4},{12,8},{16,12},{20,16},{24,20},{28,24},{1,29},{... | collective-permute-start | bytes 786440 | tf_op jit(solution)/shard_map/ppermute | solution.py:506
  77.7 25.5 %collective-permute-start.1 = (bf16[128,1024]{1,0:T(8,128)(2,1)}, bf16[128,1024]{1,0:T(8,128)(2,1)}, u32[]{:S(2)}, u32[]{:S(2)}) collective-permute-start(bf16[128,1024]{1,0:T(8,128)(2,1)} %get-tuple-element.126), channel_id=1, source_target_pairs={{0,24},{4,28},{8,0},{12,4},{16,8},{20,12},{24,16},{28,20},{1,25},{... | collective-permute-start | bytes 786440 | tf_op jit(solution)/shard_map/ppermute | solution.py:506
  78.2 28.1 %collective-permute-start.2 = (bf16[128,1024]{1,0:T(8,128)(2,1)}, bf16[128,1024]{1,0:T(8,128)(2,1)}, u32[]{:S(2)}, u32[]{:S(2)}) collective-permute-start(bf16[128,1024]{1,0:T(8,128)(2,1)} %get-tuple-element.125), channel_id=1, source_target_pairs={{0,20},{4,24},{8,28},{12,0},{16,4},{20,8},{24,12},{28,16},{1,21},{... | collective-permute-start | bytes 786440 | tf_op jit(solution)/shard_map/ppermute | solution.py:506
  78.2 44.7 %collective-permute-start.3 = (bf16[128,1024]{1,0:T(8,128)(2,1)}, bf16[128,1024]{1,0:T(8,128)(2,1)}, u32[]{:S(2)}, u32[]{:S(2)}) collective-permute-start(bf16[128,1024]{1,0:T(8,128)(2,1)} %get-tuple-element.124), channel_id=1, source_target_pairs={{0,16},{4,20},{8,24},{12,28},{16,0},{20,4},{24,8},{28,12},{1,17},{... | collective-permute-start | bytes 786440 | tf_op jit(solution)/shard_map/ppermute | solution.py:506
  81.2 41.9 %collective-permute-start.4 = (bf16[128,1024]{1,0:T(8,128)(2,1)}, bf16[128,1024]{1,0:T(8,128)(2,1)}, u32[]{:S(2)}, u32[]{:S(2)}) collective-permute-start(bf16[128,1024]{1,0:T(8,128)(2,1)} %get-tuple-element.123), channel_id=1, source_target_pairs={{0,12},{4,16},{8,20},{12,24},{16,28},{20,0},{24,4},{28,8},{1,13},{... | collective-permute-start | bytes 786440 | tf_op jit(solution)/shard_map/ppermute | solution.py:506
  101.3 23.2 %collective-permute-start.5 = (bf16[128,1024]{1,0:T(8,128)(2,1)}, bf16[128,1024]{1,0:T(8,128)(2,1)S(1)}, u32[]{:S(2)}, u32[]{:S(2)}) collective-permute-start(bf16[128,1024]{1,0:T(8,128)(2,1)} %get-tuple-element.122), channel_id=1, source_target_pairs={{0,8},{4,12},{8,16},{12,20},{16,24},{20,28},{24,0},{28,4},{1,9},{5... | collective-permute-start | bytes 786440 | tf_op jit(solution)/shard_map/ppermute | solution.py:506
  103.2 21.3 %collective-permute-start.6 = (bf16[128,1024]{1,0:T(8,128)(2,1)S(1)}, bf16[128,1024]{1,0:T(8,128)(2,1)S(1)}, u32[]{:S(2)}, u32[]{:S(2)}) collective-permute-start(bf16[128,1024]{1,0:T(8,128)(2,1)S(1)} %get-tuple-element.121), channel_id=1, source_target_pairs={{0,4},{4,8},{8,12},{12,16},{16,20},{20,24},{24,28},{28,0},{1,5},{5... | collective-permute-start | bytes 786440 | tf_op jit(solution)/shard_map/ppermute | solution.py:506
  106.3 111.5 %collective-permute-start.11 = (bf16[256,3072]{1,0:T(8,128)(2,1)}, bf16[256,3072]{1,0:T(8,128)(2,1)}, u32[]{:S(2)}, u32[]{:S(2)}) collective-permute-start(bf16[256,3072]{1,0:T(8,128)(2,1)} %param.24), channel_id=1, source_target_pairs={{0,2},{1,3},{2,0},{3,1},{4,6},{5,7},{6,4},{7,5},{8,10},{9,11},{10,... | collective-permute-start | bytes 4718600 | tf_op jit(solution)/shard_map/ppermute | solution.py:379
  122.9 115.5 %collective-permute-start.10 = (bf16[256,1536]{1,0:T(8,128)(2,1)}, bf16[256,1536]{1,0:T(8,128)(2,1)}, u32[]{:S(2)}, u32[]{:S(2)}) collective-permute-start(bf16[256,1536]{1,0:T(8,128)(2,1)} %reshape.560), channel_id=1, source_target_pairs={{0,1},{1,0},{2,3},{3,2},{4,5},{5,4},{6,7},{7,6},{8,9},{9,8},{10,11... | collective-permute-start | bytes 2359304 | tf_op jit(solution)/shard_map/ppermute | solution.py:382
  123.1 112.9 %collective-permute-start.13 = (bf16[256,1024]{1,0:T(8,128)(2,1)}, bf16[256,1024]{1,0:T(8,128)(2,1)}, u32[]{:S(2)}, u32[]{:S(2)}) collective-permute-start(bf16[256,1024]{1,0:T(8,128)(2,1)} %param.25), channel_id=1, source_target_pairs={{0,2},{1,3},{2,0},{3,1},{4,6},{5,7},{6,4},{7,5},{8,10},{9,11},{10,... | collective-permute-start | bytes 1572872 | tf_op jit(solution)/shard_map/ppermute | solution.py:379
  192.5 25.2 %collective-permute-start.7 = (bf16[4,128,1024]{2,1,0:T(8,128)(2,1)S(1)}, bf16[4,128,1024]{2,1,0:T(8,128)(2,1)S(1)}, u32[]{:S(2)}, u32[]{:S(2)}) collective-permute-start(bf16[4,128,1024]{2,1,0:T(8,128)(2,1)S(1)} %get-tuple-element.119), channel_id=1, source_target_pairs={{0,2},{1,3},{2,0},{3,1},{4,6},{5,7},{6,4},{7,5},{8,10},{9,11},{10,... | collective-permute-start | bytes 3145736 | tf_op jit(solution)/shard_map/ppermute | solution.py:379
  194.4 53.9 %collective-permute-start.8 = (bf16[4,128,1024]{2,1,0:T(8,128)(2,1)S(1)}, bf16[4,128,1024]{2,1,0:T(8,128)(2,1)S(1)}, u32[]{:S(2)}, u32[]{:S(2)}) collective-permute-start(bf16[4,128,1024]{2,1,0:T(8,128)(2,1)S(1)} %get-tuple-element.120.a0), channel_id=1, source_target_pairs={{0,1},{1,0},{2,3},{3,2},{4,5},{5,4},{6,7},{7,6},{8,9},{9,8},{10,11... | collective-permute-start | bytes 3145736 | tf_op jit(solution)/shard_map/ppermute | solution.py:382
  217.7 31.6 %collective-permute-start.9 = (bf16[4,128,1024]{2,1,0:T(8,128)(2,1)S(1)}, bf16[4,128,1024]{2,1,0:T(8,128)(2,1)}, u32[]{:S(2)}, u32[]{:S(2)}) collective-permute-start(bf16[4,128,1024]{2,1,0:T(8,128)(2,1)S(1)} %collective-permute-done.7.a1), channel_id=1, source_target_pairs={{0,1},{1,0},{2,3},{3,2},{4,5},{5,4},{6,7},{7,6},{8,9},{9,8},{10,11... | collective-permute-start | bytes 3145736 | tf_op jit(solution)/shard_map/ppermute | solution.py:382
  235.5 19.8 %collective-permute-start.12 = (bf16[256,1536]{1,0:T(8,128)(2,1)}, bf16[256,1536]{1,0:T(8,128)(2,1)}, u32[]{:S(2)}, u32[]{:S(2)}) collective-permute-start(bf16[256,1536]{1,0:T(8,128)(2,1)} %reshape.563), channel_id=1, source_target_pairs={{0,1},{1,0},{2,3},{3,2},{4,5},{5,4},{6,7},{7,6},{8,9},{9,8},{10,11... | collective-permute-start | bytes 2359304 | tf_op jit(solution)/shard_map/ppermute | solution.py:382
  236.0 150.3 %collective-permute-start.16 = (bf16[256,4096]{1,0:T(8,128)(2,1)}, bf16[256,4096]{1,0:T(8,128)(2,1)}, u32[]{:S(2)}, u32[]{:S(2)}) collective-permute-start(bf16[256,4096]{1,0:T(8,128)(2,1)} %param.26), channel_id=1, source_target_pairs={{0,2},{1,3},{2,0},{3,1},{4,6},{5,7},{6,4},{7,5},{8,10},{9,11},{10,... | collective-permute-start | bytes 6291464 | tf_op jit(solution)/shard_map/ppermute | solution.py:379
  292.5 106.4 %collective-permute-start.14 = (bf16[736,1024]{1,0:T(8,128)(2,1)}, bf16[736,1024]{1,0:T(8,128)(2,1)}, u32[]{:S(2)}, u32[]{:S(2)}) collective-permute-start(bf16[736,1024]{1,0:T(8,128)(2,1)} %convolution_convert_fusion.6), channel_id=1, source_target_pairs={{0,1},{1,0},{2,3},{3,2},{4,5},{5,4},{6,7},{7,6},{8,9},{9,8},{10,11... | collective-permute-start | bytes 4521992 | tf_op jit(solution)/shard_map/ppermute | solution.py:382
  312.2 97.2 %collective-permute-start.15 = (bf16[256,2048]{1,0:T(8,128)(2,1)}, bf16[256,2048]{1,0:T(8,128)(2,1)}, u32[]{:S(2)}, u32[]{:S(2)}) collective-permute-start(bf16[256,2048]{1,0:T(8,128)(2,1)} %bitcast.94), channel_id=1, source_target_pairs={{0,1},{1,0},{2,3},{3,2},{4,5},{5,4},{6,7},{7,6},{8,9},{9,8},{10,11... | collective-permute-start | bytes 3145736 | tf_op jit(solution)/shard_map/ppermute | solution.py:382
  312.7 98.5 %collective-permute-start.18 = (bf16[1024,1024]{1,0:T(8,128)(2,1)}, bf16[1024,1024]{1,0:T(8,128)(2,1)}, u32[]{:S(2)}, u32[]{:S(2)}) collective-permute-start(bf16[1024,1024]{1,0:T(8,128)(2,1)} %param.27), channel_id=1, source_target_pairs={{0,2},{1,3},{2,0},{3,1},{4,6},{5,7},{6,4},{7,5},{8,10},{9,11},{10,... | collective-permute-start | bytes 6291464 | tf_op jit(solution)/shard_map/ppermute | solution.py:379
  381.1 50.9 %collective-permute-start.23 = (bf16[4,128,1024]{2,1,0:T(8,128)(2,1)}, bf16[4,128,1024]{2,1,0:T(8,128)(2,1)}, u32[]{:S(2)}, u32[]{:S(2)}) collective-permute-start(bf16[4,128,1024]{2,1,0:T(8,128)(2,1)} %get-tuple-element.109), channel_id=1, source_target_pairs={{0,2},{1,3},{2,0},{3,1},{4,6},{5,7},{6,4},{7,5},{8,10},{9,11},{10,... | collective-permute-start | bytes 3145736 | tf_op jit(solution)/shard_map/ppermute | solution.py:379
  450.3 35.3 %collective-permute-start.21 = (bf16[736,1024]{1,0:T(8,128)(2,1)}, bf16[736,1024]{1,0:T(8,128)(2,1)S(1)}, u32[]{:S(2)}, u32[]{:S(2)}) collective-permute-start(bf16[736,1024]{1,0:T(8,128)(2,1)} %get-tuple-element.74.mine_ref), channel_id=1, source_target_pairs={{0,1},{1,0},{2,3},{3,2},{4,5},{5,4},{6,7},{7,6},{8,9},{9,8},{10,11... | collective-permute-start | bytes 4521992 | tf_op jit(solution)/shard_map/ppermute | solution.py:382
  472.6 71.7 %collective-permute-start.27 = (bf16[736,1024]{1,0:T(8,128)(2,1)}, bf16[736,1024]{1,0:T(8,128)(2,1)}, u32[]{:S(2)}, u32[]{:S(2)}) collective-permute-start(bf16[736,1024]{1,0:T(8,128)(2,1)} %convolution_convert_fusion.7), channel_id=1, source_target_pairs={{0,1},{1,0},{2,3},{3,2},{4,5},{5,4},{6,7},{7,6},{8,9},{9,8},{10,11... | collective-permute-start | bytes 4521992 | tf_op jit(solution)/shard_map/ppermute | solution.py:382
  475.6 18.5 %collective-permute-start.60 = (bf16[256,2048]{1,0:T(8,128)(2,1)}, bf16[256,2048]{1,0:T(8,128)(2,1)}, u32[]{:S(2)}, u32[]{:S(2)}) collective-permute-start(bf16[256,2048]{1,0:T(8,128)(2,1)} %convolution_convert_fusion), channel_id=1, source_target_pairs={{0,1},{1,0},{2,3},{3,2},{4,5},{5,4},{6,7},{7,6},{8,9},{9,8},{10,11... | collective-permute-start | bytes 3145736 | tf_op jit(solution)/shard_map/ppermute | solution.py:382
  482.6 152.0 %collective-permute-start.76 = (bf16[1024,1024]{1,0:T(8,128)(2,1)}, bf16[1024,1024]{1,0:T(8,128)(2,1)}, u32[]{:S(2)}, u32[]{:S(2)}) collective-permute-start(bf16[1024,1024]{1,0:T(8,128)(2,1)} %fusion.26), channel_id=1, source_target_pairs={{0,2},{1,3},{2,0},{3,1},{4,6},{5,7},{6,4},{7,5},{8,10},{9,11},{10,... | collective-permute-start | bytes 6291464 | tf_op jit(solution)/shard_map/ppermute | solution.py:379
  485.5 37.7 %collective-permute-start.59 = (bf16[256,2048]{1,0:T(8,128)(2,1)}, bf16[256,2048]{1,0:T(8,128)(2,1)}, u32[]{:S(2)}, u32[]{:S(2)}) collective-permute-start(bf16[256,2048]{1,0:T(8,128)(2,1)} %convolution_convert_fusion.2), channel_id=1, source_target_pairs={{0,1},{1,0},{2,3},{3,2},{4,5},{5,4},{6,7},{7,6},{8,9},{9,8},{10,11... | collective-permute-start | bytes 3145736 | tf_op jit(solution)/shard_map/ppermute | solution.py:382
  489.7 77.3 %collective-permute-start.22 = (bf16[4,128,1024]{2,1,0:T(8,128)(2,1)}, bf16[4,128,1024]{2,1,0:T(8,128)(2,1)}, u32[]{:S(2)}, u32[]{:S(2)}) collective-permute-start(bf16[4,128,1024]{2,1,0:T(8,128)(2,1)} %get-tuple-element.25), channel_id=1, source_target_pairs={{0,2},{1,3},{2,0},{3,1},{4,6},{5,7},{6,4},{7,5},{8,10},{9,11},{10,... | collective-permute-start | bytes 3145736 | tf_op jit(solution)/shard_map/ppermute | solution.py:379
  523.1 172.6 %collective-permute-start.61 = (bf16[256,4096]{1,0:T(8,128)(2,1)}, bf16[256,4096]{1,0:T(8,128)(2,1)}, u32[]{:S(2)}, u32[]{:S(2)}) collective-permute-start(bf16[256,4096]{1,0:T(8,128)(2,1)} %bitcast.116), channel_id=1, source_target_pairs={{0,2},{1,3},{2,0},{3,1},{4,6},{5,7},{6,4},{7,5},{8,10},{9,11},{10,... | collective-permute-start | bytes 6291464 | tf_op jit(solution)/shard_map/ppermute | solution.py:379
  554.9 88.0 %collective-permute-start.28 = (bf16[736,1024]{1,0:T(8,128)(2,1)S(1)}, bf16[736,1024]{1,0:T(8,128)(2,1)}, u32[]{:S(2)}, u32[]{:S(2)}) collective-permute-start(bf16[736,1024]{1,0:T(8,128)(2,1)S(1)} %get-tuple-element.54), channel_id=1, source_target_pairs={{0,1},{1,0},{2,3},{3,2},{4,5},{5,4},{6,7},{7,6},{8,9},{9,8},{10,11... | collective-permute-start | bytes 4521992 | tf_op jit(solution)/shard_map/ppermute | solution.py:382
  642.9 50.2 %collective-permute-start.77 = (bf16[512,1024]{1,0:T(8,128)(2,1)}, bf16[512,1024]{1,0:T(8,128)(2,1)}, u32[]{:S(2)}, u32[]{:S(2)}) collective-permute-start(bf16[512,1024]{1,0:T(8,128)(2,1)} %fusion.38), channel_id=1, source_target_pairs={{0,4},{4,0},{8,12},{12,8},{16,20},{20,16},{24,28},{28,24},{1,5},{5... | collective-permute-start | bytes 3145736 | tf_op jit(solution)/shard_map/ppermute | solution.py:297
  687.1 36.1 %collective-permute-start.40 = (bf16[256,1536]{1,0:T(8,128)(2,1)}, bf16[256,1536]{1,0:T(8,128)(2,1)}, u32[]{:S(2)}, u32[]{:S(2)}) collective-permute-start(bf16[256,1536]{1,0:T(8,128)(2,1)} %convolution_convert_fusion.3), channel_id=1, source_target_pairs={{0,1},{1,0},{2,3},{3,2},{4,5},{5,4},{6,7},{7,6},{8,9},{9,8},{10,11... | collective-permute-start | bytes 2359304 | tf_op jit(solution)/shard_map/ppermute | solution.py:382
  687.2 56.6 %collective-permute-start.39 = (bf16[256,1536]{1,0:T(8,128)(2,1)}, bf16[256,1536]{1,0:T(8,128)(2,1)}, u32[]{:S(2)}, u32[]{:S(2)}) collective-permute-start(bf16[256,1536]{1,0:T(8,128)(2,1)} %convolution_convert_fusion.5), channel_id=1, source_target_pairs={{0,1},{1,0},{2,3},{3,2},{4,5},{5,4},{6,7},{7,6},{8,9},{9,8},{10,11... | collective-permute-start | bytes 2359304 | tf_op jit(solution)/shard_map/ppermute | solution.py:382
  691.6 19.2 %collective-permute-start.42 = (bf16[256,1024]{1,0:T(8,128)(2,1)}, bf16[256,1024]{1,0:T(8,128)(2,1)}, u32[]{:S(2)}, u32[]{:S(2)}) collective-permute-start(bf16[256,1024]{1,0:T(8,128)(2,1)} %fusion.35), channel_id=1, source_target_pairs={{0,2},{1,3},{2,0},{3,1},{4,6},{5,7},{6,4},{7,5},{8,10},{9,11},{10,... | collective-permute-start | bytes 1572872 | tf_op jit(solution)/shard_map/ppermute | solution.py:379
  693.1 113.2 %collective-permute-start.29 = (bf16[736,1024]{1,0:T(8,128)(2,1)}, bf16[736,1024]{1,0:T(8,128)(2,1)}, u32[]{:S(2)}, u32[]{:S(2)}) collective-permute-start(bf16[736,1024]{1,0:T(8,128)(2,1)} %fusion.27), channel_id=1, source_target_pairs={{0,1},{1,0},{2,3},{3,2},{4,5},{5,4},{6,7},{7,6},{8,9},{9,8},{10,11... | collective-permute-start | bytes 4521992 | tf_op jit(solution)/shard_map/ppermute | solution.py:382
  695.7 14.4 %collective-permute-start.78 = (bf16[128,1024]{1,0:T(8,128)(2,1)S(1)}, bf16[128,1024]{1,0:T(8,128)(2,1)S(1)}, u32[]{:S(2)}, u32[]{:S(2)}) collective-permute-start(bf16[128,1024]{1,0:T(8,128)(2,1)S(1)} %get-tuple-element.87), channel_id=1, source_target_pairs={{0,8},{4,12},{1,9},{5,13},{2,10},{6,14},{3,11},{7,15}} | collective-permute-start | bytes 786440 | tf_op jit(solution)/shard_map/ppermute | solution.py:310
  719.0 45.4 %collective-permute-start.62 = (bf16[128,4096]{1,0:T(8,128)(2,1)}, bf16[128,4096]{1,0:T(8,128)(2,1)}, u32[]{:S(2)}, u32[]{:S(2)}) collective-permute-start(bf16[128,4096]{1,0:T(8,128)(2,1)} %fusion.37), channel_id=1, source_target_pairs={{0,4},{4,0},{8,12},{12,8},{16,20},{20,16},{24,28},{28,24},{1,5},{5... | collective-permute-start | bytes 3145736 | tf_op jit(solution)/shard_map/ppermute | solution.py:297
  721.9 40.0 %collective-permute-start.82 = (bf16[128,1024]{1,0:T(8,128)(2,1)}, bf16[128,1024]{1,0:T(8,128)(2,1)}, u32[]{:S(2)}, u32[]{:S(2)}) collective-permute-start(bf16[128,1024]{1,0:T(8,128)(2,1)} %get-tuple-element.86), channel_id=1, source_target_pairs={{16,8},{20,12},{24,16},{28,20},{17,9},{21,13},{25,17},{29,21},{18,... | collective-permute-start | bytes 786440 | tf_op jit(solution)/shard_map/ppermute | solution.py:315
  723.2 53.4 %collective-permute-start.80 = (bf16[128,1024]{1,0:T(8,128)(2,1)}, bf16[128,1024]{1,0:T(8,128)(2,1)S(1)}, u32[]{:S(2)}, u32[]{:S(2)}) collective-permute-start(bf16[128,1024]{1,0:T(8,128)(2,1)} %get-tuple-element.85), channel_id=1, source_target_pairs={{0,8},{4,12},{8,16},{12,20},{16,24},{20,28},{1,9},{5,13},{9,17},{1... | collective-permute-start | bytes 786440 | tf_op jit(solution)/shard_map/ppermute | solution.py:310
  766.0 16.6 %collective-permute-start.63 = (bf16[32,4096]{1,0:T(8,128)(2,1)S(1)}, bf16[32,4096]{1,0:T(8,128)(2,1)S(1)}, u32[]{:S(2)}, u32[]{:S(2)}) collective-permute-start(bf16[32,4096]{1,0:T(8,128)(2,1)S(1)} %get-tuple-element.93), channel_id=1, source_target_pairs={{0,8},{4,12},{1,9},{5,13},{2,10},{6,14},{3,11},{7,15}} | collective-permute-start | bytes 786440 | tf_op jit(solution)/shard_map/ppermute | solution.py:310
  775.3 26.9 %collective-permute-start.66 = (bf16[32,4096]{1,0:T(8,128)(2,1)S(1)}, bf16[32,4096]{1,0:T(8,128)(2,1)}, u32[]{:S(2)}, u32[]{:S(2)}) collective-permute-start(bf16[32,4096]{1,0:T(8,128)(2,1)S(1)} %get-tuple-element.94), channel_id=1, source_target_pairs={{24,16},{28,20},{25,17},{29,21},{26,18},{30,22},{27,19},{31,23}} | collective-permute-start | bytes 786440 | tf_op jit(solution)/shard_map/ppermute | solution.py:315
  776.7 25.8 %collective-permute-start.84 = (bf16[128,1024]{1,0:T(8,128)(2,1)S(1)}, bf16[128,1024]{1,0:T(8,128)(2,1)S(1)}, u32[]{:S(2)}, u32[]{:S(2)}) collective-permute-start(bf16[128,1024]{1,0:T(8,128)(2,1)S(1)} %fusion.67), channel_id=1, source_target_pairs={{8,0},{12,4},{16,8},{20,12},{24,16},{28,20},{9,1},{13,5},{17,9},{2... | collective-permute-start | bytes 786440 | tf_op jit(solution)/shard_map/ppermute | solution.py:331
  778.0 25.8 %collective-permute-start.87 = (bf16[128,1024]{1,0:T(8,128)(2,1)S(1)}, bf16[128,1024]{1,0:T(8,128)(2,1)S(1)}, u32[]{:S(2)}, u32[]{:S(2)}) collective-permute-start(bf16[128,1024]{1,0:T(8,128)(2,1)S(1)} %fusion.67), channel_id=1, source_target_pairs={{0,8},{4,12},{8,16},{12,20},{16,24},{20,28},{1,9},{5,13},{9,17},{1... | collective-permute-start | bytes 786440 | tf_op jit(solution)/shard_map/ppermute | solution.py:326
  782.7 21.8 %collective-permute-start.64 = (bf16[32,4096]{1,0:T(8,128)(2,1)S(1)}, bf16[32,4096]{1,0:T(8,128)(2,1)}, u32[]{:S(2)}, u32[]{:S(2)}) collective-permute-start(bf16[32,4096]{1,0:T(8,128)(2,1)S(1)} %fusion.70), channel_id=1, source_target_pairs={{0,8},{4,12},{8,16},{12,20},{1,9},{5,13},{9,17},{13,21},{2,10},{6,... | collective-permute-start | bytes 786440 | tf_op jit(solution)/shard_map/ppermute | solution.py:310
  802.2 33.9 %collective-permute-start.41 = (bf16[256,3072]{1,0:T(8,128)(2,1)}, bf16[256,3072]{1,0:T(8,128)(2,1)S(1)}, u32[]{:S(2)}, u32[]{:S(2)}) collective-permute-start(bf16[256,3072]{1,0:T(8,128)(2,1)} %reshape.571), channel_id=1, source_target_pairs={{0,2},{1,3},{2,0},{3,1},{4,6},{5,7},{6,4},{7,5},{8,10},{9,11},{10,... | collective-permute-start | bytes 4718600 | tf_op jit(solution)/shard_map/ppermute | solution.py:379
  803.8 16.4 %collective-permute-start.88 = (bf16[128,1024]{1,0:T(8,128)(2,1)S(1)}, bf16[128,1024]{1,0:T(8,128)(2,1)S(1)}, u32[]{:S(2)}, u32[]{:S(2)}) collective-permute-start(bf16[128,1024]{1,0:T(8,128)(2,1)S(1)} %collective-permute-done.87), channel_id=1, source_target_pairs={{8,16},{12,20},{16,24},{20,28},{9,17},{13,21},{17,25},{21,29},{10,... | collective-permute-start | bytes 786440 | tf_op jit(solution)/shard_map/ppermute | solution.py:326
  805.7 15.8 %collective-permute-start.67 = (bf16[32,4096]{1,0:T(8,128)(2,1)S(1)}, bf16[32,4096]{1,0:T(8,128)(2,1)S(1)}, u32[]{:S(2)}, u32[]{:S(2)}) collective-permute-start(bf16[32,4096]{1,0:T(8,128)(2,1)S(1)} %get-tuple-element.92), channel_id=1, source_target_pairs={{16,8},{20,12},{24,16},{28,20},{17,9},{21,13},{25,17},{29,21},{18,... | collective-permute-start | bytes 786440 | tf_op jit(solution)/shard_map/ppermute | solution.py:315
  812.9 78.1 %collective-permute-start.30 = (bf16[736,1024]{1,0:T(8,128)(2,1)S(1)}, bf16[736,1024]{1,0:T(8,128)(2,1)S(1)}, u32[]{:S(2)}, u32[]{:S(2)}) collective-permute-start(bf16[736,1024]{1,0:T(8,128)(2,1)S(1)} %add_convert_fusion.mine_ref), channel_id=1, source_target_pairs={{0,1},{1,0},{2,3},{3,2},{4,5},{5,4},{6,7},{7,6},{8,9},{9,8},{10,11... | collective-permute-start | bytes 4521992 | tf_op jit(solution)/shard_map/ppermute | solution.py:382
  813.0 25.6 %collective-permute-start.65 = (bf16[32,4096]{1,0:T(8,128)(2,1)S(1)}, bf16[32,4096]{1,0:T(8,128)(2,1)S(1)}, u32[]{:S(2)}, u32[]{:S(2)}) collective-permute-start(bf16[32,4096]{1,0:T(8,128)(2,1)S(1)} %get-tuple-element.91), channel_id=1, source_target_pairs={{0,8},{4,12},{8,16},{12,20},{16,24},{20,28},{1,9},{5,13},{9,17},{1... | collective-permute-start | bytes 786440 | tf_op jit(solution)/shard_map/ppermute | solution.py:310
  820.2 25.6 %collective-permute-start.86 = (bf16[128,1024]{1,0:T(8,128)(2,1)S(1)}, bf16[128,1024]{1,0:T(8,128)(2,1)S(1)}, u32[]{:S(2)}, u32[]{:S(2)}) collective-permute-start(bf16[128,1024]{1,0:T(8,128)(2,1)S(1)} %collective-permute-done.85), channel_id=1, source_target_pairs={{8,0},{12,4},{9,1},{13,5},{10,2},{14,6},{11,3},{15,7}} | collective-permute-start | bytes 786440 | tf_op jit(solution)/shard_map/ppermute | solution.py:331
  821.5 28.9 %collective-permute-start.89 = (bf16[128,1024]{1,0:T(8,128)(2,1)S(1)}, bf16[128,1024]{1,0:T(8,128)(2,1)S(1)}, u32[]{:S(2)}, u32[]{:S(2)}) collective-permute-start(bf16[128,1024]{1,0:T(8,128)(2,1)S(1)} %collective-permute-done.88), channel_id=1, source_target_pairs={{16,24},{20,28},{17,25},{21,29},{18,26},{22,30},{19,27},{23,31}} | collective-permute-start | bytes 786440 | tf_op jit(solution)/shard_map/ppermute | solution.py:326
  838.7 22.3 %collective-permute-start.45 = (bf16[128,4224]{1,0:T(8,128)(2,1)S(1)}, bf16[128,4224]{1,0:T(8,128)(2,1)S(1)}, u32[]{:S(2)}, u32[]{:S(2)}) collective-permute-start(bf16[128,4224]{1,0:T(8,128)(2,1)S(1)} %fusion.36), channel_id=1, source_target_pairs={{0,4},{4,0},{8,12},{12,8},{16,20},{20,16},{24,28},{28,24},{1,5},{5... | collective-permute-start | bytes 3244040 | tf_op jit(solution)/shard_map/ppermute | solution.py:297
  866.0 41.6 %collective-permute-start.90 = (bf16[512,1024]{1,0:T(8,128)(2,1)S(1)}, bf16[512,1024]{1,0:T(8,128)(2,1)S(1)}, u32[]{:S(2)}, u32[]{:S(2)}) collective-permute-start(bf16[512,1024]{1,0:T(8,128)(2,1)S(1)} %pad_maximum_fusion.36), channel_id=1, source_target_pairs={{0,4},{4,0},{8,12},{12,8},{16,20},{20,16},{24,28},{28,24},{1,5},{5... | collective-permute-start | bytes 3145736 | tf_op jit(solution)/shard_map/ppermute | solution.py:341
  886.4 15.2 %collective-permute-start.51 = (bf16[32,4224]{1,0:T(8,128)(2,1)S(1)}, bf16[32,4224]{1,0:T(8,128)(2,1)S(1)}, u32[]{:S(2)}, u32[]{:S(2)}) collective-permute-start(bf16[32,4224]{1,0:T(8,128)(2,1)S(1)} %fusion.57), channel_id=1, source_target_pairs={{8,0},{12,4},{16,8},{20,12},{24,16},{28,20},{9,1},{13,5},{17,9},{2... | collective-permute-start | bytes 811016 | tf_op jit(solution)/shard_map/ppermute | solution.py:315
  888.7 108.6 %collective-permute-start.75 = (bf16[128,4096]{1,0:T(8,128)(2,1)}, bf16[128,4096]{1,0:T(8,128)(2,1)}, u32[]{:S(2)}, u32[]{:S(2)}) collective-permute-start(bf16[128,4096]{1,0:T(8,128)(2,1)} %pad_maximum_fusion.35), channel_id=1, source_target_pairs={{0,4},{4,0},{8,12},{12,8},{16,20},{20,16},{24,28},{28,24},{1,5},{5... | collective-permute-start | bytes 3145736 | tf_op jit(solution)/shard_map/ppermute | solution.py:341
  893.1 22.1 %collective-permute-start.31 = (bf16[4,128,1024]{2,1,0:T(8,128)(2,1)S(1)}, bf16[4,128,1024]{2,1,0:T(8,128)(2,1)S(1)}, u32[]{:S(2)}, u32[]{:S(2)}) collective-permute-start(bf16[4,128,1024]{2,1,0:T(8,128)(2,1)S(1)} %get-tuple-element.28), channel_id=1, source_target_pairs={{0,2},{1,3},{2,0},{3,1},{4,6},{5,7},{6,4},{7,5},{8,10},{9,11},{10,... | collective-permute-start | bytes 3145736 | tf_op jit(solution)/shard_map/ppermute | solution.py:379
  910.8 70.8 %collective-permute-start.53 = (bf16[32,4224]{1,0:T(8,128)(2,1)S(1)}, bf16[32,4224]{1,0:T(8,128)(2,1)S(1)}, u32[]{:S(2)}, u32[]{:S(2)}) collective-permute-start(bf16[32,4224]{1,0:T(8,128)(2,1)S(1)} %collective-permute-done.52), channel_id=1, source_target_pairs={{8,0},{12,4},{16,8},{20,12},{9,1},{13,5},{17,9},{21,13},{10,2},{14... | collective-permute-start | bytes 811016 | tf_op jit(solution)/shard_map/ppermute | solution.py:331
  912.1 70.8 %collective-permute-start.56 = (bf16[32,4224]{1,0:T(8,128)(2,1)S(1)}, bf16[32,4224]{1,0:T(8,128)(2,1)S(1)}, u32[]{:S(2)}, u32[]{:S(2)}) collective-permute-start(bf16[32,4224]{1,0:T(8,128)(2,1)S(1)} %collective-permute-done.55), channel_id=1, source_target_pairs={{8,16},{12,20},{16,24},{20,28},{9,17},{13,21},{17,25},{21,29},{10,... | collective-permute-start | bytes 811016 | tf_op jit(solution)/shard_map/ppermute | solution.py:326
  981.6 15.2 %collective-permute-start.54 = (bf16[32,4224]{1,0:T(8,128)(2,1)S(1)}, bf16[32,4224]{1,0:T(8,128)(2,1)S(1)}, u32[]{:S(2)}, u32[]{:S(2)}) collective-permute-start(bf16[32,4224]{1,0:T(8,128)(2,1)S(1)} %collective-permute-done.53), channel_id=1, source_target_pairs={{8,0},{12,4},{9,1},{13,5},{10,2},{14,6},{11,3},{15,7}} | collective-permute-start | bytes 811016 | tf_op jit(solution)/shard_map/ppermute | solution.py:331
  986.0 17.4 %collective-permute-start.32 = (bf16[128,1024]{1,0:T(8,128)(2,1)S(1)}, bf16[128,1024]{1,0:T(8,128)(2,1)}, u32[]{:S(2)}, u32[]{:S(2)}) collective-permute-start(bf16[128,1024]{1,0:T(8,128)(2,1)S(1)} %get-tuple-element.107), channel_id=1, source_target_pairs={{0,4},{4,8},{8,12},{12,16},{16,20},{20,24},{24,28},{28,0},{1,5},{5... | collective-permute-start | bytes 786440 | tf_op jit(solution)/shard_map/ppermute | solution.py:637
  986.1 17.4 %collective-permute-start.33 = (bf16[128,1024]{1,0:T(8,128)(2,1)S(1)}, bf16[128,1024]{1,0:T(8,128)(2,1)S(1)}, u32[]{:S(2)}, u32[]{:S(2)}) collective-permute-start(bf16[128,1024]{1,0:T(8,128)(2,1)S(1)} %get-tuple-element.106), channel_id=1, source_target_pairs={{0,8},{4,12},{8,16},{12,20},{16,24},{20,28},{24,0},{28,4},{1,9},{5... | collective-permute-start | bytes 786440 | tf_op jit(solution)/shard_map/ppermute | solution.py:637
  996.8 17.4 %collective-permute-start.34 = (bf16[128,1024]{1,0:T(8,128)(2,1)S(1)}, bf16[128,1024]{1,0:T(8,128)(2,1)S(1)}, u32[]{:S(2)}, u32[]{:S(2)}) collective-permute-start(bf16[128,1024]{1,0:T(8,128)(2,1)S(1)} %get-tuple-element.105), channel_id=1, source_target_pairs={{0,12},{4,16},{8,20},{12,24},{16,28},{20,0},{24,4},{28,8},{1,13},{... | collective-permute-start | bytes 786440 | tf_op jit(solution)/shard_map/ppermute | solution.py:637
  996.8 27.4 %collective-permute-start.35 = (bf16[128,1024]{1,0:T(8,128)(2,1)S(1)}, bf16[128,1024]{1,0:T(8,128)(2,1)S(1)}, u32[]{:S(2)}, u32[]{:S(2)}) collective-permute-start(bf16[128,1024]{1,0:T(8,128)(2,1)S(1)} %get-tuple-element.104), channel_id=1, source_target_pairs={{0,16},{4,20},{8,24},{12,28},{16,0},{20,4},{24,8},{28,12},{1,17},{... | collective-permute-start | bytes 786440 | tf_op jit(solution)/shard_map/ppermute | solution.py:637
  997.3 100.5 %collective-permute-start.58 = (bf16[128,4224]{1,0:T(8,128)(2,1)S(1)}, bf16[128,4224]{1,0:T(8,128)(2,1)}, u32[]{:S(2)}, u32[]{:S(2)}) collective-permute-start(bf16[128,4224]{1,0:T(8,128)(2,1)S(1)} %pad_maximum_fusion.28), channel_id=1, source_target_pairs={{0,4},{4,0},{8,12},{12,8},{16,20},{20,16},{24,28},{28,24},{1,5},{5... | collective-permute-start | bytes 3244040 | tf_op jit(solution)/shard_map/ppermute | solution.py:341
  1003.4 20.8 %collective-permute-start.36 = (bf16[128,1024]{1,0:T(8,128)(2,1)S(1)}, bf16[128,1024]{1,0:T(8,128)(2,1)S(1)}, u32[]{:S(2)}, u32[]{:S(2)}) collective-permute-start(bf16[128,1024]{1,0:T(8,128)(2,1)S(1)} %get-tuple-element.103), channel_id=1, source_target_pairs={{0,20},{4,24},{8,28},{12,0},{16,4},{20,8},{24,12},{28,16},{1,21},{... | collective-permute-start | bytes 786440 | tf_op jit(solution)/shard_map/ppermute | solution.py:637
  1003.5 20.7 %collective-permute-start.37 = (bf16[128,1024]{1,0:T(8,128)(2,1)S(1)}, bf16[128,1024]{1,0:T(8,128)(2,1)S(1)}, u32[]{:S(2)}, u32[]{:S(2)}) collective-permute-start(bf16[128,1024]{1,0:T(8,128)(2,1)S(1)} %get-tuple-element.102), channel_id=1, source_target_pairs={{0,24},{4,28},{8,0},{12,4},{16,8},{20,12},{24,16},{28,20},{1,25},{... | collective-permute-start | bytes 786440 | tf_op jit(solution)/shard_map/ppermute | solution.py:637
  1014.3 17.4 %collective-permute-start.38 = (bf16[128,1024]{1,0:T(8,128)(2,1)S(1)}, bf16[128,1024]{1,0:T(8,128)(2,1)S(1)}, u32[]{:S(2)}, u32[]{:S(2)}) collective-permute-start(bf16[128,1024]{1,0:T(8,128)(2,1)S(1)} %get-tuple-element.101), channel_id=1, source_target_pairs={{0,28},{4,0},{8,4},{12,8},{16,12},{20,16},{24,20},{28,24},{1,29},{... | collective-permute-start | bytes 786440 | tf_op jit(solution)/shard_map/ppermute | solution.py:637
  (126 other events, 1659.1 us)

commit v2 on v1

v2 whole, which is shorter than its diff:
```python
import functools
import itertools

import jax
import jax.numpy as jnp
import numpy as np
from jax import lax
from jax.experimental import pallas as pl
from jax.experimental.pallas import tpu as pltpu
from jax.sharding import PartitionSpec as P

HEAD_SIZE = 64
CAP = 1536
HALF = CAP // 2
EPS = 1e-12
BF = jnp.bfloat16
F32 = jnp.float32
VMEM_SPEC = pl.BlockSpec(memory_space=pltpu.VMEM)
SMEM_SPEC = pl.BlockSpec(memory_space=pltpu.SMEM)
ANY_SPEC = pl.BlockSpec(memory_space=pl.ANY)
LIGHT = pl.CostEstimate(flops=0, bytes_accessed=1024, transcendentals=0)


def after(value, *others):
    return lax.optimization_barrier((value, *others))[0]


def mm(left, right):
    return jnp.dot(left, right, preferred_element_type=F32)


def mm_rows(left, right):
    return lax.dot_general(left, right, (((0,), (0,)), ((), ())), preferred_element_type=F32)


def mm_cols(left, right):
    return lax.dot_general(left, right, (((1,), (1,)), ((), ())), preferred_element_type=F32)


def _route_kernel(count, single, dst_ref, *refs):
    out_ref = refs[-1]
    for k in range(count):
        out_ref[dst_ref[k]] = refs[0][k] if single else refs[k][...]


def route(blocks, dst):
    single = not isinstance(blocks, (list, tuple))
    args = [blocks] if single else list(blocks)
    count = args[0].shape[0] if single else len(args)
    shape = args[0].shape[1:] if single else args[0].shape
    return pl.pallas_call(
        functools.partial(_route_kernel, count, single),
        out_shape=jax.ShapeDtypeStruct((count,) + shape, args[0].dtype),
        in_specs=[SMEM_SPEC] + [VMEM_SPEC] * len(args),
        out_specs=VMEM_SPEC,
        compiler_params=pltpu.CompilerParams(vmem_limit_bytes=24 << 20),
        cost_estimate=LIGHT,
        name="route",
    )(dst, *args)


def _pack_kernel(meta_ref, a0, a1, a2, a3, out_ref):
    here = meta_ref[12]
    out_ref[...] = jnp.zeros_like(out_ref)
    for slot in range(4):
        offset, length = meta_ref[slot], meta_ref[4 + slot]
        for src, flip in ((a0, 0), (a1, 2), (a2, 1), (a3, 3)):
            start = (here ^ flip) * 128
            pieces = jnp.clip((length - start + 15) // 16, 0, 8)

            @pl.loop(0, pieces)
            def _(i):
                row = pl.multiple_of(offset + start + i * 16, 16)
                out_ref[pl.ds(row, 16), :] = src[slot, pl.ds(pl.multiple_of(i * 16, 16), 16), :]


def pack(meta, own, from_x, from_core, from_both):
    return pl.pallas_call(
        _pack_kernel,
        out_shape=jax.ShapeDtypeStruct((CAP, own.shape[-1]), own.dtype),
        in_specs=[SMEM_SPEC] + [VMEM_SPEC] * 4,
        out_specs=VMEM_SPEC,
        compiler_params=pltpu.CompilerParams(vmem_limit_bytes=24 << 20),
        cost_estimate=LIGHT,
        name="pack",
    )(meta, own, from_x, from_core, from_both)


def _unpack_kernel(meta_ref, mine_ref, other_ref, own_ref, far_ref, rows_ref, sems):
    here, core = meta_ref[12], meta_ref[13]
    first = pltpu.make_async_copy(
        mine_ref, rows_ref.at[pl.ds(pl.multiple_of(core * HALF, 16), HALF)], sems.at[0]
    )
    second = pltpu.make_async_copy(
        other_ref, rows_ref.at[pl.ds(pl.multiple_of((1 - core) * HALF, 16), HALF)], sems.at[1]
    )
    first.start()
    second.start()
    first.wait()
    second.wait()
    width = rows_ref.shape[1]
    for slot in range(4):
        offset, length = meta_ref[slot], meta_ref[4 + slot]
        for dst, flip in ((own_ref, 0), (far_ref, 2)):
            start = (here ^ flip) * 128

            @pl.loop(0, 8)
            def _(i):
                position = start + i * 16
                row = pl.multiple_of(jnp.minimum(offset + position, CAP - 16), 16)
                keep = lax.broadcasted_iota(jnp.int32, (16, width), 0) + position < length
                part = rows_ref[pl.ds(row, 16), :].astype(F32)
                dst[slot, pl.ds(pl.multiple_of(i * 16, 16), 16), :] = jnp.where(
                    keep, part, 0.0
                ).astype(BF)


def unpack(meta, mine, other):
    width = mine.shape[1]
    shape = jax.ShapeDtypeStruct((4, 128, width), BF)
    return pl.pallas_call(
        _unpack_kernel,
        out_shape=(shape, shape),
        in_specs=[SMEM_SPEC, ANY_SPEC, ANY_SPEC],
        out_specs=(VMEM_SPEC, VMEM_SPEC),
        scratch_shapes=[pltpu.VMEM((CAP, width), BF), pltpu.SemaphoreType.DMA((2,))],
        compiler_params=pltpu.CompilerParams(vmem_limit_bytes=24 << 20),
        cost_estimate=LIGHT,
        name="unpack",
    )(meta, mine, other)


def _attend_kernel(meta_ref, qkv_ref, ctx_ref, lse_ref):
    ctx_ref[...] = jnp.zeros_like(ctx_ref)
    width = ctx_ref.shape[1]
    part = width // 2

    def one(slot, blocks):
        span = blocks * 128
        offset = pl.multiple_of(meta_ref[slot], 16)
        length = meta_ref[4 + slot]
        rows = pl.ds(offset, span)
        key_id = lax.broadcasted_iota(jnp.int32, (span, 1), 0)
        key_bias = jnp.where(key_id < length, 0.0, -1e30)

        @pl.loop(0, width // 128)
        def _(pair):
            lane0 = pl.multiple_of((pair // 2) * (3 * part) + (pair % 2) * 128, 128)
            keys = qkv_ref[rows, pl.ds(pl.multiple_of(part + lane0, 128), 128)]
            values = qkv_ref[rows, pl.ds(pl.multiple_of(2 * part + lane0, 128), 128)]
            values_t = values.astype(F32).T.astype(BF)
            for first in range(0, span, 256):
                step = min(span - first, 256)
                queries = qkv_ref[
                    pl.ds(pl.multiple_of(offset + first, 16), step), pl.ds(lane0, 128)
                ]
                queries = queries * jnp.asarray(HEAD_SIZE**-0.5, BF)
                lane = lax.broadcasted_iota(jnp.int32, (step, 128), 1)
                parts = []
                for half in range(2):
                    picked = jnp.where((lane >= 64) == (half == 1), queries, jnp.zeros_like(queries))
                    scores = mm_cols(keys, picked)
                    scores = scores + key_bias
                    highest = jnp.max(scores, axis=0, keepdims=True)
                    expo = jnp.exp(scores - highest)
                    total = jnp.sum(expo, axis=0, keepdims=True)
                    weighted = mm(values_t[64 * half : 64 * half + 64], expo.astype(BF))
                    parts.append(weighted * (1.0 / total))
                    lse_ref[slot, pair * 2 + half, :, first : first + step] = highest + jnp.log(total)
                mixed = jnp.concatenate(parts, axis=0).T
                out_lane = pl.multiple_of(pair * 128, 128)
                ctx_ref[pl.ds(pl.multiple_of(offset + first, 16), step), pl.ds(out_lane, 128)] = (
                    mixed.astype(BF)
                )

    @pl.loop(0, 4)
    def _(slot):
        for blocks in range(1, 5):
            pl.when(meta_ref[8 + slot] == blocks)(functools.partial(one, slot, blocks))


def attend(meta, qkv):
    width = qkv.shape[1] // 3
    return pl.pallas_call(
        _attend_kernel,
        out_shape=(
            jax.ShapeDtypeStruct((CAP, width), BF),
            jax.ShapeDtypeStruct((4, width // HEAD_SIZE, 1, 512), F32),
        ),
        in_specs=[SMEM_SPEC, VMEM_SPEC],
        out_specs=(VMEM_SPEC, VMEM_SPEC),
        compiler_params=pltpu.CompilerParams(vmem_limit_bytes=24 << 20),
        cost_estimate=LIGHT,
        name="attend",
    )(meta, qkv)


def _attend_back_kernel(block, meta_ref, qkv_ref, lse_ref, gctx_ref, out_ref):
    out_ref[...] = jnp.zeros_like(out_ref)
    part = out_ref.shape[1] // 3

    def one(slot, blocks):
        span = blocks * 128
        offset = pl.multiple_of(meta_ref[slot], 16)
        length = meta_ref[4 + slot]
        rows = pl.ds(offset, span)
        key_id = lax.broadcasted_iota(jnp.int32, (span, 1), 0)
        key_bias = jnp.where(key_id < length, 0.0, -1e30)

        @pl.loop(0, part // 128)
        def _(turn):
            pair = block * (part // 128) + turn
            out_lane = pl.multiple_of(turn * 128, 128)
            base = block * 3 * part
            lane0 = pl.multiple_of(base + turn * 128, 128)
            ctx_lane = pl.multiple_of(block * part + turn * 128, 128)
            keys = qkv_ref[rows, pl.ds(pl.multiple_of(part + lane0, 128), 128)]
            values = qkv_ref[rows, pl.ds(pl.multiple_of(2 * part + lane0, 128), 128)]
            keys_t = keys.astype(F32).T.astype(BF)
            grad_keys = jnp.zeros((span, 128), F32)
            grad_values = jnp.zeros((span, 128), F32)
            for first in range(0, span, 256):
                step = min(span - first, 256)
                here = pl.ds(pl.multiple_of(offset + first, 16), step)
                queries = qkv_ref[here, pl.ds(lane0, 128)] * jnp.asarray(HEAD_SIZE**-0.5, BF)
                grad_ctx = gctx_ref[here, pl.ds(ctx_lane, 128)]
                lane = lax.broadcasted_iota(jnp.int32, (step, 128), 1)
                row = lax.broadcasted_iota(jnp.int32, (step, 128), 0) + first
                grad_ctx = jnp.where(row < length, grad_ctx, jnp.zeros_like(grad_ctx))
                parts = []
                for half in range(2):
                    side = (lane >= 64) == (half == 1)
                    picked = jnp.where(side, queries, jnp.zeros_like(queries))
                    picked_grad = jnp.where(side, grad_ctx, jnp.zeros_like(grad_ctx))
                    scores = mm_cols(keys, picked)
                    log_total = lse_ref[slot, pair * 2 + half, :, first : first + step]
                    probs = jnp.exp(scores - log_total + key_bias)
                    grad_values = grad_values + mm(probs.astype(BF), picked_grad)
                    grad_probs = mm_cols(values, picked_grad)
                    inner = jnp.sum(probs * grad_probs, axis=0, keepdims=True)
                    grad_scores = (probs * (grad_probs - inner)).astype(BF)
                    grad_keys = grad_keys + mm(grad_scores, picked)
                    parts.append(mm(keys_t[64 * half : 64 * half + 64], grad_scores))
                grad_queries = jnp.concatenate(parts, axis=0).T * HEAD_SIZE**-0.5
                out_ref[here, pl.ds(out_lane, 128)] = grad_queries.astype(BF)
            key_lane = pl.multiple_of(part + out_lane, 128)
            value_lane = pl.multiple_of(2 * part + out_lane, 128)
            out_ref[rows, pl.ds(key_lane, 128)] = grad_keys.astype(BF)
            out_ref[rows, pl.ds(value_lane, 128)] = grad_values.astype(BF)

    @pl.loop(0, 4)
    def _(slot):
        for blocks in range(1, 5):
            pl.when(meta_ref[8 + slot] == blocks)(functools.partial(one, slot, blocks))


def attend_back(meta, qkv, lse, grad_ctx, block):
    return pl.pallas_call(
        functools.partial(_attend_back_kernel, block),
        out_shape=jax.ShapeDtypeStruct((qkv.shape[0], qkv.shape[1] // 2), BF),
        in_specs=[SMEM_SPEC] + [VMEM_SPEC] * 3,
        out_specs=VMEM_SPEC,
        compiler_params=pltpu.CompilerParams(vmem_limit_bytes=24 << 20),
        cost_estimate=LIGHT,
        name="attend_back",
    )(meta, qkv, lse, grad_ctx)


def _assemble_kernel(kinds, meta_ref, *refs):
    out_ref = refs[-1]
    here, core = meta_ref[12], meta_ref[13]
    rows, columns = refs[0].shape
    block = columns // (4 * kinds)
    for flip, src in zip((0, 2, 1, 3), refs[:4]):
        place = pl.ds(pl.multiple_of((here ^ flip) * rows, 16), rows)
        for kind in range(kinds):
            for side in range(2):
                lane = pl.multiple_of((kind * 4 + core + 2 * side) * block, 128)
                spot = (side * kinds + kind) * block
                out_ref[place, spot : spot + block] = src[:, pl.ds(lane, block)]


def assemble(meta, kinds, own, from_x, from_core, from_both):
    rows, columns = own.shape
    return pl.pallas_call(
        functools.partial(_assemble_kernel, kinds),
        out_shape=jax.ShapeDtypeStruct((4 * rows, columns // 2), BF),
        in_specs=[SMEM_SPEC] + [VMEM_SPEC] * 4,
        out_specs=VMEM_SPEC,
        compiler_params=pltpu.CompilerParams(vmem_limit_bytes=24 << 20),
        cost_estimate=LIGHT,
        name="assemble",
    )(meta, own, from_x, from_core, from_both)


def _spread_kernel(kinds, sides, meta_ref, *refs):
    out_ref = refs[-1]
    core = meta_ref[13]
    block = out_ref.shape[1] // (4 * kinds)
    for flip in range(2):
        for kind in range(kinds):
            for side in range(2):
                lane = pl.multiple_of((kind * 4 + (core ^ flip) + 2 * side) * block, 128)
                if sides:
                    src, spot = refs[2 * side + flip], kind * block
                else:
                    src, spot = refs[flip], (side * kinds + kind) * block
                out_ref[:, pl.ds(lane, block)] = src[:, spot : spot + block].astype(F32)


def spread_columns(meta, kinds, columns, *blocks):
    return pl.pallas_call(
        functools.partial(_spread_kernel, kinds, len(blocks) == 4),
        out_shape=jax.ShapeDtypeStruct((blocks[0].shape[0], columns), F32),
        in_specs=[SMEM_SPEC] + [VMEM_SPEC] * len(blocks),
        out_specs=VMEM_SPEC,
        compiler_params=pltpu.CompilerParams(vmem_limit_bytes=24 << 20),
        cost_estimate=LIGHT,
        name="spread_columns",
    )(meta, *blocks)


def _stack_kernel(place, meta_ref, mine_ref, other_ref, out_ref):
    spot = meta_ref[place]
    rows = mine_ref.shape[0]
    mine_at = pl.multiple_of(spot * rows, 16)
    other_at = pl.multiple_of((1 - spot) * rows, 16)
    out_ref[pl.ds(mine_at, rows), :] = mine_ref[...].astype(out_ref.dtype)
    out_ref[pl.ds(other_at, rows), :] = other_ref[...].astype(out_ref.dtype)


def stack_rows(meta, place, mine, other, kind=F32):
    return pl.pallas_call(
        functools.partial(_stack_kernel, place),
        out_shape=jax.ShapeDtypeStruct((2 * mine.shape[0], mine.shape[1]), kind),
        in_specs=[SMEM_SPEC] + [VMEM_SPEC] * 2,
        out_specs=VMEM_SPEC,
        compiler_params=pltpu.CompilerParams(vmem_limit_bytes=24 << 20),
        cost_estimate=LIGHT,
        name="stack_rows",
    )(meta, mine, other)


def _merge_kernel(meta_ref, own_ref, up_ref, mine_ref, other_ref, down_out, up_out):
    here_y, chip = meta_ref[14], meta_ref[18]
    rows, share = own_ref.shape[0], own_ref.shape[0] // 8
    lines = up_ref.shape[0] // 4
    width = own_ref.shape[1]
    size = mine_ref.shape[0] // 4
    down_out[pl.ds(pl.multiple_of(chip * rows, 16), rows), :] = own_ref[...]
    up_out[4 * lines :, :] = up_ref[...]
    for src, y in ((mine_ref, here_y), (other_ref, 1 - here_y)):
        for turn in range(4):
            at = (1 - chip) * rows + (y * 4 + turn) * share
            down_out[pl.ds(pl.multiple_of(at, 16), share), :] = src[
                turn * size : turn * size + share, :
            ]
            line = pl.multiple_of((y * 4 + turn) * (lines // 2), 16)
            for column in range(4):
                first = turn * size + share + column * (lines // 2)
                up_out[pl.ds(line, lines // 2), column * width : (column + 1) * width] = src[
                    first : first + lines // 2, :
                ]


def merge_shares(meta, w_down, far_up_high, mine, other):
    rows, width = w_down.shape
    return pl.pallas_call(
        _merge_kernel,
        out_shape=(
            jax.ShapeDtypeStruct((2 * rows, width), BF),
            jax.ShapeDtypeStruct((2 * far_up_high.shape[0], far_up_high.shape[1]), BF),
        ),
        in_specs=[SMEM_SPEC] + [VMEM_SPEC] * 4,
        out_specs=(VMEM_SPEC, VMEM_SPEC),
        compiler_params=pltpu.CompilerParams(vmem_limit_bytes=24 << 20),
        cost_estimate=LIGHT,
        name="merge_shares",
    )(meta, w_down, far_up_high, mine, other)


TILE = 256


def _tiles(meta_ref, count_at, out_refs, body):
    rows = out_refs[0].shape[0]
    used = jnp.minimum((meta_ref[count_at] + TILE - 1) // TILE, rows // TILE)

    @pl.loop(0, used)
    def _(tile):
        body(pl.ds(pl.multiple_of(tile * TILE, TILE), TILE))

    @pl.loop(used, rows // TILE)
    def _(tile):
        for out_ref in out_refs:
            place = pl.ds(pl.multiple_of(tile * TILE, TILE), TILE)
            out_ref[place, :] = jnp.zeros((TILE, out_ref.shape[1]), out_ref.dtype)


def _up_kernel(count_at, meta_ref, low_ref, weight_ref, bias_ref, act_ref, slope_ref):
    width = act_ref.shape[1]
    step = 512

    def body(place):
        @pl.loop(0, width // step)
        def _(turn):
            lanes = pl.ds(pl.multiple_of(turn * step, step), step)
            pre = mm(low_ref[place, :], weight_ref[:, lanes]) + bias_ref[:, lanes]
            cdf = 0.5 * (1.0 + lax.erf(pre * np.float32(0.5**0.5)))
            slope = cdf + pre * jnp.exp(-0.5 * pre * pre) * np.float32((2 * np.pi) ** -0.5)
            act_ref[place, lanes] = (pre * cdf).astype(BF)
            slope_ref[place, lanes] = slope.astype(BF)

    _tiles(meta_ref, count_at, (act_ref, slope_ref), body)


def up_product(meta, count_at, low, weight, bias):
    shape = jax.ShapeDtypeStruct((low.shape[0], weight.shape[1]), BF)
    return pl.pallas_call(
        functools.partial(_up_kernel, count_at),
        out_shape=(shape, shape),
        in_specs=[SMEM_SPEC] + [VMEM_SPEC] * 3,
        out_specs=(VMEM_SPEC, VMEM_SPEC),
        compiler_params=pltpu.CompilerParams(vmem_limit_bytes=24 << 20),
        cost_estimate=LIGHT,
        name="up_product",
    )(meta, low, weight, bias)


def _rows_kernel(count_at, turned, terms, scaled, meta_ref, *refs):
    lefts, rights = refs[:terms], refs[terms : 2 * terms]
    out_ref = refs[2 * terms + scaled]
    width = out_ref.shape[1]
    step = min(512, width)

    def body(place):
        @pl.loop(0, width // step)
        def _(turn):
            lanes = pl.ds(pl.multiple_of(turn * step, step), step)
            total = None
            for left_ref, right_ref in zip(lefts, rights):
                left = left_ref[place, :]
                if turned:
                    term = mm_cols(left, right_ref[lanes, :])
                else:
                    term = mm(left, right_ref[:, lanes])
                total = term if total is None else total + term
            if scaled:
                total = total * refs[2 * terms][place, lanes].astype(F32)
            out_ref[place, lanes] = total.astype(out_ref.dtype)

    _tiles(meta_ref, count_at, (out_ref,), body)


def rows_product(meta, count_at, lefts, rights, turned, kind, scale=None):
    width = rights[0].shape[0] if turned else rights[0].shape[1]
    args = [*lefts, *rights] + ([] if scale is None else [scale])
    return pl.pallas_call(
        functools.partial(_rows_kernel, count_at, turned, len(lefts), int(scale is not None)),
        out_shape=jax.ShapeDtypeStruct((lefts[0].shape[0], width), kind),
        in_specs=[SMEM_SPEC] + [VMEM_SPEC] * len(args),
        out_specs=VMEM_SPEC,
        compiler_params=pltpu.CompilerParams(vmem_limit_bytes=24 << 20),
        cost_estimate=LIGHT,
        name="rows_product",
    )(meta, *args)


def _grad_kernel(terms, meta_ref, at_ref, *refs):
    lefts, rights = refs[:terms], refs[terms : 2 * terms]
    out_ref, turned_ref = refs[2 * terms :]
    count, width = out_ref.shape
    first = 0
    for left_ref in lefts:
        rows = left_ref.shape[0]
        piece = left_ref[:, pl.ds(pl.multiple_of(at_ref[0], 128), count)]
        turned_ref[:, first : first + rows] = piece.astype(F32).T.astype(BF)
        first += rows
    step = 256

    @pl.loop(0, width // step)
    def _(turn):
        lanes = pl.ds(pl.multiple_of(turn * step, step), step)
        total, start = None, 0
        for right_ref in rights:
            rows = right_ref.shape[0]
            term = mm(turned_ref[:, start : start + rows], right_ref[:, lanes])
            total = term if total is None else total + term
            start += rows
        out_ref[:, lanes] = total.astype(out_ref.dtype)


def grad_product(meta, lefts, rights, start, count, kind):
    rows = sum(left.shape[0] for left in lefts)
    args = [*lefts, *rights]
    return pl.pallas_call(
        functools.partial(_grad_kernel, len(lefts)),
        out_shape=jax.ShapeDtypeStruct((count, rights[0].shape[1]), kind),
        in_specs=[SMEM_SPEC, SMEM_SPEC] + [VMEM_SPEC] * len(args),
        out_specs=VMEM_SPEC,
        scratch_shapes=[pltpu.VMEM((count, rows), BF)],
        compiler_params=pltpu.CompilerParams(vmem_limit_bytes=24 << 20),
        cost_estimate=LIGHT,
        name="grad_product",
    )(meta, jnp.asarray(start, jnp.int32)[None], *args)


def normed(inputs):
    average = jnp.mean(inputs, axis=-1, keepdims=True)
    centered = inputs - average
    variance = jnp.mean(centered * centered, axis=-1, keepdims=True)
    rstd = lax.rsqrt(variance + EPS)
    return centered * rstd, rstd


def norm_back(unit, rstd, grad, gain):
    scaled = grad * gain
    return (
        scaled
        - jnp.mean(scaled, axis=-1, keepdims=True)
        - unit * jnp.mean(scaled * unit, axis=-1, keepdims=True)
    ) * rstd


SWAP_X = [(i, i ^ 2) for i in range(4)]
SWAP_Y = [(i, i ^ 1) for i in range(8)]
SWAP_Z1 = [(i, i ^ 2) for i in range(8)]
SWAP_Z2 = [(i, i ^ 4) for i in range(8)]
AT_Y, AT_Z1, AT_Z2 = 14, 16, 17
MINE, OTHER = 19, 20


def moved(name, value, axis, pairs):
    with jax.named_scope(name):
        return lax.ppermute(value, axis, pairs)


class SeqSum:
    def __init__(self, name, meta, group_count):
        self.name, self.meta, self.whole = name, meta, group_count == 8
        index = lax.axis_index("seq")
        self.bits = {AT_Y: index % 2, AT_Z1: index // 2 % 2, AT_Z2: index // 4 % 2}

    def send(self, step, value, axis, pairs):
        self.token = value
        self.arrived = moved(f"{self.name}_{step}", value, axis, pairs)

    def start_x(self, far, own):
        self.kept = own[None]
        self.send("x", far.astype(BF), "head", SWAP_X)

    def start_y(self, far, kept):
        self.kept = kept
        self.send("y", far.astype(BF), "seq", SWAP_Y)

    def added(self, gates):
        arrived = after(self.arrived, *gates).astype(F32)
        self.kept = self.kept + arrived.reshape(self.kept.shape)

    def split(self, step, place, pairs):
        blocks, rows, columns = self.kept.shape
        halves = self.kept.reshape(blocks, 2, rows // 2, columns)
        bit = self.bits[place]
        self.kept = lax.dynamic_index_in_dim(halves, bit, 1, keepdims=False)
        sent = lax.dynamic_index_in_dim(halves, 1 - bit, 1, keepdims=False)
        self.send(step, sent.astype(BF).reshape(-1, columns), "seq", pairs)

    def step_y(self, *gates):
        self.added(gates)
        if self.whole:
            self.split("y", AT_Y, SWAP_Y)
            return
        count = self.kept.shape[1] // 2
        halves = lax.psum(self.kept[0], "seq").astype(BF).reshape(2, count, -1)
        bit = self.bits[AT_Y]
        self.mine = self.token = lax.dynamic_index_in_dim(halves, bit, 0, keepdims=False)
        self.arrived = lax.dynamic_index_in_dim(halves, 1 - bit, 0, keepdims=False)

    def step_z1(self, *gates):
        if self.whole:
            self.added(gates)
            self.split("z1", AT_Z1, SWAP_Z1)

    def step_z2(self, *gates):
        if self.whole:
            self.added(gates)
            self.split("z2", AT_Z2, SWAP_Z2)

    def step_x(self, *gates):
        if self.whole:
            self.added(gates)
            far = self.kept[1]
            self.kept = self.kept[:1]
            self.send("x", far.astype(BF), "head", SWAP_X)

    def back_z2(self, *gates):
        if self.whole:
            self.added(gates)
            self.mine = self.kept[0].astype(BF)
            self.send("back_z2", self.mine, "seq", SWAP_Z2)

    def joined(self, place, gates):
        arrived = after(self.arrived, *gates)
        self.mine = stack_rows(self.meta, place, self.mine, arrived, BF)

    def back_z1(self, *gates):
        if self.whole:
            self.joined(AT_Z2, gates)
            self.send("back_z1", self.mine, "seq", SWAP_Z1)

    def back_y(self, *gates):
        if self.whole:
            self.joined(AT_Z1, gates)
            self.send("back_y", self.mine, "seq", SWAP_Y)

    def halves(self, *gates):
        return self.mine, after(self.arrived, *gates)


def on_device(
    tokens,
    cotangent,
    lengths,
    seq_order,
    w_qkv,
    w_out,
    w_up,
    w_down,
    bias_q,
    bias_v,
    bias_out,
    bias_up,
    bias_down,
    gain_attn,
    shift_attn,
    gain_mlp,
    shift_mlp,
):
    group_count = lax.axis_size("seq")
    group_id = lax.axis_index("seq")
    here = lax.axis_index("head").astype(jnp.int32)
    core, chip = here % 2, here // 2
    slots, span_rows, width = tokens.shape
    part = width // 4
    ff_part = w_up.shape[1] // 4
    offsets = [k * group_count // slots for k in range(slots)]
    offsets[1], offsets[-1] = 1, group_count - 1
    swap_x = [(i, i ^ 2) for i in range(4)]
    swap_core = [(i, i ^ 1) for i in range(4)]

    def over_x(value, name="x"):
        with jax.named_scope(name):
            return lax.ppermute(value, "head", swap_x)

    def over_core(value, name="core"):
        with jax.named_scope(name):
            return lax.ppermute(value, "head", swap_core)

    slot_ids = jnp.arange(slots, dtype=jnp.int32)
    local_ids = group_id * slots + slot_ids
    given_slot = lax.dynamic_slice_in_dim(seq_order, group_id * slots, slots) % slots
    given_of_slot = jnp.sum(
        jnp.where(given_slot[None, :] == slot_ids[:, None], slot_ids[None, :], 0), axis=1
    )
    matches = seq_order[None, :] == local_ids[:, None]
    slot_lens = jnp.sum(jnp.where(matches, lengths[None, :], 0), axis=1)
    aligned = (slot_lens + 15) // 16 * 16
    choices = np.zeros((35, slots), np.int32)
    for row, picks in enumerate(itertools.combinations(range(1, slots), 3)):
        choices[row, [0, *picks]] = 1
    sides = jnp.sum(choices * aligned[None, :], axis=1)
    larger = jnp.maximum(sides, jnp.sum(aligned) - sides)
    squares = jnp.sum(choices * (slot_lens * slot_lens)[None, :], axis=1)
    heavier = jnp.maximum(squares, jnp.sum(slot_lens * slot_lens) - squares)
    score = larger * 1024 + heavier // 4096
    best = jnp.min(score)
    chosen = jnp.argmax(score == best)
    in_first = jnp.sum(
        jnp.where(jnp.arange(35)[:, None] == chosen, choices, 0), axis=0, dtype=jnp.int32
    )
    is_own = jnp.where(chip == 0, in_first, 1 - in_first)
    before = np.tril(np.ones((slots, slots), np.int32), -1)
    rank_own = jnp.sum(before * is_own[None, :], axis=1)
    rank_far = jnp.sum(before * (1 - is_own)[None, :], axis=1)
    list_pos = jnp.where(is_own == 1, rank_own, 4 + rank_far).astype(jnp.int32)
    at_place = list_pos[None, :] == slot_ids[:, None]
    slot_at = jnp.sum(jnp.where(at_place, slot_ids[None, :], 0), axis=1)
    own_lens = jnp.sum(jnp.where(at_place, slot_lens[None, :], 0), axis=1)[:4]
    own_aligned = (own_lens + 15) // 16 * 16
    own_offsets = jnp.sum(np.tril(np.ones((4, 4), np.int32), -1) * own_aligned[None, :], axis=1)
    total_rows = jnp.sum(own_aligned)
    meta = jnp.concatenate(
        [
            own_offsets,
            own_lens,
            (own_lens + 127) // 128,
            here[None],
            core[None],
            (group_id % 2)[None],
            (group_id // 2)[None],
            (group_id // 2 % 2)[None],
            (group_id // 4 % 2)[None],
            chip[None],
            jnp.clip(total_rows - core * HALF, 0, HALF)[None],
            jnp.clip(total_rows - (1 - core) * HALF, 0, HALF)[None],
            jnp.zeros((3,), jnp.int32),
        ]
    ).astype(jnp.int32)
    row_ids = core * HALF + jnp.arange(HALF, dtype=jnp.int32)
    row_keep = jnp.any(
        (row_ids[:, None] >= own_offsets[None, :])
        & (row_ids[:, None] < (own_offsets + own_lens)[None, :]),
        axis=1,
        keepdims=True,
    )

    def swapped(own, far):
        return own, far, over_core(own), over_core(far)

    if group_count == slots:
        spots = (group_id - given_slot) % slots
        sent_tokens = route(tokens, spots)
    else:
        sent_tokens = route(tokens, given_slot.astype(jnp.int32))
    small_here = jnp.concatenate(
        [
            bias_q,
            bias_v,
            bias_out,
            bias_down,
            gain_attn,
            shift_attn,
            gain_mlp,
            shift_mlp,
            bias_up,
        ]
    )[None, :]
    small_here = after(small_here, sent_tokens)
    small_core = over_core(small_here)

    def ordered(first, second, is_low):
        return jnp.concatenate(
            [jnp.where(is_low, first, second), jnp.where(is_low, second, first)], axis=0
        )

    small_pair = ordered(small_here, small_core, core == 0)
    small = ordered(small_pair, over_x(small_pair), chip == 0).astype(F32)

    def vector(place):
        return small[:, place * part : (place + 1) * part].reshape(1, width)

    def local_columns(rows):
        return jnp.concatenate(
            [
                lax.dynamic_index_in_dim(rows, core, 0, keepdims=False),
                lax.dynamic_index_in_dim(rows, core + 2, 0, keepdims=False),
            ]
        )

    query_bias = local_columns(small[:, 0:part])
    value_bias = local_columns(small[:, part : 2 * part])
    up_bias = local_columns(small[:, 8 * part :])[None, :]
    out_bias, down_bias = vector(2), vector(3)
    attn_gain, attn_shift, mlp_gain, mlp_shift = vector(4), vector(5), vector(6), vector(7)
    no_bias = jnp.zeros((part,), F32)
    joint_bias = jnp.concatenate(
        [query_bias[:part], no_bias, value_bias[:part], query_bias[part:], no_bias, value_bias[part:]]
    )[None, :]


    if group_count == 8:
        share = w_down.shape[0] // 8
        turn = (group_id % 2) * 4 + group_id // 4 + 2 * (group_id // 2 % 2)
        lines = w_up.shape[0] // 16
        up_lines = lax.dynamic_slice_in_dim(w_up, turn * lines, lines, axis=0)
        mixed = jnp.concatenate(
            [lax.dynamic_slice_in_dim(w_down, turn * share, share, axis=0)]
            + jnp.split(up_lines, 4, axis=1),
            axis=0,
        )
        mixed = over_x(after(mixed, small), "x_shares")
    else:
        mixed = small
    if group_count == slots:
        got = lax.all_to_all(sent_tokens, "seq", split_axis=0, concat_axis=0, tiled=True)
        came = (slot_ids - group_id) % slots
        placed = jnp.sum(
            jnp.where(came[:, None] == slot_ids[None, :], list_pos[None, :], 0), axis=1
        )
        lists = route(after(got, small, mixed), placed.astype(jnp.int32))
    else:
        arrived = [sent_tokens[0]]
        for k in range(1, slots):
            arrived.append(
                lax.ppermute(
                    sent_tokens[k],
                    "seq",
                    [(i, (i - offsets[k]) % group_count) for i in range(group_count)],
                )
            )
        lists = route(arrived, list_pos)

    def by_chip(own, far):
        return jnp.concatenate(
            [jnp.where(chip == 0, own, far), jnp.where(chip == 0, far, own)], axis=0
        )

    first_weights = over_x(
        after(jnp.concatenate([w_qkv, w_out], axis=1), mixed), "x_first_weights"
    )
    far_qkv, far_out = first_weights[:, : 3 * width], first_weights[:, 3 * width :]
    full_qkv = assemble(meta, 3, *swapped(w_qkv, far_qkv))
    full_out = by_chip(w_out, far_out)

    far_tokens = over_x(lists[4:], "x_tokens")
    if group_count == 8:
        pair = stack_rows(meta, AT_Z2, mixed, moved("share_z2", mixed, "seq", SWAP_Z2), BF)
        gate = four = stack_rows(meta, AT_Z1, pair, moved("share_z1", pair, "seq", SWAP_Z1), BF)
    else:
        gate = far_tokens
    rows_in = pack(meta, *swapped(lists[:4], after(far_tokens, gate)))
    w_up_later, _ = lax.optimization_barrier((w_up, far_tokens))
    if group_count == 8:
        far_up_high = over_x(w_up_later[part // 2 :], "x_up_weight")
        other_four = moved("share_y", four, "seq", SWAP_Y)
    else:
        far_up = over_x(w_up_later, "x_up_weight")
        full_down = by_chip(w_down, over_x(w_down))
    cot_lists = route(cotangent, list_pos)
    cot_far_in, _ = lax.optimization_barrier((cot_lists[4:], far_tokens))
    cot_rows = pack(meta, *swapped(cot_lists[:4], over_x(cot_far_in, "x_cotangent")))

    def halves(value):
        return (
            lax.dynamic_slice_in_dim(value, core * HALF, HALF, axis=0),
            lax.dynamic_slice_in_dim(value, (1 - core) * HALF, HALF, axis=0),
        )

    def in_order(mine, other):
        lower = jnp.where(core == 0, mine, other)
        upper = jnp.where(core == 0, other, mine)
        return jnp.concatenate([lower, upper], axis=0)

    def core_sum(lefts_mine, lefts_other, rights, turned):
        arriving = over_core(rows_product(meta, OTHER, lefts_other, rights, turned, BF))
        return rows_product(meta, MINE, lefts_mine, rights, turned, F32) + arriving.astype(F32)

    qkv = (mm(rows_in, full_qkv) + joint_bias).astype(BF)
    context, lse = attend(meta, qkv)
    if group_count == 8:
        context, other_four, far_up_high = lax.optimization_barrier(
            (context, other_four, far_up_high)
        )
        full_down, far_up = merge_shares(meta, w_down, far_up_high, four, other_four)
    full_up = assemble(meta, 1, *swapped(w_up, far_up))
    ctx_mine, ctx_other = halves(context)
    rows_mine, _ = halves(rows_in)
    resid_attn = (
        core_sum([ctx_mine], [ctx_other], [full_out], False) + rows_mine.astype(F32) + out_bias
    )
    unit_attn, rstd_attn = normed(resid_attn)
    hidden = unit_attn * attn_gain + attn_shift
    low_mine = hidden.astype(BF)
    low_other = over_core(low_mine)

    low_mine = after(low_mine, cot_rows)
    act_mine, slope_mine = up_product(meta, MINE, low_mine, full_up, up_bias)
    act_other, slope_other = up_product(meta, OTHER, low_other, full_up, up_bias)
    resid_mlp = core_sum([act_mine], [act_other], [full_down], False) + hidden + down_bias
    unit_mlp, rstd_mlp = normed(resid_mlp)
    final_mine = (unit_mlp * mlp_gain + mlp_shift).astype(BF)

    cot_mine, _ = halves(cot_rows)
    grad_y = jnp.where(row_keep, cot_mine.astype(F32), 0.0)
    grad_mlp2 = norm_back(unit_mlp, rstd_mlp, grad_y, mlp_gain)
    sum_gain_mlp = jnp.sum(grad_y * unit_mlp, axis=0)
    sum_shift_mlp = jnp.sum(grad_y, axis=0)
    branch_mine = grad_mlp2.astype(BF)
    branch_other = over_core(branch_mine)
    sum_bias_down = jnp.sum(branch_mine, axis=0, dtype=F32)
    def grads(lefts, rights, start, count, kind=F32):
        return grad_product(meta, lefts, rights, start, count, kind)

    down_sum = SeqSum("down", meta, group_count)
    acts, branches = [act_mine, act_other], [branch_mine, branch_other]
    if group_count == 8:
        here_y = group_id % 2
        count = ff_part // 2

        def down_term(half, kind):
            return jnp.stack(
                [
                    grads(acts, branches, side * ff_part + half * count, count, kind)
                    for side in (chip, 1 - chip)
                ]
            )

        down_sum.start_y(down_term(1 - here_y, BF).reshape(-1, width), down_term(here_y, F32))
    else:
        down_sum.start_x(
            *(grads(acts, branches, side * ff_part, ff_part) for side in (1 - chip, chip))
        )
    branch_mine, branch_other, _ = lax.optimization_barrier(
        (branch_mine, branch_other, down_sum.token)
    )
    pre_mine = rows_product(meta, MINE, [branch_mine], [full_down], True, BF, slope_mine)
    pre_other = rows_product(meta, OTHER, [branch_other], [full_down], True, BF, slope_other)
    sum_bias_up = jnp.sum(pre_mine, axis=0, dtype=F32) + jnp.sum(pre_other, axis=0, dtype=F32)

    lows, pres = [low_mine, low_other], [pre_mine, pre_other]
    up_far, up_own = (
        grads(lows, pres, side * 2 * part, 2 * part, kind)
        for side, kind in ((1 - chip, BF), (chip, F32))
    )
    up_sum = SeqSum("up", meta, group_count)
    up_sum.start_x(up_far, up_own)
    pre_mine, pre_other, _ = lax.optimization_barrier((pre_mine, pre_other, up_sum.token))
    gh_other = rows_product(meta, OTHER, [pre_other], [full_up], True, BF)
    gh_arrived = over_core(gh_other)
    if group_count == 8:
        down_sum.step_z1(gh_other)
    else:
        down_sum.step_y(gh_other)
    pre_mine = after(pre_mine, down_sum.token)
    grad_hidden = rows_product(meta, MINE, [pre_mine], [full_up], True, F32)
    grad_hidden = grad_hidden + gh_arrived.astype(F32) + grad_mlp2

    grad_attn2 = norm_back(unit_attn, rstd_attn, grad_hidden, attn_gain)
    sum_gain_attn = jnp.sum(grad_hidden * unit_attn, axis=0)
    sum_shift_attn = jnp.sum(grad_hidden, axis=0)
    attn_mine = grad_attn2.astype(BF)
    attn_other = over_core(attn_mine)
    sum_bias_out = jnp.sum(attn_mine, axis=0, dtype=F32)
    half_width = width // 2

    def out_term(side, kind):
        term = grads([ctx_mine, ctx_other], [attn_mine, attn_other], side * part, part, kind)
        return jnp.concatenate([term[:, :half_width], term[:, half_width:]], axis=0)

    out_far, out_own = out_term(1 - chip, BF), out_term(chip, F32)
    down_sum.step_z2(out_own, out_far)
    up_sum.step_y(down_sum.token)
    attn_mine, attn_other, _ = lax.optimization_barrier((attn_mine, attn_other, up_sum.token))
    grad_ctx = in_order(
        rows_product(meta, MINE, [attn_mine], [full_out], True, BF),
        rows_product(meta, OTHER, [attn_other], [full_out], True, BF),
    )
    grad_first = attend_back(meta, qkv, lse, grad_ctx, 0)
    down_sum.step_x(grad_first)
    up_sum.step_z1(down_sum.token)
    grad_first = after(grad_first, up_sum.token)
    first_far, first_own = (
        jnp.concatenate(
            [grads([rows_in], [grad_first], side * 2 * part, 2 * part, out.dtype), out], axis=1
        )
        for side, out in ((1 - chip, out_far), (chip, out_own))
    )
    first_sum = SeqSum("first", meta, group_count)
    first_sum.start_x(first_far, first_own)
    down_sum.back_z2(first_sum.token, first_own)
    grad_last = attend_back(meta, qkv, lse, after(grad_ctx, down_sum.token), 1)
    up_sum.step_z2(grad_last)
    down_sum.back_z1(up_sum.token)
    grad_last = after(grad_last, down_sum.token)
    last_far, last_own = (
        grads([rows_in], [grad_last], side * 2 * part, 2 * part, kind)
        for side, kind in ((1 - chip, BF), (chip, F32))
    )
    first_sums = jnp.sum(grad_first, axis=0, dtype=F32)
    last_sums = jnp.sum(grad_last, axis=0, dtype=F32)
    sum_bias_q = jnp.concatenate([first_sums[:part], last_sums[:part]])
    sum_bias_v = jnp.concatenate([first_sums[2 * part :], last_sums[2 * part :]])

    def whole_row(value):
        return value.reshape(4, part)

    def spread(value, size):
        result = jnp.zeros((4, size), F32)
        result = lax.dynamic_update_slice(result, value[None, :size], (core, 0))
        return lax.dynamic_update_slice(result, value[None, size:], (core + 2, 0))

    terms = jnp.concatenate(
        [
            spread(sum_bias_q, part),
            spread(sum_bias_v, part),
            whole_row(sum_bias_out),
            whole_row(sum_bias_down),
            whole_row(sum_gain_attn),
            whole_row(sum_shift_attn),
            whole_row(sum_gain_mlp),
            whole_row(sum_shift_mlp),
            spread(sum_bias_up, ff_part),
        ],
        axis=1,
    )

    def shard(value, flip):
        return lax.dynamic_index_in_dim(value, here ^ flip, 0, keepdims=True)

    from_core = over_core(jnp.concatenate([shard(terms, 1), shard(terms, 3)]).astype(BF))
    near_term = shard(terms, 0)[0] + from_core[0].astype(F32)
    far_term = shard(terms, 2)[0] + from_core[1].astype(F32)
    lanes = near_term.shape[0] // (2 * part)

    def as_columns(term):
        return jnp.pad(term.reshape(lanes, 2 * part).T, ((0, 0), (0, 128 - lanes)))

    last_far = jnp.concatenate([last_far, as_columns(far_term).astype(BF)], axis=1)
    last_own = jnp.concatenate([last_own, as_columns(near_term)], axis=1)
    last_sum = SeqSum("last", meta, group_count)
    last_sum.start_x(last_far, last_own)
    first_sum.step_y(last_sum.token)
    up_sum.back_z2(first_sum.token)
    grad_last = after(grad_last, up_sum.token)

    qkv_blocks = [full_qkv[:, : 3 * part], full_qkv[:, 3 * part :]]
    first_mine, first_other = halves(grad_first)
    last_mine, last_other = halves(grad_last)
    gx_other = rows_product(meta, OTHER, [first_other, last_other], qkv_blocks, True, BF)
    gx_arrived = over_core(gx_other)
    down_sum.back_y(gx_other)
    first_sum.step_z1(down_sum.token)
    last_mine = after(last_mine, first_sum.token)
    gx_mine = rows_product(meta, MINE, [first_mine, last_mine], qkv_blocks, True, F32)
    gx_mine = (gx_mine + gx_arrived.astype(F32) + grad_attn2).astype(BF)

    def listed(own, arriving):
        parts = [own[k] for k in range(4)] + [arriving[k] for k in range(4)]
        return route(parts, slot_at.astype(jnp.int32))

    up_sum.back_z1(gx_mine)
    gx_own, gx_far = unpack(meta, gx_mine, over_core(after(gx_mine, up_sum.token)))
    last_sum.step_y(gx_far)
    gx_arrived = over_x(after(gx_far, last_sum.token), "x_grad")
    first_sum.step_z2(last_sum.token)
    up_sum.back_y(first_sum.token)
    last_sum.step_z1(up_sum.token)
    first_sum.back_z2(last_sum.token)
    last_sum.step_z2(first_sum.token)
    back = listed(gx_own, after(gx_arrived, last_sum.token))
    y_own, y_far = unpack(meta, final_mine, over_core(after(final_mine, gx_far)))
    activations = listed(y_own, over_x(after(y_far, gx_arrived), "x_activations"))
    if group_count == slots:
        spots = (group_id + slot_ids) % slots
        got = lax.all_to_all(
            route(back, spots.astype(jnp.int32)), "seq", split_axis=0, concat_axis=0, tiled=True
        )
        came = (group_id - slot_ids) % slots
        home = jnp.sum(
            jnp.where(came[:, None] == slot_ids[None, :], given_of_slot[None, :], 0), axis=1
        )
        input_grad = route(got, home.astype(jnp.int32))
    else:
        returned = [back[0]]
        for k in range(1, slots):
            returned.append(
                lax.ppermute(
                    back[k],
                    "seq",
                    [(i, (i + offsets[k]) % group_count) for i in range(group_count)],
                )
            )
        input_grad = route(returned, given_of_slot.astype(jnp.int32))

    def my_block(mine, other):
        aligned_here = (group_id % 2) == core
        return jnp.where(aligned_here, mine, other), jnp.where(aligned_here, other, mine)

    first_sum.back_z1(back)
    grad_down = stack_rows(meta, AT_Y, *down_sum.halves(first_sum.token))
    last_sum.back_z2(grad_down)
    first_sum.back_y(last_sum.token)
    last_sum.back_z1(first_sum.token)
    kept, sent = my_block(*up_sum.halves(last_sum.token))
    grad_w_up = spread_columns(meta, 1, 4 * ff_part, kept, over_core(sent))
    last_sum.back_y(kept)
    first_halves = first_sum.halves(last_sum.token)
    last_halves = last_sum.halves()
    blocks = []
    for mine, other in (first_halves, last_halves):
        kept, sent = my_block(mine[:, : 3 * part], other[:, : 3 * part])
        blocks += [kept, over_core(sent)]
    grad_w_qkv = spread_columns(meta, 3, 3 * width, *blocks)

    def by_y(mine, other, axis):
        lower = jnp.where(group_id % 2 == 0, mine, other)
        upper = jnp.where(group_id % 2 == 0, other, mine)
        return jnp.concatenate([lower, upper], axis=axis).astype(F32)

    grad_w_out = by_y(*(half[:, 3 * part :] for half in first_halves), 1)
    sums = by_y(*(half[:, 3 * part :] for half in last_halves), 0)[:, :lanes].T.reshape(-1)

    def piece(place):
        return sums[place * part : (place + 1) * part]

    return (
        activations,
        input_grad,
        grad_w_qkv,
        grad_w_out,
        grad_w_up,
        grad_down,
        piece(0),
        piece(1),
        piece(2),
        sums[8 * part :],
        piece(3),
        piece(4),
        piece(5),
        piece(6),
        piece(7),
    )


def solution(mesh):
    rows = P("seq", "head", None)
    weight, vector = P("head", None), P("head")
    in_specs = (rows, rows, P(), P()) + (weight,) * 4 + (vector,) * 9
    out_specs = (rows, rows) + (weight,) * 4 + (vector,) * 9
    return jax.shard_map(
        on_device, mesh=mesh, in_specs=in_specs, out_specs=out_specs, check_vma=False
    )
```

time: 1120 us -> 615 us (0.55)
  Pallas kernels: 451 us -> 198 us
  matrix products: 129 us -> 5.31 us
  local copies, waits for them, and re-layouts: 176 us -> 65.7 us
  waiting for transfers between devices: 116 us -> 206 us
  starting transfers between devices: 135 us -> 68.5 us
  other arithmetic: 93.7 us -> 59.6 us
    pallas_call x6 -> x7, Pallas kernels: 392 us -> 7.4 us  [route(): pl.pallas_call(functools.partial(_route_kernel, count, single), out_shape...]
    pallas_call x1 -> x44, Pallas kernels: 25 us -> 159 us  [the longest x12 49 us: rows_product(): pl.pallas_call(functools.partial(_rows_kernel, count_at, turned, len(left...]
    dot_general x20 -> x0, matrix products: 97.2 us -> none  [the longest x12 53.3 us: mm_rows(): lax.dot_general(left, right, (((0,), (0,)), ((), ())), preferred_element_...]
    ppermute x56 -> x31, starting transfers between devices: 119 us -> 37.1 us  [moved(): return lax.ppermute(value, axis, pairs)]
    ppermute x56 -> x31, waiting for transfers between devices: 72.8 us -> 145 us  [moved(): return lax.ppermute(value, axis, pairs)]
    reshape x10 -> x1, local copies, waits for them, and re-layouts: 32.1 us -> 1.32 us  [on_device(): by_y(*(half[:, 3 * part:] for half in last_halves), 0)[:, :lanes]]
    slice x13 -> x10, local copies, waits for them, and re-layouts: 34.7 us -> 6.28 us  [the longest x1 1.85 us: on_device(): qkv_blocks = [full_qkv[:, :3 * part], full_qkv[:, 3 * part:]]]
    all_to_all x0 -> x2, waiting for transfers between devices: none -> 27.9 us  [the longest x1 27.9 us: on_device(): lax.all_to_all(sent_tokens, 'seq', split_axis=0, concat_axis=0, tiled=True)]
  transfers between devices with their start and end apart: 91 -> 63, of which waited for: 19 -> 23; matrix products, arithmetic and copies ran while one was open for 32% -> 15% of each run, Pallas kernels for 35% -> 30%
where the time goes in v2:
time: 615 us; the launch traced here: 609 us
  waiting for transfers between devices  206 us (33%)
  Pallas kernels  198 us (32%)
  starting transfers between devices  68.5 us (11%)
  local copies, waits for them, and re-layouts  65.7 us (11%)
  other arithmetic  59.6 us (10%)
    ppermute x31, waiting for transfers between devices, moved(): return lax.ppermute(value, axis, pairs)  145 us
    pallas_call x12, Pallas kernels, rows_product(): pl.pallas_call(functools.partial(_rows_kernel, count_at, turned, len(left...  49 us
    pallas_call x12, Pallas kernels, grad_product(): pl.pallas_call(functools.partial(_grad_kernel, len(lefts)), out_shape=jax...  49 us
    ppermute x31, starting transfers between devices, moved(): return lax.ppermute(value, axis, pairs)  37.1 us
    unnamed x255, local copies, waits for them, and re-layouts  36.5 us
    all_to_all x1, waiting for transfers between devices, on_device(): lax.all_to_all(sent_tokens, 'seq', split_axis=0, concat_axis=0, tiled=True)  27.9 us
    ppermute x8, waiting for transfers between devices, over_x(): return lax.ppermute(value, 'head', swap_x)  26.9 us
    pallas_call x2, Pallas kernels, attend_back(): pl.pallas_call(functools.partial(_attend_back_kernel, block), out_shape=j...  23.8 us
  transfers between devices with their start and end apart: 63, of which 23 were waited for; matrix products, arithmetic and copies ran while one was open for 15% of the time, Pallas kernels for 30%

profile of v2, /device:TPU:0, one launch (start us, length us, event | category | flops | bytes accessed | tf_op | source)
XLA Modules:
  0.0 608.5 jit_solution(10771097746217392272)
XLA Ops:
  5.7 7.4 %all-to-all-start = ((bf16[8,128,1024]{2,1,0:T(8,128)(2,1)}), bf16[8,128,1024]{2,1,0:T(8,128)(2,1)S(1)}, u32[]{:S(2)}, u32[]{:S(2)}) async-start(bf16[8,128,1024]{2,1,0:T(8,128)(2,1)} %copy-done.44), calls=%async_computation | async-start | bytes 4194304 | tf_op jit(solution)/shard_map/all_to_all | solution.py:785
  26.7 2.9 pad_maximum_fusion
  29.6 6.2 %collective-permute-done.2.mine_ref = bf16[192,1024]{1,0:T(8,128)(2,1)S(1)} collective-permute-done((bf16[192,1024]{1,0:T(8,128)(2,1)S(1)}, bf16[192,1024]{1,0:T(8,128)(2,1)S(1)}, u32[]{:S(2)}, u32[]{:S(2)}) %collective-permute-start.2) | collective-permute-done | bytes 393248 | tf_op jit(solution)/shard_map/x_shares/ppermute | solution.py:653
  40.3 2.9 collective-permute-start.4
  43.2 27.9 %all-to-all-done.refs_0_ = bf16[8,128,1024]{2,1,0:T(8,128)(2,1)S(1)} async-done(((bf16[8,128,1024]{2,1,0:T(8,128)(2,1)}), bf16[8,128,1024]{2,1,0:T(8,128)(2,1)S(1)}, u32[]{:S(2)}, u32[]{:S(2)}) %all-to-all-start) | async-done | bytes 2097184 | tf_op jit(solution)/shard_map/all_to_all | solution.py:785
  79.7 5.0 collective-permute-done.8
  86.4 11.7 %collective-permute-done.5.other_ref = bf16[384,1024]{1,0:T(8,128)(2,1)} collective-permute-done((bf16[384,1024]{1,0:T(8,128)(2,1)}, bf16[384,1024]{1,0:T(8,128)(2,1)}, u32[]{:S(2)}, u32[]{:S(2)}) %collective-permute-start.5) | collective-permute-done | bytes 786464 | tf_op jit(solution)/shard_map/share_z1/ppermute | solution.py:535
  99.7 5.1 collective-permute-done.3.a1
  108.2 2.7 assemble.2
  115.1 5.3 add_convert_fusion.qkv_ref
  120.4 21.3 %attend.1 = (bf16[1536,512]{1,0:T(8,128)(2,1)S(1)}, f32[4,8,1,512]{3,2,1,0:T(1,128)S(1)}) custom-call(s32[24]{0:T(128)S(1)} %concatenate.62.meta_ref, bf16[1536,1536]{1,0:T(8,128)(2,1)S(1)} %add_convert_fusion.qkv_ref), custom_call_target="tpu_custom_call" | custom-call | bytes 1024 | tf_op jit(solution)/shard_map/attend/pallas_call | solution.py:184
  155.8 5.7 up_product.3
  161.5 3.5 rows_product.15
  165.0 4.2 collective-permute-start.20
  169.3 9.2 %collective-permute-done.14.a1 = bf16[4,128,1024]{2,1,0:T(8,128)(2,1)S(1)} collective-permute-done((bf16[4,128,1024]{2,1,0:T(8,128)(2,1)S(1)}, bf16[4,128,1024]{2,1,0:T(8,128)(2,1)S(1)}, u32[]{:S(2)}, u32[]{:S(2)}) %collective-permute-start.14) | collective-permute-done | bytes 1048608 | tf_op jit(solution)/shard_map/x_cotangent/ppermute | solution.py:653
  178.6 2.5 collective-permute-done.16.a3
  182.6 8.0 %up_product.2 = (bf16[768,2048]{1,0:T(8,128)(2,1)S(1)}, bf16[768,2048]{1,0:T(8,128)(2,1)S(1)}) custom-call(s32[24]{0:T(128)S(1)} %concatenate.62.meta_ref, bf16[768,1024]{1,0:T(8,128)(2,1)S(1)} %fusion.3.low_ref.refs_0_, bf16[1024,2048]{1,0:T(8,128)(2,1)S(1)} %assemble.3.weight_ref.refs_1_, f32[1,2048]{1,0:T(1,128)S(1)} %bitcast.169), custom_call_target="tpu_custom_call" | custom-call | bytes 1024 | tf_op jit(solution)/shard_map/up_product/pallas_call | solution.py:419
  190.7 5.3 rows_product.14
  202.0 3.7 collective-permute-done.21.refs_3_.refs_0_
  209.5 4.7 grad_product.13
  214.2 4.7 grad_product.12
  226.2 7.2 %rows_product.16.refs_2_.refs_0_ = bf16[768,2048]{1,0:T(8,128)(2,1)S(1)} custom-call(s32[24]{0:T(128)S(1)} %concatenate.62.meta_ref, bf16[768,1024]{1,0:T(8,128)(2,1)} %get-tuple-element.101.refs_2_.refs_0_, bf16[2048,1024]{1,0:T(8,128)(2,1)S(1)} %copy-done.15, bf16[768,2048]{1,0:T(8,128)(2,1)S(1)} %copy-done.61), custom_call_target="tpu_custom_call" | custom-call | bytes 1024 | tf_op jit(solution)/shard_map/rows_product/pallas_call | solution.py:458
  233.5 6.4 %rows_product.17.refs_3_.refs_0_ = bf16[768,2048]{1,0:T(8,128)(2,1)S(1)} custom-call(s32[24]{0:T(128)S(1)} %concatenate.62.meta_ref, bf16[768,1024]{1,0:T(8,128)(2,1)} %collective-permute-done.21.refs_3_.refs_0_, bf16[2048,1024]{1,0:T(8,128)(2,1)S(1)} %copy-done.15, bf16[768,2048]{1,0:T(8,128)(2,1)S(1)} %copy-done.59), custom_call_target="tpu_custom_call" | custom-call | bytes 1024 | tf_op jit(solution)/shard_map/rows_product/pallas_call | solution.py:458
  240.0 5.7 grad_product.14
  247.1 4.7 rows_product.18
  264.2 4.7 grad_product.16
  269.0 4.9 grad_product.15
  273.9 5.7 grad_product.17
  281.7 2.8 maximum_add_fusion
  288.2 5.0 rows_product.19
  293.3 5.7 multiply_reduce_fusion.1
  299.0 2.8 convert_reduce_fusion.5
  303.6 8.2 %collective-permute-done.26 = bf16[512,1024]{1,0:T(8,128)(2,1)} collective-permute-done((bf16[512,1024]{1,0:T(8,128)(2,1)}, bf16[512,1024]{1,0:T(8,128)(2,1)}, u32[]{:S(2)}, u32[]{:S(2)}) %collective-permute-start.26) | collective-permute-done | bytes 1048608 | tf_op jit(solution)/shard_map/down_z1/ppermute | solution.py:535
  319.2 3.0 rows_product.20
  322.3 2.5 rows_product.21
  325.0 12.0 %attend_back.2.refs_1_ = bf16[1536,768]{1,0:T(8,128)(2,1)S(1)} custom-call(s32[24]{0:T(128)S(1)} %concatenate.62.meta_ref, bf16[1536,1536]{1,0:T(8,128)(2,1)S(1)} %bitcast.163, f32[4,8,1,512]{3,2,1,0:T(1,128)S(1)} %get-tuple-element.100.lse_ref, bf16[1536,512]{1,0:T(8,128)(2,1)S(1)} %pad_maximum_fusion.2.gctx_ref), custom_call_target="tpu_custom_call" | custom-call | bytes 1024 | tf_op jit(solution)/shard_map/attend_back/pallas_call | solution.py:258
  339.4 3.7 grad_product.19
  343.1 3.7 grad_product.18
  350.8 2.7 grad_product.20
  354.7 2.8 collective-permute-start.30
  359.1 11.8 %attend_back.3.refs_1_ = bf16[1536,768]{1,0:T(8,128)(2,1)S(1)} custom-call(s32[24]{0:T(128)S(1)} %concatenate.62.meta_ref, bf16[1536,1536]{1,0:T(8,128)(2,1)S(1)} %bitcast.163, f32[4,8,1,512]{3,2,1,0:T(1,128)S(1)} %get-tuple-element.100.lse_ref, bf16[1536,512]{1,0:T(8,128)(2,1)S(1)} %pad_maximum_fusion.2.gctx_ref), custom_call_target="tpu_custom_call" | custom-call | bytes 1024 | tf_op jit(solution)/shard_map/attend_back/pallas_call | solution.py:258
  378.0 3.4 constant_dynamic-slice_fusion.1
  381.4 2.7 grad_product.21
  384.3 2.7 grad_product.22
  390.4 2.5 convert_add_fusion.1
  393.0 5.6 collective-permute-done.32
  399.8 3.0 rows_product.22
  404.2 2.5 collective-permute-start.35
  409.0 16.8 %collective-permute-done.36.other_ref = bf16[256,1024]{1,0:T(8,128)(2,1)S(1)} collective-permute-done((bf16[256,1024]{1,0:T(8,128)(2,1)S(1)}, bf16[256,1024]{1,0:T(8,128)(2,1)S(1)}, u32[]{:S(2)}, u32[]{:S(2)}) %collective-permute-start.36) | collective-permute-done | bytes 524320 | tf_op jit(solution)/shard_map/down_back_z1/ppermute | solution.py:535
  427.6 4.2 rows_product.23
  438.0 2.7 grad_product.23
  444.6 3.3 unpack.2
  447.9 10.6 %collective-permute-done.41 = bf16[512,896]{1,0:T(8,128)(2,1)} collective-permute-done((bf16[512,896]{1,0:T(8,128)(2,1)}, bf16[512,896]{1,0:T(8,128)(2,1)}, u32[]{:S(2)}, u32[]{:S(2)}) %collective-permute-start.41) | collective-permute-done | bytes 917536 | tf_op jit(solution)/shard_map/last_x/ppermute | solution.py:535
  464.3 13.2 %collective-permute-done.44 = bf16[256,896]{1,0:T(8,128)(2,1)S(1)} collective-permute-done((bf16[256,896]{1,0:T(8,128)(2,1)S(1)}, bf16[256,896]{1,0:T(8,128)(2,1)S(1)}, u32[]{:S(2)}, u32[]{:S(2)}) %collective-permute-start.44) | collective-permute-done | bytes 458784 | tf_op jit(solution)/shard_map/last_y/ppermute | solution.py:535
  477.8 6.8 %collective-permute-done.47 = bf16[128,896]{1,0:T(8,128)(2,1)S(1)} collective-permute-done((bf16[128,896]{1,0:T(8,128)(2,1)S(1)}, bf16[128,896]{1,0:T(8,128)(2,1)S(1)}, u32[]{:S(2)}, u32[]{:S(2)}) %collective-permute-start.47) | collective-permute-done | bytes 229408 | tf_op jit(solution)/shard_map/last_z1/ppermute | solution.py:535
  488.3 4.0 all-to-all-start.1
  497.5 52.6 %collective-permute-done.49.other_ref = bf16[64,1280]{1,0:T(8,128)(2,1)S(1)} collective-permute-done((bf16[64,1280]{1,0:T(8,128)(2,1)S(1)}, bf16[64,1280]{1,0:T(8,128)(2,1)S(1)}, u32[]{:S(2)}, u32[]{:S(2)}) %collective-permute-start.49) | collective-permute-done | bytes 163872 | tf_op jit(solution)/shard_map/first_back_z2/ppermute | solution.py:535
  551.7 3.6 stack_rows.18
  556.4 3.8 collective-permute-done.50.other_ref
  564.3 2.7 broadcast_select_fusion
  567.0 3.9 unpack.3
  576.4 10.0 %collective-permute-done.58 = bf16[256,896]{1,0:T(8,128)(2,1)S(1)} collective-permute-done((bf16[256,896]{1,0:T(8,128)(2,1)S(1)}, bf16[256,896]{1,0:T(8,128)(2,1)S(1)}, u32[]{:S(2)}, u32[]{:S(2)}) %collective-permute-start.58) | collective-permute-done | bytes 458784 | tf_op jit(solution)/shard_map/last_back_y/ppermute | solution.py:535
  596.0 3.6 spread_columns.3
  599.6 3.1 spread_columns.2
  (526 shorter events, 179.6 us)
Async XLA Ops:
  5.7 65.5 %all-to-all-start = ((bf16[8,128,1024]{2,1,0:T(8,128)(2,1)}), bf16[8,128,1024]{2,1,0:T(8,128)(2,1)S(1)}, u32[]{:S(2)}, u32[]{:S(2)}) async-start(bf16[8,128,1024]{2,1,0:T(8,128)(2,1)} %copy-done.44), calls=%async_computation | async-start | bytes 4194304 | tf_op jit(solution)/shard_map/all_to_all | solution.py:785
  14.9 6.3 %collective-permute-start = (bf16[1,3072]{1,0:T(2,128)(2,1)S(1)}, bf16[1,3072]{1,0:T(2,128)(2,1)S(1)}, u32[]{:S(2)}, u32[]{:S(2)}) collective-permute-start(bf16[1,3072]{1,0:T(2,128)(2,1)S(1)} %broadcast_in_dim.215), channel_id=1, source_target_pairs={{0,1},{1,0},{2,3},{3,2},{4,5},{5,4},{6,7},{7,6},{8,9},{9,8},{10,11... | collective-permute-start | bytes 18440 | tf_op jit(solution)/shard_map/core/ppermute | solution.py:657
  21.3 3.8 collective-permute-start.1
  25.1 10.7 %collective-permute-start.2 = (bf16[192,1024]{1,0:T(8,128)(2,1)S(1)}, bf16[192,1024]{1,0:T(8,128)(2,1)S(1)}, u32[]{:S(2)}, u32[]{:S(2)}) collective-permute-start(bf16[192,1024]{1,0:T(8,128)(2,1)S(1)} %dynamic-slice_dynamic-update-slice_fusion.1), channel_id=1, source_target_pairs={{0,2},{1,3},{2,0},{3,1},{4,6},{5,7},{6,4},{7,5},{8,10},{9,11},{10,... | collective-permute-start | bytes 1179656 | tf_op jit(solution)/shard_map/x_shares/ppermute | solution.py:653
  35.8 48.9 %collective-permute-start.8 = (bf16[256,4096]{1,0:T(8,128)(2,1)}, bf16[256,4096]{1,0:T(8,128)(2,1)}, u32[]{:S(2)}, u32[]{:S(2)}) collective-permute-start(bf16[256,4096]{1,0:T(8,128)(2,1)} %pad_maximum_fusion), channel_id=1, source_target_pairs={{0,2},{1,3},{2,0},{3,1},{4,6},{5,7},{6,4},{7,5},{8,10},{9,11},{10,... | collective-permute-start | bytes 6291464 | tf_op jit(solution)/shard_map/x_first_weights/ppermute | solution.py:653
  40.3 37.8 %collective-permute-start.4 = (bf16[192,1024]{1,0:T(8,128)(2,1)S(1)}, bf16[192,1024]{1,0:T(8,128)(2,1)S(1)}, u32[]{:S(2)}, u32[]{:S(2)}) collective-permute-start(bf16[192,1024]{1,0:T(8,128)(2,1)S(1)} %collective-permute-done.2.mine_ref), channel_id=1, source_target_pairs={{0,16},{4,20},{8,24},{12,28},{16,0},{20,4},{24,8},{28,12},{1,17},{... | collective-permute-start | bytes 1179656 | tf_op jit(solution)/shard_map/share_z2/ppermute | solution.py:535
  73.4 31.4 %collective-permute-start.3 = (bf16[4,128,1024]{2,1,0:T(8,128)(2,1)}, bf16[4,128,1024]{2,1,0:T(8,128)(2,1)}, u32[]{:S(2)}, u32[]{:S(2)}) collective-permute-start(bf16[4,128,1024]{2,1,0:T(8,128)(2,1)} %get-tuple-element.199), channel_id=1, source_target_pairs={{0,2},{1,3},{2,0},{3,1},{4,6},{5,7},{6,4},{7,5},{8,10},{9,11},{10,... | collective-permute-start | bytes 3145736 | tf_op jit(solution)/shard_map/x_tokens/ppermute | solution.py:653
  79.6 18.5 %collective-permute-start.5 = (bf16[384,1024]{1,0:T(8,128)(2,1)}, bf16[384,1024]{1,0:T(8,128)(2,1)}, u32[]{:S(2)}, u32[]{:S(2)}) collective-permute-start(bf16[384,1024]{1,0:T(8,128)(2,1)} %stack_rows.11.mine_ref), channel_id=1, source_target_pairs={{0,8},{4,12},{8,0},{12,4},{16,24},{20,28},{24,16},{28,20},{1,9},{5... | collective-permute-start | bytes 2359304 | tf_op jit(solution)/shard_map/share_z1/ppermute | solution.py:535
  79.7 28.5 %collective-permute-start.9 = (bf16[256,3072]{1,0:T(8,128)(2,1)S(1)}, bf16[256,3072]{1,0:T(8,128)(2,1)}, u32[]{:S(2)}, u32[]{:S(2)}) collective-permute-start(bf16[256,3072]{1,0:T(8,128)(2,1)S(1)} %copy-done.46), channel_id=1, source_target_pairs={{0,1},{1,0},{2,3},{3,2},{4,5},{5,4},{6,7},{7,6},{8,9},{9,8},{10,11... | collective-permute-start | bytes 4718600 | tf_op jit(solution)/shard_map/core/ppermute | solution.py:657
  86.2 22.0 %collective-permute-start.10 = (bf16[256,3072]{1,0:T(8,128)(2,1)S(1)}, bf16[256,3072]{1,0:T(8,128)(2,1)}, u32[]{:S(2)}, u32[]{:S(2)}) collective-permute-start(bf16[256,3072]{1,0:T(8,128)(2,1)S(1)} %slice.276.refs_1_), channel_id=1, source_target_pairs={{0,1},{1,0},{2,3},{3,2},{4,5},{5,4},{6,7},{7,6},{8,9},{9,8},{10,11... | collective-permute-start | bytes 4718600 | tf_op jit(solution)/shard_map/core/ppermute | solution.py:657
  99.6 13.1 %collective-permute-start.6 = (bf16[4,128,1024]{2,1,0:T(8,128)(2,1)S(1)}, bf16[4,128,1024]{2,1,0:T(8,128)(2,1)S(1)}, u32[]{:S(2)}, u32[]{:S(2)}) collective-permute-start(bf16[4,128,1024]{2,1,0:T(8,128)(2,1)S(1)} %copy-done.57), channel_id=1, source_target_pairs={{0,1},{1,0},{2,3},{3,2},{4,5},{5,4},{6,7},{7,6},{8,9},{9,8},{10,11... | collective-permute-start | bytes 3145736 | tf_op jit(solution)/shard_map/core/ppermute | solution.py:657
  104.8 7.9 %collective-permute-start.7 = (bf16[4,128,1024]{2,1,0:T(8,128)(2,1)}, bf16[4,128,1024]{2,1,0:T(8,128)(2,1)S(1)}, u32[]{:S(2)}, u32[]{:S(2)}) collective-permute-start(bf16[4,128,1024]{2,1,0:T(8,128)(2,1)} %collective-permute-done.3.a1), channel_id=1, source_target_pairs={{0,1},{1,0},{2,3},{3,2},{4,5},{5,4},{6,7},{7,6},{8,9},{9,8},{10,11... | collective-permute-start | bytes 3145736 | tf_op jit(solution)/shard_map/core/ppermute | solution.py:657
  104.9 37.1 %collective-permute-start.11 = (bf16[768,1024]{1,0:T(8,128)(2,1)S(1)}, bf16[768,1024]{1,0:T(8,128)(2,1)S(1)}, u32[]{:S(2)}, u32[]{:S(2)}) collective-permute-start(bf16[768,1024]{1,0:T(8,128)(2,1)S(1)} %stack_rows.12.mine_ref), channel_id=1, source_target_pairs={{0,4},{4,0},{8,12},{12,8},{16,20},{20,16},{24,28},{28,24},{1,5},{5... | collective-permute-start | bytes 4718600 | tf_op jit(solution)/shard_map/share_y/ppermute | solution.py:535
  111.2 30.8 %collective-permute-start.12 = (bf16[128,4096]{1,0:T(8,128)(2,1)S(1)}, bf16[128,4096]{1,0:T(8,128)(2,1)S(1)}, u32[]{:S(2)}, u32[]{:S(2)}) collective-permute-start(bf16[128,4096]{1,0:T(8,128)(2,1)S(1)} %slice.212), channel_id=1, source_target_pairs={{0,2},{1,3},{2,0},{3,1},{4,6},{5,7},{6,4},{7,5},{8,10},{9,11},{10,... | collective-permute-start | bytes 3145736 | tf_op jit(solution)/shard_map/x_up_weight/ppermute | solution.py:653
  144.0 4.1 collective-permute-start.13
  144.5 10.4 %collective-permute-start.17 = (bf16[256,4096]{1,0:T(8,128)(2,1)S(1)}, bf16[256,4096]{1,0:T(8,128)(2,1)S(1)}, u32[]{:S(2)}, u32[]{:S(2)}) collective-permute-start(bf16[256,4096]{1,0:T(8,128)(2,1)S(1)} %copy-done.51), channel_id=1, source_target_pairs={{0,1},{1,0},{2,3},{3,2},{4,5},{5,4},{6,7},{7,6},{8,9},{9,8},{10,11... | collective-permute-start | bytes 6291464 | tf_op jit(solution)/shard_map/core/ppermute | solution.py:657
  148.0 6.9 %collective-permute-start.18 = (bf16[256,4096]{1,0:T(8,128)(2,1)S(1)}, bf16[256,4096]{1,0:T(8,128)(2,1)S(1)}, u32[]{:S(2)}, u32[]{:S(2)}) collective-permute-start(bf16[256,4096]{1,0:T(8,128)(2,1)S(1)} %get-tuple-element.96.refs_1_), channel_id=1, source_target_pairs={{0,1},{1,0},{2,3},{3,2},{4,5},{5,4},{6,7},{7,6},{8,9},{9,8},{10,11... | collective-permute-start | bytes 6291464 | tf_op jit(solution)/shard_map/core/ppermute | solution.py:657
  149.9 5.9 collective-permute-start.19
  153.3 25.2 %collective-permute-start.14 = (bf16[4,128,1024]{2,1,0:T(8,128)(2,1)S(1)}, bf16[4,128,1024]{2,1,0:T(8,128)(2,1)S(1)}, u32[]{:S(2)}, u32[]{:S(2)}) collective-permute-start(bf16[4,128,1024]{2,1,0:T(8,128)(2,1)S(1)} %get-tuple-element.92), channel_id=1, source_target_pairs={{0,2},{1,3},{2,0},{3,1},{4,6},{5,7},{6,4},{7,5},{8,10},{9,11},{10,... | collective-permute-start | bytes 3145736 | tf_op jit(solution)/shard_map/x_cotangent/ppermute | solution.py:653
  165.0 31.0 %collective-permute-start.20 = (bf16[768,1024]{1,0:T(8,128)(2,1)S(1)}, bf16[768,1024]{1,0:T(8,128)(2,1)S(1)}, u32[]{:S(2)}, u32[]{:S(2)}) collective-permute-start(bf16[768,1024]{1,0:T(8,128)(2,1)S(1)} %rows_product.15), channel_id=1, source_target_pairs={{0,1},{1,0},{2,3},{3,2},{4,5},{5,4},{6,7},{7,6},{8,9},{9,8},{10,11... | collective-permute-start | bytes 4718600 | tf_op jit(solution)/shard_map/core/ppermute | solution.py:657
  169.2 9.4 %collective-permute-start.15 = (bf16[4,128,1024]{2,1,0:T(8,128)(2,1)S(1)}, bf16[4,128,1024]{2,1,0:T(8,128)(2,1)S(1)}, u32[]{:S(2)}, u32[]{:S(2)}) collective-permute-start(bf16[4,128,1024]{2,1,0:T(8,128)(2,1)S(1)} %get-tuple-element.198.a0), channel_id=1, source_target_pairs={{0,1},{1,0},{2,3},{3,2},{4,5},{5,4},{6,7},{7,6},{8,9},{9,8},{10,11... | collective-permute-start | bytes 3145736 | tf_op jit(solution)/shard_map/core/ppermute | solution.py:657
  178.5 2.7 collective-permute-start.16
  202.0 3.8 collective-permute-start.21
  220.5 61.2 %collective-permute-start.22 = (bf16[1024,1024]{1,0:T(8,128)(2,1)}, bf16[1024,1024]{1,0:T(8,128)(2,1)}, u32[]{:S(2)}, u32[]{:S(2)}) collective-permute-start(bf16[1024,1024]{1,0:T(8,128)(2,1)} %bitcast.20), channel_id=1, source_target_pairs={{0,4},{4,0},{8,12},{12,8},{16,20},{20,16},{24,28},{28,24},{1,5},{5... | collective-permute-start | bytes 6291464 | tf_op jit(solution)/shard_map/down_y/ppermute | solution.py:535
  251.8 41.4 %collective-permute-start.23 = (bf16[768,1024]{1,0:T(8,128)(2,1)}, bf16[768,1024]{1,0:T(8,128)(2,1)}, u32[]{:S(2)}, u32[]{:S(2)}) collective-permute-start(bf16[768,1024]{1,0:T(8,128)(2,1)} %rows_product.18), channel_id=1, source_target_pairs={{0,1},{1,0},{2,3},{3,2},{4,5},{5,4},{6,7},{7,6},{8,9},{9,8},{10,11... | collective-permute-start | bytes 4718600 | tf_op jit(solution)/shard_map/core/ppermute | solution.py:657
  255.6 60.5 %collective-permute-start.25 = (bf16[512,2048]{1,0:T(8,128)(2,1)}, bf16[512,2048]{1,0:T(8,128)(2,1)}, u32[]{:S(2)}, u32[]{:S(2)}) collective-permute-start(bf16[512,2048]{1,0:T(8,128)(2,1)} %copy-done.70), channel_id=1, source_target_pairs={{0,2},{1,3},{2,0},{3,1},{4,6},{5,7},{6,4},{7,5},{8,10},{9,11},{10,... | collective-permute-start | bytes 6291464 | tf_op jit(solution)/shard_map/up_x/ppermute | solution.py:535
  286.8 25.1 %collective-permute-start.26 = (bf16[512,1024]{1,0:T(8,128)(2,1)}, bf16[512,1024]{1,0:T(8,128)(2,1)}, u32[]{:S(2)}, u32[]{:S(2)}) collective-permute-start(bf16[512,1024]{1,0:T(8,128)(2,1)} %bitcast.27), channel_id=1, source_target_pairs={{0,8},{4,12},{8,0},{12,4},{16,24},{20,28},{24,16},{28,20},{1,9},{5... | collective-permute-start | bytes 3145736 | tf_op jit(solution)/shard_map/down_z1/ppermute | solution.py:535
  301.9 17.4 %collective-permute-start.24 = (bf16[768,1024]{1,0:T(8,128)(2,1)}, bf16[768,1024]{1,0:T(8,128)(2,1)}, u32[]{:S(2)}, u32[]{:S(2)}) collective-permute-start(bf16[768,1024]{1,0:T(8,128)(2,1)} %get-tuple-element.111.refs_2_.refs_0_), channel_id=1, source_target_pairs={{0,1},{1,0},{2,3},{3,2},{4,5},{5,4},{6,7},{7,6},{8,9},{9,8},{10,11... | collective-permute-start | bytes 4718600 | tf_op jit(solution)/shard_map/core/ppermute | solution.py:657
  313.7 24.9 %collective-permute-start.28 = (bf16[256,1024]{1,0:T(8,128)(2,1)S(1)}, bf16[256,1024]{1,0:T(8,128)(2,1)S(1)}, u32[]{:S(2)}, u32[]{:S(2)}) collective-permute-start(bf16[256,1024]{1,0:T(8,128)(2,1)S(1)} %bitcast.191), channel_id=1, source_target_pairs={{0,16},{4,20},{8,24},{12,28},{16,0},{20,4},{24,8},{28,12},{1,17},{... | collective-permute-start | bytes 1572872 | tf_op jit(solution)/shard_map/down_z2/ppermute | solution.py:535
  318.6 29.4 %collective-permute-start.27 = (bf16[256,2048]{1,0:T(8,128)(2,1)S(1)}, bf16[256,2048]{1,0:T(8,128)(2,1)S(1)}, u32[]{:S(2)}, u32[]{:S(2)}) collective-permute-start(bf16[256,2048]{1,0:T(8,128)(2,1)S(1)} %fusion.6), channel_id=1, source_target_pairs={{0,4},{4,0},{8,12},{12,8},{16,20},{20,16},{24,28},{28,24},{1,5},{5... | collective-permute-start | bytes 3145736 | tf_op jit(solution)/shard_map/up_y/ppermute | solution.py:535
  338.8 15.9 %collective-permute-start.29 = (bf16[128,1024]{1,0:T(8,128)(2,1)S(1)}, bf16[128,1024]{1,0:T(8,128)(2,1)S(1)}, u32[]{:S(2)}, u32[]{:S(2)}) collective-permute-start(bf16[128,1024]{1,0:T(8,128)(2,1)S(1)} %fusion.16), channel_id=1, source_target_pairs={{0,2},{1,3},{2,0},{3,1},{4,6},{5,7},{6,4},{7,5},{8,10},{9,11},{10,... | collective-permute-start | bytes 786440 | tf_op jit(solution)/shard_map/down_x/ppermute | solution.py:535
  349.7 23.4 %collective-permute-start.31 = (bf16[128,2048]{1,0:T(8,128)(2,1)}, bf16[128,2048]{1,0:T(8,128)(2,1)}, u32[]{:S(2)}, u32[]{:S(2)}) collective-permute-start(bf16[128,2048]{1,0:T(8,128)(2,1)} %fusion.9), channel_id=1, source_target_pairs={{0,8},{4,12},{8,0},{12,4},{16,24},{20,28},{24,16},{28,20},{1,9},{5... | collective-permute-start | bytes 1572872 | tf_op jit(solution)/shard_map/up_z1/ppermute | solution.py:535
  354.7 21.1 %collective-permute-start.30 = (bf16[128,1024]{1,0:T(8,128)(2,1)S(1)}, bf16[128,1024]{1,0:T(8,128)(2,1)}, u32[]{:S(2)}, u32[]{:S(2)}) collective-permute-start(bf16[128,1024]{1,0:T(8,128)(2,1)S(1)} %fusion.17.mine_ref), channel_id=1, source_target_pairs={{0,16},{4,20},{8,24},{12,28},{16,0},{20,4},{24,8},{28,12},{1,17},{... | collective-permute-start | bytes 786440 | tf_op jit(solution)/shard_map/down_back_z2/ppermute | solution.py:535
  357.6 32.8 %collective-permute-start.33 = (bf16[512,1280]{1,0:T(8,128)(2,1)}, bf16[512,1280]{1,0:T(8,128)(2,1)}, u32[]{:S(2)}, u32[]{:S(2)}) collective-permute-start(bf16[512,1280]{1,0:T(8,128)(2,1)} %maximum_maximum_fusion.1), channel_id=1, source_target_pairs={{0,2},{1,3},{2,0},{3,1},{4,6},{5,7},{6,4},{7,5},{8,10},{9,11},{10,... | collective-permute-start | bytes 3932168 | tf_op jit(solution)/shard_map/first_x/ppermute | solution.py:535
  378.0 10.0 %collective-permute-start.34 = (bf16[2,3072]{1,0:T(2,128)(2,1)S(1)}, bf16[2,3072]{1,0:T(2,128)(2,1)S(1)}, u32[]{:S(2)}, u32[]{:S(2)}) collective-permute-start(bf16[2,3072]{1,0:T(2,128)(2,1)S(1)} %pad_maximum_fusion.6), channel_id=1, source_target_pairs={{0,1},{1,0},{2,3},{3,2},{4,5},{5,4},{6,7},{7,6},{8,9},{9,8},{10,11... | collective-permute-start | bytes 36872 | tf_op jit(solution)/shard_map/core/ppermute | solution.py:657
  384.2 14.4 %collective-permute-start.32 = (bf16[64,2048]{1,0:T(8,128)(2,1)}, bf16[64,2048]{1,0:T(8,128)(2,1)}, u32[]{:S(2)}, u32[]{:S(2)}) collective-permute-start(bf16[64,2048]{1,0:T(8,128)(2,1)} %fusion.15), channel_id=1, source_target_pairs={{0,16},{4,20},{8,24},{12,28},{16,0},{20,4},{24,8},{28,12},{1,17},{... | collective-permute-start | bytes 786440 | tf_op jit(solution)/shard_map/up_z2/ppermute | solution.py:535
  402.9 29.0 %collective-permute-start.37 = (bf16[768,1024]{1,0:T(8,128)(2,1)S(1)}, bf16[768,1024]{1,0:T(8,128)(2,1)S(1)}, u32[]{:S(2)}, u32[]{:S(2)}) collective-permute-start(bf16[768,1024]{1,0:T(8,128)(2,1)S(1)} %rows_product.22), channel_id=1, source_target_pairs={{0,1},{1,0},{2,3},{3,2},{4,5},{5,4},{6,7},{7,6},{8,9},{9,8},{10,11... | collective-permute-start | bytes 4718600 | tf_op jit(solution)/shard_map/core/ppermute | solution.py:657
  404.2 22.3 %collective-permute-start.35 = (bf16[256,1280]{1,0:T(8,128)(2,1)S(1)}, bf16[256,1280]{1,0:T(8,128)(2,1)S(1)}, u32[]{:S(2)}, u32[]{:S(2)}) collective-permute-start(bf16[256,1280]{1,0:T(8,128)(2,1)S(1)} %fusion.8), channel_id=1, source_target_pairs={{0,4},{4,0},{8,12},{12,8},{16,20},{20,16},{24,28},{28,24},{1,5},{5... | collective-permute-start | bytes 1966088 | tf_op jit(solution)/shard_map/first_y/ppermute | solution.py:535
  406.6 19.2 %collective-permute-start.36 = (bf16[256,1024]{1,0:T(8,128)(2,1)S(1)}, bf16[256,1024]{1,0:T(8,128)(2,1)S(1)}, u32[]{:S(2)}, u32[]{:S(2)}) collective-permute-start(bf16[256,1024]{1,0:T(8,128)(2,1)S(1)} %copy-done.65), channel_id=1, source_target_pairs={{0,8},{4,12},{8,0},{12,4},{16,24},{20,28},{24,16},{28,20},{1,9},{5... | collective-permute-start | bytes 1572872 | tf_op jit(solution)/shard_map/down_back_z1/ppermute | solution.py:535
  406.6 27.4 %collective-permute-start.38 = (bf16[64,2048]{1,0:T(8,128)(2,1)S(1)}, bf16[64,2048]{1,0:T(8,128)(2,1)S(1)}, u32[]{:S(2)}, u32[]{:S(2)}) collective-permute-start(bf16[64,2048]{1,0:T(8,128)(2,1)S(1)} %fusion.11.mine_ref), channel_id=1, source_target_pairs={{0,16},{4,20},{8,24},{12,28},{16,0},{20,4},{24,8},{28,12},{1,17},{... | collective-permute-start | bytes 786440 | tf_op jit(solution)/shard_map/up_back_z2/ppermute | solution.py:535
  435.4 9.2 %collective-permute-start.39 = (bf16[768,1024]{1,0:T(8,128)(2,1)}, bf16[768,1024]{1,0:T(8,128)(2,1)}, u32[]{:S(2)}, u32[]{:S(2)}) collective-permute-start(bf16[768,1024]{1,0:T(8,128)(2,1)} %add_convert_fusion.1.mine_ref), channel_id=1, source_target_pairs={{0,1},{1,0},{2,3},{3,2},{4,5},{5,4},{6,7},{7,6},{8,9},{9,8},{10,11... | collective-permute-start | bytes 4718600 | tf_op jit(solution)/shard_map/core/ppermute | solution.py:657
  435.4 23.1 %collective-permute-start.41 = (bf16[512,896]{1,0:T(8,128)(2,1)}, bf16[512,896]{1,0:T(8,128)(2,1)}, u32[]{:S(2)}, u32[]{:S(2)}) collective-permute-start(bf16[512,896]{1,0:T(8,128)(2,1)} %fusion.7), channel_id=1, source_target_pairs={{0,2},{1,3},{2,0},{3,1},{4,6},{5,7},{6,4},{7,5},{8,10},{9,11},{10,... | collective-permute-start | bytes 2752520 | tf_op jit(solution)/shard_map/last_x/ppermute | solution.py:535
  442.1 109.6 %collective-permute-start.52 = (bf16[512,1024]{1,0:T(8,128)(2,1)}, bf16[512,1024]{1,0:T(8,128)(2,1)}, u32[]{:S(2)}, u32[]{:S(2)}) collective-permute-start(bf16[512,1024]{1,0:T(8,128)(2,1)} %copy-done.54), channel_id=1, source_target_pairs={{0,4},{4,0},{8,12},{12,8},{16,20},{20,16},{24,28},{28,24},{1,5},{5... | collective-permute-start | bytes 3145736 | tf_op jit(solution)/shard_map/down_back_y/ppermute | solution.py:535
  442.6 18.8 %collective-permute-start.46 = (bf16[128,1280]{1,0:T(8,128)(2,1)}, bf16[128,1280]{1,0:T(8,128)(2,1)S(1)}, u32[]{:S(2)}, u32[]{:S(2)}) collective-permute-start(bf16[128,1280]{1,0:T(8,128)(2,1)} %fusion.13), channel_id=1, source_target_pairs={{0,8},{4,12},{8,0},{12,4},{16,24},{20,28},{24,16},{28,20},{1,9},{5... | collective-permute-start | bytes 983048 | tf_op jit(solution)/shard_map/first_z1/ppermute | solution.py:535
  442.6 21.0 %collective-permute-start.45 = (bf16[128,2048]{1,0:T(8,128)(2,1)}, bf16[128,2048]{1,0:T(8,128)(2,1)S(1)}, u32[]{:S(2)}, u32[]{:S(2)}) collective-permute-start(bf16[128,2048]{1,0:T(8,128)(2,1)} %copy-done.66), channel_id=1, source_target_pairs={{0,8},{4,12},{8,0},{12,4},{16,24},{20,28},{24,16},{28,20},{1,9},{5... | collective-permute-start | bytes 1572872 | tf_op jit(solution)/shard_map/up_back_z1/ppermute | solution.py:535
  459.9 17.6 %collective-permute-start.44 = (bf16[256,896]{1,0:T(8,128)(2,1)S(1)}, bf16[256,896]{1,0:T(8,128)(2,1)S(1)}, u32[]{:S(2)}, u32[]{:S(2)}) collective-permute-start(bf16[256,896]{1,0:T(8,128)(2,1)S(1)} %fusion.12), channel_id=1, source_target_pairs={{0,4},{4,0},{8,12},{12,8},{16,20},{20,16},{24,28},{28,24},{1,5},{5... | collective-permute-start | bytes 1376264 | tf_op jit(solution)/shard_map/last_y/ppermute | solution.py:535
  460.4 25.1 %collective-permute-start.42 = (bf16[4,128,1024]{2,1,0:T(8,128)(2,1)S(1)}, bf16[4,128,1024]{2,1,0:T(8,128)(2,1)S(1)}, u32[]{:S(2)}, u32[]{:S(2)}) collective-permute-start(bf16[4,128,1024]{2,1,0:T(8,128)(2,1)S(1)} %get-tuple-element.134), channel_id=1, source_target_pairs={{0,2},{1,3},{2,0},{3,1},{4,6},{5,7},{6,4},{7,5},{8,10},{9,11},{10,... | collective-permute-start | bytes 3145736 | tf_op jit(solution)/shard_map/x_grad/ppermute | solution.py:653
  461.4 16.3 %collective-permute-start.48 = (bf16[64,1280]{1,0:T(8,128)(2,1)S(1)}, bf16[64,1280]{1,0:T(8,128)(2,1)S(1)}, u32[]{:S(2)}, u32[]{:S(2)}) collective-permute-start(bf16[64,1280]{1,0:T(8,128)(2,1)S(1)} %fusion.20), channel_id=1, source_target_pairs={{0,16},{4,20},{8,24},{12,28},{16,0},{20,4},{24,8},{28,12},{1,17},{... | collective-permute-start | bytes 491528 | tf_op jit(solution)/shard_map/first_z2/ppermute | solution.py:535
  477.6 7.0 %collective-permute-start.47 = (bf16[128,896]{1,0:T(8,128)(2,1)S(1)}, bf16[128,896]{1,0:T(8,128)(2,1)S(1)}, u32[]{:S(2)}, u32[]{:S(2)}) collective-permute-start(bf16[128,896]{1,0:T(8,128)(2,1)S(1)} %fusion.18), channel_id=1, source_target_pairs={{0,8},{4,12},{8,0},{12,4},{16,24},{20,28},{24,16},{28,20},{1,9},{5... | collective-permute-start | bytes 688136 | tf_op jit(solution)/shard_map/last_z1/ppermute | solution.py:535
  488.3 63.4 %copy-start.55 = (bf16[512,1024]{1,0:T(8,128)(2,1)S(1)}, bf16[512,1024]{1,0:T(8,128)(2,1)}, u32[]{:S(2)}) copy-start(bf16[512,1024]{1,0:T(8,128)(2,1)} %copy-done.54) | copy-start | bytes 3145732
  488.3 117.8 %all-to-all-start.1 = ((bf16[8,128,1024]{2,1,0:T(8,128)(2,1)}), bf16[8,128,1024]{2,1,0:T(8,128)(2,1)S(1)}, u32[]{:S(2)}, u32[]{:S(2)}) async-start(bf16[8,128,1024]{2,1,0:T(8,128)(2,1)} %copy-done.45), calls=%async_computation.1 | async-start | bytes 4194304 | tf_op jit(solution)/shard_map/all_to_all | solution.py:1045
  492.3 72.0 %collective-permute-start.56 = (bf16[256,2048]{1,0:T(8,128)(2,1)}, bf16[256,2048]{1,0:T(8,128)(2,1)}, u32[]{:S(2)}, u32[]{:S(2)}) collective-permute-start(bf16[256,2048]{1,0:T(8,128)(2,1)} %copy-done.56), channel_id=1, source_target_pairs={{0,4},{4,0},{8,12},{12,8},{16,20},{20,16},{24,28},{28,24},{1,5},{5... | collective-permute-start | bytes 3145736 | tf_op jit(solution)/shard_map/up_back_y/ppermute | solution.py:535
  494.4 72.5 %collective-permute-start.40 = (bf16[768,1024]{1,0:T(8,128)(2,1)}, bf16[768,1024]{1,0:T(8,128)(2,1)}, u32[]{:S(2)}, u32[]{:S(2)}) collective-permute-start(bf16[768,1024]{1,0:T(8,128)(2,1)} %get-tuple-element.130.mine_ref), channel_id=1, source_target_pairs={{0,1},{1,0},{2,3},{3,2},{4,5},{5,4},{6,7},{7,6},{8,9},{9,8},{10,11... | collective-permute-start | bytes 4718600 | tf_op jit(solution)/shard_map/core/ppermute | solution.py:657
  494.4 55.7 %collective-permute-start.49 = (bf16[64,1280]{1,0:T(8,128)(2,1)S(1)}, bf16[64,1280]{1,0:T(8,128)(2,1)S(1)}, u32[]{:S(2)}, u32[]{:S(2)}) collective-permute-start(bf16[64,1280]{1,0:T(8,128)(2,1)S(1)} %fusion.14.mine_ref), channel_id=1, source_target_pairs={{0,16},{4,20},{8,24},{12,28},{16,0},{20,4},{24,8},{28,12},{1,17},{... | collective-permute-start | bytes 491528 | tf_op jit(solution)/shard_map/first_back_z2/ppermute | solution.py:535
  496.8 58.5 %collective-permute-start.51 = (bf16[64,896]{1,0:T(8,128)(2,1)}, bf16[64,896]{1,0:T(8,128)(2,1)S(1)}, u32[]{:S(2)}, u32[]{:S(2)}) collective-permute-start(bf16[64,896]{1,0:T(8,128)(2,1)} %fusion.21), channel_id=1, source_target_pairs={{0,16},{4,20},{8,24},{12,28},{16,0},{20,4},{24,8},{28,12},{1,17},{... | collective-permute-start | bytes 344072 | tf_op jit(solution)/shard_map/last_z2/ppermute | solution.py:535
  551.6 8.6 %collective-permute-start.50 = (bf16[128,1280]{1,0:T(8,128)(2,1)S(1)}, bf16[128,1280]{1,0:T(8,128)(2,1)}, u32[]{:S(2)}, u32[]{:S(2)}) collective-permute-start(bf16[128,1280]{1,0:T(8,128)(2,1)S(1)} %stack_rows.17.mine_ref), channel_id=1, source_target_pairs={{0,8},{4,12},{8,0},{12,4},{16,24},{20,28},{24,16},{28,20},{1,9},{5... | collective-permute-start | bytes 983048 | tf_op jit(solution)/shard_map/first_back_z1/ppermute | solution.py:535
  555.3 8.4 %collective-permute-start.54 = (bf16[64,896]{1,0:T(8,128)(2,1)S(1)}, bf16[64,896]{1,0:T(8,128)(2,1)S(1)}, u32[]{:S(2)}, u32[]{:S(2)}) collective-permute-start(bf16[64,896]{1,0:T(8,128)(2,1)S(1)} %fusion.19.mine_ref), channel_id=1, source_target_pairs={{0,16},{4,20},{8,24},{12,28},{16,0},{20,4},{24,8},{28,12},{1,17},{... | collective-permute-start | bytes 344072 | tf_op jit(solution)/shard_map/last_back_z2/ppermute | solution.py:535
  561.3 13.2 %collective-permute-start.53 = (bf16[256,1280]{1,0:T(8,128)(2,1)S(1)}, bf16[256,1280]{1,0:T(8,128)(2,1)S(1)}, u32[]{:S(2)}, u32[]{:S(2)}) collective-permute-start(bf16[256,1280]{1,0:T(8,128)(2,1)S(1)} %stack_rows.19), channel_id=1, source_target_pairs={{0,4},{4,0},{8,12},{12,8},{16,20},{20,16},{24,28},{28,24},{1,5},{5... | collective-permute-start | bytes 1966088 | tf_op jit(solution)/shard_map/first_back_y/ppermute | solution.py:535
  564.2 8.9 %collective-permute-start.55 = (bf16[128,896]{1,0:T(8,128)(2,1)S(1)}, bf16[128,896]{1,0:T(8,128)(2,1)S(1)}, u32[]{:S(2)}, u32[]{:S(2)}) collective-permute-start(bf16[128,896]{1,0:T(8,128)(2,1)S(1)} %stack_rows.20.mine_ref), channel_id=1, source_target_pairs={{0,8},{4,12},{8,0},{12,4},{16,24},{20,28},{24,16},{28,20},{1,9},{5... | collective-permute-start | bytes 688136 | tf_op jit(solution)/shard_map/last_back_z1/ppermute | solution.py:535
  567.0 29.0 %collective-permute-start.60 = (bf16[256,2048]{1,0:T(8,128)(2,1)}, bf16[256,2048]{1,0:T(8,128)(2,1)}, u32[]{:S(2)}, u32[]{:S(2)}) collective-permute-start(bf16[256,2048]{1,0:T(8,128)(2,1)} %get-tuple-element.195), channel_id=1, source_target_pairs={{0,1},{1,0},{2,3},{3,2},{4,5},{5,4},{6,7},{7,6},{8,9},{9,8},{10,11... | collective-permute-start | bytes 3145736 | tf_op jit(solution)/shard_map/core/ppermute | solution.py:657
  570.8 31.9 %collective-permute-start.43 = (bf16[4,128,1024]{2,1,0:T(8,128)(2,1)}, bf16[4,128,1024]{2,1,0:T(8,128)(2,1)}, u32[]{:S(2)}, u32[]{:S(2)}) collective-permute-start(bf16[4,128,1024]{2,1,0:T(8,128)(2,1)} %get-tuple-element.135), channel_id=1, source_target_pairs={{0,2},{1,3},{2,0},{3,1},{4,6},{5,7},{6,4},{7,5},{8,10},{9,11},{10,... | collective-permute-start | bytes 3145736 | tf_op jit(solution)/shard_map/x_activations/ppermute | solution.py:653
  573.7 12.7 %collective-permute-start.58 = (bf16[256,896]{1,0:T(8,128)(2,1)S(1)}, bf16[256,896]{1,0:T(8,128)(2,1)S(1)}, u32[]{:S(2)}, u32[]{:S(2)}) collective-permute-start(bf16[256,896]{1,0:T(8,128)(2,1)S(1)} %stack_rows.21), channel_id=1, source_target_pairs={{0,4},{4,0},{8,12},{12,8},{16,20},{20,16},{24,28},{28,24},{1,5},{5... | collective-permute-start | bytes 1376264 | tf_op jit(solution)/shard_map/last_back_y/ppermute | solution.py:535
  575.3 24.3 %collective-permute-start.57 = (bf16[256,768]{1,0:T(8,128)(2,1)}, bf16[256,768]{1,0:T(8,128)(2,1)}, u32[]{:S(2)}, u32[]{:S(2)}) collective-permute-start(bf16[256,768]{1,0:T(8,128)(2,1)} %get-tuple-element.207), channel_id=1, source_target_pairs={{0,1},{1,0},{2,3},{3,2},{4,5},{5,4},{6,7},{7,6},{8,9},{9,8},{10,11... | collective-permute-start | bytes 1179656 | tf_op jit(solution)/shard_map/core/ppermute | solution.py:657
  587.4 12.2 %collective-permute-start.59 = (bf16[256,768]{1,0:T(8,128)(2,1)}, bf16[256,768]{1,0:T(8,128)(2,1)}, u32[]{:S(2)}, u32[]{:S(2)}) collective-permute-start(bf16[256,768]{1,0:T(8,128)(2,1)} %get-tuple-element.229), channel_id=1, source_target_pairs={{0,1},{1,0},{2,3},{3,2},{4,5},{5,4},{6,7},{7,6},{8,9},{9,8},{10,11... | collective-permute-start | bytes 1179656 | tf_op jit(solution)/shard_map/core/ppermute | solution.py:657
  (110 other events, 875.6 us)

commit v3 on v2

--- a/solution.py
+++ b/solution.py
@@ -53,7 +53,7 @@
         out_shape=jax.ShapeDtypeStruct((count,) + shape, args[0].dtype),
         in_specs=[SMEM_SPEC] + [VMEM_SPEC] * len(args),
         out_specs=VMEM_SPEC,
-        compiler_params=pltpu.CompilerParams(vmem_limit_bytes=24 << 20),
+        compiler_params=pltpu.CompilerParams(vmem_limit_bytes=12 << 20),
         cost_estimate=LIGHT,
         name="route",
     )(dst, *args)
@@ -80,7 +80,7 @@
         out_shape=jax.ShapeDtypeStruct((CAP, own.shape[-1]), own.dtype),
         in_specs=[SMEM_SPEC] + [VMEM_SPEC] * 4,
         out_specs=VMEM_SPEC,
-        compiler_params=pltpu.CompilerParams(vmem_limit_bytes=24 << 20),
+        compiler_params=pltpu.CompilerParams(vmem_limit_bytes=12 << 20),
         cost_estimate=LIGHT,
         name="pack",
     )(meta, own, from_x, from_core, from_both)
@@ -124,7 +124,7 @@
         in_specs=[SMEM_SPEC, ANY_SPEC, ANY_SPEC],
         out_specs=(VMEM_SPEC, VMEM_SPEC),
         scratch_shapes=[pltpu.VMEM((CAP, width), BF), pltpu.SemaphoreType.DMA((2,))],
-        compiler_params=pltpu.CompilerParams(vmem_limit_bytes=24 << 20),
+        compiler_params=pltpu.CompilerParams(vmem_limit_bytes=12 << 20),
         cost_estimate=LIGHT,
         name="unpack",
     )(meta, mine, other)
@@ -189,7 +189,7 @@
         ),
         in_specs=[SMEM_SPEC, VMEM_SPEC],
         out_specs=(VMEM_SPEC, VMEM_SPEC),
-        compiler_params=pltpu.CompilerParams(vmem_limit_bytes=24 << 20),
+        compiler_params=pltpu.CompilerParams(vmem_limit_bytes=12 << 20),
         cost_estimate=LIGHT,
         name="attend",
     )(meta, qkv)
@@ -260,7 +260,7 @@
         out_shape=jax.ShapeDtypeStruct((qkv.shape[0], qkv.shape[1] // 2), BF),
         in_specs=[SMEM_SPEC] + [VMEM_SPEC] * 3,
         out_specs=VMEM_SPEC,
-        compiler_params=pltpu.CompilerParams(vmem_limit_bytes=24 << 20),
+        compiler_params=pltpu.CompilerParams(vmem_limit_bytes=12 << 20),
         cost_estimate=LIGHT,
         name="attend_back",
     )(meta, qkv, lse, grad_ctx)
@@ -287,7 +287,7 @@
         out_shape=jax.ShapeDtypeStruct((4 * rows, columns // 2), BF),
         in_specs=[SMEM_SPEC] + [VMEM_SPEC] * 4,
         out_specs=VMEM_SPEC,
-        compiler_params=pltpu.CompilerParams(vmem_limit_bytes=24 << 20),
+        compiler_params=pltpu.CompilerParams(vmem_limit_bytes=12 << 20),
         cost_estimate=LIGHT,
         name="assemble",
     )(meta, own, from_x, from_core, from_both)
@@ -314,7 +314,7 @@
         out_shape=jax.ShapeDtypeStruct((blocks[0].shape[0], columns), F32),
         in_specs=[SMEM_SPEC] + [VMEM_SPEC] * len(blocks),
         out_specs=VMEM_SPEC,
-        compiler_params=pltpu.CompilerParams(vmem_limit_bytes=24 << 20),
+        compiler_params=pltpu.CompilerParams(vmem_limit_bytes=12 << 20),
         cost_estimate=LIGHT,
         name="spread_columns",
     )(meta, *blocks)
@@ -335,7 +335,7 @@
         out_shape=jax.ShapeDtypeStruct((2 * mine.shape[0], mine.shape[1]), kind),
         in_specs=[SMEM_SPEC] + [VMEM_SPEC] * 2,
         out_specs=VMEM_SPEC,
-        compiler_params=pltpu.CompilerParams(vmem_limit_bytes=24 << 20),
+        compiler_params=pltpu.CompilerParams(vmem_limit_bytes=12 << 20),
         cost_estimate=LIGHT,
         name="stack_rows",
     )(meta, mine, other)
@@ -373,7 +373,7 @@
         ),
         in_specs=[SMEM_SPEC] + [VMEM_SPEC] * 4,
         out_specs=(VMEM_SPEC, VMEM_SPEC),
-        compiler_params=pltpu.CompilerParams(vmem_limit_bytes=24 << 20),
+        compiler_params=pltpu.CompilerParams(vmem_limit_bytes=12 << 20),
         cost_estimate=LIGHT,
         name="merge_shares",
     )(meta, w_down, far_up_high, mine, other)
@@ -421,7 +421,7 @@
         out_shape=(shape, shape),
         in_specs=[SMEM_SPEC] + [VMEM_SPEC] * 3,
         out_specs=(VMEM_SPEC, VMEM_SPEC),
-        compiler_params=pltpu.CompilerParams(vmem_limit_bytes=24 << 20),
+        compiler_params=pltpu.CompilerParams(vmem_limit_bytes=12 << 20),
         cost_estimate=LIGHT,
         name="up_product",
     )(meta, low, weight, bias)
@@ -460,7 +460,7 @@
         out_shape=jax.ShapeDtypeStruct((lefts[0].shape[0], width), kind),
         in_specs=[SMEM_SPEC] + [VMEM_SPEC] * len(args),
         out_specs=VMEM_SPEC,
-        compiler_params=pltpu.CompilerParams(vmem_limit_bytes=24 << 20),
+        compiler_params=pltpu.CompilerParams(vmem_limit_bytes=12 << 20),
         cost_estimate=LIGHT,
         name="rows_product",
     )(meta, *args)
@@ -499,7 +499,7 @@
         in_specs=[SMEM_SPEC, SMEM_SPEC] + [VMEM_SPEC] * len(args),
         out_specs=VMEM_SPEC,
         scratch_shapes=[pltpu.VMEM((count, rows), BF)],
-        compiler_params=pltpu.CompilerParams(vmem_limit_bytes=24 << 20),
+        compiler_params=pltpu.CompilerParams(vmem_limit_bytes=12 << 20),
         cost_estimate=LIGHT,
         name="grad_product",
     )(meta, jnp.asarray(start, jnp.int32)[None], *args)
@@ -768,6 +768,9 @@
     )[None, :]
 
 
+    first_weights = over_x(
+        after(jnp.concatenate([w_qkv, w_out], axis=1), sent_tokens), "x_first_weights"
+    )
     if group_count == 8:
         share = w_down.shape[0] // 8
         turn = (group_id % 2) * 4 + group_id // 4 + 2 * (group_id // 2 % 2)
@@ -778,7 +781,7 @@
             + jnp.split(up_lines, 4, axis=1),
             axis=0,
         )
-        mixed = over_x(after(mixed, small), "x_shares")
+        mixed = over_x(after(mixed, sent_tokens), "x_shares")
     else:
         mixed = small
     if group_count == slots:
@@ -787,7 +790,7 @@
         placed = jnp.sum(
             jnp.where(came[:, None] == slot_ids[None, :], list_pos[None, :], 0), axis=1
         )
-        lists = route(after(got, small, mixed), placed.astype(jnp.int32))
+        lists = route(got, placed.astype(jnp.int32))
     else:
         arrived = [sent_tokens[0]]
         for k in range(1, slots):
@@ -805,20 +808,18 @@
             [jnp.where(chip == 0, own, far), jnp.where(chip == 0, far, own)], axis=0
         )
 
-    first_weights = over_x(
-        after(jnp.concatenate([w_qkv, w_out], axis=1), mixed), "x_first_weights"
-    )
     far_qkv, far_out = first_weights[:, : 3 * width], first_weights[:, 3 * width :]
     full_qkv = assemble(meta, 3, *swapped(w_qkv, far_qkv))
     full_out = by_chip(w_out, far_out)
 
+    cot_lists = route(cotangent, list_pos)
     far_tokens = over_x(lists[4:], "x_tokens")
     if group_count == 8:
         pair = stack_rows(meta, AT_Z2, mixed, moved("share_z2", mixed, "seq", SWAP_Z2), BF)
         gate = four = stack_rows(meta, AT_Z1, pair, moved("share_z1", pair, "seq", SWAP_Z1), BF)
     else:
         gate = far_tokens
-    rows_in = pack(meta, *swapped(lists[:4], after(far_tokens, gate)))
+    rows_in = pack(meta, *swapped(lists[:4], after(far_tokens, gate, cot_lists)))
     w_up_later, _ = lax.optimization_barrier((w_up, far_tokens))
     if group_count == 8:
         far_up_high = over_x(w_up_later[part // 2 :], "x_up_weight")
@@ -826,10 +827,7 @@
     else:
         far_up = over_x(w_up_later, "x_up_weight")
         full_down = by_chip(w_down, over_x(w_down))
-    cot_lists = route(cotangent, list_pos)
-    cot_far_in, _ = lax.optimization_barrier((cot_lists[4:], far_tokens))
-    cot_rows = pack(meta, *swapped(cot_lists[:4], over_x(cot_far_in, "x_cotangent")))
-
+        cot_far_in = cot_lists[4:]
     def halves(value):
         return (
             lax.dynamic_slice_in_dim(value, core * HALF, HALF, axis=0),
@@ -851,8 +849,10 @@
         context, other_four, far_up_high = lax.optimization_barrier(
             (context, other_four, far_up_high)
         )
+        cot_far_in = after(cot_lists[4:], far_up_high)
         full_down, far_up = merge_shares(meta, w_down, far_up_high, four, other_four)
     full_up = assemble(meta, 1, *swapped(w_up, far_up))
+    cot_arrived = over_x(cot_far_in, "x_cotangent")
     ctx_mine, ctx_other = halves(context)
     rows_mine, _ = halves(rows_in)
     resid_attn = (
@@ -863,9 +863,9 @@
     low_mine = hidden.astype(BF)
     low_other = over_core(low_mine)
 
-    low_mine = after(low_mine, cot_rows)
     act_mine, slope_mine = up_product(meta, MINE, low_mine, full_up, up_bias)
     act_other, slope_other = up_product(meta, OTHER, low_other, full_up, up_bias)
+    cot_rows = pack(meta, *swapped(cot_lists[:4], after(cot_arrived, act_mine)))
     resid_mlp = core_sum([act_mine], [act_other], [full_down], False) + hidden + down_bias
     unit_mlp, rstd_mlp = normed(resid_mlp)
     final_mine = (unit_mlp * mlp_gain + mlp_shift).astype(BF)
@@ -945,10 +945,13 @@
         rows_product(meta, MINE, [attn_mine], [full_out], True, BF),
         rows_product(meta, OTHER, [attn_other], [full_out], True, BF),
     )
-    grad_first = attend_back(meta, qkv, lse, grad_ctx, 0)
+    y_own, y_far = unpack(meta, final_mine, over_core(after(final_mine, gh_other)))
+    y_arrived = over_x(y_far, "x_activations")
+    grad_first = attend_back(meta, qkv, lse, after(grad_ctx, y_far), 0)
     down_sum.step_x(grad_first)
     up_sum.step_z1(down_sum.token)
     grad_first = after(grad_first, up_sum.token)
+
     first_far, first_own = (
         jnp.concatenate(
             [grads([rows_in], [grad_first], side * 2 * part, 2 * part, out.dtype), out], axis=1
@@ -959,9 +962,27 @@
     first_sum.start_x(first_far, first_own)
     down_sum.back_z2(first_sum.token, first_own)
     grad_last = attend_back(meta, qkv, lse, after(grad_ctx, down_sum.token), 1)
-    up_sum.step_z2(grad_last)
-    down_sum.back_z1(up_sum.token)
-    grad_last = after(grad_last, down_sum.token)
+    grad_last = after(grad_last, y_arrived)
+    down_sum.back_z1(grad_last)
+    up_sum.step_z2(down_sum.token)
+    grad_last = after(grad_last, up_sum.token)
+
+    qkv_blocks = [full_qkv[:, : 3 * part], full_qkv[:, 3 * part :]]
+    first_mine, first_other = halves(grad_first)
+    last_mine, last_other = halves(grad_last)
+    gx_other = rows_product(meta, OTHER, [first_other, last_other], qkv_blocks, True, BF)
+    gx_arrived = over_core(gx_other)
+    gx_mine = rows_product(meta, MINE, [first_mine, last_mine], qkv_blocks, True, F32)
+    gx_mine = (gx_mine + gx_arrived.astype(F32) + grad_attn2).astype(BF)
+    gx_other = over_core(gx_mine)
+    first_sum.step_y(gx_mine)
+    down_sum.back_y(first_sum.token)
+    up_sum.back_z2(down_sum.token)
+    gx_mine = after(gx_mine, up_sum.token)
+    gx_own, gx_far = unpack(meta, gx_mine, gx_other)
+    gx_arrived = over_x(gx_far, "x_grad")
+    up_sum.back_z1(gx_far)
+    grad_last = after(grad_last, up_sum.token)
     last_far, last_own = (
         grads([rows_in], [grad_last], side * 2 * part, 2 * part, kind)
         for side, kind in ((1 - chip, BF), (chip, F32))
@@ -1009,73 +1030,50 @@
     last_own = jnp.concatenate([last_own, as_columns(near_term)], axis=1)
     last_sum = SeqSum("last", meta, group_count)
     last_sum.start_x(last_far, last_own)
-    first_sum.step_y(last_sum.token)
-    up_sum.back_z2(first_sum.token)
-    grad_last = after(grad_last, up_sum.token)
-
-    qkv_blocks = [full_qkv[:, : 3 * part], full_qkv[:, 3 * part :]]
-    first_mine, first_other = halves(grad_first)
-    last_mine, last_other = halves(grad_last)
-    gx_other = rows_product(meta, OTHER, [first_other, last_other], qkv_blocks, True, BF)
-    gx_arrived = over_core(gx_other)
-    down_sum.back_y(gx_other)
-    first_sum.step_z1(down_sum.token)
-    last_mine = after(last_mine, first_sum.token)
-    gx_mine = rows_product(meta, MINE, [first_mine, last_mine], qkv_blocks, True, F32)
-    gx_mine = (gx_mine + gx_arrived.astype(F32) + grad_attn2).astype(BF)
+
+    def my_block(mine, other):
+        aligned_here = (group_id % 2) == core
+        return jnp.where(aligned_here, mine, other), jnp.where(aligned_here, other, mine)
 
     def listed(own, arriving):
         parts = [own[k] for k in range(4)] + [arriving[k] for k in range(4)]
         return route(parts, slot_at.astype(jnp.int32))
 
-    up_sum.back_z1(gx_mine)
-    gx_own, gx_far = unpack(meta, gx_mine, over_core(after(gx_mine, up_sum.token)))
-    last_sum.step_y(gx_far)
-    gx_arrived = over_x(after(gx_far, last_sum.token), "x_grad")
-    first_sum.step_z2(last_sum.token)
-    up_sum.back_y(first_sum.token)
-    last_sum.step_z1(up_sum.token)
+    first_sum.step_z1(last_sum.token)
+    grad_down = stack_rows(meta, AT_Y, *down_sum.halves(first_sum.token))
+    back = listed(gx_own, after(gx_arrived, grad_down))
+    returned = [back[0]]
+
+    def send_back(count, *gates):
+        for _ in range(count):
+            k = len(returned)
+            pairs = [(i, (i + offsets[k]) % group_count) for i in range(group_count)]
+            returned.append(moved("return", after(back[k], *gates), "seq", pairs))
+
+    send_back(2, grad_down)
+    last_sum.step_y(back)
+    up_sum.back_y(last_sum.token)
+    first_sum.step_z2(up_sum.token, returned[1])
+    send_back(1, first_sum.token)
+    last_sum.step_z1(first_sum.token, returned[2])
     first_sum.back_z2(last_sum.token)
-    last_sum.step_z2(first_sum.token)
-    back = listed(gx_own, after(gx_arrived, last_sum.token))
-    y_own, y_far = unpack(meta, final_mine, over_core(after(final_mine, gx_far)))
-    activations = listed(y_own, over_x(after(y_far, gx_arrived), "x_activations"))
-    if group_count == slots:
-        spots = (group_id + slot_ids) % slots
-        got = lax.all_to_all(
-            route(back, spots.astype(jnp.int32)), "seq", split_axis=0, concat_axis=0, tiled=True
-        )
-        came = (group_id - slot_ids) % slots
-        home = jnp.sum(
-            jnp.where(came[:, None] == slot_ids[None, :], given_of_slot[None, :], 0), axis=1
-        )
-        input_grad = route(got, home.astype(jnp.int32))
-    else:
-        returned = [back[0]]
-        for k in range(1, slots):
-            returned.append(
-                lax.ppermute(
-                    back[k],
-                    "seq",
-                    [(i, (i + offsets[k]) % group_count) for i in range(group_count)],
-                )
-            )
-        input_grad = route(returned, given_of_slot.astype(jnp.int32))
-
-    def my_block(mine, other):
-        aligned_here = (group_id % 2) == core
-        return jnp.where(aligned_here, mine, other), jnp.where(aligned_here, other, mine)
-
-    first_sum.back_z1(back)
-    grad_down = stack_rows(meta, AT_Y, *down_sum.halves(first_sum.token))
-    last_sum.back_z2(grad_down)
-    first_sum.back_y(last_sum.token)
-    last_sum.back_z1(first_sum.token)
+    send_back(1, last_sum.token)
+    last_sum.step_z2(first_sum.token, returned[3])
+    first_sum.back_z1(last_sum.token)
+    send_back(1, last_sum.token)
+    last_sum.back_z2(first_sum.token, returned[4])
     kept, sent = my_block(*up_sum.halves(last_sum.token))
     grad_w_up = spread_columns(meta, 1, 4 * ff_part, kept, over_core(sent))
-    last_sum.back_y(kept)
+    first_sum.back_y(kept)
+    send_back(1, last_sum.token)
+    last_sum.back_z1(first_sum.token, returned[5])
+    send_back(1, first_sum.token)
+    last_sum.back_y(last_sum.token, returned[6])
     first_halves = first_sum.halves(last_sum.token)
-    last_halves = last_sum.halves()
+    last_halves = last_sum.halves(returned[7])
+    activations = listed(y_own, after(y_arrived, last_sum.token))
+    input_grad = route(returned, given_of_slot.astype(jnp.int32))
+
     blocks = []
     for mine, other in (first_halves, last_halves):
         kept, sent = my_block(mine[:, : 3 * part], other[:, : 3 * part])

time: 615 us -> 574 us (0.933)
  waiting for transfers between devices: 206 us -> 141 us
  starting transfers between devices: 68.5 us -> 94.4 us
  Pallas kernels: 198 us -> 190 us
    ppermute x31 -> x38, waiting for transfers between devices: 145 us -> 101 us  [moved(): return lax.ppermute(value, axis, pairs)]
    ppermute x31 -> x38, starting transfers between devices: 37.1 us -> 68.9 us  [moved(): return lax.ppermute(value, axis, pairs)]
    ppermute x8, waiting for transfers between devices: 26.9 us -> 0.09 us  [over_x(): return lax.ppermute(value, 'head', swap_x)]
    unnamed x255 -> x292, local copies, waits for them, and re-layouts: 36.5 us -> 46.5 us
    all_to_all x1, waiting for transfers between devices: 27.9 us -> 35.8 us  [on_device(): lax.all_to_all(sent_tokens, 'seq', split_axis=0, concat_axis=0, tiled=True)]
  transfers between devices with their start and end apart: 63 -> 69, of which waited for: 23 -> 25; matrix products, arithmetic and copies ran while one was open for 15% -> 16% of each run, Pallas kernels for 30% -> 30%
where the time goes in v3:
time: 574 us; the launch traced here: 564 us
  Pallas kernels  190 us (33%)
  waiting for transfers between devices  141 us (25%)
  starting transfers between devices  94.4 us (16%)
  local copies, waits for them, and re-layouts  67.8 us (12%)
  other arithmetic  60.6 us (11%)
    ppermute x38, waiting for transfers between devices, moved(): return lax.ppermute(value, axis, pairs)  101 us
    ppermute x38, starting transfers between devices, moved(): return lax.ppermute(value, axis, pairs)  68.9 us
    pallas_call x12, Pallas kernels, rows_product(): pl.pallas_call(functools.partial(_rows_kernel, count_at, turned, len(left...  48 us
    unnamed x292, local copies, waits for them, and re-layouts  46.5 us
    pallas_call x12, Pallas kernels, grad_product(): pl.pallas_call(functools.partial(_grad_kernel, len(lefts)), out_shape=jax...  46.3 us
    all_to_all x1, waiting for transfers between devices, on_device(): lax.all_to_all(sent_tokens, 'seq', split_axis=0, concat_axis=0, tiled=True)  35.8 us
    pallas_call x2, Pallas kernels, attend_back(): pl.pallas_call(functools.partial(_attend_back_kernel, block), out_shape=j...  22.3 us
    pallas_call x1, Pallas kernels, attend(): pl.pallas_call(_attend_kernel, out_shape=(jax.ShapeDtypeStruct((CAP, widt...  20.6 us
  transfers between devices with their start and end apart: 69, of which 25 were waited for; matrix products, arithmetic and copies ran while one was open for 16% of the time, Pallas kernels for 30%

profile of v3, /device:TPU:0, one launch (start us, length us, event | category | flops | bytes accessed | tf_op | source)
XLA Modules:
  0.0 563.8 jit_solution(10468326500005134680)
XLA Ops:
  5.6 7.4 %all-to-all-start = ((bf16[8,128,1024]{2,1,0:T(8,128)(2,1)}), bf16[8,128,1024]{2,1,0:T(8,128)(2,1)S(1)}, u32[]{:S(2)}, u32[]{:S(2)}) async-start(bf16[8,128,1024]{2,1,0:T(8,128)(2,1)} %copy-done.48), calls=%async_computation | async-start | bytes 4194304 | tf_op jit(solution)/shard_map/all_to_all | solution.py:788
  20.7 2.9 pad_maximum_fusion
  32.4 2.9 collective-permute-start.2
  35.3 35.8 %all-to-all-done.refs_0_ = bf16[8,128,1024]{2,1,0:T(8,128)(2,1)S(1)} async-done(((bf16[8,128,1024]{2,1,0:T(8,128)(2,1)}), bf16[8,128,1024]{2,1,0:T(8,128)(2,1)S(1)}, u32[]{:S(2)}, u32[]{:S(2)}) %all-to-all-start) | async-done | bytes 2097184 | tf_op jit(solution)/shard_map/all_to_all | solution.py:788
  84.0 13.5 %collective-permute-done.3.other_ref = bf16[384,1024]{1,0:T(8,128)(2,1)S(1)} collective-permute-done((bf16[384,1024]{1,0:T(8,128)(2,1)S(1)}, bf16[384,1024]{1,0:T(8,128)(2,1)S(1)}, u32[]{:S(2)}, u32[]{:S(2)}) %collective-permute-start.3) | collective-permute-done | bytes 786464 | tf_op jit(solution)/shard_map/share_z1/ppermute | solution.py:535
  112.3 2.7 pack.2.refs_0_
  115.0 5.3 add_convert_fusion.qkv_ref
  120.3 20.6 %attend.1 = (bf16[1536,512]{1,0:T(8,128)(2,1)S(1)}, f32[4,8,1,512]{3,2,1,0:T(1,128)S(1)}) custom-call(s32[24]{0:T(128)S(1)} %concatenate.62.meta_ref, bf16[1536,1536]{1,0:T(8,128)(2,1)S(1)} %add_convert_fusion.qkv_ref), custom_call_target="tpu_custom_call" | custom-call | bytes 1024 | tf_op jit(solution)/shard_map/attend/pallas_call | solution.py:184
  155.5 5.7 %up_product.3 = (bf16[768,2048]{1,0:T(8,128)(2,1)S(1)}, bf16[768,2048]{1,0:T(8,128)(2,1)S(1)}) custom-call(s32[24]{0:T(128)S(1)} %concatenate.62.meta_ref, bf16[768,1024]{1,0:T(8,128)(2,1)S(1)} %collective-permute-done.16.low_ref.refs_1_, bf16[1024,2048]{1,0:T(8,128)(2,1)S(1)} %assemble.3.weight_ref.refs_1_, f32[1,2048]{1,0:T(1,128)S(1)} %bitcast.184), custom_call_target="tpu_custom_call" | custom-call | bytes 1024 | tf_op jit(solution)/shard_map/up_product/pallas_call | solution.py:419
  161.2 3.5 rows_product.15
  164.7 4.0 collective-permute-start.17
  168.8 8.0 %up_product.2 = (bf16[768,2048]{1,0:T(8,128)(2,1)S(1)}, bf16[768,2048]{1,0:T(8,128)(2,1)S(1)}) custom-call(s32[24]{0:T(128)S(1)} %concatenate.62.meta_ref, bf16[768,1024]{1,0:T(8,128)(2,1)S(1)} %fusion.3.low_ref.refs_0_, bf16[1024,2048]{1,0:T(8,128)(2,1)S(1)} %assemble.3.weight_ref.refs_1_, f32[1,2048]{1,0:T(1,128)S(1)} %bitcast.185), custom_call_target="tpu_custom_call" | custom-call | bytes 1024 | tf_op jit(solution)/shard_map/up_product/pallas_call | solution.py:419
  178.7 4.9 rows_product.14
  191.2 3.7 collective-permute-done.21.refs_3_.refs_0_
  198.7 4.7 grad_product.13
  203.4 4.7 grad_product.12
  215.5 7.2 %rows_product.16.refs_2_.refs_0_ = bf16[768,2048]{1,0:T(8,128)(2,1)S(1)} custom-call(s32[24]{0:T(128)S(1)} %concatenate.62.meta_ref, bf16[768,1024]{1,0:T(8,128)(2,1)} %get-tuple-element.106.refs_2_.refs_0_, bf16[2048,1024]{1,0:T(8,128)(2,1)S(1)} %copy-done.15, bf16[768,2048]{1,0:T(8,128)(2,1)S(1)} %copy-done.64), custom_call_target="tpu_custom_call" | custom-call | bytes 1024 | tf_op jit(solution)/shard_map/rows_product/pallas_call | solution.py:458
  222.8 6.4 %rows_product.17.refs_3_.refs_0_ = bf16[768,2048]{1,0:T(8,128)(2,1)S(1)} custom-call(s32[24]{0:T(128)S(1)} %concatenate.62.meta_ref, bf16[768,1024]{1,0:T(8,128)(2,1)} %collective-permute-done.21.refs_3_.refs_0_, bf16[2048,1024]{1,0:T(8,128)(2,1)S(1)} %copy-done.15, bf16[768,2048]{1,0:T(8,128)(2,1)S(1)} %copy-done.62), custom_call_target="tpu_custom_call" | custom-call | bytes 1024 | tf_op jit(solution)/shard_map/rows_product/pallas_call | solution.py:458
  229.3 5.7 %grad_product.14 = bf16[512,2048]{1,0:T(8,128)(2,1)S(1)} custom-call(s32[24]{0:T(128)S(1)} %concatenate.62.meta_ref, s32[1]{0:T(128)} %bitcast.21.at_ref, bf16[768,1024]{1,0:T(8,128)(2,1)S(1)} %copy-done.27, bf16[768,1024]{1,0:T(8,128)(2,1)S(1)} %copy-done.38, bf16[768,2048]{1,0:T(8,128)(2,1)S(1)} %rows_product.16.refs_2_.refs_0_, ...), custom_call_target="tpu_custom_call" | custom-call | bytes 1024 | tf_op jit(solution)/shard_map/grad_product/pallas_call | solution.py:496
  235.1 4.8 rows_product.18
  246.4 4.7 grad_product.16
  251.2 4.9 grad_product.15
  256.1 5.7 %grad_product.17 = f32[512,2048]{1,0:T(8,128)S(1)} custom-call(s32[24]{0:T(128)S(1)} %concatenate.62.meta_ref, s32[1]{0:T(128)} %bitcast.26.at_ref, bf16[768,1024]{1,0:T(8,128)(2,1)S(1)} %copy-done.28, bf16[768,1024]{1,0:T(8,128)(2,1)S(1)} %copy-done.39, bf16[768,2048]{1,0:T(8,128)(2,1)S(1)} %copy-done.4, bf16[768,2048]{1,0:T(8,128)(2,1)S(1)} %copy-done.6), custom_call_target="tpu_custom_call" | custom-call | bytes 1024 | tf_op jit(solution)/shard_map/grad_product/pallas_call | solution.py:496
  261.9 2.8 maximum_add_fusion
  268.7 5.0 rows_product.19
  273.7 5.0 multiply_reduce_fusion.1
  278.9 2.5 convert_reduce_fusion.5
  282.4 9.7 %collective-permute-done.28 = bf16[512,1024]{1,0:T(8,128)(2,1)S(1)} collective-permute-done((bf16[512,1024]{1,0:T(8,128)(2,1)}, bf16[512,1024]{1,0:T(8,128)(2,1)S(1)}, u32[]{:S(2)}, u32[]{:S(2)}) %collective-permute-start.28) | collective-permute-done | bytes 1048608 | tf_op jit(solution)/shard_map/down_z1/ppermute | solution.py:535
  292.7 2.6 collective-permute-start.29
  295.3 2.5 convert_add_fusion
  304.6 11.4 %attend_back.2.refs_1_ = bf16[1536,768]{1,0:T(8,128)(2,1)S(1)} custom-call(s32[24]{0:T(128)S(1)} %concatenate.62.meta_ref, bf16[1536,1536]{1,0:T(8,128)(2,1)S(1)} %bitcast.179, f32[4,8,1,512]{3,2,1,0:T(1,128)S(1)} %get-tuple-element.114.lse_ref, bf16[1536,512]{1,0:T(8,128)(2,1)S(1)} %pad_maximum_fusion.2.gctx_ref), custom_call_target="tpu_custom_call" | custom-call | bytes 1024 | tf_op jit(solution)/shard_map/attend_back/pallas_call | solution.py:258
  323.7 2.7 grad_product.20
  330.1 10.9 %attend_back.3.refs_1_ = bf16[1536,768]{1,0:T(8,128)(2,1)S(1)} custom-call(s32[24]{0:T(128)S(1)} %concatenate.62.meta_ref, bf16[1536,1536]{1,0:T(8,128)(2,1)S(1)} %bitcast.179, f32[4,8,1,512]{3,2,1,0:T(1,128)S(1)} %get-tuple-element.114.lse_ref, bf16[1536,512]{1,0:T(8,128)(2,1)S(1)} %pad_maximum_fusion.2.gctx_ref), custom_call_target="tpu_custom_call" | custom-call | bytes 1024 | tf_op jit(solution)/shard_map/attend_back/pallas_call | solution.py:258
  345.5 4.3 rows_product.23
  362.2 2.7 grad_product.21
  369.9 4.2 rows_product.22
  374.1 3.6 add_convert_fusion.1.mine_ref
  377.7 3.7 collective-permute-done.36
  392.2 4.3 unpack.3
  397.4 4.1 collective-permute-done.38.other_ref
  403.7 2.7 grad_product.22
  413.1 2.7 grad_product.23
  421.0 8.0 %collective-permute-done.44 = bf16[256,1280]{1,0:T(8,128)(2,1)} collective-permute-done((bf16[256,1280]{1,0:T(8,128)(2,1)}, bf16[256,1280]{1,0:T(8,128)(2,1)}, u32[]{:S(2)}, u32[]{:S(2)}) %collective-permute-start.44) | collective-permute-done | bytes 655392 | tf_op jit(solution)/shard_map/first_y/ppermute | solution.py:535
  433.4 3.5 stack_rows.16
  440.0 11.5 %collective-permute-done.41 = bf16[512,896]{1,0:T(8,128)(2,1)} collective-permute-done((bf16[512,896]{1,0:T(8,128)(2,1)}, bf16[512,896]{1,0:T(8,128)(2,1)}, u32[]{:S(2)}, u32[]{:S(2)}) %collective-permute-start.41) | collective-permute-done | bytes 917536 | tf_op jit(solution)/shard_map/last_x/ppermute | solution.py:535
  451.5 3.2 collective-permute-start.48
  462.7 3.7 collective-permute-start.52
  468.9 8.1 %collective-permute-done.45 = bf16[256,896]{1,0:T(8,128)(2,1)S(1)} collective-permute-done((bf16[256,896]{1,0:T(8,128)(2,1)S(1)}, bf16[256,896]{1,0:T(8,128)(2,1)S(1)}, u32[]{:S(2)}, u32[]{:S(2)}) %collective-permute-start.45) | collective-permute-done | bytes 458784 | tf_op jit(solution)/shard_map/last_y/ppermute | solution.py:535
  477.2 4.4 collective-permute-done.51
  481.6 2.9 collective-permute-start.55
  484.5 11.7 %collective-permute-done.52.refs_3_ = bf16[128,1024]{1,0:T(8,128)(2,1)S(1)} collective-permute-done((bf16[128,1024]{1,0:T(8,128)(2,1)S(1)}, bf16[128,1024]{1,0:T(8,128)(2,1)S(1)}, u32[]{:S(2)}, u32[]{:S(2)}) %collective-permute-start.52) | collective-permute-done | bytes 262176 | tf_op jit(solution)/shard_map/return/ppermute | solution.py:535
  497.1 2.5 collective-permute-start.57
  499.6 6.1 %collective-permute-start.59 = (bf16[128,1024]{1,0:T(8,128)(2,1)}, bf16[128,1024]{1,0:T(8,128)(2,1)}, u32[]{:S(2)}, u32[]{:S(2)}) collective-permute-start(bf16[128,1024]{1,0:T(8,128)(2,1)} %get-tuple-element.157), channel_id=1, source_target_pairs={{0,20},{4,24},{8,28},{12,0},{16,4},{20,8},{24,12},{28,16},{1,21},{... | collective-permute-start | bytes 786440 | tf_op jit(solution)/shard_map/return/ppermute | solution.py:535
  508.7 4.2 collective-permute-done.57.other_ref
  513.5 3.8 collective-permute-start.63
  517.3 4.1 collective-permute-start.56
  523.4 3.3 collective-permute-done.56.other_ref
  527.4 5.8 %collective-permute-start.60 = (bf16[128,896]{1,0:T(8,128)(2,1)S(1)}, bf16[128,896]{1,0:T(8,128)(2,1)S(1)}, u32[]{:S(2)}, u32[]{:S(2)}) collective-permute-start(bf16[128,896]{1,0:T(8,128)(2,1)S(1)} %stack_rows.20.mine_ref), channel_id=1, source_target_pairs={{0,8},{4,12},{8,0},{12,4},{16,24},{20,28},{24,16},{28,20},{1,9},{5... | collective-permute-start | bytes 688136 | tf_op jit(solution)/shard_map/last_back_z1/ppermute | solution.py:535
  533.2 2.7 collective-permute-start.62
  536.0 3.7 collective-permute-done.60.other_ref
  543.0 2.5 route.11
  549.4 3.0 collective-permute-done.65
  557.9 2.8 spread_columns.3
  560.7 2.9 spread_columns.2
  (574 shorter events, 197.2 us)
Async XLA Ops:
  5.6 65.5 %all-to-all-start = ((bf16[8,128,1024]{2,1,0:T(8,128)(2,1)}), bf16[8,128,1024]{2,1,0:T(8,128)(2,1)S(1)}, u32[]{:S(2)}, u32[]{:S(2)}) async-start(bf16[8,128,1024]{2,1,0:T(8,128)(2,1)} %copy-done.48), calls=%async_computation | async-start | bytes 4194304 | tf_op jit(solution)/shard_map/all_to_all | solution.py:788
  14.9 15.3 %collective-permute-start.9 = (bf16[1,3072]{1,0:T(2,128)(2,1)S(1)}, bf16[1,3072]{1,0:T(2,128)(2,1)S(1)}, u32[]{:S(2)}, u32[]{:S(2)}) collective-permute-start(bf16[1,3072]{1,0:T(2,128)(2,1)S(1)} %broadcast_in_dim.204), channel_id=1, source_target_pairs={{0,1},{1,0},{2,3},{3,2},{4,5},{5,4},{6,7},{7,6},{8,9},{9,8},{10,11... | collective-permute-start | bytes 18440 | tf_op jit(solution)/shard_map/core/ppermute | solution.py:657
  19.1 13.4 %collective-permute-start.1 = (bf16[192,1024]{1,0:T(8,128)(2,1)S(1)}, bf16[192,1024]{1,0:T(8,128)(2,1)S(1)}, u32[]{:S(2)}, u32[]{:S(2)}) collective-permute-start(bf16[192,1024]{1,0:T(8,128)(2,1)S(1)} %dynamic-slice_dynamic-update-slice_fusion.1), channel_id=1, source_target_pairs={{0,2},{1,3},{2,0},{3,1},{4,6},{5,7},{6,4},{7,5},{8,10},{9,11},{10,... | collective-permute-start | bytes 1179656 | tf_op jit(solution)/shard_map/x_shares/ppermute | solution.py:653
  20.6 87.6 %collective-permute-start.7 = (bf16[256,3072]{1,0:T(8,128)(2,1)}, bf16[256,3072]{1,0:T(8,128)(2,1)}, u32[]{:S(2)}, u32[]{:S(2)}) collective-permute-start(bf16[256,3072]{1,0:T(8,128)(2,1)} %refs_0_.6), channel_id=1, source_target_pairs={{0,1},{1,0},{2,3},{3,2},{4,5},{5,4},{6,7},{7,6},{8,9},{9,8},{10,11... | collective-permute-start | bytes 4718600 | tf_op jit(solution)/shard_map/core/ppermute | solution.py:657
  23.6 56.6 %collective-permute-start.6 = (bf16[256,4096]{1,0:T(8,128)(2,1)}, bf16[256,4096]{1,0:T(8,128)(2,1)}, u32[]{:S(2)}, u32[]{:S(2)}) collective-permute-start(bf16[256,4096]{1,0:T(8,128)(2,1)} %pad_maximum_fusion), channel_id=1, source_target_pairs={{0,2},{1,3},{2,0},{3,1},{4,6},{5,7},{6,4},{7,5},{8,10},{9,11},{10,... | collective-permute-start | bytes 6291464 | tf_op jit(solution)/shard_map/x_first_weights/ppermute | solution.py:653
  30.9 51.0 %collective-permute-start.10 = (bf16[2,3072]{1,0:T(2,128)(2,1)}, bf16[2,3072]{1,0:T(2,128)(2,1)}, u32[]{:S(2)}, u32[]{:S(2)}) collective-permute-start(bf16[2,3072]{1,0:T(2,128)(2,1)} %pad_maximum_fusion.5), channel_id=1, source_target_pairs={{0,2},{1,3},{2,0},{3,1},{4,6},{5,7},{6,4},{7,5},{8,10},{9,11},{10,... | collective-permute-start | bytes 36872 | tf_op jit(solution)/shard_map/x/ppermute | solution.py:653
  32.4 46.6 %collective-permute-start.2 = (bf16[192,1024]{1,0:T(8,128)(2,1)S(1)}, bf16[192,1024]{1,0:T(8,128)(2,1)}, u32[]{:S(2)}, u32[]{:S(2)}) collective-permute-start(bf16[192,1024]{1,0:T(8,128)(2,1)S(1)} %collective-permute-done.1.mine_ref), channel_id=1, source_target_pairs={{0,16},{4,20},{8,24},{12,28},{16,0},{20,4},{24,8},{28,12},{1,17},{... | collective-permute-start | bytes 1179656 | tf_op jit(solution)/shard_map/share_z2/ppermute | solution.py:535
  73.0 25.4 %collective-permute-start = (bf16[4,128,1024]{2,1,0:T(8,128)(2,1)}, bf16[4,128,1024]{2,1,0:T(8,128)(2,1)}, u32[]{:S(2)}, u32[]{:S(2)}) collective-permute-start(bf16[4,128,1024]{2,1,0:T(8,128)(2,1)} %get-tuple-element.221), channel_id=1, source_target_pairs={{0,2},{1,3},{2,0},{3,1},{4,6},{5,7},{6,4},{7,5},{8,10},{9,11},{10,... | collective-permute-start | bytes 3145736 | tf_op jit(solution)/shard_map/x_tokens/ppermute | solution.py:653
  80.2 17.3 %collective-permute-start.3 = (bf16[384,1024]{1,0:T(8,128)(2,1)S(1)}, bf16[384,1024]{1,0:T(8,128)(2,1)S(1)}, u32[]{:S(2)}, u32[]{:S(2)}) collective-permute-start(bf16[384,1024]{1,0:T(8,128)(2,1)S(1)} %stack_rows.11.mine_ref), channel_id=1, source_target_pairs={{0,8},{4,12},{8,0},{12,4},{16,24},{20,28},{24,16},{28,20},{1,9},{5... | collective-permute-start | bytes 2359304 | tf_op jit(solution)/shard_map/share_z1/ppermute | solution.py:535
  81.8 26.4 %collective-permute-start.8 = (bf16[256,3072]{1,0:T(8,128)(2,1)S(1)}, bf16[256,3072]{1,0:T(8,128)(2,1)S(1)}, u32[]{:S(2)}, u32[]{:S(2)}) collective-permute-start(bf16[256,3072]{1,0:T(8,128)(2,1)S(1)} %slice.308.refs_1_), channel_id=1, source_target_pairs={{0,1},{1,0},{2,3},{3,2},{4,5},{5,4},{6,7},{7,6},{8,9},{9,8},{10,11... | collective-permute-start | bytes 4718600 | tf_op jit(solution)/shard_map/core/ppermute | solution.py:657
  98.2 14.1 %collective-permute-start.4 = (bf16[4,128,1024]{2,1,0:T(8,128)(2,1)S(1)}, bf16[4,128,1024]{2,1,0:T(8,128)(2,1)S(1)}, u32[]{:S(2)}, u32[]{:S(2)}) collective-permute-start(bf16[4,128,1024]{2,1,0:T(8,128)(2,1)S(1)} %get-tuple-element.222.a0), channel_id=1, source_target_pairs={{0,1},{1,0},{2,3},{3,2},{4,5},{5,4},{6,7},{7,6},{8,9},{9,8},{10,11... | collective-permute-start | bytes 3145736 | tf_op jit(solution)/shard_map/core/ppermute | solution.py:657
  98.3 14.0 %collective-permute-start.5 = (bf16[4,128,1024]{2,1,0:T(8,128)(2,1)}, bf16[4,128,1024]{2,1,0:T(8,128)(2,1)S(1)}, u32[]{:S(2)}, u32[]{:S(2)}) collective-permute-start(bf16[4,128,1024]{2,1,0:T(8,128)(2,1)} %collective-permute-done.a1), channel_id=1, source_target_pairs={{0,1},{1,0},{2,3},{3,2},{4,5},{5,4},{6,7},{7,6},{8,9},{9,8},{10,11... | collective-permute-start | bytes 3145736 | tf_op jit(solution)/shard_map/core/ppermute | solution.py:657
  105.1 36.6 %collective-permute-start.11 = (bf16[768,1024]{1,0:T(8,128)(2,1)S(1)}, bf16[768,1024]{1,0:T(8,128)(2,1)S(1)}, u32[]{:S(2)}, u32[]{:S(2)}) collective-permute-start(bf16[768,1024]{1,0:T(8,128)(2,1)S(1)} %stack_rows.12.mine_ref), channel_id=1, source_target_pairs={{0,4},{4,0},{8,12},{12,8},{16,20},{20,16},{24,28},{28,24},{1,5},{5... | collective-permute-start | bytes 4718600 | tf_op jit(solution)/shard_map/share_y/ppermute | solution.py:535
  110.7 31.1 %collective-permute-start.12 = (bf16[128,4096]{1,0:T(8,128)(2,1)S(1)}, bf16[128,4096]{1,0:T(8,128)(2,1)S(1)}, u32[]{:S(2)}, u32[]{:S(2)}) collective-permute-start(bf16[128,4096]{1,0:T(8,128)(2,1)S(1)} %slice.236), channel_id=1, source_target_pairs={{0,2},{1,3},{2,0},{3,1},{4,6},{5,7},{6,4},{7,5},{8,10},{9,11},{10,... | collective-permute-start | bytes 3145736 | tf_op jit(solution)/shard_map/x_up_weight/ppermute | solution.py:653
  144.0 10.1 %collective-permute-start.14 = (bf16[256,4096]{1,0:T(8,128)(2,1)S(1)}, bf16[256,4096]{1,0:T(8,128)(2,1)S(1)}, u32[]{:S(2)}, u32[]{:S(2)}) collective-permute-start(bf16[256,4096]{1,0:T(8,128)(2,1)S(1)} %copy-done.54), channel_id=1, source_target_pairs={{0,1},{1,0},{2,3},{3,2},{4,5},{5,4},{6,7},{7,6},{8,9},{9,8},{10,11... | collective-permute-start | bytes 6291464 | tf_op jit(solution)/shard_map/core/ppermute | solution.py:657
  152.4 26.1 %collective-permute-start.18 = (bf16[4,128,1024]{2,1,0:T(8,128)(2,1)S(1)}, bf16[4,128,1024]{2,1,0:T(8,128)(2,1)S(1)}, u32[]{:S(2)}, u32[]{:S(2)}) collective-permute-start(bf16[4,128,1024]{2,1,0:T(8,128)(2,1)S(1)} %get-tuple-element.104), channel_id=1, source_target_pairs={{0,2},{1,3},{2,0},{3,1},{4,6},{5,7},{6,4},{7,5},{8,10},{9,11},{10,... | collective-permute-start | bytes 3145736 | tf_op jit(solution)/shard_map/x_cotangent/ppermute | solution.py:653
  164.7 20.5 %collective-permute-start.17 = (bf16[768,1024]{1,0:T(8,128)(2,1)S(1)}, bf16[768,1024]{1,0:T(8,128)(2,1)S(1)}, u32[]{:S(2)}, u32[]{:S(2)}) collective-permute-start(bf16[768,1024]{1,0:T(8,128)(2,1)S(1)} %rows_product.15), channel_id=1, source_target_pairs={{0,1},{1,0},{2,3},{3,2},{4,5},{5,4},{6,7},{7,6},{8,9},{9,8},{10,11... | collective-permute-start | bytes 4718600 | tf_op jit(solution)/shard_map/core/ppermute | solution.py:657
  168.7 14.8 %collective-permute-start.19 = (bf16[4,128,1024]{2,1,0:T(8,128)(2,1)S(1)}, bf16[4,128,1024]{2,1,0:T(8,128)(2,1)S(1)}, u32[]{:S(2)}, u32[]{:S(2)}) collective-permute-start(bf16[4,128,1024]{2,1,0:T(8,128)(2,1)S(1)} %get-tuple-element.220.a0), channel_id=1, source_target_pairs={{0,1},{1,0},{2,3},{3,2},{4,5},{5,4},{6,7},{7,6},{8,9},{9,8},{10,11... | collective-permute-start | bytes 3145736 | tf_op jit(solution)/shard_map/core/ppermute | solution.py:657
  209.7 52.2 %collective-permute-start.24 = (bf16[1024,1024]{1,0:T(8,128)(2,1)}, bf16[1024,1024]{1,0:T(8,128)(2,1)}, u32[]{:S(2)}, u32[]{:S(2)}) collective-permute-start(bf16[1024,1024]{1,0:T(8,128)(2,1)} %bitcast.20), channel_id=1, source_target_pairs={{0,4},{4,0},{8,12},{12,8},{16,20},{20,16},{24,28},{28,24},{1,5},{5... | collective-permute-start | bytes 6291464 | tf_op jit(solution)/shard_map/down_y/ppermute | solution.py:535
  239.9 33.8 %collective-permute-start.25 = (bf16[768,1024]{1,0:T(8,128)(2,1)}, bf16[768,1024]{1,0:T(8,128)(2,1)}, u32[]{:S(2)}, u32[]{:S(2)}) collective-permute-start(bf16[768,1024]{1,0:T(8,128)(2,1)} %rows_product.18), channel_id=1, source_target_pairs={{0,1},{1,0},{2,3},{3,2},{4,5},{5,4},{6,7},{7,6},{8,9},{9,8},{10,11... | collective-permute-start | bytes 4718600 | tf_op jit(solution)/shard_map/core/ppermute | solution.py:657
  241.2 54.1 %collective-permute-start.27 = (bf16[512,2048]{1,0:T(8,128)(2,1)}, bf16[512,2048]{1,0:T(8,128)(2,1)}, u32[]{:S(2)}, u32[]{:S(2)}) collective-permute-start(bf16[512,2048]{1,0:T(8,128)(2,1)} %copy-done.71), channel_id=1, source_target_pairs={{0,2},{1,3},{2,0},{3,1},{4,6},{5,7},{6,4},{7,5},{8,10},{9,11},{10,... | collective-permute-start | bytes 6291464 | tf_op jit(solution)/shard_map/up_x/ppermute | solution.py:535
  267.1 25.1 %collective-permute-start.28 = (bf16[512,1024]{1,0:T(8,128)(2,1)}, bf16[512,1024]{1,0:T(8,128)(2,1)S(1)}, u32[]{:S(2)}, u32[]{:S(2)}) collective-permute-start(bf16[512,1024]{1,0:T(8,128)(2,1)} %bitcast.32), channel_id=1, source_target_pairs={{0,8},{4,12},{8,0},{12,4},{16,24},{20,28},{24,16},{28,20},{1,9},{5... | collective-permute-start | bytes 3145736 | tf_op jit(solution)/shard_map/down_z1/ppermute | solution.py:535
  278.8 19.8 %collective-permute-start.22 = (bf16[768,1024]{1,0:T(8,128)(2,1)S(1)}, bf16[768,1024]{1,0:T(8,128)(2,1)S(1)}, u32[]{:S(2)}, u32[]{:S(2)}) collective-permute-start(bf16[768,1024]{1,0:T(8,128)(2,1)S(1)} %get-tuple-element.111.mine_ref), channel_id=1, source_target_pairs={{0,1},{1,0},{2,3},{3,2},{4,5},{5,4},{6,7},{7,6},{8,9},{9,8},{10,11... | collective-permute-start | bytes 4718600 | tf_op jit(solution)/shard_map/core/ppermute | solution.py:657
  281.4 19.4 %collective-permute-start.26 = (bf16[768,1024]{1,0:T(8,128)(2,1)S(1)}, bf16[768,1024]{1,0:T(8,128)(2,1)S(1)}, u32[]{:S(2)}, u32[]{:S(2)}) collective-permute-start(bf16[768,1024]{1,0:T(8,128)(2,1)S(1)} %get-tuple-element.120.refs_2_.refs_0_), channel_id=1, source_target_pairs={{0,1},{1,0},{2,3},{3,2},{4,5},{5,4},{6,7},{7,6},{8,9},{9,8},{10,11... | collective-permute-start | bytes 4718600 | tf_op jit(solution)/shard_map/core/ppermute | solution.py:657
  292.7 25.0 %collective-permute-start.29 = (bf16[256,1024]{1,0:T(8,128)(2,1)S(1)}, bf16[256,1024]{1,0:T(8,128)(2,1)S(1)}, u32[]{:S(2)}, u32[]{:S(2)}) collective-permute-start(bf16[256,1024]{1,0:T(8,128)(2,1)S(1)} %bitcast.208), channel_id=1, source_target_pairs={{0,16},{4,20},{8,24},{12,28},{16,0},{20,4},{24,8},{28,12},{1,17},{... | collective-permute-start | bytes 1572872 | tf_op jit(solution)/shard_map/down_z2/ppermute | solution.py:535
  297.9 23.8 %collective-permute-start.31 = (bf16[256,2048]{1,0:T(8,128)(2,1)S(1)}, bf16[256,2048]{1,0:T(8,128)(2,1)S(1)}, u32[]{:S(2)}, u32[]{:S(2)}) collective-permute-start(bf16[256,2048]{1,0:T(8,128)(2,1)S(1)} %fusion.6), channel_id=1, source_target_pairs={{0,4},{4,0},{8,12},{12,8},{16,20},{20,16},{24,28},{28,24},{1,5},{5... | collective-permute-start | bytes 3145736 | tf_op jit(solution)/shard_map/up_y/ppermute | solution.py:535
  300.1 42.3 %collective-permute-start.23 = (bf16[4,128,1024]{2,1,0:T(8,128)(2,1)S(1)}, bf16[4,128,1024]{2,1,0:T(8,128)(2,1)S(1)}, u32[]{:S(2)}, u32[]{:S(2)}) collective-permute-start(bf16[4,128,1024]{2,1,0:T(8,128)(2,1)S(1)} %get-tuple-element.113), channel_id=1, source_target_pairs={{0,2},{1,3},{2,0},{3,1},{4,6},{5,7},{6,4},{7,5},{8,10},{9,11},{10,... | collective-permute-start | bytes 3145736 | tf_op jit(solution)/shard_map/x_activations/ppermute | solution.py:653
  317.8 11.4 %collective-permute-start.30 = (bf16[128,1024]{1,0:T(8,128)(2,1)S(1)}, bf16[128,1024]{1,0:T(8,128)(2,1)S(1)}, u32[]{:S(2)}, u32[]{:S(2)}) collective-permute-start(bf16[128,1024]{1,0:T(8,128)(2,1)S(1)} %fusion.17), channel_id=1, source_target_pairs={{0,2},{1,3},{2,0},{3,1},{4,6},{5,7},{6,4},{7,5},{8,10},{9,11},{10,... | collective-permute-start | bytes 786440 | tf_op jit(solution)/shard_map/down_x/ppermute | solution.py:535
  322.1 20.9 %collective-permute-start.32 = (bf16[128,2048]{1,0:T(8,128)(2,1)S(1)}, bf16[128,2048]{1,0:T(8,128)(2,1)S(1)}, u32[]{:S(2)}, u32[]{:S(2)}) collective-permute-start(bf16[128,2048]{1,0:T(8,128)(2,1)S(1)} %fusion.9), channel_id=1, source_target_pairs={{0,8},{4,12},{8,0},{12,4},{16,24},{20,28},{24,16},{28,20},{1,9},{5... | collective-permute-start | bytes 1572872 | tf_op jit(solution)/shard_map/up_z1/ppermute | solution.py:535
  329.3 13.2 %collective-permute-start.33 = (bf16[128,1024]{1,0:T(8,128)(2,1)S(1)}, bf16[128,1024]{1,0:T(8,128)(2,1)S(1)}, u32[]{:S(2)}, u32[]{:S(2)}) collective-permute-start(bf16[128,1024]{1,0:T(8,128)(2,1)S(1)} %fusion.16.mine_ref), channel_id=1, source_target_pairs={{0,16},{4,20},{8,24},{12,28},{16,0},{20,4},{24,8},{28,12},{1,17},{... | collective-permute-start | bytes 786440 | tf_op jit(solution)/shard_map/down_back_z2/ppermute | solution.py:535
  349.8 24.3 %collective-permute-start.37 = (bf16[768,1024]{1,0:T(8,128)(2,1)}, bf16[768,1024]{1,0:T(8,128)(2,1)}, u32[]{:S(2)}, u32[]{:S(2)}) collective-permute-start(bf16[768,1024]{1,0:T(8,128)(2,1)} %rows_product.23), channel_id=1, source_target_pairs={{0,1},{1,0},{2,3},{3,2},{4,5},{5,4},{6,7},{7,6},{8,9},{9,8},{10,11... | collective-permute-start | bytes 4718600 | tf_op jit(solution)/shard_map/core/ppermute | solution.py:657
  349.8 31.6 %collective-permute-start.36 = (bf16[512,1280]{1,0:T(8,128)(2,1)}, bf16[512,1280]{1,0:T(8,128)(2,1)}, u32[]{:S(2)}, u32[]{:S(2)}) collective-permute-start(bf16[512,1280]{1,0:T(8,128)(2,1)} %maximum_maximum_fusion.1), channel_id=1, source_target_pairs={{0,2},{1,3},{2,0},{3,1},{4,6},{5,7},{6,4},{7,5},{8,10},{9,11},{10,... | collective-permute-start | bytes 3932168 | tf_op jit(solution)/shard_map/first_x/ppermute | solution.py:535
  364.9 22.2 %collective-permute-start.34 = (bf16[64,2048]{1,0:T(8,128)(2,1)S(1)}, bf16[64,2048]{1,0:T(8,128)(2,1)S(1)}, u32[]{:S(2)}, u32[]{:S(2)}) collective-permute-start(bf16[64,2048]{1,0:T(8,128)(2,1)S(1)} %fusion.15), channel_id=1, source_target_pairs={{0,16},{4,20},{8,24},{12,28},{16,0},{20,4},{24,8},{28,12},{1,17},{... | collective-permute-start | bytes 786440 | tf_op jit(solution)/shard_map/up_z2/ppermute | solution.py:535
  367.4 18.2 %collective-permute-start.35 = (bf16[256,1024]{1,0:T(8,128)(2,1)S(1)}, bf16[256,1024]{1,0:T(8,128)(2,1)S(1)}, u32[]{:S(2)}, u32[]{:S(2)}) collective-permute-start(bf16[256,1024]{1,0:T(8,128)(2,1)S(1)} %copy-done.68), channel_id=1, source_target_pairs={{0,8},{4,12},{8,0},{12,4},{16,24},{20,28},{24,16},{28,20},{1,9},{5... | collective-permute-start | bytes 1572872 | tf_op jit(solution)/shard_map/down_back_z1/ppermute | solution.py:535
  377.7 14.5 %collective-permute-start.39 = (bf16[768,1024]{1,0:T(8,128)(2,1)}, bf16[768,1024]{1,0:T(8,128)(2,1)}, u32[]{:S(2)}, u32[]{:S(2)}) collective-permute-start(bf16[768,1024]{1,0:T(8,128)(2,1)} %add_convert_fusion.1.mine_ref), channel_id=1, source_target_pairs={{0,1},{1,0},{2,3},{3,2},{4,5},{5,4},{6,7},{7,6},{8,9},{9,8},{10,11... | collective-permute-start | bytes 4718600 | tf_op jit(solution)/shard_map/core/ppermute | solution.py:657
  387.2 14.3 %collective-permute-start.38 = (bf16[64,2048]{1,0:T(8,128)(2,1)S(1)}, bf16[64,2048]{1,0:T(8,128)(2,1)}, u32[]{:S(2)}, u32[]{:S(2)}) collective-permute-start(bf16[64,2048]{1,0:T(8,128)(2,1)S(1)} %fusion.11.mine_ref), channel_id=1, source_target_pairs={{0,16},{4,20},{8,24},{12,28},{16,0},{20,4},{24,8},{28,12},{1,17},{... | collective-permute-start | bytes 786440 | tf_op jit(solution)/shard_map/up_back_z2/ppermute | solution.py:535
  390.1 43.3 %collective-permute-start.43 = (bf16[512,1024]{1,0:T(8,128)(2,1)}, bf16[512,1024]{1,0:T(8,128)(2,1)}, u32[]{:S(2)}, u32[]{:S(2)}) collective-permute-start(bf16[512,1024]{1,0:T(8,128)(2,1)} %copy-done.57), channel_id=1, source_target_pairs={{0,4},{4,0},{8,12},{12,8},{16,20},{20,16},{24,28},{28,24},{1,5},{5... | collective-permute-start | bytes 3145736 | tf_op jit(solution)/shard_map/down_back_y/ppermute | solution.py:535
  391.1 37.9 %collective-permute-start.44 = (bf16[256,1280]{1,0:T(8,128)(2,1)}, bf16[256,1280]{1,0:T(8,128)(2,1)}, u32[]{:S(2)}, u32[]{:S(2)}) collective-permute-start(bf16[256,1280]{1,0:T(8,128)(2,1)} %fusion.8), channel_id=1, source_target_pairs={{0,4},{4,0},{8,12},{12,8},{16,20},{20,16},{24,28},{28,24},{1,5},{5... | collective-permute-start | bytes 1966088 | tf_op jit(solution)/shard_map/first_y/ppermute | solution.py:535
  407.6 29.3 %collective-permute-start.42 = (bf16[4,128,1024]{2,1,0:T(8,128)(2,1)}, bf16[4,128,1024]{2,1,0:T(8,128)(2,1)}, u32[]{:S(2)}, u32[]{:S(2)}) collective-permute-start(bf16[4,128,1024]{2,1,0:T(8,128)(2,1)} %get-tuple-element.136), channel_id=1, source_target_pairs={{0,2},{1,3},{2,0},{3,1},{4,6},{5,7},{6,4},{7,5},{8,10},{9,11},{10,... | collective-permute-start | bytes 3145736 | tf_op jit(solution)/shard_map/x_grad/ppermute | solution.py:653
  408.9 47.5 %collective-permute-start.47 = (bf16[128,2048]{1,0:T(8,128)(2,1)}, bf16[128,2048]{1,0:T(8,128)(2,1)}, u32[]{:S(2)}, u32[]{:S(2)}) collective-permute-start(bf16[128,2048]{1,0:T(8,128)(2,1)} %stack_rows.15.mine_ref), channel_id=1, source_target_pairs={{0,8},{4,12},{8,0},{12,4},{16,24},{20,28},{24,16},{28,20},{1,9},{5... | collective-permute-start | bytes 1572872 | tf_op jit(solution)/shard_map/up_back_z1/ppermute | solution.py:535
  409.2 7.6 %collective-permute-start.40 = (bf16[2,3072]{1,0:T(2,128)(2,1)S(1)}, bf16[2,3072]{1,0:T(2,128)(2,1)S(1)}, u32[]{:S(2)}, u32[]{:S(2)}) collective-permute-start(bf16[2,3072]{1,0:T(2,128)(2,1)S(1)} %pad_maximum_fusion.6), channel_id=1, source_target_pairs={{0,1},{1,0},{2,3},{3,2},{4,5},{5,4},{6,7},{7,6},{8,9},{9,8},{10,11... | collective-permute-start | bytes 36872 | tf_op jit(solution)/shard_map/core/ppermute | solution.py:657
  419.7 31.8 %collective-permute-start.41 = (bf16[512,896]{1,0:T(8,128)(2,1)}, bf16[512,896]{1,0:T(8,128)(2,1)}, u32[]{:S(2)}, u32[]{:S(2)}) collective-permute-start(bf16[512,896]{1,0:T(8,128)(2,1)} %fusion.7), channel_id=1, source_target_pairs={{0,2},{1,3},{2,0},{3,1},{4,6},{5,7},{6,4},{7,5},{8,10},{9,11},{10,... | collective-permute-start | bytes 2752520 | tf_op jit(solution)/shard_map/last_x/ppermute | solution.py:535
  431.8 28.0 %collective-permute-start.46 = (bf16[128,1280]{1,0:T(8,128)(2,1)S(1)}, bf16[128,1280]{1,0:T(8,128)(2,1)S(1)}, u32[]{:S(2)}, u32[]{:S(2)}) collective-permute-start(bf16[128,1280]{1,0:T(8,128)(2,1)S(1)} %fusion.13), channel_id=1, source_target_pairs={{0,8},{4,12},{8,0},{12,4},{16,24},{20,28},{24,16},{28,20},{1,9},{5... | collective-permute-start | bytes 983048 | tf_op jit(solution)/shard_map/first_z1/ppermute | solution.py:535
  451.5 10.7 %collective-permute-start.48 = (bf16[128,1024]{1,0:T(8,128)(2,1)S(1)}, bf16[128,1024]{1,0:T(8,128)(2,1)S(1)}, u32[]{:S(2)}, u32[]{:S(2)}) collective-permute-start(bf16[128,1024]{1,0:T(8,128)(2,1)S(1)} %get-tuple-element.145), channel_id=1, source_target_pairs={{0,4},{4,8},{8,12},{12,16},{16,20},{20,24},{24,28},{28,0},{1,5},{5... | collective-permute-start | bytes 786440 | tf_op jit(solution)/shard_map/return/ppermute | solution.py:535
  456.3 20.6 %collective-permute-start.45 = (bf16[256,896]{1,0:T(8,128)(2,1)S(1)}, bf16[256,896]{1,0:T(8,128)(2,1)S(1)}, u32[]{:S(2)}, u32[]{:S(2)}) collective-permute-start(bf16[256,896]{1,0:T(8,128)(2,1)S(1)} %fusion.12), channel_id=1, source_target_pairs={{0,4},{4,0},{8,12},{12,8},{16,20},{20,16},{24,28},{28,24},{1,5},{5... | collective-permute-start | bytes 1376264 | tf_op jit(solution)/shard_map/last_y/ppermute | solution.py:535
  457.7 11.2 %collective-permute-start.49 = (bf16[128,1024]{1,0:T(8,128)(2,1)S(1)}, bf16[128,1024]{1,0:T(8,128)(2,1)S(1)}, u32[]{:S(2)}, u32[]{:S(2)}) collective-permute-start(bf16[128,1024]{1,0:T(8,128)(2,1)S(1)} %get-tuple-element.147), channel_id=1, source_target_pairs={{0,8},{4,12},{8,16},{12,20},{16,24},{20,28},{24,0},{28,4},{1,9},{5... | collective-permute-start | bytes 786440 | tf_op jit(solution)/shard_map/return/ppermute | solution.py:535
  457.7 48.6 %collective-permute-start.58 = (bf16[256,2048]{1,0:T(8,128)(2,1)S(1)}, bf16[256,2048]{1,0:T(8,128)(2,1)}, u32[]{:S(2)}, u32[]{:S(2)}) collective-permute-start(bf16[256,2048]{1,0:T(8,128)(2,1)S(1)} %stack_rows.17), channel_id=1, source_target_pairs={{0,4},{4,0},{8,12},{12,8},{16,20},{20,16},{24,28},{28,24},{1,5},{5... | collective-permute-start | bytes 3145736 | tf_op jit(solution)/shard_map/up_back_y/ppermute | solution.py:535
  462.3 19.2 %collective-permute-start.51 = (bf16[64,1280]{1,0:T(8,128)(2,1)S(1)}, bf16[64,1280]{1,0:T(8,128)(2,1)S(1)}, u32[]{:S(2)}, u32[]{:S(2)}) collective-permute-start(bf16[64,1280]{1,0:T(8,128)(2,1)S(1)} %fusion.20), channel_id=1, source_target_pairs={{0,16},{4,20},{8,24},{12,28},{16,0},{20,4},{24,8},{28,12},{1,17},{... | collective-permute-start | bytes 491528 | tf_op jit(solution)/shard_map/first_z2/ppermute | solution.py:535
  462.7 33.6 %collective-permute-start.52 = (bf16[128,1024]{1,0:T(8,128)(2,1)S(1)}, bf16[128,1024]{1,0:T(8,128)(2,1)S(1)}, u32[]{:S(2)}, u32[]{:S(2)}) collective-permute-start(bf16[128,1024]{1,0:T(8,128)(2,1)S(1)} %get-tuple-element.150), channel_id=1, source_target_pairs={{0,12},{4,16},{8,20},{12,24},{16,28},{20,0},{24,4},{28,8},{1,13},{... | collective-permute-start | bytes 786440 | tf_op jit(solution)/shard_map/return/ppermute | solution.py:535
  477.1 19.2 %collective-permute-start.50 = (bf16[128,896]{1,0:T(8,128)(2,1)S(1)}, bf16[128,896]{1,0:T(8,128)(2,1)S(1)}, u32[]{:S(2)}, u32[]{:S(2)}) collective-permute-start(bf16[128,896]{1,0:T(8,128)(2,1)S(1)} %fusion.18), channel_id=1, source_target_pairs={{0,8},{4,12},{8,0},{12,4},{16,24},{20,28},{24,16},{28,20},{1,9},{5... | collective-permute-start | bytes 688136 | tf_op jit(solution)/shard_map/last_z1/ppermute | solution.py:535
  481.6 14.9 %collective-permute-start.54 = (bf16[64,1280]{1,0:T(8,128)(2,1)S(1)}, bf16[64,1280]{1,0:T(8,128)(2,1)S(1)}, u32[]{:S(2)}, u32[]{:S(2)}) collective-permute-start(bf16[64,1280]{1,0:T(8,128)(2,1)S(1)} %fusion.14.mine_ref), channel_id=1, source_target_pairs={{0,16},{4,20},{8,24},{12,28},{16,0},{20,4},{24,8},{28,12},{1,17},{... | collective-permute-start | bytes 491528 | tf_op jit(solution)/shard_map/first_back_z2/ppermute | solution.py:535
  481.6 24.0 %collective-permute-start.55 = (bf16[128,1024]{1,0:T(8,128)(2,1)}, bf16[128,1024]{1,0:T(8,128)(2,1)S(1)}, u32[]{:S(2)}, u32[]{:S(2)}) collective-permute-start(bf16[128,1024]{1,0:T(8,128)(2,1)} %get-tuple-element.153), channel_id=1, source_target_pairs={{0,16},{4,20},{8,24},{12,28},{16,0},{20,4},{24,8},{28,12},{1,17},{... | collective-permute-start | bytes 786440 | tf_op jit(solution)/shard_map/return/ppermute | solution.py:535
  496.4 9.3 %collective-permute-start.53 = (bf16[64,896]{1,0:T(8,128)(2,1)S(1)}, bf16[64,896]{1,0:T(8,128)(2,1)S(1)}, u32[]{:S(2)}, u32[]{:S(2)}) collective-permute-start(bf16[64,896]{1,0:T(8,128)(2,1)S(1)} %fusion.21), channel_id=1, source_target_pairs={{0,16},{4,20},{8,24},{12,28},{16,0},{20,4},{24,8},{28,12},{1,17},{... | collective-permute-start | bytes 344072 | tf_op jit(solution)/shard_map/last_z2/ppermute | solution.py:535
  497.1 15.8 %collective-permute-start.57 = (bf16[128,1280]{1,0:T(8,128)(2,1)S(1)}, bf16[128,1280]{1,0:T(8,128)(2,1)S(1)}, u32[]{:S(2)}, u32[]{:S(2)}) collective-permute-start(bf16[128,1280]{1,0:T(8,128)(2,1)S(1)} %stack_rows.18.mine_ref), channel_id=1, source_target_pairs={{0,8},{4,12},{8,0},{12,4},{16,24},{20,28},{24,16},{28,20},{1,9},{5... | collective-permute-start | bytes 983048 | tf_op jit(solution)/shard_map/first_back_z1/ppermute | solution.py:535
  499.6 27.2 %collective-permute-start.59 = (bf16[128,1024]{1,0:T(8,128)(2,1)}, bf16[128,1024]{1,0:T(8,128)(2,1)}, u32[]{:S(2)}, u32[]{:S(2)}) collective-permute-start(bf16[128,1024]{1,0:T(8,128)(2,1)} %get-tuple-element.157), channel_id=1, source_target_pairs={{0,20},{4,24},{8,28},{12,0},{16,4},{20,8},{24,12},{28,16},{1,21},{... | collective-permute-start | bytes 786440 | tf_op jit(solution)/shard_map/return/ppermute | solution.py:535
  513.5 32.0 %collective-permute-start.63 = (bf16[256,1280]{1,0:T(8,128)(2,1)S(1)}, bf16[256,1280]{1,0:T(8,128)(2,1)}, u32[]{:S(2)}, u32[]{:S(2)}) collective-permute-start(bf16[256,1280]{1,0:T(8,128)(2,1)S(1)} %stack_rows.19), channel_id=1, source_target_pairs={{0,4},{4,0},{8,12},{12,8},{16,20},{20,16},{24,28},{28,24},{1,5},{5... | collective-permute-start | bytes 1966088 | tf_op jit(solution)/shard_map/first_back_y/ppermute | solution.py:535
  517.3 9.5 %collective-permute-start.56 = (bf16[64,896]{1,0:T(8,128)(2,1)S(1)}, bf16[64,896]{1,0:T(8,128)(2,1)S(1)}, u32[]{:S(2)}, u32[]{:S(2)}) collective-permute-start(bf16[64,896]{1,0:T(8,128)(2,1)S(1)} %fusion.19.mine_ref), channel_id=1, source_target_pairs={{0,16},{4,20},{8,24},{12,28},{16,0},{20,4},{24,8},{28,12},{1,17},{... | collective-permute-start | bytes 344072 | tf_op jit(solution)/shard_map/last_back_z2/ppermute | solution.py:535
  521.4 14.6 %collective-permute-start.61 = (bf16[128,1024]{1,0:T(8,128)(2,1)}, bf16[128,1024]{1,0:T(8,128)(2,1)}, u32[]{:S(2)}, u32[]{:S(2)}) collective-permute-start(bf16[128,1024]{1,0:T(8,128)(2,1)} %get-tuple-element.159), channel_id=1, source_target_pairs={{0,24},{4,28},{8,0},{12,4},{16,8},{20,12},{24,16},{28,20},{1,25},{... | collective-permute-start | bytes 786440 | tf_op jit(solution)/shard_map/return/ppermute | solution.py:535
  527.4 12.3 %collective-permute-start.60 = (bf16[128,896]{1,0:T(8,128)(2,1)S(1)}, bf16[128,896]{1,0:T(8,128)(2,1)S(1)}, u32[]{:S(2)}, u32[]{:S(2)}) collective-permute-start(bf16[128,896]{1,0:T(8,128)(2,1)S(1)} %stack_rows.20.mine_ref), channel_id=1, source_target_pairs={{0,8},{4,12},{8,0},{12,4},{16,24},{20,28},{24,16},{28,20},{1,9},{5... | collective-permute-start | bytes 688136 | tf_op jit(solution)/shard_map/last_back_z1/ppermute | solution.py:535
  533.2 9.9 %collective-permute-start.62 = (bf16[128,1024]{1,0:T(8,128)(2,1)}, bf16[128,1024]{1,0:T(8,128)(2,1)S(1)}, u32[]{:S(2)}, u32[]{:S(2)}) collective-permute-start(bf16[128,1024]{1,0:T(8,128)(2,1)} %get-tuple-element.162), channel_id=1, source_target_pairs={{0,28},{4,0},{8,4},{12,8},{16,12},{20,16},{24,20},{28,24},{1,29},{... | collective-permute-start | bytes 786440 | tf_op jit(solution)/shard_map/return/ppermute | solution.py:535
  535.9 21.9 %collective-permute-start.67 = (bf16[256,2048]{1,0:T(8,128)(2,1)}, bf16[256,2048]{1,0:T(8,128)(2,1)S(1)}, u32[]{:S(2)}, u32[]{:S(2)}) collective-permute-start(bf16[256,2048]{1,0:T(8,128)(2,1)} %get-tuple-element.209), channel_id=1, source_target_pairs={{0,1},{1,0},{2,3},{3,2},{4,5},{5,4},{6,7},{7,6},{8,9},{9,8},{10,11... | collective-permute-start | bytes 3145736 | tf_op jit(solution)/shard_map/core/ppermute | solution.py:657
  540.3 12.1 %collective-permute-start.65 = (bf16[256,896]{1,0:T(8,128)(2,1)S(1)}, bf16[256,896]{1,0:T(8,128)(2,1)S(1)}, u32[]{:S(2)}, u32[]{:S(2)}) collective-permute-start(bf16[256,896]{1,0:T(8,128)(2,1)S(1)} %stack_rows.21), channel_id=1, source_target_pairs={{0,4},{4,0},{8,12},{12,8},{16,20},{20,16},{24,28},{28,24},{1,5},{5... | collective-permute-start | bytes 1376264 | tf_op jit(solution)/shard_map/last_back_y/ppermute | solution.py:535
  547.4 13.4 %collective-permute-start.64 = (bf16[256,768]{1,0:T(8,128)(2,1)}, bf16[256,768]{1,0:T(8,128)(2,1)S(1)}, u32[]{:S(2)}, u32[]{:S(2)}) collective-permute-start(bf16[256,768]{1,0:T(8,128)(2,1)} %get-tuple-element.229), channel_id=1, source_target_pairs={{0,1},{1,0},{2,3},{3,2},{4,5},{5,4},{6,7},{7,6},{8,9},{9,8},{10,11... | collective-permute-start | bytes 1179656 | tf_op jit(solution)/shard_map/core/ppermute | solution.py:657
  553.3 7.4 %collective-permute-start.66 = (bf16[256,768]{1,0:T(8,128)(2,1)}, bf16[256,768]{1,0:T(8,128)(2,1)}, u32[]{:S(2)}, u32[]{:S(2)}) collective-permute-start(bf16[256,768]{1,0:T(8,128)(2,1)} %get-tuple-element.251), channel_id=1, source_target_pairs={{0,1},{1,0},{2,3},{3,2},{4,5},{5,4},{6,7},{7,6},{8,9},{9,8},{10,11... | collective-permute-start | bytes 1179656 | tf_op jit(solution)/shard_map/core/ppermute | solution.py:657
  (135 other events, 1159.3 us)

commit v4 on v3

--- a/solution.py
+++ b/solution.py
@@ -12,6 +12,7 @@
 HEAD_SIZE = 64
 CAP = 1536
 HALF = CAP // 2
+STEP = 512
 EPS = 1e-12
 BF = jnp.bfloat16
 F32 = jnp.float32
@@ -130,6 +131,13 @@
     )(meta, mine, other)
 
 
+def masked(scores, key_bias):
+    first = scores.shape[0] - 128
+    if first == 0:
+        return scores + key_bias
+    return jnp.concatenate([scores[:first], scores[first:] + key_bias], axis=0)
+
+
 def _attend_kernel(meta_ref, qkv_ref, ctx_ref, lse_ref):
     ctx_ref[...] = jnp.zeros_like(ctx_ref)
     width = ctx_ref.shape[1]
@@ -140,17 +148,17 @@
         offset = pl.multiple_of(meta_ref[slot], 16)
         length = meta_ref[4 + slot]
         rows = pl.ds(offset, span)
-        key_id = lax.broadcasted_iota(jnp.int32, (span, 1), 0)
+        key_id = lax.broadcasted_iota(jnp.int32, (128, 1), 0) + (span - 128)
         key_bias = jnp.where(key_id < length, 0.0, -1e30)
 
-        @pl.loop(0, width // 128)
+        @pl.loop(0, width // 128, unroll=2)
         def _(pair):
             lane0 = pl.multiple_of((pair // 2) * (3 * part) + (pair % 2) * 128, 128)
             keys = qkv_ref[rows, pl.ds(pl.multiple_of(part + lane0, 128), 128)]
             values = qkv_ref[rows, pl.ds(pl.multiple_of(2 * part + lane0, 128), 128)]
             values_t = values.astype(F32).T.astype(BF)
-            for first in range(0, span, 256):
-                step = min(span - first, 256)
+            for first in range(0, span, STEP):
+                step = min(span - first, STEP)
                 queries = qkv_ref[
                     pl.ds(pl.multiple_of(offset + first, 16), step), pl.ds(lane0, 128)
                 ]
@@ -160,7 +168,7 @@
                 for half in range(2):
                     picked = jnp.where((lane >= 64) == (half == 1), queries, jnp.zeros_like(queries))
                     scores = mm_cols(keys, picked)
-                    scores = scores + key_bias
+                    scores = masked(scores, key_bias)
                     highest = jnp.max(scores, axis=0, keepdims=True)
                     expo = jnp.exp(scores - highest)
                     total = jnp.sum(expo, axis=0, keepdims=True)
@@ -204,10 +212,10 @@
         offset = pl.multiple_of(meta_ref[slot], 16)
         length = meta_ref[4 + slot]
         rows = pl.ds(offset, span)
-        key_id = lax.broadcasted_iota(jnp.int32, (span, 1), 0)
+        key_id = lax.broadcasted_iota(jnp.int32, (128, 1), 0) + (span - 128)
         key_bias = jnp.where(key_id < length, 0.0, -1e30)
 
-        @pl.loop(0, part // 128)
+        @pl.loop(0, part // 128, unroll=2)
         def _(turn):
             pair = block * (part // 128) + turn
             out_lane = pl.multiple_of(turn * 128, 128)
@@ -219,8 +227,8 @@
             keys_t = keys.astype(F32).T.astype(BF)
             grad_keys = jnp.zeros((span, 128), F32)
             grad_values = jnp.zeros((span, 128), F32)
-            for first in range(0, span, 256):
-                step = min(span - first, 256)
+            for first in range(0, span, STEP):
+                step = min(span - first, STEP)
                 here = pl.ds(pl.multiple_of(offset + first, 16), step)
                 queries = qkv_ref[here, pl.ds(lane0, 128)] * jnp.asarray(HEAD_SIZE**-0.5, BF)
                 grad_ctx = gctx_ref[here, pl.ds(ctx_lane, 128)]
@@ -234,7 +242,9 @@
                     picked_grad = jnp.where(side, grad_ctx, jnp.zeros_like(grad_ctx))
                     scores = mm_cols(keys, picked)
                     log_total = lse_ref[slot, pair * 2 + half, :, first : first + step]
-                    probs = jnp.exp(scores - log_total + key_bias)
+                    scores = scores - log_total
+                    scores = masked(scores, key_bias)
+                    probs = jnp.exp(scores)
                     grad_values = grad_values + mm(probs.astype(BF), picked_grad)
                     grad_probs = mm_cols(values, picked_grad)
                     inner = jnp.sum(probs * grad_probs, axis=0, keepdims=True)
@@ -341,42 +351,35 @@
     )(meta, mine, other)
 
 
-def _merge_kernel(meta_ref, own_ref, up_ref, mine_ref, other_ref, down_out, up_out):
+def _merge_kernel(meta_ref, down_ref, out_weight_ref, mine_ref, other_ref, down_out, out_out):
     here_y, chip = meta_ref[14], meta_ref[18]
-    rows, share = own_ref.shape[0], own_ref.shape[0] // 8
-    lines = up_ref.shape[0] // 4
-    width = own_ref.shape[1]
     size = mine_ref.shape[0] // 4
-    down_out[pl.ds(pl.multiple_of(chip * rows, 16), rows), :] = own_ref[...]
-    up_out[4 * lines :, :] = up_ref[...]
-    for src, y in ((mine_ref, here_y), (other_ref, 1 - here_y)):
-        for turn in range(4):
-            at = (1 - chip) * rows + (y * 4 + turn) * share
-            down_out[pl.ds(pl.multiple_of(at, 16), share), :] = src[
-                turn * size : turn * size + share, :
-            ]
-            line = pl.multiple_of((y * 4 + turn) * (lines // 2), 16)
-            for column in range(4):
-                first = turn * size + share + column * (lines // 2)
-                up_out[pl.ds(line, lines // 2), column * width : (column + 1) * width] = src[
-                    first : first + lines // 2, :
+    first = 0
+    for own_ref, out_ref in ((down_ref, down_out), (out_weight_ref, out_out)):
+        rows, share = own_ref.shape[0], own_ref.shape[0] // 8
+        out_ref[pl.ds(pl.multiple_of(chip * rows, 16), rows), :] = own_ref[...]
+        for src, y in ((mine_ref, here_y), (other_ref, 1 - here_y)):
+            for turn in range(4):
+                at = (1 - chip) * rows + (y * 4 + turn) * share
+                out_ref[pl.ds(pl.multiple_of(at, 16), share), :] = src[
+                    turn * size + first : turn * size + first + share, :
                 ]
-
-
-def merge_shares(meta, w_down, far_up_high, mine, other):
-    rows, width = w_down.shape
+        first += share
+
+
+def merge_shares(meta, w_down, w_out, mine, other):
     return pl.pallas_call(
         _merge_kernel,
-        out_shape=(
-            jax.ShapeDtypeStruct((2 * rows, width), BF),
-            jax.ShapeDtypeStruct((2 * far_up_high.shape[0], far_up_high.shape[1]), BF),
+        out_shape=tuple(
+            jax.ShapeDtypeStruct((2 * weight.shape[0], weight.shape[1]), BF)
+            for weight in (w_down, w_out)
         ),
         in_specs=[SMEM_SPEC] + [VMEM_SPEC] * 4,
         out_specs=(VMEM_SPEC, VMEM_SPEC),
         compiler_params=pltpu.CompilerParams(vmem_limit_bytes=12 << 20),
         cost_estimate=LIGHT,
         name="merge_shares",
-    )(meta, w_down, far_up_high, mine, other)
+    )(meta, w_down, w_out, mine, other)
 
 
 TILE = 256
@@ -421,10 +424,34 @@
         out_shape=(shape, shape),
         in_specs=[SMEM_SPEC] + [VMEM_SPEC] * 3,
         out_specs=(VMEM_SPEC, VMEM_SPEC),
-        compiler_params=pltpu.CompilerParams(vmem_limit_bytes=12 << 20),
+        compiler_params=pltpu.CompilerParams(vmem_limit_bytes=8 << 20),
         cost_estimate=LIGHT,
         name="up_product",
     )(meta, low, weight, bias)
+
+
+def _qkv_kernel(meta_ref, rows_ref, weight_ref, bias_ref, out_ref):
+    step = out_ref.shape[1] // 2
+
+    def body(place):
+        for first in (0, step):
+            lanes = slice(first, first + step)
+            product = mm(rows_ref[place, :], weight_ref[:, lanes]) + bias_ref[:, lanes]
+            out_ref[place, lanes] = product.astype(BF)
+
+    _tiles(meta_ref, ALL, (out_ref,), body)
+
+
+def qkv_product(meta, rows, weight, bias):
+    return pl.pallas_call(
+        _qkv_kernel,
+        out_shape=jax.ShapeDtypeStruct((rows.shape[0], weight.shape[1]), BF),
+        in_specs=[SMEM_SPEC] + [VMEM_SPEC] * 3,
+        out_specs=VMEM_SPEC,
+        compiler_params=pltpu.CompilerParams(vmem_limit_bytes=8 << 20),
+        cost_estimate=LIGHT,
+        name="qkv_product",
+    )(meta, rows, weight, bias)
 
 
 def _rows_kernel(count_at, turned, terms, scaled, meta_ref, *refs):
@@ -460,7 +487,7 @@
         out_shape=jax.ShapeDtypeStruct((lefts[0].shape[0], width), kind),
         in_specs=[SMEM_SPEC] + [VMEM_SPEC] * len(args),
         out_specs=VMEM_SPEC,
-        compiler_params=pltpu.CompilerParams(vmem_limit_bytes=12 << 20),
+        compiler_params=pltpu.CompilerParams(vmem_limit_bytes=8 << 20),
         cost_estimate=LIGHT,
         name="rows_product",
     )(meta, *args)
@@ -527,7 +554,7 @@
 SWAP_Z1 = [(i, i ^ 2) for i in range(8)]
 SWAP_Z2 = [(i, i ^ 4) for i in range(8)]
 AT_Y, AT_Z1, AT_Z2 = 14, 16, 17
-MINE, OTHER = 19, 20
+MINE, OTHER, ALL = 19, 20, 21
 
 
 def moved(name, value, axis, pairs):
@@ -703,7 +730,8 @@
             chip[None],
             jnp.clip(total_rows - core * HALF, 0, HALF)[None],
             jnp.clip(total_rows - (1 - core) * HALF, 0, HALF)[None],
-            jnp.zeros((3,), jnp.int32),
+            total_rows[None],
+            jnp.zeros((2,), jnp.int32),
         ]
     ).astype(jnp.int32)
     row_ids = core * HALF + jnp.arange(HALF, dtype=jnp.int32)
@@ -768,17 +796,16 @@
     )[None, :]
 
 
-    first_weights = over_x(
-        after(jnp.concatenate([w_qkv, w_out], axis=1), sent_tokens), "x_first_weights"
-    )
+    far_qkv = over_x(after(w_qkv, sent_tokens), "x_first_weights")
     if group_count == 8:
-        share = w_down.shape[0] // 8
         turn = (group_id % 2) * 4 + group_id // 4 + 2 * (group_id // 2 % 2)
-        lines = w_up.shape[0] // 16
-        up_lines = lax.dynamic_slice_in_dim(w_up, turn * lines, lines, axis=0)
         mixed = jnp.concatenate(
-            [lax.dynamic_slice_in_dim(w_down, turn * share, share, axis=0)]
-            + jnp.split(up_lines, 4, axis=1),
+            [
+                lax.dynamic_slice_in_dim(
+                    weight, turn * (weight.shape[0] // 8), weight.shape[0] // 8, axis=0
+                )
+                for weight in (w_down, w_out)
+            ],
             axis=0,
         )
         mixed = over_x(after(mixed, sent_tokens), "x_shares")
@@ -808,26 +835,28 @@
             [jnp.where(chip == 0, own, far), jnp.where(chip == 0, far, own)], axis=0
         )
 
-    far_qkv, far_out = first_weights[:, : 3 * width], first_weights[:, 3 * width :]
     full_qkv = assemble(meta, 3, *swapped(w_qkv, far_qkv))
-    full_out = by_chip(w_out, far_out)
 
     cot_lists = route(cotangent, list_pos)
     far_tokens = over_x(lists[4:], "x_tokens")
     if group_count == 8:
+        mixed = after(mixed, lists)
         pair = stack_rows(meta, AT_Z2, mixed, moved("share_z2", mixed, "seq", SWAP_Z2), BF)
-        gate = four = stack_rows(meta, AT_Z1, pair, moved("share_z1", pair, "seq", SWAP_Z1), BF)
+        gate = pair
+        four = stack_rows(meta, AT_Z1, pair, moved("share_z1", pair, "seq", SWAP_Z1), BF)
     else:
         gate = far_tokens
-    rows_in = pack(meta, *swapped(lists[:4], after(far_tokens, gate, cot_lists)))
+    here_blocks = swapped(lists[:4], after(far_tokens, gate, cot_lists))
+    if group_count == 8:
+        here_blocks = (*here_blocks[:3], after(here_blocks[3], four))
+    rows_in = pack(meta, *here_blocks)
     w_up_later, _ = lax.optimization_barrier((w_up, far_tokens))
+    far_up = over_x(w_up_later, "x_up_weight")
     if group_count == 8:
-        far_up_high = over_x(w_up_later[part // 2 :], "x_up_weight")
         other_four = moved("share_y", four, "seq", SWAP_Y)
     else:
-        far_up = over_x(w_up_later, "x_up_weight")
-        full_down = by_chip(w_down, over_x(w_down))
-        cot_far_in = cot_lists[4:]
+        full_down, full_out = by_chip(w_down, over_x(w_down)), by_chip(w_out, over_x(w_out))
+
     def halves(value):
         return (
             lax.dynamic_slice_in_dim(value, core * HALF, HALF, axis=0),
@@ -843,14 +872,12 @@
         arriving = over_core(rows_product(meta, OTHER, lefts_other, rights, turned, BF))
         return rows_product(meta, MINE, lefts_mine, rights, turned, F32) + arriving.astype(F32)
 
-    qkv = (mm(rows_in, full_qkv) + joint_bias).astype(BF)
+    qkv = qkv_product(meta, rows_in, full_qkv, joint_bias)
     context, lse = attend(meta, qkv)
     if group_count == 8:
-        context, other_four, far_up_high = lax.optimization_barrier(
-            (context, other_four, far_up_high)
-        )
-        cot_far_in = after(cot_lists[4:], far_up_high)
-        full_down, far_up = merge_shares(meta, w_down, far_up_high, four, other_four)
+        context, other_four = lax.optimization_barrier((context, other_four))
+        full_down, full_out = merge_shares(meta, w_down, w_out, four, other_four)
+    cot_far_in = after(cot_lists[4:], far_up)
     full_up = assemble(meta, 1, *swapped(w_up, far_up))
     cot_arrived = over_x(cot_far_in, "x_cotangent")
     ctx_mine, ctx_other = halves(context)

time: 574 us -> 569 us (level)
  waiting for transfers between devices: 141 us -> 181 us
  starting transfers between devices: 94.4 us -> 72.9 us
  local copies, waits for them, and re-layouts: 67.8 us -> 61 us
  other arithmetic: 60.6 us -> 54.3 us
    ppermute x38, waiting for transfers between devices: 101 us -> 128 us  [moved(): return lax.ppermute(value, axis, pairs)]
    ppermute x38, starting transfers between devices: 68.9 us -> 47.5 us  [moved(): return lax.ppermute(value, axis, pairs)]
    ppermute x8, waiting for transfers between devices: 0.09 us -> 12.6 us  [over_x(): return lax.ppermute(value, 'head', swap_x)]
    pallas_call x1, Pallas kernels: 20.6 us -> 13.7 us  [attend(): pl.pallas_call(_attend_kernel, out_shape=(jax.ShapeDtypeStruct((CAP, widt...]
    unnamed x292 -> x260, local copies, waits for them, and re-layouts: 46.5 us -> 42.3 us
  transfers between devices with their start and end apart: 69 -> 69, of which waited for: 25 -> 25; matrix products, arithmetic and copies ran while one was open for 16% -> 12% of each run, Pallas kernels for 30% -> 30%
where the time goes in v4:
time: 569 us; the launch traced here: 560 us
  Pallas kernels  186 us (33%)
  waiting for transfers between devices  181 us (32%)
  starting transfers between devices  72.9 us (13%)
  local copies, waits for them, and re-layouts  61 us (11%)
  other arithmetic  54.3 us (10%)
    ppermute x38, waiting for transfers between devices, moved(): return lax.ppermute(value, axis, pairs)  128 us
    pallas_call x12, Pallas kernels, rows_product(): pl.pallas_call(functools.partial(_rows_kernel, count_at, turned, len(left...  48.1 us
    ppermute x38, starting transfers between devices, moved(): return lax.ppermute(value, axis, pairs)  47.5 us
    pallas_call x12, Pallas kernels, grad_product(): pl.pallas_call(functools.partial(_grad_kernel, len(lefts)), out_shape=jax...  46.3 us
    unnamed x260, local copies, waits for them, and re-layouts  42.3 us
    all_to_all x1, waiting for transfers between devices, on_device(): lax.all_to_all(sent_tokens, 'seq', split_axis=0, concat_axis=0, tiled=True)  36.1 us
    pallas_call x2, Pallas kernels, attend_back(): pl.pallas_call(functools.partial(_attend_back_kernel, block), out_shape=j...  18.7 us
    pallas_call x2, Pallas kernels, up_product(): pl.pallas_call(functools.partial(_up_kernel, count_at), out_shape=(shape,...  13.7 us
  transfers between devices with their start and end apart: 69, of which 25 were waited for; matrix products, arithmetic and copies ran while one was open for 12% of the time, Pallas kernels for 30%

profile of v4, /device:TPU:0, one launch (start us, length us, event | category | flops | bytes accessed | tf_op | source)
XLA Modules:
  0.0 559.8 jit_solution(5539083762472823240)
XLA Ops:
  5.6 7.4 %all-to-all-start = ((bf16[8,128,1024]{2,1,0:T(8,128)(2,1)}), bf16[8,128,1024]{2,1,0:T(8,128)(2,1)S(1)}, u32[]{:S(2)}, u32[]{:S(2)}) async-start(bf16[8,128,1024]{2,1,0:T(8,128)(2,1)} %copy-done.48), calls=%async_computation | async-start | bytes 4194304 | tf_op jit(solution)/shard_map/all_to_all | solution.py:815
  25.2 36.1 %all-to-all-done.refs_0_ = bf16[8,128,1024]{2,1,0:T(8,128)(2,1)S(1)} async-done(((bf16[8,128,1024]{2,1,0:T(8,128)(2,1)}), bf16[8,128,1024]{2,1,0:T(8,128)(2,1)S(1)}, u32[]{:S(2)}, u32[]{:S(2)}) %all-to-all-start) | async-done | bytes 2097184 | tf_op jit(solution)/shard_map/all_to_all | solution.py:815
  66.8 11.5 %collective-permute-done.2.other_ref = bf16[160,1024]{1,0:T(8,128)(2,1)S(1)} collective-permute-done((bf16[160,1024]{1,0:T(8,128)(2,1)S(1)}, bf16[160,1024]{1,0:T(8,128)(2,1)S(1)}, u32[]{:S(2)}, u32[]{:S(2)}) %collective-permute-start.2) | collective-permute-done | bytes 327712 | tf_op jit(solution)/shard_map/share_z2/ppermute | solution.py:562
  84.2 10.5 %collective-permute-done.5.other_ref = bf16[320,1024]{1,0:T(8,128)(2,1)} collective-permute-done((bf16[320,1024]{1,0:T(8,128)(2,1)S(1)}, bf16[320,1024]{1,0:T(8,128)(2,1)}, u32[]{:S(2)}, u32[]{:S(2)}) %collective-permute-start.5) | collective-permute-done | bytes 655392 | tf_op jit(solution)/shard_map/share_z1/ppermute | solution.py:562
  95.9 2.7 collective-permute-start.11
  103.1 3.0 pack.2.rows_ref.refs_0_
  106.0 5.7 %qkv_product.1.qkv_ref = bf16[1536,1536]{1,0:T(8,128)(2,1)S(1)} custom-call(s32[24]{0:T(128)S(1)} %concatenate.56.meta_ref, bf16[1536,1024]{1,0:T(8,128)(2,1)S(1)} %pack.2.rows_ref.refs_0_, bf16[1024,1536]{1,0:T(8,128)(2,1)S(1)} %assemble.2.weight_ref, f32[1,1536]{1,0:T(1,128)S(1)} %broadcast_in_dim.212.bias_ref), custom_call_target="tpu_custom_call" | custom-call | bytes 1024 | tf_op jit(solution)/shard_map/qkv_product/pallas_call | solution.py:446
  111.8 13.7 %attend.1 = (bf16[1536,512]{1,0:T(8,128)(2,1)S(1)}, f32[4,8,1,512]{3,2,1,0:T(1,128)S(1)}) custom-call(s32[24]{0:T(128)S(1)} %concatenate.56.meta_ref, bf16[1536,1536]{1,0:T(8,128)(2,1)S(1)} %qkv_product.1.qkv_ref), custom_call_target="tpu_custom_call" | custom-call | bytes 1024 | tf_op jit(solution)/shard_map/attend/pallas_call | solution.py:192
  134.5 12.5 %collective-permute-done.13.refs_1_ = bf16[256,4096]{1,0:T(8,128)(2,1)S(1)} collective-permute-done((bf16[256,4096]{1,0:T(8,128)(2,1)}, bf16[256,4096]{1,0:T(8,128)(2,1)S(1)}, u32[]{:S(2)}, u32[]{:S(2)}) %collective-permute-start.13) | collective-permute-done | bytes 2097184 | tf_op jit(solution)/shard_map/x_up_weight/ppermute | solution.py:680
  153.8 5.7 %up_product.3 = (bf16[768,2048]{1,0:T(8,128)(2,1)S(1)}, bf16[768,2048]{1,0:T(8,128)(2,1)S(1)}) custom-call(s32[24]{0:T(128)S(1)} %concatenate.56.meta_ref, bf16[768,1024]{1,0:T(8,128)(2,1)S(1)} %collective-permute-done.16.low_ref.refs_1_, bf16[1024,2048]{1,0:T(8,128)(2,1)S(1)} %assemble.3.weight_ref.refs_1_, f32[1,2048]{1,0:T(1,128)S(1)} %bitcast.183), custom_call_target="tpu_custom_call" | custom-call | bytes 1024 | tf_op jit(solution)/shard_map/up_product/pallas_call | solution.py:422
  159.5 3.5 rows_product.15
  163.0 4.1 collective-permute-start.17
  167.2 8.0 %up_product.2 = (bf16[768,2048]{1,0:T(8,128)(2,1)S(1)}, bf16[768,2048]{1,0:T(8,128)(2,1)S(1)}) custom-call(s32[24]{0:T(128)S(1)} %concatenate.56.meta_ref, bf16[768,1024]{1,0:T(8,128)(2,1)S(1)} %fusion.3.low_ref.refs_0_, bf16[1024,2048]{1,0:T(8,128)(2,1)S(1)} %assemble.3.weight_ref.refs_1_, f32[1,2048]{1,0:T(1,128)S(1)} %bitcast.184), custom_call_target="tpu_custom_call" | custom-call | bytes 1024 | tf_op jit(solution)/shard_map/up_product/pallas_call | solution.py:422
  177.0 4.9 rows_product.14
  189.8 3.7 collective-permute-done.21.refs_3_.refs_0_
  197.4 4.7 grad_product.13
  202.1 4.7 grad_product.12
  212.5 7.2 %rows_product.16.refs_2_.refs_0_ = bf16[768,2048]{1,0:T(8,128)(2,1)S(1)} custom-call(s32[24]{0:T(128)S(1)} %concatenate.56.meta_ref, bf16[768,1024]{1,0:T(8,128)(2,1)} %get-tuple-element.108.refs_2_.refs_0_, bf16[2048,1024]{1,0:T(8,128)(2,1)S(1)} %copy-done.16, bf16[768,2048]{1,0:T(8,128)(2,1)S(1)} %copy-done.62), custom_call_target="tpu_custom_call" | custom-call | bytes 1024 | tf_op jit(solution)/shard_map/rows_product/pallas_call | solution.py:485
  219.8 6.4 %rows_product.17.refs_3_.refs_0_ = bf16[768,2048]{1,0:T(8,128)(2,1)S(1)} custom-call(s32[24]{0:T(128)S(1)} %concatenate.56.meta_ref, bf16[768,1024]{1,0:T(8,128)(2,1)} %collective-permute-done.21.refs_3_.refs_0_, bf16[2048,1024]{1,0:T(8,128)(2,1)S(1)} %copy-done.16, bf16[768,2048]{1,0:T(8,128)(2,1)S(1)} %copy-done.60), custom_call_target="tpu_custom_call" | custom-call | bytes 1024 | tf_op jit(solution)/shard_map/rows_product/pallas_call | solution.py:485
  226.3 5.7 %grad_product.14 = bf16[512,2048]{1,0:T(8,128)(2,1)S(1)} custom-call(s32[24]{0:T(128)S(1)} %concatenate.56.meta_ref, s32[1]{0:T(128)} %bitcast.22.at_ref, bf16[768,1024]{1,0:T(8,128)(2,1)S(1)} %copy-done.27, bf16[768,1024]{1,0:T(8,128)(2,1)S(1)} %copy-done.40, bf16[768,2048]{1,0:T(8,128)(2,1)S(1)} %rows_product.16.refs_2_.refs_0_, ...), custom_call_target="tpu_custom_call" | custom-call | bytes 1024 | tf_op jit(solution)/shard_map/grad_product/pallas_call | solution.py:523
  233.4 4.8 rows_product.18
  244.9 4.7 grad_product.16
  249.7 4.9 grad_product.15
  254.6 5.7 %grad_product.17 = f32[512,2048]{1,0:T(8,128)S(1)} custom-call(s32[24]{0:T(128)S(1)} %concatenate.56.meta_ref, s32[1]{0:T(128)} %bitcast.27.at_ref, bf16[768,1024]{1,0:T(8,128)(2,1)S(1)} %copy-done.28, bf16[768,1024]{1,0:T(8,128)(2,1)S(1)} %copy-done.41, bf16[768,2048]{1,0:T(8,128)(2,1)S(1)} %copy-done.4, bf16[768,2048]{1,0:T(8,128)(2,1)S(1)} %copy-done.6), custom_call_target="tpu_custom_call" | custom-call | bytes 1024 | tf_op jit(solution)/shard_map/grad_product/pallas_call | solution.py:523
  260.4 2.8 maximum_add_fusion
  265.8 5.2 rows_product.19
  271.1 5.0 multiply_reduce_fusion.1
  276.2 2.5 convert_reduce_fusion.5
  279.8 10.8 %collective-permute-done.28 = bf16[512,1024]{1,0:T(8,128)(2,1)S(1)} collective-permute-done((bf16[512,1024]{1,0:T(8,128)(2,1)}, bf16[512,1024]{1,0:T(8,128)(2,1)S(1)}, u32[]{:S(2)}, u32[]{:S(2)}) %collective-permute-start.28) | collective-permute-done | bytes 1048608 | tf_op jit(solution)/shard_map/down_z1/ppermute | solution.py:562
  301.8 9.2 %attend_back.2.refs_1_ = bf16[1536,768]{1,0:T(8,128)(2,1)S(1)} custom-call(s32[24]{0:T(128)S(1)} %concatenate.56.meta_ref, bf16[1536,1536]{1,0:T(8,128)(2,1)S(1)} %bitcast.178, f32[4,8,1,512]{3,2,1,0:T(1,128)S(1)} %get-tuple-element.116.lse_ref, bf16[1536,512]{1,0:T(8,128)(2,1)S(1)} %pad_maximum_fusion.1.gctx_ref), custom_call_target="tpu_custom_call" | custom-call | bytes 1024 | tf_op jit(solution)/shard_map/attend_back/pallas_call | solution.py:268
  311.1 4.6 collective-permute-done.29
  320.0 2.7 grad_product.20
  323.9 2.6 collective-permute-done.30
  326.6 2.7 collective-permute-start.33
  329.5 9.5 %attend_back.3.refs_1_ = bf16[1536,768]{1,0:T(8,128)(2,1)S(1)} custom-call(s32[24]{0:T(128)S(1)} %concatenate.56.meta_ref, bf16[1536,1536]{1,0:T(8,128)(2,1)S(1)} %bitcast.178, f32[4,8,1,512]{3,2,1,0:T(1,128)S(1)} %get-tuple-element.116.lse_ref, bf16[1536,512]{1,0:T(8,128)(2,1)S(1)} %pad_maximum_fusion.1.gctx_ref), custom_call_target="tpu_custom_call" | custom-call | bytes 1024 | tf_op jit(solution)/shard_map/attend_back/pallas_call | solution.py:268
  343.7 4.2 rows_product.23
  348.4 2.7 convert_reduce_fusion.1
  359.5 2.7 grad_product.21
  365.3 4.3 rows_product.22
  369.7 3.6 add_convert_fusion.mine_ref
  373.3 6.1 %collective-permute-done.36 = bf16[512,1280]{1,0:T(8,128)(2,1)} collective-permute-done((bf16[512,1280]{1,0:T(8,128)(2,1)}, bf16[512,1280]{1,0:T(8,128)(2,1)}, u32[]{:S(2)}, u32[]{:S(2)}) %collective-permute-start.36) | collective-permute-done | bytes 1310752 | tf_op jit(solution)/shard_map/first_x/ppermute | solution.py:562
  389.1 4.3 unpack.3
  394.4 4.9 collective-permute-done.38.other_ref
  401.5 2.7 grad_product.22
  410.7 2.7 grad_product.23
  417.6 8.1 %collective-permute-done.44 = bf16[256,1280]{1,0:T(8,128)(2,1)} collective-permute-done((bf16[256,1280]{1,0:T(8,128)(2,1)}, bf16[256,1280]{1,0:T(8,128)(2,1)}, u32[]{:S(2)}, u32[]{:S(2)}) %collective-permute-start.44) | collective-permute-done | bytes 655392 | tf_op jit(solution)/shard_map/first_y/ppermute | solution.py:562
  429.9 3.5 stack_rows.16
  436.5 13.9 %collective-permute-done.41 = bf16[512,896]{1,0:T(8,128)(2,1)} collective-permute-done((bf16[512,896]{1,0:T(8,128)(2,1)}, bf16[512,896]{1,0:T(8,128)(2,1)}, u32[]{:S(2)}, u32[]{:S(2)}) %collective-permute-start.41) | collective-permute-done | bytes 917536 | tf_op jit(solution)/shard_map/last_x/ppermute | solution.py:562
  455.5 7.0 %collective-permute-done.48.refs_1_ = bf16[128,1024]{1,0:T(8,128)(2,1)S(1)} collective-permute-done((bf16[128,1024]{1,0:T(8,128)(2,1)S(1)}, bf16[128,1024]{1,0:T(8,128)(2,1)S(1)}, u32[]{:S(2)}, u32[]{:S(2)}) %collective-permute-start.48) | collective-permute-done | bytes 262176 | tf_op jit(solution)/shard_map/return/ppermute | solution.py:562
  462.8 3.2 collective-permute-done.49.refs_2_
  466.0 5.7 %collective-permute-done.45 = bf16[256,896]{1,0:T(8,128)(2,1)S(1)} collective-permute-done((bf16[256,896]{1,0:T(8,128)(2,1)S(1)}, bf16[256,896]{1,0:T(8,128)(2,1)S(1)}, u32[]{:S(2)}, u32[]{:S(2)}) %collective-permute-start.45) | collective-permute-done | bytes 458784 | tf_op jit(solution)/shard_map/last_y/ppermute | solution.py:562
  472.2 6.3 %collective-permute-done.51 = bf16[64,1280]{1,0:T(8,128)(2,1)S(1)} collective-permute-done((bf16[64,1280]{1,0:T(8,128)(2,1)S(1)}, bf16[64,1280]{1,0:T(8,128)(2,1)S(1)}, u32[]{:S(2)}, u32[]{:S(2)}) %collective-permute-start.51) | collective-permute-done | bytes 163872 | tf_op jit(solution)/shard_map/first_z2/ppermute | solution.py:562
  478.7 2.9 collective-permute-start.55
  481.6 13.3 %collective-permute-done.52.refs_3_ = bf16[128,1024]{1,0:T(8,128)(2,1)S(1)} collective-permute-done((bf16[128,1024]{1,0:T(8,128)(2,1)S(1)}, bf16[128,1024]{1,0:T(8,128)(2,1)S(1)}, u32[]{:S(2)}, u32[]{:S(2)}) %collective-permute-start.52) | collective-permute-done | bytes 262176 | tf_op jit(solution)/shard_map/return/ppermute | solution.py:562
  496.3 3.6 collective-permute-start.59
  503.6 8.0 %collective-permute-done.57.other_ref = bf16[128,1280]{1,0:T(8,128)(2,1)S(1)} collective-permute-done((bf16[128,1280]{1,0:T(8,128)(2,1)S(1)}, bf16[128,1280]{1,0:T(8,128)(2,1)S(1)}, u32[]{:S(2)}, u32[]{:S(2)}) %collective-permute-start.57) | collective-permute-done | bytes 327712 | tf_op jit(solution)/shard_map/first_back_z1/ppermute | solution.py:562
  512.1 3.8 collective-permute-start.63
  515.9 2.7 collective-permute-start.56
  520.6 3.8 collective-permute-done.56.other_ref
  525.0 6.1 %collective-permute-start.60 = (bf16[128,896]{1,0:T(8,128)(2,1)S(1)}, bf16[128,896]{1,0:T(8,128)(2,1)S(1)}, u32[]{:S(2)}, u32[]{:S(2)}) collective-permute-start(bf16[128,896]{1,0:T(8,128)(2,1)S(1)} %stack_rows.20.mine_ref), channel_id=1, source_target_pairs={{0,8},{4,12},{8,0},{12,4},{16,24},{20,28},{24,16},{28,20},{1,9},{5... | collective-permute-start | bytes 688136 | tf_op jit(solution)/shard_map/last_back_z1/ppermute | solution.py:562
  531.1 2.7 collective-permute-start.62
  548.3 3.0 collective-permute-done.65
  553.8 2.8 spread_columns.3
  556.6 3.0 spread_columns.2
  (540 shorter events, 173.9 us)
Async XLA Ops:
  5.6 55.7 %all-to-all-start = ((bf16[8,128,1024]{2,1,0:T(8,128)(2,1)}), bf16[8,128,1024]{2,1,0:T(8,128)(2,1)S(1)}, u32[]{:S(2)}, u32[]{:S(2)}) async-start(bf16[8,128,1024]{2,1,0:T(8,128)(2,1)} %copy-done.48), calls=%async_computation | async-start | bytes 4194304 | tf_op jit(solution)/shard_map/all_to_all | solution.py:815
  14.9 64.1 %collective-permute-start.9 = (bf16[1,3072]{1,0:T(2,128)(2,1)S(1)}, bf16[1,3072]{1,0:T(2,128)(2,1)S(1)}, u32[]{:S(2)}, u32[]{:S(2)}) collective-permute-start(bf16[1,3072]{1,0:T(2,128)(2,1)S(1)} %broadcast_in_dim.210), channel_id=1, source_target_pairs={{0,1},{1,0},{2,3},{3,2},{4,5},{5,4},{6,7},{7,6},{8,9},{9,8},{10,11... | collective-permute-start | bytes 18440 | tf_op jit(solution)/shard_map/core/ppermute | solution.py:684
  16.9 45.1 %collective-permute-start.1 = (bf16[160,1024]{1,0:T(8,128)(2,1)S(1)}, bf16[160,1024]{1,0:T(8,128)(2,1)S(1)}, u32[]{:S(2)}, u32[]{:S(2)}) collective-permute-start(bf16[160,1024]{1,0:T(8,128)(2,1)S(1)} %pad_maximum_fusion.2), channel_id=1, source_target_pairs={{0,2},{1,3},{2,0},{3,1},{4,6},{5,7},{6,4},{7,5},{8,10},{9,11},{10,... | collective-permute-start | bytes 983048 | tf_op jit(solution)/shard_map/x_shares/ppermute | solution.py:680
  18.4 80.6 %collective-permute-start.7 = (bf16[256,3072]{1,0:T(8,128)(2,1)}, bf16[256,3072]{1,0:T(8,128)(2,1)}, u32[]{:S(2)}, u32[]{:S(2)}) collective-permute-start(bf16[256,3072]{1,0:T(8,128)(2,1)} %refs_0_.6), channel_id=1, source_target_pairs={{0,1},{1,0},{2,3},{3,2},{4,5},{5,4},{6,7},{7,6},{8,9},{9,8},{10,11... | collective-permute-start | bytes 4718600 | tf_op jit(solution)/shard_map/core/ppermute | solution.py:684
  18.6 65.6 %collective-permute-start.6 = (bf16[256,3072]{1,0:T(8,128)(2,1)}, bf16[256,3072]{1,0:T(8,128)(2,1)}, u32[]{:S(2)}, u32[]{:S(2)}) collective-permute-start(bf16[256,3072]{1,0:T(8,128)(2,1)} %refs_0_.6), channel_id=1, source_target_pairs={{0,2},{1,3},{2,0},{3,1},{4,6},{5,7},{6,4},{7,5},{8,10},{9,11},{10,... | collective-permute-start | bytes 4718600 | tf_op jit(solution)/shard_map/x_first_weights/ppermute | solution.py:680
  62.0 16.3 %collective-permute-start.2 = (bf16[160,1024]{1,0:T(8,128)(2,1)S(1)}, bf16[160,1024]{1,0:T(8,128)(2,1)S(1)}, u32[]{:S(2)}, u32[]{:S(2)}) collective-permute-start(bf16[160,1024]{1,0:T(8,128)(2,1)S(1)} %collective-permute-done.1.mine_ref), channel_id=1, source_target_pairs={{0,16},{4,20},{8,24},{12,28},{16,0},{20,4},{24,8},{28,12},{1,17},{... | collective-permute-start | bytes 983048 | tf_op jit(solution)/shard_map/share_z2/ppermute | solution.py:562
  63.2 32.7 %collective-permute-start = (bf16[4,128,1024]{2,1,0:T(8,128)(2,1)}, bf16[4,128,1024]{2,1,0:T(8,128)(2,1)}, u32[]{:S(2)}, u32[]{:S(2)}) collective-permute-start(bf16[4,128,1024]{2,1,0:T(8,128)(2,1)} %get-tuple-element.221), channel_id=1, source_target_pairs={{0,2},{1,3},{2,0},{3,1},{4,6},{5,7},{6,4},{7,5},{8,10},{9,11},{10,... | collective-permute-start | bytes 3145736 | tf_op jit(solution)/shard_map/x_tokens/ppermute | solution.py:680
  78.9 15.8 %collective-permute-start.5 = (bf16[320,1024]{1,0:T(8,128)(2,1)S(1)}, bf16[320,1024]{1,0:T(8,128)(2,1)}, u32[]{:S(2)}, u32[]{:S(2)}) collective-permute-start(bf16[320,1024]{1,0:T(8,128)(2,1)S(1)} %stack_rows.11.mine_ref), channel_id=1, source_target_pairs={{0,8},{4,12},{8,0},{12,4},{16,24},{20,28},{24,16},{28,20},{1,9},{5... | collective-permute-start | bytes 1966088 | tf_op jit(solution)/shard_map/share_z1/ppermute | solution.py:562
  79.1 19.6 %collective-permute-start.10 = (bf16[2,3072]{1,0:T(2,128)(2,1)S(1)}, bf16[2,3072]{1,0:T(2,128)(2,1)S(1)}, u32[]{:S(2)}, u32[]{:S(2)}) collective-permute-start(bf16[2,3072]{1,0:T(2,128)(2,1)S(1)} %pad_maximum_fusion.4), channel_id=1, source_target_pairs={{0,2},{1,3},{2,0},{3,1},{4,6},{5,7},{6,4},{7,5},{8,10},{9,11},{10,... | collective-permute-start | bytes 36872 | tf_op jit(solution)/shard_map/x/ppermute | solution.py:680
  84.2 16.4 %collective-permute-start.8 = (bf16[256,3072]{1,0:T(8,128)(2,1)}, bf16[256,3072]{1,0:T(8,128)(2,1)S(1)}, u32[]{:S(2)}, u32[]{:S(2)}) collective-permute-start(bf16[256,3072]{1,0:T(8,128)(2,1)} %collective-permute-done.6.refs_1_), channel_id=1, source_target_pairs={{0,1},{1,0},{2,3},{3,2},{4,5},{5,4},{6,7},{7,6},{8,9},{9,8},{10,11... | collective-permute-start | bytes 4718600 | tf_op jit(solution)/shard_map/core/ppermute | solution.py:684
  94.7 8.4 %collective-permute-start.3 = (bf16[4,128,1024]{2,1,0:T(8,128)(2,1)S(1)}, bf16[4,128,1024]{2,1,0:T(8,128)(2,1)S(1)}, u32[]{:S(2)}, u32[]{:S(2)}) collective-permute-start(bf16[4,128,1024]{2,1,0:T(8,128)(2,1)S(1)} %get-tuple-element.222.a0), channel_id=1, source_target_pairs={{0,1},{1,0},{2,3},{3,2},{4,5},{5,4},{6,7},{7,6},{8,9},{9,8},{10,11... | collective-permute-start | bytes 3145736 | tf_op jit(solution)/shard_map/core/ppermute | solution.py:684
  95.9 32.2 %collective-permute-start.11 = (bf16[640,1024]{1,0:T(8,128)(2,1)S(1)}, bf16[640,1024]{1,0:T(8,128)(2,1)S(1)}, u32[]{:S(2)}, u32[]{:S(2)}) collective-permute-start(bf16[640,1024]{1,0:T(8,128)(2,1)S(1)} %stack_rows.12.mine_ref), channel_id=1, source_target_pairs={{0,4},{4,0},{8,12},{12,8},{16,20},{20,16},{24,28},{28,24},{1,5},{5... | collective-permute-start | bytes 3932168 | tf_op jit(solution)/shard_map/share_y/ppermute | solution.py:562
  99.0 48.1 %collective-permute-start.13 = (bf16[256,4096]{1,0:T(8,128)(2,1)}, bf16[256,4096]{1,0:T(8,128)(2,1)S(1)}, u32[]{:S(2)}, u32[]{:S(2)}) collective-permute-start(bf16[256,4096]{1,0:T(8,128)(2,1)} %refs_0_.7), channel_id=1, source_target_pairs={{0,2},{1,3},{2,0},{3,1},{4,6},{5,7},{6,4},{7,5},{8,10},{9,11},{10,... | collective-permute-start | bytes 6291464 | tf_op jit(solution)/shard_map/x_up_weight/ppermute | solution.py:680
  130.9 16.1 %collective-permute-start.12 = (bf16[768,1024]{1,0:T(8,128)(2,1)S(1)}, bf16[768,1024]{1,0:T(8,128)(2,1)S(1)}, u32[]{:S(2)}, u32[]{:S(2)}) collective-permute-start(bf16[768,1024]{1,0:T(8,128)(2,1)S(1)} %rows_product.13), channel_id=1, source_target_pairs={{0,1},{1,0},{2,3},{3,2},{4,5},{5,4},{6,7},{7,6},{8,9},{9,8},{10,11... | collective-permute-start | bytes 4718600 | tf_op jit(solution)/shard_map/core/ppermute | solution.py:684
  132.1 20.8 %collective-permute-start.14 = (bf16[256,4096]{1,0:T(8,128)(2,1)S(1)}, bf16[256,4096]{1,0:T(8,128)(2,1)S(1)}, u32[]{:S(2)}, u32[]{:S(2)}) collective-permute-start(bf16[256,4096]{1,0:T(8,128)(2,1)S(1)} %copy-done.65), channel_id=1, source_target_pairs={{0,1},{1,0},{2,3},{3,2},{4,5},{5,4},{6,7},{7,6},{8,9},{9,8},{10,11... | collective-permute-start | bytes 6291464 | tf_op jit(solution)/shard_map/core/ppermute | solution.py:684
  147.1 5.8 %collective-permute-start.15 = (bf16[256,4096]{1,0:T(8,128)(2,1)S(1)}, bf16[256,4096]{1,0:T(8,128)(2,1)S(1)}, u32[]{:S(2)}, u32[]{:S(2)}) collective-permute-start(bf16[256,4096]{1,0:T(8,128)(2,1)S(1)} %collective-permute-done.13.refs_1_), channel_id=1, source_target_pairs={{0,1},{1,0},{2,3},{3,2},{4,5},{5,4},{6,7},{7,6},{8,9},{9,8},{10,11... | collective-permute-start | bytes 6291464 | tf_op jit(solution)/shard_map/core/ppermute | solution.py:684
  151.3 25.6 %collective-permute-start.18 = (bf16[4,128,1024]{2,1,0:T(8,128)(2,1)S(1)}, bf16[4,128,1024]{2,1,0:T(8,128)(2,1)S(1)}, u32[]{:S(2)}, u32[]{:S(2)}) collective-permute-start(bf16[4,128,1024]{2,1,0:T(8,128)(2,1)S(1)} %get-tuple-element.106), channel_id=1, source_target_pairs={{0,2},{1,3},{2,0},{3,1},{4,6},{5,7},{6,4},{7,5},{8,10},{9,11},{10,... | collective-permute-start | bytes 3145736 | tf_op jit(solution)/shard_map/x_cotangent/ppermute | solution.py:680
  163.0 20.8 %collective-permute-start.17 = (bf16[768,1024]{1,0:T(8,128)(2,1)S(1)}, bf16[768,1024]{1,0:T(8,128)(2,1)S(1)}, u32[]{:S(2)}, u32[]{:S(2)}) collective-permute-start(bf16[768,1024]{1,0:T(8,128)(2,1)S(1)} %rows_product.15), channel_id=1, source_target_pairs={{0,1},{1,0},{2,3},{3,2},{4,5},{5,4},{6,7},{7,6},{8,9},{9,8},{10,11... | collective-permute-start | bytes 4718600 | tf_op jit(solution)/shard_map/core/ppermute | solution.py:684
  167.1 14.8 %collective-permute-start.19 = (bf16[4,128,1024]{2,1,0:T(8,128)(2,1)S(1)}, bf16[4,128,1024]{2,1,0:T(8,128)(2,1)S(1)}, u32[]{:S(2)}, u32[]{:S(2)}) collective-permute-start(bf16[4,128,1024]{2,1,0:T(8,128)(2,1)S(1)} %get-tuple-element.220.a0), channel_id=1, source_target_pairs={{0,1},{1,0},{2,3},{3,2},{4,5},{5,4},{6,7},{7,6},{8,9},{9,8},{10,11... | collective-permute-start | bytes 3145736 | tf_op jit(solution)/shard_map/core/ppermute | solution.py:684
  208.3 52.1 %collective-permute-start.24 = (bf16[1024,1024]{1,0:T(8,128)(2,1)}, bf16[1024,1024]{1,0:T(8,128)(2,1)}, u32[]{:S(2)}, u32[]{:S(2)}) collective-permute-start(bf16[1024,1024]{1,0:T(8,128)(2,1)} %bitcast.21), channel_id=1, source_target_pairs={{0,4},{4,0},{8,12},{12,8},{16,20},{20,16},{24,28},{28,24},{1,5},{5... | collective-permute-start | bytes 6291464 | tf_op jit(solution)/shard_map/down_y/ppermute | solution.py:562
  238.2 32.9 %collective-permute-start.25 = (bf16[768,1024]{1,0:T(8,128)(2,1)}, bf16[768,1024]{1,0:T(8,128)(2,1)}, u32[]{:S(2)}, u32[]{:S(2)}) collective-permute-start(bf16[768,1024]{1,0:T(8,128)(2,1)} %rows_product.18), channel_id=1, source_target_pairs={{0,1},{1,0},{2,3},{3,2},{4,5},{5,4},{6,7},{7,6},{8,9},{9,8},{10,11... | collective-permute-start | bytes 4718600 | tf_op jit(solution)/shard_map/core/ppermute | solution.py:684
  239.6 51.7 %collective-permute-start.27 = (bf16[512,2048]{1,0:T(8,128)(2,1)}, bf16[512,2048]{1,0:T(8,128)(2,1)}, u32[]{:S(2)}, u32[]{:S(2)}) collective-permute-start(bf16[512,2048]{1,0:T(8,128)(2,1)} %copy-done.70), channel_id=1, source_target_pairs={{0,2},{1,3},{2,0},{3,1},{4,6},{5,7},{6,4},{7,5},{8,10},{9,11},{10,... | collective-permute-start | bytes 6291464 | tf_op jit(solution)/shard_map/up_x/ppermute | solution.py:562
  265.6 25.0 %collective-permute-start.28 = (bf16[512,1024]{1,0:T(8,128)(2,1)}, bf16[512,1024]{1,0:T(8,128)(2,1)S(1)}, u32[]{:S(2)}, u32[]{:S(2)}) collective-permute-start(bf16[512,1024]{1,0:T(8,128)(2,1)} %bitcast.33), channel_id=1, source_target_pairs={{0,8},{4,12},{8,0},{12,4},{16,24},{20,28},{24,16},{28,20},{1,9},{5... | collective-permute-start | bytes 3145736 | tf_op jit(solution)/shard_map/down_z1/ppermute | solution.py:562
  276.1 19.7 %collective-permute-start.22 = (bf16[768,1024]{1,0:T(8,128)(2,1)S(1)}, bf16[768,1024]{1,0:T(8,128)(2,1)S(1)}, u32[]{:S(2)}, u32[]{:S(2)}) collective-permute-start(bf16[768,1024]{1,0:T(8,128)(2,1)S(1)} %get-tuple-element.113.mine_ref), channel_id=1, source_target_pairs={{0,1},{1,0},{2,3},{3,2},{4,5},{5,4},{6,7},{7,6},{8,9},{9,8},{10,11... | collective-permute-start | bytes 4718600 | tf_op jit(solution)/shard_map/core/ppermute | solution.py:684
  278.7 19.3 %collective-permute-start.26 = (bf16[768,1024]{1,0:T(8,128)(2,1)S(1)}, bf16[768,1024]{1,0:T(8,128)(2,1)S(1)}, u32[]{:S(2)}, u32[]{:S(2)}) collective-permute-start(bf16[768,1024]{1,0:T(8,128)(2,1)S(1)} %get-tuple-element.122.refs_2_.refs_0_), channel_id=1, source_target_pairs={{0,1},{1,0},{2,3},{3,2},{4,5},{5,4},{6,7},{7,6},{8,9},{9,8},{10,11... | collective-permute-start | bytes 4718600 | tf_op jit(solution)/shard_map/core/ppermute | solution.py:684
  291.1 24.6 %collective-permute-start.29 = (bf16[256,1024]{1,0:T(8,128)(2,1)S(1)}, bf16[256,1024]{1,0:T(8,128)(2,1)S(1)}, u32[]{:S(2)}, u32[]{:S(2)}) collective-permute-start(bf16[256,1024]{1,0:T(8,128)(2,1)S(1)} %bitcast.207), channel_id=1, source_target_pairs={{0,16},{4,20},{8,24},{12,28},{16,0},{20,4},{24,8},{28,12},{1,17},{... | collective-permute-start | bytes 1572872 | tf_op jit(solution)/shard_map/down_z2/ppermute | solution.py:562
  294.0 24.9 %collective-permute-start.31 = (bf16[256,2048]{1,0:T(8,128)(2,1)S(1)}, bf16[256,2048]{1,0:T(8,128)(2,1)S(1)}, u32[]{:S(2)}, u32[]{:S(2)}) collective-permute-start(bf16[256,2048]{1,0:T(8,128)(2,1)S(1)} %fusion.6), channel_id=1, source_target_pairs={{0,4},{4,0},{8,12},{12,8},{16,20},{20,16},{24,28},{28,24},{1,5},{5... | collective-permute-start | bytes 3145736 | tf_op jit(solution)/shard_map/up_y/ppermute | solution.py:562
  297.5 43.1 %collective-permute-start.23 = (bf16[4,128,1024]{2,1,0:T(8,128)(2,1)S(1)}, bf16[4,128,1024]{2,1,0:T(8,128)(2,1)S(1)}, u32[]{:S(2)}, u32[]{:S(2)}) collective-permute-start(bf16[4,128,1024]{2,1,0:T(8,128)(2,1)S(1)} %get-tuple-element.115), channel_id=1, source_target_pairs={{0,2},{1,3},{2,0},{3,1},{4,6},{5,7},{6,4},{7,5},{8,10},{9,11},{10,... | collective-permute-start | bytes 3145736 | tf_op jit(solution)/shard_map/x_activations/ppermute | solution.py:680
  315.9 10.7 %collective-permute-start.30 = (bf16[128,1024]{1,0:T(8,128)(2,1)S(1)}, bf16[128,1024]{1,0:T(8,128)(2,1)S(1)}, u32[]{:S(2)}, u32[]{:S(2)}) collective-permute-start(bf16[128,1024]{1,0:T(8,128)(2,1)S(1)} %fusion.17), channel_id=1, source_target_pairs={{0,2},{1,3},{2,0},{3,1},{4,6},{5,7},{6,4},{7,5},{8,10},{9,11},{10,... | collective-permute-start | bytes 786440 | tf_op jit(solution)/shard_map/down_x/ppermute | solution.py:562
  319.4 21.8 %collective-permute-start.32 = (bf16[128,2048]{1,0:T(8,128)(2,1)S(1)}, bf16[128,2048]{1,0:T(8,128)(2,1)S(1)}, u32[]{:S(2)}, u32[]{:S(2)}) collective-permute-start(bf16[128,2048]{1,0:T(8,128)(2,1)S(1)} %fusion.9), channel_id=1, source_target_pairs={{0,8},{4,12},{8,0},{12,4},{16,24},{20,28},{24,16},{28,20},{1,9},{5... | collective-permute-start | bytes 1572872 | tf_op jit(solution)/shard_map/up_z1/ppermute | solution.py:562
  326.6 13.9 %collective-permute-start.33 = (bf16[128,1024]{1,0:T(8,128)(2,1)S(1)}, bf16[128,1024]{1,0:T(8,128)(2,1)S(1)}, u32[]{:S(2)}, u32[]{:S(2)}) collective-permute-start(bf16[128,1024]{1,0:T(8,128)(2,1)S(1)} %fusion.16.mine_ref), channel_id=1, source_target_pairs={{0,16},{4,20},{8,24},{12,28},{16,0},{20,4},{24,8},{28,12},{1,17},{... | collective-permute-start | bytes 786440 | tf_op jit(solution)/shard_map/down_back_z2/ppermute | solution.py:562
  347.8 21.9 %collective-permute-start.37 = (bf16[768,1024]{1,0:T(8,128)(2,1)}, bf16[768,1024]{1,0:T(8,128)(2,1)}, u32[]{:S(2)}, u32[]{:S(2)}) collective-permute-start(bf16[768,1024]{1,0:T(8,128)(2,1)} %rows_product.23), channel_id=1, source_target_pairs={{0,1},{1,0},{2,3},{3,2},{4,5},{5,4},{6,7},{7,6},{8,9},{9,8},{10,11... | collective-permute-start | bytes 4718600 | tf_op jit(solution)/shard_map/core/ppermute | solution.py:684
  347.8 31.6 %collective-permute-start.36 = (bf16[512,1280]{1,0:T(8,128)(2,1)}, bf16[512,1280]{1,0:T(8,128)(2,1)}, u32[]{:S(2)}, u32[]{:S(2)}) collective-permute-start(bf16[512,1280]{1,0:T(8,128)(2,1)} %maximum_maximum_fusion.1), channel_id=1, source_target_pairs={{0,2},{1,3},{2,0},{3,1},{4,6},{5,7},{6,4},{7,5},{8,10},{9,11},{10,... | collective-permute-start | bytes 3932168 | tf_op jit(solution)/shard_map/first_x/ppermute | solution.py:562
  362.2 22.1 %collective-permute-start.34 = (bf16[64,2048]{1,0:T(8,128)(2,1)S(1)}, bf16[64,2048]{1,0:T(8,128)(2,1)S(1)}, u32[]{:S(2)}, u32[]{:S(2)}) collective-permute-start(bf16[64,2048]{1,0:T(8,128)(2,1)S(1)} %fusion.15), channel_id=1, source_target_pairs={{0,16},{4,20},{8,24},{12,28},{16,0},{20,4},{24,8},{28,12},{1,17},{... | collective-permute-start | bytes 786440 | tf_op jit(solution)/shard_map/up_z2/ppermute | solution.py:562
  363.4 19.3 %collective-permute-start.35 = (bf16[256,1024]{1,0:T(8,128)(2,1)S(1)}, bf16[256,1024]{1,0:T(8,128)(2,1)S(1)}, u32[]{:S(2)}, u32[]{:S(2)}) collective-permute-start(bf16[256,1024]{1,0:T(8,128)(2,1)S(1)} %copy-done.67), channel_id=1, source_target_pairs={{0,8},{4,12},{8,0},{12,4},{16,24},{20,28},{24,16},{28,20},{1,9},{5... | collective-permute-start | bytes 1572872 | tf_op jit(solution)/shard_map/down_back_z1/ppermute | solution.py:562
  373.3 15.8 %collective-permute-start.39 = (bf16[768,1024]{1,0:T(8,128)(2,1)}, bf16[768,1024]{1,0:T(8,128)(2,1)}, u32[]{:S(2)}, u32[]{:S(2)}) collective-permute-start(bf16[768,1024]{1,0:T(8,128)(2,1)} %add_convert_fusion.mine_ref), channel_id=1, source_target_pairs={{0,1},{1,0},{2,3},{3,2},{4,5},{5,4},{6,7},{7,6},{8,9},{9,8},{10,11... | collective-permute-start | bytes 4718600 | tf_op jit(solution)/shard_map/core/ppermute | solution.py:684
  384.4 14.9 %collective-permute-start.38 = (bf16[64,2048]{1,0:T(8,128)(2,1)S(1)}, bf16[64,2048]{1,0:T(8,128)(2,1)}, u32[]{:S(2)}, u32[]{:S(2)}) collective-permute-start(bf16[64,2048]{1,0:T(8,128)(2,1)S(1)} %fusion.11.mine_ref), channel_id=1, source_target_pairs={{0,16},{4,20},{8,24},{12,28},{16,0},{20,4},{24,8},{28,12},{1,17},{... | collective-permute-start | bytes 786440 | tf_op jit(solution)/shard_map/up_back_z2/ppermute | solution.py:562
  387.1 42.9 %collective-permute-start.43 = (bf16[512,1024]{1,0:T(8,128)(2,1)}, bf16[512,1024]{1,0:T(8,128)(2,1)}, u32[]{:S(2)}, u32[]{:S(2)}) collective-permute-start(bf16[512,1024]{1,0:T(8,128)(2,1)} %copy-done.55), channel_id=1, source_target_pairs={{0,4},{4,0},{8,12},{12,8},{16,20},{20,16},{24,28},{28,24},{1,5},{5... | collective-permute-start | bytes 3145736 | tf_op jit(solution)/shard_map/down_back_y/ppermute | solution.py:562
  387.1 38.5 %collective-permute-start.44 = (bf16[256,1280]{1,0:T(8,128)(2,1)}, bf16[256,1280]{1,0:T(8,128)(2,1)}, u32[]{:S(2)}, u32[]{:S(2)}) collective-permute-start(bf16[256,1280]{1,0:T(8,128)(2,1)} %fusion.8), channel_id=1, source_target_pairs={{0,4},{4,0},{8,12},{12,8},{16,20},{20,16},{24,28},{28,24},{1,5},{5... | collective-permute-start | bytes 1966088 | tf_op jit(solution)/shard_map/first_y/ppermute | solution.py:562
  405.4 28.1 %collective-permute-start.42 = (bf16[4,128,1024]{2,1,0:T(8,128)(2,1)}, bf16[4,128,1024]{2,1,0:T(8,128)(2,1)}, u32[]{:S(2)}, u32[]{:S(2)}) collective-permute-start(bf16[4,128,1024]{2,1,0:T(8,128)(2,1)} %get-tuple-element.138), channel_id=1, source_target_pairs={{0,2},{1,3},{2,0},{3,1},{4,6},{5,7},{6,4},{7,5},{8,10},{9,11},{10,... | collective-permute-start | bytes 3145736 | tf_op jit(solution)/shard_map/x_grad/ppermute | solution.py:680
  406.6 46.3 %collective-permute-start.47 = (bf16[128,2048]{1,0:T(8,128)(2,1)}, bf16[128,2048]{1,0:T(8,128)(2,1)}, u32[]{:S(2)}, u32[]{:S(2)}) collective-permute-start(bf16[128,2048]{1,0:T(8,128)(2,1)} %stack_rows.15.mine_ref), channel_id=1, source_target_pairs={{0,8},{4,12},{8,0},{12,4},{16,24},{20,28},{24,16},{28,20},{1,9},{5... | collective-permute-start | bytes 1572872 | tf_op jit(solution)/shard_map/up_back_z1/ppermute | solution.py:562
  406.8 7.5 %collective-permute-start.40 = (bf16[2,3072]{1,0:T(2,128)(2,1)S(1)}, bf16[2,3072]{1,0:T(2,128)(2,1)S(1)}, u32[]{:S(2)}, u32[]{:S(2)}) collective-permute-start(bf16[2,3072]{1,0:T(2,128)(2,1)S(1)} %pad_maximum_fusion.5), channel_id=1, source_target_pairs={{0,1},{1,0},{2,3},{3,2},{4,5},{5,4},{6,7},{7,6},{8,9},{9,8},{10,11... | collective-permute-start | bytes 36872 | tf_op jit(solution)/shard_map/core/ppermute | solution.py:684
  416.8 33.6 %collective-permute-start.41 = (bf16[512,896]{1,0:T(8,128)(2,1)}, bf16[512,896]{1,0:T(8,128)(2,1)}, u32[]{:S(2)}, u32[]{:S(2)}) collective-permute-start(bf16[512,896]{1,0:T(8,128)(2,1)} %fusion.7), channel_id=1, source_target_pairs={{0,2},{1,3},{2,0},{3,1},{4,6},{5,7},{6,4},{7,5},{8,10},{9,11},{10,... | collective-permute-start | bytes 2752520 | tf_op jit(solution)/shard_map/last_x/ppermute | solution.py:562
  428.4 27.1 %collective-permute-start.46 = (bf16[128,1280]{1,0:T(8,128)(2,1)S(1)}, bf16[128,1280]{1,0:T(8,128)(2,1)S(1)}, u32[]{:S(2)}, u32[]{:S(2)}) collective-permute-start(bf16[128,1280]{1,0:T(8,128)(2,1)S(1)} %fusion.13), channel_id=1, source_target_pairs={{0,8},{4,12},{8,0},{12,4},{16,24},{20,28},{24,16},{28,20},{1,9},{5... | collective-permute-start | bytes 983048 | tf_op jit(solution)/shard_map/first_z1/ppermute | solution.py:562
  450.4 12.1 %collective-permute-start.48 = (bf16[128,1024]{1,0:T(8,128)(2,1)S(1)}, bf16[128,1024]{1,0:T(8,128)(2,1)S(1)}, u32[]{:S(2)}, u32[]{:S(2)}) collective-permute-start(bf16[128,1024]{1,0:T(8,128)(2,1)S(1)} %get-tuple-element.147), channel_id=1, source_target_pairs={{0,4},{4,8},{8,12},{12,16},{16,20},{20,24},{24,28},{28,0},{1,5},{5... | collective-permute-start | bytes 786440 | tf_op jit(solution)/shard_map/return/ppermute | solution.py:562
  452.0 19.7 %collective-permute-start.45 = (bf16[256,896]{1,0:T(8,128)(2,1)S(1)}, bf16[256,896]{1,0:T(8,128)(2,1)S(1)}, u32[]{:S(2)}, u32[]{:S(2)}) collective-permute-start(bf16[256,896]{1,0:T(8,128)(2,1)S(1)} %fusion.12), channel_id=1, source_target_pairs={{0,4},{4,0},{8,12},{12,8},{16,20},{20,16},{24,28},{28,24},{1,5},{5... | collective-permute-start | bytes 1376264 | tf_op jit(solution)/shard_map/last_y/ppermute | solution.py:562
  454.2 11.8 %collective-permute-start.49 = (bf16[128,1024]{1,0:T(8,128)(2,1)S(1)}, bf16[128,1024]{1,0:T(8,128)(2,1)S(1)}, u32[]{:S(2)}, u32[]{:S(2)}) collective-permute-start(bf16[128,1024]{1,0:T(8,128)(2,1)S(1)} %get-tuple-element.149), channel_id=1, source_target_pairs={{0,8},{4,12},{8,16},{12,20},{16,24},{20,28},{24,0},{28,4},{1,9},{5... | collective-permute-start | bytes 786440 | tf_op jit(solution)/shard_map/return/ppermute | solution.py:562
  454.9 46.4 %collective-permute-start.58 = (bf16[256,2048]{1,0:T(8,128)(2,1)S(1)}, bf16[256,2048]{1,0:T(8,128)(2,1)}, u32[]{:S(2)}, u32[]{:S(2)}) collective-permute-start(bf16[256,2048]{1,0:T(8,128)(2,1)S(1)} %stack_rows.17), channel_id=1, source_target_pairs={{0,4},{4,0},{8,12},{12,8},{16,20},{20,16},{24,28},{28,24},{1,5},{5... | collective-permute-start | bytes 3145736 | tf_op jit(solution)/shard_map/up_back_y/ppermute | solution.py:562
  462.6 16.0 %collective-permute-start.51 = (bf16[64,1280]{1,0:T(8,128)(2,1)S(1)}, bf16[64,1280]{1,0:T(8,128)(2,1)S(1)}, u32[]{:S(2)}, u32[]{:S(2)}) collective-permute-start(bf16[64,1280]{1,0:T(8,128)(2,1)S(1)} %fusion.20), channel_id=1, source_target_pairs={{0,16},{4,20},{8,24},{12,28},{16,0},{20,4},{24,8},{28,12},{1,17},{... | collective-permute-start | bytes 491528 | tf_op jit(solution)/shard_map/first_z2/ppermute | solution.py:562
  462.7 32.2 %collective-permute-start.52 = (bf16[128,1024]{1,0:T(8,128)(2,1)S(1)}, bf16[128,1024]{1,0:T(8,128)(2,1)S(1)}, u32[]{:S(2)}, u32[]{:S(2)}) collective-permute-start(bf16[128,1024]{1,0:T(8,128)(2,1)S(1)} %get-tuple-element.152), channel_id=1, source_target_pairs={{0,12},{4,16},{8,20},{12,24},{16,28},{20,0},{24,4},{28,8},{1,13},{... | collective-permute-start | bytes 786440 | tf_op jit(solution)/shard_map/return/ppermute | solution.py:562
  471.9 23.0 %collective-permute-start.50 = (bf16[128,896]{1,0:T(8,128)(2,1)S(1)}, bf16[128,896]{1,0:T(8,128)(2,1)S(1)}, u32[]{:S(2)}, u32[]{:S(2)}) collective-permute-start(bf16[128,896]{1,0:T(8,128)(2,1)S(1)} %fusion.18), channel_id=1, source_target_pairs={{0,8},{4,12},{8,0},{12,4},{16,24},{20,28},{24,16},{28,20},{1,9},{5... | collective-permute-start | bytes 688136 | tf_op jit(solution)/shard_map/last_z1/ppermute | solution.py:562
  478.6 16.5 %collective-permute-start.54 = (bf16[64,1280]{1,0:T(8,128)(2,1)S(1)}, bf16[64,1280]{1,0:T(8,128)(2,1)S(1)}, u32[]{:S(2)}, u32[]{:S(2)}) collective-permute-start(bf16[64,1280]{1,0:T(8,128)(2,1)S(1)} %fusion.14.mine_ref), channel_id=1, source_target_pairs={{0,16},{4,20},{8,24},{12,28},{16,0},{20,4},{24,8},{28,12},{1,17},{... | collective-permute-start | bytes 491528 | tf_op jit(solution)/shard_map/first_back_z2/ppermute | solution.py:562
  478.7 21.2 %collective-permute-start.55 = (bf16[128,1024]{1,0:T(8,128)(2,1)S(1)}, bf16[128,1024]{1,0:T(8,128)(2,1)S(1)}, u32[]{:S(2)}, u32[]{:S(2)}) collective-permute-start(bf16[128,1024]{1,0:T(8,128)(2,1)S(1)} %get-tuple-element.155), channel_id=1, source_target_pairs={{0,16},{4,20},{8,24},{12,28},{16,0},{20,4},{24,8},{28,12},{1,17},{... | collective-permute-start | bytes 786440 | tf_op jit(solution)/shard_map/return/ppermute | solution.py:562
  495.0 6.2 %collective-permute-start.53 = (bf16[64,896]{1,0:T(8,128)(2,1)S(1)}, bf16[64,896]{1,0:T(8,128)(2,1)S(1)}, u32[]{:S(2)}, u32[]{:S(2)}) collective-permute-start(bf16[64,896]{1,0:T(8,128)(2,1)S(1)} %fusion.21), channel_id=1, source_target_pairs={{0,16},{4,20},{8,24},{12,28},{16,0},{20,4},{24,8},{28,12},{1,17},{... | collective-permute-start | bytes 344072 | tf_op jit(solution)/shard_map/last_z2/ppermute | solution.py:562
  496.2 15.3 %collective-permute-start.57 = (bf16[128,1280]{1,0:T(8,128)(2,1)S(1)}, bf16[128,1280]{1,0:T(8,128)(2,1)S(1)}, u32[]{:S(2)}, u32[]{:S(2)}) collective-permute-start(bf16[128,1280]{1,0:T(8,128)(2,1)S(1)} %stack_rows.18.mine_ref), channel_id=1, source_target_pairs={{0,8},{4,12},{8,0},{12,4},{16,24},{20,28},{24,16},{28,20},{1,9},{5... | collective-permute-start | bytes 983048 | tf_op jit(solution)/shard_map/first_back_z1/ppermute | solution.py:562
  496.3 28.2 %collective-permute-start.59 = (bf16[128,1024]{1,0:T(8,128)(2,1)}, bf16[128,1024]{1,0:T(8,128)(2,1)}, u32[]{:S(2)}, u32[]{:S(2)}) collective-permute-start(bf16[128,1024]{1,0:T(8,128)(2,1)} %get-tuple-element.159), channel_id=1, source_target_pairs={{0,20},{4,24},{8,28},{12,0},{16,4},{20,8},{24,12},{28,16},{1,21},{... | collective-permute-start | bytes 786440 | tf_op jit(solution)/shard_map/return/ppermute | solution.py:562
  512.1 32.2 %collective-permute-start.63 = (bf16[256,1280]{1,0:T(8,128)(2,1)S(1)}, bf16[256,1280]{1,0:T(8,128)(2,1)}, u32[]{:S(2)}, u32[]{:S(2)}) collective-permute-start(bf16[256,1280]{1,0:T(8,128)(2,1)S(1)} %stack_rows.19), channel_id=1, source_target_pairs={{0,4},{4,0},{8,12},{12,8},{16,20},{20,16},{24,28},{28,24},{1,5},{5... | collective-permute-start | bytes 1966088 | tf_op jit(solution)/shard_map/first_back_y/ppermute | solution.py:562
  515.9 8.5 %collective-permute-start.56 = (bf16[64,896]{1,0:T(8,128)(2,1)S(1)}, bf16[64,896]{1,0:T(8,128)(2,1)S(1)}, u32[]{:S(2)}, u32[]{:S(2)}) collective-permute-start(bf16[64,896]{1,0:T(8,128)(2,1)S(1)} %fusion.19.mine_ref), channel_id=1, source_target_pairs={{0,16},{4,20},{8,24},{12,28},{16,0},{20,4},{24,8},{28,12},{1,17},{... | collective-permute-start | bytes 344072 | tf_op jit(solution)/shard_map/last_back_z2/ppermute | solution.py:562
  518.6 16.6 %collective-permute-start.61 = (bf16[128,1024]{1,0:T(8,128)(2,1)}, bf16[128,1024]{1,0:T(8,128)(2,1)}, u32[]{:S(2)}, u32[]{:S(2)}) collective-permute-start(bf16[128,1024]{1,0:T(8,128)(2,1)} %get-tuple-element.161), channel_id=1, source_target_pairs={{0,24},{4,28},{8,0},{12,4},{16,8},{20,12},{24,16},{28,20},{1,25},{... | collective-permute-start | bytes 786440 | tf_op jit(solution)/shard_map/return/ppermute | solution.py:562
  525.0 12.5 %collective-permute-start.60 = (bf16[128,896]{1,0:T(8,128)(2,1)S(1)}, bf16[128,896]{1,0:T(8,128)(2,1)S(1)}, u32[]{:S(2)}, u32[]{:S(2)}) collective-permute-start(bf16[128,896]{1,0:T(8,128)(2,1)S(1)} %stack_rows.20.mine_ref), channel_id=1, source_target_pairs={{0,8},{4,12},{8,0},{12,4},{16,24},{20,28},{24,16},{28,20},{1,9},{5... | collective-permute-start | bytes 688136 | tf_op jit(solution)/shard_map/last_back_z1/ppermute | solution.py:562
  531.1 10.8 %collective-permute-start.62 = (bf16[128,1024]{1,0:T(8,128)(2,1)}, bf16[128,1024]{1,0:T(8,128)(2,1)S(1)}, u32[]{:S(2)}, u32[]{:S(2)}) collective-permute-start(bf16[128,1024]{1,0:T(8,128)(2,1)} %get-tuple-element.164), channel_id=1, source_target_pairs={{0,28},{4,0},{8,4},{12,8},{16,12},{20,16},{24,20},{28,24},{1,29},{... | collective-permute-start | bytes 786440 | tf_op jit(solution)/shard_map/return/ppermute | solution.py:562
  535.0 18.7 %collective-permute-start.67 = (bf16[256,2048]{1,0:T(8,128)(2,1)}, bf16[256,2048]{1,0:T(8,128)(2,1)S(1)}, u32[]{:S(2)}, u32[]{:S(2)}) collective-permute-start(bf16[256,2048]{1,0:T(8,128)(2,1)} %get-tuple-element.209), channel_id=1, source_target_pairs={{0,1},{1,0},{2,3},{3,2},{4,5},{5,4},{6,7},{7,6},{8,9},{9,8},{10,11... | collective-permute-start | bytes 3145736 | tf_op jit(solution)/shard_map/core/ppermute | solution.py:684
  538.1 13.2 %collective-permute-start.65 = (bf16[256,896]{1,0:T(8,128)(2,1)S(1)}, bf16[256,896]{1,0:T(8,128)(2,1)S(1)}, u32[]{:S(2)}, u32[]{:S(2)}) collective-permute-start(bf16[256,896]{1,0:T(8,128)(2,1)S(1)} %stack_rows.21), channel_id=1, source_target_pairs={{0,4},{4,0},{8,12},{12,8},{16,20},{20,16},{24,28},{28,24},{1,5},{5... | collective-permute-start | bytes 1376264 | tf_op jit(solution)/shard_map/last_back_y/ppermute | solution.py:562
  546.2 10.4 %collective-permute-start.64 = (bf16[256,768]{1,0:T(8,128)(2,1)}, bf16[256,768]{1,0:T(8,128)(2,1)}, u32[]{:S(2)}, u32[]{:S(2)}) collective-permute-start(bf16[256,768]{1,0:T(8,128)(2,1)} %get-tuple-element.229), channel_id=1, source_target_pairs={{0,1},{1,0},{2,3},{3,2},{4,5},{5,4},{6,7},{7,6},{8,9},{9,8},{10,11... | collective-permute-start | bytes 1179656 | tf_op jit(solution)/shard_map/core/ppermute | solution.py:684
  (121 other events, 930.1 us)

commit v5 on v4

--- a/solution.py
+++ b/solution.py
@@ -105,15 +105,28 @@
         for dst, flip in ((own_ref, 0), (far_ref, 2)):
             start = (here ^ flip) * 128
 
-            @pl.loop(0, 8)
+            whole = jnp.clip((length - start) // 16, 0, 8)
+            some = jnp.clip((length - start + 15) // 16, 0, 8)
+
+            def piece(i):
+                row = pl.multiple_of(jnp.minimum(offset + start + i * 16, CAP - 16), 16)
+                return rows_ref[pl.ds(row, 16), :]
+
+            def put(i, value):
+                dst[slot, pl.ds(pl.multiple_of(i * 16, 16), 16), :] = value
+
+            @pl.loop(0, whole)
             def _(i):
-                position = start + i * 16
-                row = pl.multiple_of(jnp.minimum(offset + position, CAP - 16), 16)
-                keep = lax.broadcasted_iota(jnp.int32, (16, width), 0) + position < length
-                part = rows_ref[pl.ds(row, 16), :].astype(F32)
-                dst[slot, pl.ds(pl.multiple_of(i * 16, 16), 16), :] = jnp.where(
-                    keep, part, 0.0
-                ).astype(BF)
+                put(i, piece(i))
+
+            @pl.loop(whole, some)
+            def _(i):
+                keep = lax.broadcasted_iota(jnp.int32, (16, width), 0) + (start + i * 16) < length
+                put(i, jnp.where(keep, piece(i).astype(F32), 0.0).astype(BF))
+
+            @pl.loop(some, 8)
+            def _(i):
+                put(i, jnp.zeros((16, width), BF))
 
 
 def unpack(meta, mine, other):

time: 569 us -> 568 us (level)
  transfers between devices with their start and end apart: 69 -> 69, of which waited for: 25 -> 24; matrix products, arithmetic and copies ran while one was open for 12% -> 12% of each run, Pallas kernels for 30% -> 31%
where the time goes in v5:
time: 568 us; the launch traced here: 560 us
  Pallas kernels  188 us (33%)
  waiting for transfers between devices  180 us (32%)
  starting transfers between devices  71.9 us (13%)
  local copies, waits for them, and re-layouts  61.2 us (11%)
  other arithmetic  54.2 us (10%)
    ppermute x38, waiting for transfers between devices, moved(): return lax.ppermute(value, axis, pairs)  128 us
    pallas_call x12, Pallas kernels, rows_product(): pl.pallas_call(functools.partial(_rows_kernel, count_at, turned, len(left...  48.1 us
    ppermute x38, starting transfers between devices, moved(): return lax.ppermute(value, axis, pairs)  47 us
    pallas_call x12, Pallas kernels, grad_product(): pl.pallas_call(functools.partial(_grad_kernel, len(lefts)), out_shape=jax...  46.3 us
    unnamed x260, local copies, waits for them, and re-layouts  42.4 us
    all_to_all x1, waiting for transfers between devices, on_device(): lax.all_to_all(sent_tokens, 'seq', split_axis=0, concat_axis=0, tiled=True)  36.1 us
    pallas_call x2, Pallas kernels, attend_back(): pl.pallas_call(functools.partial(_attend_back_kernel, block), out_shape=j...  20.4 us
    pallas_call x1, Pallas kernels, attend(): pl.pallas_call(_attend_kernel, out_shape=(jax.ShapeDtypeStruct((CAP, widt...  14.9 us
  transfers between devices with their start and end apart: 69, of which 24 were waited for; matrix products, arithmetic and copies ran while one was open for 12% of the time, Pallas kernels for 31%

profile of v5, /device:TPU:0, one launch (start us, length us, event | category | flops | bytes accessed | tf_op | source)
XLA Modules:
  0.0 560.3 jit_solution(15662574056275882639)
XLA Ops:
  5.6 7.4 %all-to-all-start = ((bf16[8,128,1024]{2,1,0:T(8,128)(2,1)}), bf16[8,128,1024]{2,1,0:T(8,128)(2,1)S(1)}, u32[]{:S(2)}, u32[]{:S(2)}) async-start(bf16[8,128,1024]{2,1,0:T(8,128)(2,1)} %copy-done.48), calls=%async_computation | async-start | bytes 4194304 | tf_op jit(solution)/shard_map/all_to_all | solution.py:828
  25.2 36.1 %all-to-all-done.refs_0_ = bf16[8,128,1024]{2,1,0:T(8,128)(2,1)S(1)} async-done(((bf16[8,128,1024]{2,1,0:T(8,128)(2,1)}), bf16[8,128,1024]{2,1,0:T(8,128)(2,1)S(1)}, u32[]{:S(2)}, u32[]{:S(2)}) %all-to-all-start) | async-done | bytes 2097184 | tf_op jit(solution)/shard_map/all_to_all | solution.py:828
  66.8 11.5 %collective-permute-done.2.other_ref = bf16[160,1024]{1,0:T(8,128)(2,1)S(1)} collective-permute-done((bf16[160,1024]{1,0:T(8,128)(2,1)S(1)}, bf16[160,1024]{1,0:T(8,128)(2,1)S(1)}, u32[]{:S(2)}, u32[]{:S(2)}) %collective-permute-start.2) | collective-permute-done | bytes 327712 | tf_op jit(solution)/shard_map/share_z2/ppermute | solution.py:575
  84.2 10.5 %collective-permute-done.5.other_ref = bf16[320,1024]{1,0:T(8,128)(2,1)} collective-permute-done((bf16[320,1024]{1,0:T(8,128)(2,1)S(1)}, bf16[320,1024]{1,0:T(8,128)(2,1)}, u32[]{:S(2)}, u32[]{:S(2)}) %collective-permute-start.5) | collective-permute-done | bytes 655392 | tf_op jit(solution)/shard_map/share_z1/ppermute | solution.py:575
  95.9 2.7 collective-permute-start.11
  103.1 3.0 pack.2.rows_ref.refs_0_
  106.0 5.7 %qkv_product.1.qkv_ref = bf16[1536,1536]{1,0:T(8,128)(2,1)S(1)} custom-call(s32[24]{0:T(128)S(1)} %concatenate.56.meta_ref, bf16[1536,1024]{1,0:T(8,128)(2,1)S(1)} %pack.2.rows_ref.refs_0_, bf16[1024,1536]{1,0:T(8,128)(2,1)S(1)} %assemble.2.weight_ref, f32[1,1536]{1,0:T(1,128)S(1)} %broadcast_in_dim.212.bias_ref), custom_call_target="tpu_custom_call" | custom-call | bytes 1024 | tf_op jit(solution)/shard_map/qkv_product/pallas_call | solution.py:459
  111.8 14.9 %attend.1 = (bf16[1536,512]{1,0:T(8,128)(2,1)S(1)}, f32[4,8,1,512]{3,2,1,0:T(1,128)S(1)}) custom-call(s32[24]{0:T(128)S(1)} %concatenate.56.meta_ref, bf16[1536,1536]{1,0:T(8,128)(2,1)S(1)} %qkv_product.1.qkv_ref), custom_call_target="tpu_custom_call" | custom-call | bytes 1024 | tf_op jit(solution)/shard_map/attend/pallas_call | solution.py:205
  135.4 11.7 %collective-permute-done.13.refs_1_ = bf16[256,4096]{1,0:T(8,128)(2,1)S(1)} collective-permute-done((bf16[256,4096]{1,0:T(8,128)(2,1)}, bf16[256,4096]{1,0:T(8,128)(2,1)S(1)}, u32[]{:S(2)}, u32[]{:S(2)}) %collective-permute-start.13) | collective-permute-done | bytes 2097184 | tf_op jit(solution)/shard_map/x_up_weight/ppermute | solution.py:693
  153.8 5.7 %up_product.3 = (bf16[768,2048]{1,0:T(8,128)(2,1)S(1)}, bf16[768,2048]{1,0:T(8,128)(2,1)S(1)}) custom-call(s32[24]{0:T(128)S(1)} %concatenate.56.meta_ref, bf16[768,1024]{1,0:T(8,128)(2,1)S(1)} %collective-permute-done.16.low_ref.refs_1_, bf16[1024,2048]{1,0:T(8,128)(2,1)S(1)} %assemble.3.weight_ref.refs_1_, f32[1,2048]{1,0:T(1,128)S(1)} %bitcast.183), custom_call_target="tpu_custom_call" | custom-call | bytes 1024 | tf_op jit(solution)/shard_map/up_product/pallas_call | solution.py:435
  159.5 3.5 rows_product.15
  163.0 4.1 collective-permute-start.17
  167.2 8.0 %up_product.2 = (bf16[768,2048]{1,0:T(8,128)(2,1)S(1)}, bf16[768,2048]{1,0:T(8,128)(2,1)S(1)}) custom-call(s32[24]{0:T(128)S(1)} %concatenate.56.meta_ref, bf16[768,1024]{1,0:T(8,128)(2,1)S(1)} %fusion.3.low_ref.refs_0_, bf16[1024,2048]{1,0:T(8,128)(2,1)S(1)} %assemble.3.weight_ref.refs_1_, f32[1,2048]{1,0:T(1,128)S(1)} %bitcast.184), custom_call_target="tpu_custom_call" | custom-call | bytes 1024 | tf_op jit(solution)/shard_map/up_product/pallas_call | solution.py:435
  177.0 4.9 rows_product.14
  189.8 3.7 collective-permute-done.21.refs_3_.refs_0_
  197.4 4.7 grad_product.13
  202.1 4.7 grad_product.12
  212.5 7.2 %rows_product.16.refs_2_.refs_0_ = bf16[768,2048]{1,0:T(8,128)(2,1)S(1)} custom-call(s32[24]{0:T(128)S(1)} %concatenate.56.meta_ref, bf16[768,1024]{1,0:T(8,128)(2,1)} %get-tuple-element.108.refs_2_.refs_0_, bf16[2048,1024]{1,0:T(8,128)(2,1)S(1)} %copy-done.16, bf16[768,2048]{1,0:T(8,128)(2,1)S(1)} %copy-done.62), custom_call_target="tpu_custom_call" | custom-call | bytes 1024 | tf_op jit(solution)/shard_map/rows_product/pallas_call | solution.py:498
  219.8 6.4 %rows_product.17.refs_3_.refs_0_ = bf16[768,2048]{1,0:T(8,128)(2,1)S(1)} custom-call(s32[24]{0:T(128)S(1)} %concatenate.56.meta_ref, bf16[768,1024]{1,0:T(8,128)(2,1)} %collective-permute-done.21.refs_3_.refs_0_, bf16[2048,1024]{1,0:T(8,128)(2,1)S(1)} %copy-done.16, bf16[768,2048]{1,0:T(8,128)(2,1)S(1)} %copy-done.60), custom_call_target="tpu_custom_call" | custom-call | bytes 1024 | tf_op jit(solution)/shard_map/rows_product/pallas_call | solution.py:498
  226.3 5.7 %grad_product.14 = bf16[512,2048]{1,0:T(8,128)(2,1)S(1)} custom-call(s32[24]{0:T(128)S(1)} %concatenate.56.meta_ref, s32[1]{0:T(128)} %bitcast.22.at_ref, bf16[768,1024]{1,0:T(8,128)(2,1)S(1)} %copy-done.27, bf16[768,1024]{1,0:T(8,128)(2,1)S(1)} %copy-done.40, bf16[768,2048]{1,0:T(8,128)(2,1)S(1)} %rows_product.16.refs_2_.refs_0_, ...), custom_call_target="tpu_custom_call" | custom-call | bytes 1024 | tf_op jit(solution)/shard_map/grad_product/pallas_call | solution.py:536
  233.4 4.8 rows_product.18
  244.9 4.7 grad_product.16
  249.7 4.9 grad_product.15
  254.6 5.7 %grad_product.17 = f32[512,2048]{1,0:T(8,128)S(1)} custom-call(s32[24]{0:T(128)S(1)} %concatenate.56.meta_ref, s32[1]{0:T(128)} %bitcast.27.at_ref, bf16[768,1024]{1,0:T(8,128)(2,1)S(1)} %copy-done.28, bf16[768,1024]{1,0:T(8,128)(2,1)S(1)} %copy-done.41, bf16[768,2048]{1,0:T(8,128)(2,1)S(1)} %copy-done.4, bf16[768,2048]{1,0:T(8,128)(2,1)S(1)} %copy-done.6), custom_call_target="tpu_custom_call" | custom-call | bytes 1024 | tf_op jit(solution)/shard_map/grad_product/pallas_call | solution.py:536
  260.4 2.8 maximum_add_fusion
  265.8 5.2 rows_product.19
  271.1 5.0 multiply_reduce_fusion.1
  276.2 2.5 convert_reduce_fusion.5
  279.8 10.7 %collective-permute-done.28 = bf16[512,1024]{1,0:T(8,128)(2,1)S(1)} collective-permute-done((bf16[512,1024]{1,0:T(8,128)(2,1)}, bf16[512,1024]{1,0:T(8,128)(2,1)S(1)}, u32[]{:S(2)}, u32[]{:S(2)}) %collective-permute-start.28) | collective-permute-done | bytes 1048608 | tf_op jit(solution)/shard_map/down_z1/ppermute | solution.py:575
  301.6 10.0 %attend_back.2.refs_1_ = bf16[1536,768]{1,0:T(8,128)(2,1)S(1)} custom-call(s32[24]{0:T(128)S(1)} %concatenate.56.meta_ref, bf16[1536,1536]{1,0:T(8,128)(2,1)S(1)} %bitcast.178, f32[4,8,1,512]{3,2,1,0:T(1,128)S(1)} %get-tuple-element.116.lse_ref, bf16[1536,512]{1,0:T(8,128)(2,1)S(1)} %pad_maximum_fusion.1.gctx_ref), custom_call_target="tpu_custom_call" | custom-call | bytes 1024 | tf_op jit(solution)/shard_map/attend_back/pallas_call | solution.py:281
  311.7 3.9 collective-permute-done.29
  320.0 2.7 grad_product.20
  326.4 2.7 collective-permute-start.33
  329.3 10.4 %attend_back.3.refs_1_ = bf16[1536,768]{1,0:T(8,128)(2,1)S(1)} custom-call(s32[24]{0:T(128)S(1)} %concatenate.56.meta_ref, bf16[1536,1536]{1,0:T(8,128)(2,1)S(1)} %bitcast.178, f32[4,8,1,512]{3,2,1,0:T(1,128)S(1)} %get-tuple-element.116.lse_ref, bf16[1536,512]{1,0:T(8,128)(2,1)S(1)} %pad_maximum_fusion.1.gctx_ref), custom_call_target="tpu_custom_call" | custom-call | bytes 1024 | tf_op jit(solution)/shard_map/attend_back/pallas_call | solution.py:281
  344.3 4.2 rows_product.23
  348.6 2.5 convert_reduce_fusion.1
  359.7 2.7 grad_product.21
  362.8 2.9 collective-permute-start.35
  365.7 4.3 rows_product.22
  370.1 3.6 add_convert_fusion.mine_ref
  373.6 6.4 %collective-permute-done.36 = bf16[512,1280]{1,0:T(8,128)(2,1)} collective-permute-done((bf16[512,1280]{1,0:T(8,128)(2,1)}, bf16[512,1280]{1,0:T(8,128)(2,1)}, u32[]{:S(2)}, u32[]{:S(2)}) %collective-permute-start.36) | collective-permute-done | bytes 1310752 | tf_op jit(solution)/shard_map/first_x/ppermute | solution.py:575
  389.3 4.0 unpack.3
  394.3 5.6 collective-permute-done.38.other_ref
  402.1 2.7 grad_product.22
  410.7 2.7 grad_product.23
  418.2 7.9 %collective-permute-done.44 = bf16[256,1280]{1,0:T(8,128)(2,1)} collective-permute-done((bf16[256,1280]{1,0:T(8,128)(2,1)}, bf16[256,1280]{1,0:T(8,128)(2,1)}, u32[]{:S(2)}, u32[]{:S(2)}) %collective-permute-start.44) | collective-permute-done | bytes 655392 | tf_op jit(solution)/shard_map/first_y/ppermute | solution.py:575
  430.4 3.5 stack_rows.16
  437.0 14.1 %collective-permute-done.41 = bf16[512,896]{1,0:T(8,128)(2,1)} collective-permute-done((bf16[512,896]{1,0:T(8,128)(2,1)}, bf16[512,896]{1,0:T(8,128)(2,1)}, u32[]{:S(2)}, u32[]{:S(2)}) %collective-permute-start.41) | collective-permute-done | bytes 917536 | tf_op jit(solution)/shard_map/last_x/ppermute | solution.py:575
  456.1 7.0 %collective-permute-done.48.refs_1_ = bf16[128,1024]{1,0:T(8,128)(2,1)S(1)} collective-permute-done((bf16[128,1024]{1,0:T(8,128)(2,1)S(1)}, bf16[128,1024]{1,0:T(8,128)(2,1)S(1)}, u32[]{:S(2)}, u32[]{:S(2)}) %collective-permute-start.48) | collective-permute-done | bytes 262176 | tf_op jit(solution)/shard_map/return/ppermute | solution.py:575
  463.4 3.2 collective-permute-done.49.refs_2_
  466.6 5.6 %collective-permute-done.45 = bf16[256,896]{1,0:T(8,128)(2,1)S(1)} collective-permute-done((bf16[256,896]{1,0:T(8,128)(2,1)S(1)}, bf16[256,896]{1,0:T(8,128)(2,1)S(1)}, u32[]{:S(2)}, u32[]{:S(2)}) %collective-permute-start.45) | collective-permute-done | bytes 458784 | tf_op jit(solution)/shard_map/last_y/ppermute | solution.py:575
  472.7 6.3 %collective-permute-done.51 = bf16[64,1280]{1,0:T(8,128)(2,1)S(1)} collective-permute-done((bf16[64,1280]{1,0:T(8,128)(2,1)S(1)}, bf16[64,1280]{1,0:T(8,128)(2,1)S(1)}, u32[]{:S(2)}, u32[]{:S(2)}) %collective-permute-start.51) | collective-permute-done | bytes 163872 | tf_op jit(solution)/shard_map/first_z2/ppermute | solution.py:575
  479.2 2.9 collective-permute-start.55
  482.1 13.4 %collective-permute-done.52.refs_3_ = bf16[128,1024]{1,0:T(8,128)(2,1)S(1)} collective-permute-done((bf16[128,1024]{1,0:T(8,128)(2,1)S(1)}, bf16[128,1024]{1,0:T(8,128)(2,1)S(1)}, u32[]{:S(2)}, u32[]{:S(2)}) %collective-permute-start.52) | collective-permute-done | bytes 262176 | tf_op jit(solution)/shard_map/return/ppermute | solution.py:575
  496.9 3.6 collective-permute-start.59
  504.1 8.0 %collective-permute-done.57.other_ref = bf16[128,1280]{1,0:T(8,128)(2,1)S(1)} collective-permute-done((bf16[128,1280]{1,0:T(8,128)(2,1)S(1)}, bf16[128,1280]{1,0:T(8,128)(2,1)S(1)}, u32[]{:S(2)}, u32[]{:S(2)}) %collective-permute-start.57) | collective-permute-done | bytes 327712 | tf_op jit(solution)/shard_map/first_back_z1/ppermute | solution.py:575
  512.7 3.8 collective-permute-start.63
  516.5 2.6 collective-permute-start.56
  521.1 4.0 collective-permute-done.56.other_ref
  525.7 5.9 %collective-permute-start.60 = (bf16[128,896]{1,0:T(8,128)(2,1)S(1)}, bf16[128,896]{1,0:T(8,128)(2,1)S(1)}, u32[]{:S(2)}, u32[]{:S(2)}) collective-permute-start(bf16[128,896]{1,0:T(8,128)(2,1)S(1)} %stack_rows.20.mine_ref), channel_id=1, source_target_pairs={{0,8},{4,12},{8,0},{12,4},{16,24},{20,28},{24,16},{28,20},{1,9},{5... | collective-permute-start | bytes 688136 | tf_op jit(solution)/shard_map/last_back_z1/ppermute | solution.py:575
  531.6 2.7 collective-permute-start.62
  548.8 3.0 collective-permute-done.65
  554.3 2.8 spread_columns.3
  557.1 3.0 spread_columns.2
  (540 shorter events, 172.1 us)
Async XLA Ops:
  5.6 55.7 %all-to-all-start = ((bf16[8,128,1024]{2,1,0:T(8,128)(2,1)}), bf16[8,128,1024]{2,1,0:T(8,128)(2,1)S(1)}, u32[]{:S(2)}, u32[]{:S(2)}) async-start(bf16[8,128,1024]{2,1,0:T(8,128)(2,1)} %copy-done.48), calls=%async_computation | async-start | bytes 4194304 | tf_op jit(solution)/shard_map/all_to_all | solution.py:828
  14.9 64.1 %collective-permute-start.9 = (bf16[1,3072]{1,0:T(2,128)(2,1)S(1)}, bf16[1,3072]{1,0:T(2,128)(2,1)S(1)}, u32[]{:S(2)}, u32[]{:S(2)}) collective-permute-start(bf16[1,3072]{1,0:T(2,128)(2,1)S(1)} %broadcast_in_dim.210), channel_id=1, source_target_pairs={{0,1},{1,0},{2,3},{3,2},{4,5},{5,4},{6,7},{7,6},{8,9},{9,8},{10,11... | collective-permute-start | bytes 18440 | tf_op jit(solution)/shard_map/core/ppermute | solution.py:697
  16.9 45.1 %collective-permute-start.1 = (bf16[160,1024]{1,0:T(8,128)(2,1)S(1)}, bf16[160,1024]{1,0:T(8,128)(2,1)S(1)}, u32[]{:S(2)}, u32[]{:S(2)}) collective-permute-start(bf16[160,1024]{1,0:T(8,128)(2,1)S(1)} %pad_maximum_fusion.2), channel_id=1, source_target_pairs={{0,2},{1,3},{2,0},{3,1},{4,6},{5,7},{6,4},{7,5},{8,10},{9,11},{10,... | collective-permute-start | bytes 983048 | tf_op jit(solution)/shard_map/x_shares/ppermute | solution.py:693
  18.4 80.6 %collective-permute-start.7 = (bf16[256,3072]{1,0:T(8,128)(2,1)}, bf16[256,3072]{1,0:T(8,128)(2,1)}, u32[]{:S(2)}, u32[]{:S(2)}) collective-permute-start(bf16[256,3072]{1,0:T(8,128)(2,1)} %refs_0_.6), channel_id=1, source_target_pairs={{0,1},{1,0},{2,3},{3,2},{4,5},{5,4},{6,7},{7,6},{8,9},{9,8},{10,11... | collective-permute-start | bytes 4718600 | tf_op jit(solution)/shard_map/core/ppermute | solution.py:697
  18.6 65.6 %collective-permute-start.6 = (bf16[256,3072]{1,0:T(8,128)(2,1)}, bf16[256,3072]{1,0:T(8,128)(2,1)}, u32[]{:S(2)}, u32[]{:S(2)}) collective-permute-start(bf16[256,3072]{1,0:T(8,128)(2,1)} %refs_0_.6), channel_id=1, source_target_pairs={{0,2},{1,3},{2,0},{3,1},{4,6},{5,7},{6,4},{7,5},{8,10},{9,11},{10,... | collective-permute-start | bytes 4718600 | tf_op jit(solution)/shard_map/x_first_weights/ppermute | solution.py:693
  62.0 16.3 %collective-permute-start.2 = (bf16[160,1024]{1,0:T(8,128)(2,1)S(1)}, bf16[160,1024]{1,0:T(8,128)(2,1)S(1)}, u32[]{:S(2)}, u32[]{:S(2)}) collective-permute-start(bf16[160,1024]{1,0:T(8,128)(2,1)S(1)} %collective-permute-done.1.mine_ref), channel_id=1, source_target_pairs={{0,16},{4,20},{8,24},{12,28},{16,0},{20,4},{24,8},{28,12},{1,17},{... | collective-permute-start | bytes 983048 | tf_op jit(solution)/shard_map/share_z2/ppermute | solution.py:575
  63.2 32.7 %collective-permute-start = (bf16[4,128,1024]{2,1,0:T(8,128)(2,1)}, bf16[4,128,1024]{2,1,0:T(8,128)(2,1)}, u32[]{:S(2)}, u32[]{:S(2)}) collective-permute-start(bf16[4,128,1024]{2,1,0:T(8,128)(2,1)} %get-tuple-element.221), channel_id=1, source_target_pairs={{0,2},{1,3},{2,0},{3,1},{4,6},{5,7},{6,4},{7,5},{8,10},{9,11},{10,... | collective-permute-start | bytes 3145736 | tf_op jit(solution)/shard_map/x_tokens/ppermute | solution.py:693
  78.9 15.8 %collective-permute-start.5 = (bf16[320,1024]{1,0:T(8,128)(2,1)S(1)}, bf16[320,1024]{1,0:T(8,128)(2,1)}, u32[]{:S(2)}, u32[]{:S(2)}) collective-permute-start(bf16[320,1024]{1,0:T(8,128)(2,1)S(1)} %stack_rows.11.mine_ref), channel_id=1, source_target_pairs={{0,8},{4,12},{8,0},{12,4},{16,24},{20,28},{24,16},{28,20},{1,9},{5... | collective-permute-start | bytes 1966088 | tf_op jit(solution)/shard_map/share_z1/ppermute | solution.py:575
  79.1 19.6 %collective-permute-start.10 = (bf16[2,3072]{1,0:T(2,128)(2,1)S(1)}, bf16[2,3072]{1,0:T(2,128)(2,1)S(1)}, u32[]{:S(2)}, u32[]{:S(2)}) collective-permute-start(bf16[2,3072]{1,0:T(2,128)(2,1)S(1)} %pad_maximum_fusion.4), channel_id=1, source_target_pairs={{0,2},{1,3},{2,0},{3,1},{4,6},{5,7},{6,4},{7,5},{8,10},{9,11},{10,... | collective-permute-start | bytes 36872 | tf_op jit(solution)/shard_map/x/ppermute | solution.py:693
  84.2 16.4 %collective-permute-start.8 = (bf16[256,3072]{1,0:T(8,128)(2,1)}, bf16[256,3072]{1,0:T(8,128)(2,1)S(1)}, u32[]{:S(2)}, u32[]{:S(2)}) collective-permute-start(bf16[256,3072]{1,0:T(8,128)(2,1)} %collective-permute-done.6.refs_1_), channel_id=1, source_target_pairs={{0,1},{1,0},{2,3},{3,2},{4,5},{5,4},{6,7},{7,6},{8,9},{9,8},{10,11... | collective-permute-start | bytes 4718600 | tf_op jit(solution)/shard_map/core/ppermute | solution.py:697
  94.7 8.4 %collective-permute-start.3 = (bf16[4,128,1024]{2,1,0:T(8,128)(2,1)S(1)}, bf16[4,128,1024]{2,1,0:T(8,128)(2,1)S(1)}, u32[]{:S(2)}, u32[]{:S(2)}) collective-permute-start(bf16[4,128,1024]{2,1,0:T(8,128)(2,1)S(1)} %get-tuple-element.222.a0), channel_id=1, source_target_pairs={{0,1},{1,0},{2,3},{3,2},{4,5},{5,4},{6,7},{7,6},{8,9},{9,8},{10,11... | collective-permute-start | bytes 3145736 | tf_op jit(solution)/shard_map/core/ppermute | solution.py:697
  95.9 33.0 %collective-permute-start.11 = (bf16[640,1024]{1,0:T(8,128)(2,1)S(1)}, bf16[640,1024]{1,0:T(8,128)(2,1)S(1)}, u32[]{:S(2)}, u32[]{:S(2)}) collective-permute-start(bf16[640,1024]{1,0:T(8,128)(2,1)S(1)} %stack_rows.12.mine_ref), channel_id=1, source_target_pairs={{0,4},{4,0},{8,12},{12,8},{16,20},{20,16},{24,28},{28,24},{1,5},{5... | collective-permute-start | bytes 3932168 | tf_op jit(solution)/shard_map/share_y/ppermute | solution.py:575
  99.0 48.1 %collective-permute-start.13 = (bf16[256,4096]{1,0:T(8,128)(2,1)}, bf16[256,4096]{1,0:T(8,128)(2,1)S(1)}, u32[]{:S(2)}, u32[]{:S(2)}) collective-permute-start(bf16[256,4096]{1,0:T(8,128)(2,1)} %refs_0_.7), channel_id=1, source_target_pairs={{0,2},{1,3},{2,0},{3,1},{4,6},{5,7},{6,4},{7,5},{8,10},{9,11},{10,... | collective-permute-start | bytes 6291464 | tf_op jit(solution)/shard_map/x_up_weight/ppermute | solution.py:693
  131.7 15.3 %collective-permute-start.12 = (bf16[768,1024]{1,0:T(8,128)(2,1)S(1)}, bf16[768,1024]{1,0:T(8,128)(2,1)S(1)}, u32[]{:S(2)}, u32[]{:S(2)}) collective-permute-start(bf16[768,1024]{1,0:T(8,128)(2,1)S(1)} %rows_product.13), channel_id=1, source_target_pairs={{0,1},{1,0},{2,3},{3,2},{4,5},{5,4},{6,7},{7,6},{8,9},{9,8},{10,11... | collective-permute-start | bytes 4718600 | tf_op jit(solution)/shard_map/core/ppermute | solution.py:697
  132.9 20.0 %collective-permute-start.14 = (bf16[256,4096]{1,0:T(8,128)(2,1)S(1)}, bf16[256,4096]{1,0:T(8,128)(2,1)S(1)}, u32[]{:S(2)}, u32[]{:S(2)}) collective-permute-start(bf16[256,4096]{1,0:T(8,128)(2,1)S(1)} %copy-done.65), channel_id=1, source_target_pairs={{0,1},{1,0},{2,3},{3,2},{4,5},{5,4},{6,7},{7,6},{8,9},{9,8},{10,11... | collective-permute-start | bytes 6291464 | tf_op jit(solution)/shard_map/core/ppermute | solution.py:697
  147.1 5.8 %collective-permute-start.15 = (bf16[256,4096]{1,0:T(8,128)(2,1)S(1)}, bf16[256,4096]{1,0:T(8,128)(2,1)S(1)}, u32[]{:S(2)}, u32[]{:S(2)}) collective-permute-start(bf16[256,4096]{1,0:T(8,128)(2,1)S(1)} %collective-permute-done.13.refs_1_), channel_id=1, source_target_pairs={{0,1},{1,0},{2,3},{3,2},{4,5},{5,4},{6,7},{7,6},{8,9},{9,8},{10,11... | collective-permute-start | bytes 6291464 | tf_op jit(solution)/shard_map/core/ppermute | solution.py:697
  151.3 25.6 %collective-permute-start.18 = (bf16[4,128,1024]{2,1,0:T(8,128)(2,1)S(1)}, bf16[4,128,1024]{2,1,0:T(8,128)(2,1)S(1)}, u32[]{:S(2)}, u32[]{:S(2)}) collective-permute-start(bf16[4,128,1024]{2,1,0:T(8,128)(2,1)S(1)} %get-tuple-element.106), channel_id=1, source_target_pairs={{0,2},{1,3},{2,0},{3,1},{4,6},{5,7},{6,4},{7,5},{8,10},{9,11},{10,... | collective-permute-start | bytes 3145736 | tf_op jit(solution)/shard_map/x_cotangent/ppermute | solution.py:693
  163.0 20.8 %collective-permute-start.17 = (bf16[768,1024]{1,0:T(8,128)(2,1)S(1)}, bf16[768,1024]{1,0:T(8,128)(2,1)S(1)}, u32[]{:S(2)}, u32[]{:S(2)}) collective-permute-start(bf16[768,1024]{1,0:T(8,128)(2,1)S(1)} %rows_product.15), channel_id=1, source_target_pairs={{0,1},{1,0},{2,3},{3,2},{4,5},{5,4},{6,7},{7,6},{8,9},{9,8},{10,11... | collective-permute-start | bytes 4718600 | tf_op jit(solution)/shard_map/core/ppermute | solution.py:697
  167.1 14.8 %collective-permute-start.19 = (bf16[4,128,1024]{2,1,0:T(8,128)(2,1)S(1)}, bf16[4,128,1024]{2,1,0:T(8,128)(2,1)S(1)}, u32[]{:S(2)}, u32[]{:S(2)}) collective-permute-start(bf16[4,128,1024]{2,1,0:T(8,128)(2,1)S(1)} %get-tuple-element.220.a0), channel_id=1, source_target_pairs={{0,1},{1,0},{2,3},{3,2},{4,5},{5,4},{6,7},{7,6},{8,9},{9,8},{10,11... | collective-permute-start | bytes 3145736 | tf_op jit(solution)/shard_map/core/ppermute | solution.py:697
  208.3 52.0 %collective-permute-start.24 = (bf16[1024,1024]{1,0:T(8,128)(2,1)}, bf16[1024,1024]{1,0:T(8,128)(2,1)}, u32[]{:S(2)}, u32[]{:S(2)}) collective-permute-start(bf16[1024,1024]{1,0:T(8,128)(2,1)} %bitcast.21), channel_id=1, source_target_pairs={{0,4},{4,0},{8,12},{12,8},{16,20},{20,16},{24,28},{28,24},{1,5},{5... | collective-permute-start | bytes 6291464 | tf_op jit(solution)/shard_map/down_y/ppermute | solution.py:575
  238.2 32.9 %collective-permute-start.25 = (bf16[768,1024]{1,0:T(8,128)(2,1)}, bf16[768,1024]{1,0:T(8,128)(2,1)}, u32[]{:S(2)}, u32[]{:S(2)}) collective-permute-start(bf16[768,1024]{1,0:T(8,128)(2,1)} %rows_product.18), channel_id=1, source_target_pairs={{0,1},{1,0},{2,3},{3,2},{4,5},{5,4},{6,7},{7,6},{8,9},{9,8},{10,11... | collective-permute-start | bytes 4718600 | tf_op jit(solution)/shard_map/core/ppermute | solution.py:697
  239.7 51.7 %collective-permute-start.27 = (bf16[512,2048]{1,0:T(8,128)(2,1)}, bf16[512,2048]{1,0:T(8,128)(2,1)}, u32[]{:S(2)}, u32[]{:S(2)}) collective-permute-start(bf16[512,2048]{1,0:T(8,128)(2,1)} %copy-done.70), channel_id=1, source_target_pairs={{0,2},{1,3},{2,0},{3,1},{4,6},{5,7},{6,4},{7,5},{8,10},{9,11},{10,... | collective-permute-start | bytes 6291464 | tf_op jit(solution)/shard_map/up_x/ppermute | solution.py:575
  265.5 25.0 %collective-permute-start.28 = (bf16[512,1024]{1,0:T(8,128)(2,1)}, bf16[512,1024]{1,0:T(8,128)(2,1)S(1)}, u32[]{:S(2)}, u32[]{:S(2)}) collective-permute-start(bf16[512,1024]{1,0:T(8,128)(2,1)} %bitcast.33), channel_id=1, source_target_pairs={{0,8},{4,12},{8,0},{12,4},{16,24},{20,28},{24,16},{28,20},{1,9},{5... | collective-permute-start | bytes 3145736 | tf_op jit(solution)/shard_map/down_z1/ppermute | solution.py:575
  276.1 19.7 %collective-permute-start.22 = (bf16[768,1024]{1,0:T(8,128)(2,1)S(1)}, bf16[768,1024]{1,0:T(8,128)(2,1)S(1)}, u32[]{:S(2)}, u32[]{:S(2)}) collective-permute-start(bf16[768,1024]{1,0:T(8,128)(2,1)S(1)} %get-tuple-element.113.mine_ref), channel_id=1, source_target_pairs={{0,1},{1,0},{2,3},{3,2},{4,5},{5,4},{6,7},{7,6},{8,9},{9,8},{10,11... | collective-permute-start | bytes 4718600 | tf_op jit(solution)/shard_map/core/ppermute | solution.py:697
  278.7 19.1 %collective-permute-start.26 = (bf16[768,1024]{1,0:T(8,128)(2,1)S(1)}, bf16[768,1024]{1,0:T(8,128)(2,1)S(1)}, u32[]{:S(2)}, u32[]{:S(2)}) collective-permute-start(bf16[768,1024]{1,0:T(8,128)(2,1)S(1)} %get-tuple-element.122.refs_2_.refs_0_), channel_id=1, source_target_pairs={{0,1},{1,0},{2,3},{3,2},{4,5},{5,4},{6,7},{7,6},{8,9},{9,8},{10,11... | collective-permute-start | bytes 4718600 | tf_op jit(solution)/shard_map/core/ppermute | solution.py:697
  291.1 24.6 %collective-permute-start.29 = (bf16[256,1024]{1,0:T(8,128)(2,1)S(1)}, bf16[256,1024]{1,0:T(8,128)(2,1)S(1)}, u32[]{:S(2)}, u32[]{:S(2)}) collective-permute-start(bf16[256,1024]{1,0:T(8,128)(2,1)S(1)} %bitcast.207), channel_id=1, source_target_pairs={{0,16},{4,20},{8,24},{12,28},{16,0},{20,4},{24,8},{28,12},{1,17},{... | collective-permute-start | bytes 1572872 | tf_op jit(solution)/shard_map/down_z2/ppermute | solution.py:575
  294.0 24.9 %collective-permute-start.31 = (bf16[256,2048]{1,0:T(8,128)(2,1)S(1)}, bf16[256,2048]{1,0:T(8,128)(2,1)S(1)}, u32[]{:S(2)}, u32[]{:S(2)}) collective-permute-start(bf16[256,2048]{1,0:T(8,128)(2,1)S(1)} %fusion.6), channel_id=1, source_target_pairs={{0,4},{4,0},{8,12},{12,8},{16,20},{20,16},{24,28},{28,24},{1,5},{5... | collective-permute-start | bytes 3145736 | tf_op jit(solution)/shard_map/up_y/ppermute | solution.py:575
  297.3 43.9 %collective-permute-start.23 = (bf16[4,128,1024]{2,1,0:T(8,128)(2,1)S(1)}, bf16[4,128,1024]{2,1,0:T(8,128)(2,1)S(1)}, u32[]{:S(2)}, u32[]{:S(2)}) collective-permute-start(bf16[4,128,1024]{2,1,0:T(8,128)(2,1)S(1)} %get-tuple-element.115), channel_id=1, source_target_pairs={{0,2},{1,3},{2,0},{3,1},{4,6},{5,7},{6,4},{7,5},{8,10},{9,11},{10,... | collective-permute-start | bytes 3145736 | tf_op jit(solution)/shard_map/x_activations/ppermute | solution.py:693
  315.9 10.5 %collective-permute-start.30 = (bf16[128,1024]{1,0:T(8,128)(2,1)S(1)}, bf16[128,1024]{1,0:T(8,128)(2,1)S(1)}, u32[]{:S(2)}, u32[]{:S(2)}) collective-permute-start(bf16[128,1024]{1,0:T(8,128)(2,1)S(1)} %fusion.17), channel_id=1, source_target_pairs={{0,2},{1,3},{2,0},{3,1},{4,6},{5,7},{6,4},{7,5},{8,10},{9,11},{10,... | collective-permute-start | bytes 786440 | tf_op jit(solution)/shard_map/down_x/ppermute | solution.py:575
  319.4 22.4 %collective-permute-start.32 = (bf16[128,2048]{1,0:T(8,128)(2,1)S(1)}, bf16[128,2048]{1,0:T(8,128)(2,1)S(1)}, u32[]{:S(2)}, u32[]{:S(2)}) collective-permute-start(bf16[128,2048]{1,0:T(8,128)(2,1)S(1)} %fusion.9), channel_id=1, source_target_pairs={{0,8},{4,12},{8,0},{12,4},{16,24},{20,28},{24,16},{28,20},{1,9},{5... | collective-permute-start | bytes 1572872 | tf_op jit(solution)/shard_map/up_z1/ppermute | solution.py:575
  326.4 14.7 %collective-permute-start.33 = (bf16[128,1024]{1,0:T(8,128)(2,1)S(1)}, bf16[128,1024]{1,0:T(8,128)(2,1)S(1)}, u32[]{:S(2)}, u32[]{:S(2)}) collective-permute-start(bf16[128,1024]{1,0:T(8,128)(2,1)S(1)} %fusion.16.mine_ref), channel_id=1, source_target_pairs={{0,16},{4,20},{8,24},{12,28},{16,0},{20,4},{24,8},{28,12},{1,17},{... | collective-permute-start | bytes 786440 | tf_op jit(solution)/shard_map/down_back_z2/ppermute | solution.py:575
  348.4 21.6 %collective-permute-start.37 = (bf16[768,1024]{1,0:T(8,128)(2,1)}, bf16[768,1024]{1,0:T(8,128)(2,1)}, u32[]{:S(2)}, u32[]{:S(2)}) collective-permute-start(bf16[768,1024]{1,0:T(8,128)(2,1)} %rows_product.23), channel_id=1, source_target_pairs={{0,1},{1,0},{2,3},{3,2},{4,5},{5,4},{6,7},{7,6},{8,9},{9,8},{10,11... | collective-permute-start | bytes 4718600 | tf_op jit(solution)/shard_map/core/ppermute | solution.py:697
  348.5 31.6 %collective-permute-start.36 = (bf16[512,1280]{1,0:T(8,128)(2,1)}, bf16[512,1280]{1,0:T(8,128)(2,1)}, u32[]{:S(2)}, u32[]{:S(2)}) collective-permute-start(bf16[512,1280]{1,0:T(8,128)(2,1)} %maximum_maximum_fusion.1), channel_id=1, source_target_pairs={{0,2},{1,3},{2,0},{3,1},{4,6},{5,7},{6,4},{7,5},{8,10},{9,11},{10,... | collective-permute-start | bytes 3932168 | tf_op jit(solution)/shard_map/first_x/ppermute | solution.py:575
  362.4 22.5 %collective-permute-start.34 = (bf16[64,2048]{1,0:T(8,128)(2,1)S(1)}, bf16[64,2048]{1,0:T(8,128)(2,1)S(1)}, u32[]{:S(2)}, u32[]{:S(2)}) collective-permute-start(bf16[64,2048]{1,0:T(8,128)(2,1)S(1)} %fusion.15), channel_id=1, source_target_pairs={{0,16},{4,20},{8,24},{12,28},{16,0},{20,4},{24,8},{28,12},{1,17},{... | collective-permute-start | bytes 786440 | tf_op jit(solution)/shard_map/up_z2/ppermute | solution.py:575
  362.8 20.6 %collective-permute-start.35 = (bf16[256,1024]{1,0:T(8,128)(2,1)S(1)}, bf16[256,1024]{1,0:T(8,128)(2,1)S(1)}, u32[]{:S(2)}, u32[]{:S(2)}) collective-permute-start(bf16[256,1024]{1,0:T(8,128)(2,1)S(1)} %copy-done.67), channel_id=1, source_target_pairs={{0,8},{4,12},{8,0},{12,4},{16,24},{20,28},{24,16},{28,20},{1,9},{5... | collective-permute-start | bytes 1572872 | tf_op jit(solution)/shard_map/down_back_z1/ppermute | solution.py:575
  373.6 15.6 %collective-permute-start.39 = (bf16[768,1024]{1,0:T(8,128)(2,1)}, bf16[768,1024]{1,0:T(8,128)(2,1)}, u32[]{:S(2)}, u32[]{:S(2)}) collective-permute-start(bf16[768,1024]{1,0:T(8,128)(2,1)} %add_convert_fusion.mine_ref), channel_id=1, source_target_pairs={{0,1},{1,0},{2,3},{3,2},{4,5},{5,4},{6,7},{7,6},{8,9},{9,8},{10,11... | collective-permute-start | bytes 4718600 | tf_op jit(solution)/shard_map/core/ppermute | solution.py:697
  385.0 14.9 %collective-permute-start.38 = (bf16[64,2048]{1,0:T(8,128)(2,1)S(1)}, bf16[64,2048]{1,0:T(8,128)(2,1)}, u32[]{:S(2)}, u32[]{:S(2)}) collective-permute-start(bf16[64,2048]{1,0:T(8,128)(2,1)S(1)} %fusion.11.mine_ref), channel_id=1, source_target_pairs={{0,16},{4,20},{8,24},{12,28},{16,0},{20,4},{24,8},{28,12},{1,17},{... | collective-permute-start | bytes 786440 | tf_op jit(solution)/shard_map/up_back_z2/ppermute | solution.py:575
  387.2 43.2 %collective-permute-start.43 = (bf16[512,1024]{1,0:T(8,128)(2,1)}, bf16[512,1024]{1,0:T(8,128)(2,1)}, u32[]{:S(2)}, u32[]{:S(2)}) collective-permute-start(bf16[512,1024]{1,0:T(8,128)(2,1)} %copy-done.55), channel_id=1, source_target_pairs={{0,4},{4,0},{8,12},{12,8},{16,20},{20,16},{24,28},{28,24},{1,5},{5... | collective-permute-start | bytes 3145736 | tf_op jit(solution)/shard_map/down_back_y/ppermute | solution.py:575
  387.2 38.8 %collective-permute-start.44 = (bf16[256,1280]{1,0:T(8,128)(2,1)}, bf16[256,1280]{1,0:T(8,128)(2,1)}, u32[]{:S(2)}, u32[]{:S(2)}) collective-permute-start(bf16[256,1280]{1,0:T(8,128)(2,1)} %fusion.8), channel_id=1, source_target_pairs={{0,4},{4,0},{8,12},{12,8},{16,20},{20,16},{24,28},{28,24},{1,5},{5... | collective-permute-start | bytes 1966088 | tf_op jit(solution)/shard_map/first_y/ppermute | solution.py:575
  406.0 27.9 %collective-permute-start.42 = (bf16[4,128,1024]{2,1,0:T(8,128)(2,1)}, bf16[4,128,1024]{2,1,0:T(8,128)(2,1)}, u32[]{:S(2)}, u32[]{:S(2)}) collective-permute-start(bf16[4,128,1024]{2,1,0:T(8,128)(2,1)} %get-tuple-element.138), channel_id=1, source_target_pairs={{0,2},{1,3},{2,0},{3,1},{4,6},{5,7},{6,4},{7,5},{8,10},{9,11},{10,... | collective-permute-start | bytes 3145736 | tf_op jit(solution)/shard_map/x_grad/ppermute | solution.py:693
  406.6 46.8 %collective-permute-start.47 = (bf16[128,2048]{1,0:T(8,128)(2,1)}, bf16[128,2048]{1,0:T(8,128)(2,1)}, u32[]{:S(2)}, u32[]{:S(2)}) collective-permute-start(bf16[128,2048]{1,0:T(8,128)(2,1)} %stack_rows.15.mine_ref), channel_id=1, source_target_pairs={{0,8},{4,12},{8,0},{12,4},{16,24},{20,28},{24,16},{28,20},{1,9},{5... | collective-permute-start | bytes 1572872 | tf_op jit(solution)/shard_map/up_back_z1/ppermute | solution.py:575
  406.9 7.5 %collective-permute-start.40 = (bf16[2,3072]{1,0:T(2,128)(2,1)S(1)}, bf16[2,3072]{1,0:T(2,128)(2,1)S(1)}, u32[]{:S(2)}, u32[]{:S(2)}) collective-permute-start(bf16[2,3072]{1,0:T(2,128)(2,1)S(1)} %pad_maximum_fusion.5), channel_id=1, source_target_pairs={{0,1},{1,0},{2,3},{3,2},{4,5},{5,4},{6,7},{7,6},{8,9},{9,8},{10,11... | collective-permute-start | bytes 36872 | tf_op jit(solution)/shard_map/core/ppermute | solution.py:697
  416.8 34.2 %collective-permute-start.41 = (bf16[512,896]{1,0:T(8,128)(2,1)}, bf16[512,896]{1,0:T(8,128)(2,1)}, u32[]{:S(2)}, u32[]{:S(2)}) collective-permute-start(bf16[512,896]{1,0:T(8,128)(2,1)} %fusion.7), channel_id=1, source_target_pairs={{0,2},{1,3},{2,0},{3,1},{4,6},{5,7},{6,4},{7,5},{8,10},{9,11},{10,... | collective-permute-start | bytes 2752520 | tf_op jit(solution)/shard_map/last_x/ppermute | solution.py:575
  428.8 27.3 %collective-permute-start.46 = (bf16[128,1280]{1,0:T(8,128)(2,1)S(1)}, bf16[128,1280]{1,0:T(8,128)(2,1)S(1)}, u32[]{:S(2)}, u32[]{:S(2)}) collective-permute-start(bf16[128,1280]{1,0:T(8,128)(2,1)S(1)} %fusion.13), channel_id=1, source_target_pairs={{0,8},{4,12},{8,0},{12,4},{16,24},{20,28},{24,16},{28,20},{1,9},{5... | collective-permute-start | bytes 983048 | tf_op jit(solution)/shard_map/first_z1/ppermute | solution.py:575
  451.0 12.1 %collective-permute-start.48 = (bf16[128,1024]{1,0:T(8,128)(2,1)S(1)}, bf16[128,1024]{1,0:T(8,128)(2,1)S(1)}, u32[]{:S(2)}, u32[]{:S(2)}) collective-permute-start(bf16[128,1024]{1,0:T(8,128)(2,1)S(1)} %get-tuple-element.147), channel_id=1, source_target_pairs={{0,4},{4,8},{8,12},{12,16},{16,20},{20,24},{24,28},{28,0},{1,5},{5... | collective-permute-start | bytes 786440 | tf_op jit(solution)/shard_map/return/ppermute | solution.py:575
  452.6 19.6 %collective-permute-start.45 = (bf16[256,896]{1,0:T(8,128)(2,1)S(1)}, bf16[256,896]{1,0:T(8,128)(2,1)S(1)}, u32[]{:S(2)}, u32[]{:S(2)}) collective-permute-start(bf16[256,896]{1,0:T(8,128)(2,1)S(1)} %fusion.12), channel_id=1, source_target_pairs={{0,4},{4,0},{8,12},{12,8},{16,20},{20,16},{24,28},{28,24},{1,5},{5... | collective-permute-start | bytes 1376264 | tf_op jit(solution)/shard_map/last_y/ppermute | solution.py:575
  454.7 11.9 %collective-permute-start.49 = (bf16[128,1024]{1,0:T(8,128)(2,1)S(1)}, bf16[128,1024]{1,0:T(8,128)(2,1)S(1)}, u32[]{:S(2)}, u32[]{:S(2)}) collective-permute-start(bf16[128,1024]{1,0:T(8,128)(2,1)S(1)} %get-tuple-element.149), channel_id=1, source_target_pairs={{0,8},{4,12},{8,16},{12,20},{16,24},{20,28},{24,0},{28,4},{1,9},{5... | collective-permute-start | bytes 786440 | tf_op jit(solution)/shard_map/return/ppermute | solution.py:575
  455.5 46.3 %collective-permute-start.58 = (bf16[256,2048]{1,0:T(8,128)(2,1)S(1)}, bf16[256,2048]{1,0:T(8,128)(2,1)}, u32[]{:S(2)}, u32[]{:S(2)}) collective-permute-start(bf16[256,2048]{1,0:T(8,128)(2,1)S(1)} %stack_rows.17), channel_id=1, source_target_pairs={{0,4},{4,0},{8,12},{12,8},{16,20},{20,16},{24,28},{28,24},{1,5},{5... | collective-permute-start | bytes 3145736 | tf_op jit(solution)/shard_map/up_back_y/ppermute | solution.py:575
  463.2 15.8 %collective-permute-start.51 = (bf16[64,1280]{1,0:T(8,128)(2,1)S(1)}, bf16[64,1280]{1,0:T(8,128)(2,1)S(1)}, u32[]{:S(2)}, u32[]{:S(2)}) collective-permute-start(bf16[64,1280]{1,0:T(8,128)(2,1)S(1)} %fusion.20), channel_id=1, source_target_pairs={{0,16},{4,20},{8,24},{12,28},{16,0},{20,4},{24,8},{28,12},{1,17},{... | collective-permute-start | bytes 491528 | tf_op jit(solution)/shard_map/first_z2/ppermute | solution.py:575
  463.3 32.2 %collective-permute-start.52 = (bf16[128,1024]{1,0:T(8,128)(2,1)S(1)}, bf16[128,1024]{1,0:T(8,128)(2,1)S(1)}, u32[]{:S(2)}, u32[]{:S(2)}) collective-permute-start(bf16[128,1024]{1,0:T(8,128)(2,1)S(1)} %get-tuple-element.152), channel_id=1, source_target_pairs={{0,12},{4,16},{8,20},{12,24},{16,28},{20,0},{24,4},{28,8},{1,13},{... | collective-permute-start | bytes 786440 | tf_op jit(solution)/shard_map/return/ppermute | solution.py:575
  472.4 23.1 %collective-permute-start.50 = (bf16[128,896]{1,0:T(8,128)(2,1)S(1)}, bf16[128,896]{1,0:T(8,128)(2,1)S(1)}, u32[]{:S(2)}, u32[]{:S(2)}) collective-permute-start(bf16[128,896]{1,0:T(8,128)(2,1)S(1)} %fusion.18), channel_id=1, source_target_pairs={{0,8},{4,12},{8,0},{12,4},{16,24},{20,28},{24,16},{28,20},{1,9},{5... | collective-permute-start | bytes 688136 | tf_op jit(solution)/shard_map/last_z1/ppermute | solution.py:575
  479.1 16.6 %collective-permute-start.54 = (bf16[64,1280]{1,0:T(8,128)(2,1)S(1)}, bf16[64,1280]{1,0:T(8,128)(2,1)S(1)}, u32[]{:S(2)}, u32[]{:S(2)}) collective-permute-start(bf16[64,1280]{1,0:T(8,128)(2,1)S(1)} %fusion.14.mine_ref), channel_id=1, source_target_pairs={{0,16},{4,20},{8,24},{12,28},{16,0},{20,4},{24,8},{28,12},{1,17},{... | collective-permute-start | bytes 491528 | tf_op jit(solution)/shard_map/first_back_z2/ppermute | solution.py:575
  479.2 21.3 %collective-permute-start.55 = (bf16[128,1024]{1,0:T(8,128)(2,1)S(1)}, bf16[128,1024]{1,0:T(8,128)(2,1)S(1)}, u32[]{:S(2)}, u32[]{:S(2)}) collective-permute-start(bf16[128,1024]{1,0:T(8,128)(2,1)S(1)} %get-tuple-element.155), channel_id=1, source_target_pairs={{0,16},{4,20},{8,24},{12,28},{16,0},{20,4},{24,8},{28,12},{1,17},{... | collective-permute-start | bytes 786440 | tf_op jit(solution)/shard_map/return/ppermute | solution.py:575
  495.6 6.2 %collective-permute-start.53 = (bf16[64,896]{1,0:T(8,128)(2,1)S(1)}, bf16[64,896]{1,0:T(8,128)(2,1)S(1)}, u32[]{:S(2)}, u32[]{:S(2)}) collective-permute-start(bf16[64,896]{1,0:T(8,128)(2,1)S(1)} %fusion.21), channel_id=1, source_target_pairs={{0,16},{4,20},{8,24},{12,28},{16,0},{20,4},{24,8},{28,12},{1,17},{... | collective-permute-start | bytes 344072 | tf_op jit(solution)/shard_map/last_z2/ppermute | solution.py:575
  496.8 15.3 %collective-permute-start.57 = (bf16[128,1280]{1,0:T(8,128)(2,1)S(1)}, bf16[128,1280]{1,0:T(8,128)(2,1)S(1)}, u32[]{:S(2)}, u32[]{:S(2)}) collective-permute-start(bf16[128,1280]{1,0:T(8,128)(2,1)S(1)} %stack_rows.18.mine_ref), channel_id=1, source_target_pairs={{0,8},{4,12},{8,0},{12,4},{16,24},{20,28},{24,16},{28,20},{1,9},{5... | collective-permute-start | bytes 983048 | tf_op jit(solution)/shard_map/first_back_z1/ppermute | solution.py:575
  496.9 28.2 %collective-permute-start.59 = (bf16[128,1024]{1,0:T(8,128)(2,1)}, bf16[128,1024]{1,0:T(8,128)(2,1)}, u32[]{:S(2)}, u32[]{:S(2)}) collective-permute-start(bf16[128,1024]{1,0:T(8,128)(2,1)} %get-tuple-element.159), channel_id=1, source_target_pairs={{0,20},{4,24},{8,28},{12,0},{16,4},{20,8},{24,12},{28,16},{1,21},{... | collective-permute-start | bytes 786440 | tf_op jit(solution)/shard_map/return/ppermute | solution.py:575
  512.7 32.2 %collective-permute-start.63 = (bf16[256,1280]{1,0:T(8,128)(2,1)S(1)}, bf16[256,1280]{1,0:T(8,128)(2,1)}, u32[]{:S(2)}, u32[]{:S(2)}) collective-permute-start(bf16[256,1280]{1,0:T(8,128)(2,1)S(1)} %stack_rows.19), channel_id=1, source_target_pairs={{0,4},{4,0},{8,12},{12,8},{16,20},{20,16},{24,28},{28,24},{1,5},{5... | collective-permute-start | bytes 1966088 | tf_op jit(solution)/shard_map/first_back_y/ppermute | solution.py:575
  516.5 8.6 %collective-permute-start.56 = (bf16[64,896]{1,0:T(8,128)(2,1)S(1)}, bf16[64,896]{1,0:T(8,128)(2,1)S(1)}, u32[]{:S(2)}, u32[]{:S(2)}) collective-permute-start(bf16[64,896]{1,0:T(8,128)(2,1)S(1)} %fusion.19.mine_ref), channel_id=1, source_target_pairs={{0,16},{4,20},{8,24},{12,28},{16,0},{20,4},{24,8},{28,12},{1,17},{... | collective-permute-start | bytes 344072 | tf_op jit(solution)/shard_map/last_back_z2/ppermute | solution.py:575
  519.1 16.6 %collective-permute-start.61 = (bf16[128,1024]{1,0:T(8,128)(2,1)}, bf16[128,1024]{1,0:T(8,128)(2,1)}, u32[]{:S(2)}, u32[]{:S(2)}) collective-permute-start(bf16[128,1024]{1,0:T(8,128)(2,1)} %get-tuple-element.161), channel_id=1, source_target_pairs={{0,24},{4,28},{8,0},{12,4},{16,8},{20,12},{24,16},{28,20},{1,25},{... | collective-permute-start | bytes 786440 | tf_op jit(solution)/shard_map/return/ppermute | solution.py:575
  525.7 12.3 %collective-permute-start.60 = (bf16[128,896]{1,0:T(8,128)(2,1)S(1)}, bf16[128,896]{1,0:T(8,128)(2,1)S(1)}, u32[]{:S(2)}, u32[]{:S(2)}) collective-permute-start(bf16[128,896]{1,0:T(8,128)(2,1)S(1)} %stack_rows.20.mine_ref), channel_id=1, source_target_pairs={{0,8},{4,12},{8,0},{12,4},{16,24},{20,28},{24,16},{28,20},{1,9},{5... | collective-permute-start | bytes 688136 | tf_op jit(solution)/shard_map/last_back_z1/ppermute | solution.py:575
  531.6 10.8 %collective-permute-start.62 = (bf16[128,1024]{1,0:T(8,128)(2,1)}, bf16[128,1024]{1,0:T(8,128)(2,1)S(1)}, u32[]{:S(2)}, u32[]{:S(2)}) collective-permute-start(bf16[128,1024]{1,0:T(8,128)(2,1)} %get-tuple-element.164), channel_id=1, source_target_pairs={{0,28},{4,0},{8,4},{12,8},{16,12},{20,16},{24,20},{28,24},{1,29},{... | collective-permute-start | bytes 786440 | tf_op jit(solution)/shard_map/return/ppermute | solution.py:575
  535.6 18.7 %collective-permute-start.67 = (bf16[256,2048]{1,0:T(8,128)(2,1)}, bf16[256,2048]{1,0:T(8,128)(2,1)S(1)}, u32[]{:S(2)}, u32[]{:S(2)}) collective-permute-start(bf16[256,2048]{1,0:T(8,128)(2,1)} %get-tuple-element.209), channel_id=1, source_target_pairs={{0,1},{1,0},{2,3},{3,2},{4,5},{5,4},{6,7},{7,6},{8,9},{9,8},{10,11... | collective-permute-start | bytes 3145736 | tf_op jit(solution)/shard_map/core/ppermute | solution.py:697
  538.6 13.2 %collective-permute-start.65 = (bf16[256,896]{1,0:T(8,128)(2,1)S(1)}, bf16[256,896]{1,0:T(8,128)(2,1)S(1)}, u32[]{:S(2)}, u32[]{:S(2)}) collective-permute-start(bf16[256,896]{1,0:T(8,128)(2,1)S(1)} %stack_rows.21), channel_id=1, source_target_pairs={{0,4},{4,0},{8,12},{12,8},{16,20},{20,16},{24,28},{28,24},{1,5},{5... | collective-permute-start | bytes 1376264 | tf_op jit(solution)/shard_map/last_back_y/ppermute | solution.py:575
  546.7 10.4 %collective-permute-start.64 = (bf16[256,768]{1,0:T(8,128)(2,1)}, bf16[256,768]{1,0:T(8,128)(2,1)}, u32[]{:S(2)}, u32[]{:S(2)}) collective-permute-start(bf16[256,768]{1,0:T(8,128)(2,1)} %get-tuple-element.229), channel_id=1, source_target_pairs={{0,1},{1,0},{2,3},{3,2},{4,5},{5,4},{6,7},{7,6},{8,9},{9,8},{10,11... | collective-permute-start | bytes 1179656 | tf_op jit(solution)/shard_map/core/ppermute | solution.py:697
  (121 other events, 931.0 us)
